TPU v7x, 32 devices: a whole 2x2x4 slice. The times are simulated.
32 devices in a mesh: grp: 2 (over y), clu: 4 (over z), sub: 2 (over x), rep: 2 (over core).
Axes of the slice: x: 2, y: 2, z: 4, core: 2. Of those that a mesh axis runs over, the one named last changes fastest.
Arguments:
- charges: float32 [1024, 256], P(('grp', 'clu'), 'sub'), parts along dimension 0, may hold values from -0.6 to 0.6
- panel_mask: int32 [1024, 256], P(('grp', 'clu'), 'sub'), parts along dimension 0, may hold values from 0 to 1, as said below
- geometry: float32 [1024, 4, 256], P(('grp', 'clu')), parts along dimension 0
- remote_source: int32 [8, 4, 32], P(('grp', 'clu'), None, 'rep'), parts along dimension 0, may hold values from 0 to 127
- remote_target: int32 [8, 4, 32], P(('grp', 'clu'), None, 'rep'), parts along dimension 0, may hold values from 0 to 127
- remote_live: int32 [8, 4, 32], P(('grp', 'clu'), None, 'rep'), parts along dimension 0, may hold values from 0 to 1, as said below
- local_pairs: int32 [8, 256, 2], P(('grp', 'clu'), 'rep'), parts along dimension 0, may hold values from 0 to 127, as said below
- basis: float32 [1024, 256, 32], P(('grp', 'clu'), 'sub'), parts along dimension 0, may hold values from -0.9 to 0.9
- transfer: float32 [1024, 32, 32], P(('grp', 'clu')), parts along dimension 0, may hold values from -1 to 1
- parent_of: int32 [1024], P(('grp', 'clu')), parts along dimension 0, may hold values from 0 to 15, as said below
- far_list: int32 [128, 8], P(('grp', 'clu')), parts along dimension 0, may hold values from 0 to 63
- coupling: float32 [128, 8, 32, 32], P(('grp', 'clu')), parts along dimension 0, may hold values from -0.375 to 0.375
Outputs:
- potential: float32 [1024, 256], P(('grp', 'clu'), 'sub'), parts along dimension 0
There are 2 independent parts, one for each index of `grp`. A program takes and returns all parts, laid end to end along the dimension named above; each array names one. Nothing has to cross between parts.
Inputs may be any that keep to these rules, and one draw needn't show every extreme that they name: `panel_mask`: within each cluster the real panels come first, and at least 128 are real. `remote_live`: live slots come first in each slot list [c, d]; the list [c, c] is empty; the lists between clu neighbours at cycle distance 1 are full (32 live). `local_pairs`: the two clusters of a local pair differ. `parent_of`: each of the 16 parents of a clu device has exactly 8 children on that device.
All inputs are finite; a program needn't handle non-finite values.
Results may differ from a plain program's by a relative error of at most 0.000064.
Values sent between devices are 32-bit elements; how exact they have to be, the bound alone decides.
No kernel may reach another device: no remote copies, remote signals or barrier semaphores. Data moves between devices by JAX's collectives and lax.ppermute only.
A program may use at most 64 MiB of HBM per device.

v0:
```python
import math

import jax
import jax.numpy as jnp
from jax import lax
from jax.sharding import PartitionSpec as P


def kernel_tile(rows_geo, cols_geo):
    delta = rows_geo[:, :3, :, None] - cols_geo[:, :3, None, :]
    dist_sq = jnp.sum(delta * delta, axis=1)
    radius_sq = (
        rows_geo[:, 3, :, None] * rows_geo[:, 3, :, None]
        + cols_geo[:, 3, None, :] * cols_geo[:, 3, None, :]
    )
    return lax.rsqrt(dist_sq + radius_sq)


def pair_apply(rows_geo, rows_q, cols_geo, cols_q):
    total = rows_geo.shape[0]
    step_len = math.gcd(total, 32)

    def single(args):
        row_g, row_q, col_g, col_q = args
        tile = kernel_tile(row_g, col_g)
        return (
            jnp.sum(tile * col_q[:, None, :], axis=2),
            jnp.sum(tile * row_q[:, :, None], axis=1),
        )

    shaped = tuple(
        (
            x.reshape((total // step_len, step_len) + x.shape[1:])
            for x in (rows_geo, rows_q, cols_geo, cols_q)
        )
    )
    forward, backward = lax.map(single, shaped)
    return (forward.reshape(total, -1), backward.reshape(total, -1))


def on_device(
    charges,
    panel_mask,
    geometry,
    remote_source,
    remote_target,
    remote_live,
    local_pairs,
    basis,
    transfer,
    parent_of,
    far_list,
    coupling,
):
    highest = lax.Precision.HIGHEST
    cl_local, slice_len = charges.shape
    panels = geometry.shape[2]
    sub_index = lax.axis_index("sub")
    rep_index = lax.axis_index("rep")
    rep_count = lax.axis_size("rep")
    owners = lax.axis_size("clu")
    maskf = panel_mask.astype(jnp.float32)
    masked = charges * maskf
    full_q = lax.all_gather(masked, "sub", axis=1, tiled=True)
    geo_slice = lax.dynamic_slice_in_dim(geometry, sub_index * slice_len, slice_len, 2)
    rows_acc = jnp.zeros((cl_local, panels), jnp.float32)
    cols_acc = jnp.zeros((cl_local, slice_len), jnp.float32)
    self_count = cl_local // rep_count
    self_idx = rep_index * self_count + jnp.arange(self_count, dtype=jnp.int32)
    self_fwd, unused_back = pair_apply(
        geometry[self_idx], full_q[self_idx], geo_slice[self_idx], masked[self_idx]
    )
    rows_acc = rows_acc.at[self_idx].add(self_fwd)
    local_a = local_pairs[0, :, 0]
    local_b = local_pairs[0, :, 1]
    local_fwd, local_back = pair_apply(
        geometry[local_a], full_q[local_a], geo_slice[local_b], masked[local_b]
    )
    rows_acc = rows_acc.at[local_a].add(local_fwd)
    cols_acc = cols_acc.at[local_b].add(local_back)
    source_rows = remote_source[0]
    target_rows = remote_target[0]
    live_rows = remote_live[0]
    slot_count = source_rows.shape[1]
    target_flat = target_rows.reshape(-1)
    live_flat = live_rows.reshape(-1).astype(jnp.float32)
    ask_ints = jnp.stack([source_rows, live_rows], axis=1)
    target_pack = jnp.concatenate([geometry[target_flat], full_q[target_flat][:, None, :]], axis=1)
    target_pack = target_pack.reshape(owners, slot_count * 5 * panels)
    got_ints, got_targets = (
        lax.all_to_all(ask_ints, "clu", split_axis=0, concat_axis=0, tiled=True),
        lax.all_to_all(target_pack, "clu", split_axis=0, concat_axis=0, tiled=True),
    )
    asked_flat = got_ints[:, 0].reshape(-1)
    asked_live = got_ints[:, 1].reshape(-1).astype(jnp.float32)
    target_data = got_targets.reshape(-1, 5, panels)
    owner_fwd, owner_back = pair_apply(
        geo_slice[asked_flat], masked[asked_flat], target_data[:, :4], target_data[:, 4]
    )
    cols_acc = cols_acc.at[asked_flat].add(owner_fwd * asked_live[:, None])
    source_pack = jnp.concatenate([geo_slice[asked_flat], masked[asked_flat][:, None, :]], axis=1)
    source_pack = source_pack.reshape(owners, slot_count * 5 * slice_len)
    arrived = lax.all_to_all(source_pack, "clu", split_axis=0, concat_axis=0, tiled=True).reshape(
        -1, 5, slice_len
    )
    remote_fwd, remote_back = pair_apply(
        geometry[target_flat], full_q[target_flat], arrived[:, :4], arrived[:, 4]
    )
    rows_acc = rows_acc.at[target_flat].add(remote_fwd * live_flat[:, None])
    near_rows = lax.psum_scatter(rows_acc, "sub", scatter_dimension=1, tiled=True)
    near = lax.psum(near_rows + cols_acc, "rep")
    leaf_part = jnp.einsum("cpr,cp->cr", basis, masked, precision=highest)
    leaf = lax.psum(leaf_part, "sub")
    lifted = jnp.einsum("crs,cr->cs", transfer, leaf, precision=highest)
    par_local = far_list.shape[0]
    onehot = (parent_of[None, :] == jnp.arange(par_local, dtype=jnp.int32)[:, None]).astype(
        jnp.float32
    )
    parent_coeff = jnp.dot(onehot, lifted, precision=highest, preferred_element_type=jnp.float32)
    all_parents = lax.all_gather(parent_coeff, "clu", axis=0, tiled=True)
    field = jnp.einsum("pkrs,pks->pr", coupling, all_parents[far_list], precision=highest)
    down_field = jnp.dot(onehot.T, field, precision=highest, preferred_element_type=jnp.float32)
    leaf_field = jnp.einsum("crs,cs->cr", transfer, down_field, precision=highest)
    far = jnp.einsum("cpr,cr->cp", basis, leaf_field, precision=highest)
    return maskf * (near + far)


def solution(mesh):
    placed = (
        P(("grp", "clu"), "sub"),
        P(("grp", "clu"), "sub"),
        P(("grp", "clu"), None, None),
        P(("grp", "clu"), None, "rep"),
        P(("grp", "clu"), None, "rep"),
        P(("grp", "clu"), None, "rep"),
        P(("grp", "clu"), "rep", None),
        P(("grp", "clu"), "sub", None),
        P(("grp", "clu"), None, None),
        P(("grp", "clu")),
        P(("grp", "clu"), None),
        P(("grp", "clu"), None, None, None),
    )
    return jax.shard_map(
        on_device, mesh=mesh, in_specs=placed, out_specs=P(("grp", "clu"), "sub"), check_vma=False
    )
```

profile of v0, /device:TPU:0, one launch (start us, length us, event | category | flops | bytes accessed | tf_op | source)
XLA Modules:
  0.0 211.7 jit_solution(2548999337480439340)
XLA Ops:
  8.0 6.3 %all-to-all-start = ((s32[4,2,16]{2,1,0:T(2,128)}), s32[4,2,16]{2,1,0:T(2,128)S(1)}, u32[]{:S(2)}, u32[]{:S(2)}) async-start(s32[4,2,16]{2,1,0:T(2,128)} %copy.82), calls=%async_computation | async-start | bytes 8192 | tf_op jit(solution)/shard_map/all_to_all | solution.py:91
  15.9 4.9 %all_gather.6 = f32[128,256]{1,0:T(8,128)S(1)} all-gather(f32[128,128]{1,0:T(8,128)S(1)} %convert_multiply_fusion), channel_id=1, replica_groups=mesh['grp'=2,'clu'=4,'sub'=2,'rep'=2] {'sub'}, dimensions={1}, use_global_device_ids=true | all-gather | bytes 196608 | tf_op jit(solution)/shard_map/all_gather | solution.py:64
  20.9 1.2 gather_fusion.5
  23.1 1.4 gather_fusion.4
  25.8 1.8 gather_fusion
  27.6 1.9 gather_fusion.3
  29.5 1.4 gather_fusion.6
  30.9 46.4 %while.43 = (s32[]{:T(128)}, f32[4,32,256]{2,1,0:T(8,128)}, f32[4,32,128]{2,1,0:T(8,128)}, f32[4,32,4,256]{3,2,1,0:T(4,128)S(1)}, f32[4,32,4,128]{3,2,1,0:T(4,12...) while((s32[]{:T(128)}, f32[4,32,256]{2,1,0:T(8,128)}, f32[4,32,128]{2,1,0:T(8,128)}, ...), condition=%wide.region_9.10_spmd, body=%wide.region_5.9_spmd.sunk | while | flops 14680066 | bytes 10355813 | solution.py:37
  32.0 4.1 %multiply_reduce_fusion.20 = f32[32,256,128]{2,1,0:T(8,128)S(1)} fusion(f32[32,3,128]{2,1,0:T(4,128)S(1)} %copy.167, f32[32,3,256]{2,1,0:T(4,128)S(1)} %copy.169), kind=kLoop, calls=%fused_computation.29.clone.1 | loop fusion | flops 8388608 | bytes 4341760 | tf_op jit(solution)/shard_map/while/body/eval_jaxpr/reduce_sum | solution.py:11
  37.6 3.7 %multiply_reduce_fusion.21 = (f32[32,128]{1,0:T(8,128)S(1)}, f32[32,256]{1,0:T(8,128)S(1)}) fusion(f32[32,256,128]{2,1,0:T(8,128)S(1)} %multiply_reduce_fusion.20, f32[32,256]{1,0:T(8,128)S(1)} %dynamic-slice_bitcast_fusion.11, f32[32,128]{1,0:T(8,128)S(1)} %fusion.44, f32[32,256]{1,0:T(8,128)S(1)} %fusion.45, ...), kind=kLoop, calls=%fused_computation.30.clone.1 | loop fusion | flops 6279168 | bytes 4341760 | tf_op jit(solution)/shard_map/while/body/eval_jaxpr/reduce_sum | solution.py:28
  43.6 4.1 %multiply_reduce_fusion.20 = f32[32,256,128]{2,1,0:T(8,128)S(1)} fusion(f32[32,3,128]{2,1,0:T(4,128)S(1)} %copy.167, f32[32,3,256]{2,1,0:T(4,128)S(1)} %copy.169), kind=kLoop, calls=%fused_computation.29.clone.1 | loop fusion | flops 8388608 | bytes 4341760 | tf_op jit(solution)/shard_map/while/body/eval_jaxpr/reduce_sum | solution.py:11
  49.2 3.7 %multiply_reduce_fusion.21 = (f32[32,128]{1,0:T(8,128)S(1)}, f32[32,256]{1,0:T(8,128)S(1)}) fusion(f32[32,256,128]{2,1,0:T(8,128)S(1)} %multiply_reduce_fusion.20, f32[32,256]{1,0:T(8,128)S(1)} %dynamic-slice_bitcast_fusion.11, f32[32,128]{1,0:T(8,128)S(1)} %fusion.44, f32[32,256]{1,0:T(8,128)S(1)} %fusion.45, ...), kind=kLoop, calls=%fused_computation.30.clone.1 | loop fusion | flops 6279168 | bytes 4341760 | tf_op jit(solution)/shard_map/while/body/eval_jaxpr/reduce_sum | solution.py:28
  55.2 4.1 %multiply_reduce_fusion.20 = f32[32,256,128]{2,1,0:T(8,128)S(1)} fusion(f32[32,3,128]{2,1,0:T(4,128)S(1)} %copy.167, f32[32,3,256]{2,1,0:T(4,128)S(1)} %copy.169), kind=kLoop, calls=%fused_computation.29.clone.1 | loop fusion | flops 8388608 | bytes 4341760 | tf_op jit(solution)/shard_map/while/body/eval_jaxpr/reduce_sum | solution.py:11
  60.9 3.7 %multiply_reduce_fusion.21 = (f32[32,128]{1,0:T(8,128)S(1)}, f32[32,256]{1,0:T(8,128)S(1)}) fusion(f32[32,256,128]{2,1,0:T(8,128)S(1)} %multiply_reduce_fusion.20, f32[32,256]{1,0:T(8,128)S(1)} %dynamic-slice_bitcast_fusion.11, f32[32,128]{1,0:T(8,128)S(1)} %fusion.44, f32[32,256]{1,0:T(8,128)S(1)} %fusion.45, ...), kind=kLoop, calls=%fused_computation.30.clone.1 | loop fusion | flops 6279168 | bytes 4341760 | tf_op jit(solution)/shard_map/while/body/eval_jaxpr/reduce_sum | solution.py:28
  66.8 4.1 %multiply_reduce_fusion.20 = f32[32,256,128]{2,1,0:T(8,128)S(1)} fusion(f32[32,3,128]{2,1,0:T(4,128)S(1)} %copy.167, f32[32,3,256]{2,1,0:T(4,128)S(1)} %copy.169), kind=kLoop, calls=%fused_computation.29.clone.1 | loop fusion | flops 8388608 | bytes 4341760 | tf_op jit(solution)/shard_map/while/body/eval_jaxpr/reduce_sum | solution.py:11
  72.5 3.7 %multiply_reduce_fusion.21 = (f32[32,128]{1,0:T(8,128)S(1)}, f32[32,256]{1,0:T(8,128)S(1)}) fusion(f32[32,256,128]{2,1,0:T(8,128)S(1)} %multiply_reduce_fusion.20, f32[32,256]{1,0:T(8,128)S(1)} %dynamic-slice_bitcast_fusion.11, f32[32,128]{1,0:T(8,128)S(1)} %fusion.44, f32[32,256]{1,0:T(8,128)S(1)} %fusion.45, ...), kind=kLoop, calls=%fused_computation.30.clone.1 | loop fusion | flops 6279168 | bytes 4341760 | tf_op jit(solution)/shard_map/while/body/eval_jaxpr/reduce_sum | solution.py:28
  77.4 13.8 %while.42 = (s32[]{:T(128)}, f32[2,32,256]{2,1,0:T(8,128)S(1)}, f32[2,32,4,256]{3,2,1,0:T(4,128)S(1)}, f32[2,32,4,128]{3,2,1,0:T(4,128)S(1)}, f32[2,32,128]{2,1,0:T(8,128)S(1)}, /*index=5*/s32[]{:T(128)}) while((s32[]{:T(128)}, f32[2,32,256]{2,1,0:T(8,128)S(1)}, f32[2,32,4,256]{3,2,1,0:T(4,128)S(1)}, f32[2,32,4,128]{3,2,1,0:T(4,128)S(1)}, ...), condition=%wide.region_3.4_spmd, body=%wide.region_0.3_spmd.sunk | while | flops 12587010 | bytes 10207317 | solution.py:37
  77.6 4.1 %multiply_reduce_fusion.18 = f32[32,256,128]{2,1,0:T(8,128)S(1)} fusion(f32[32,3,128]{2,1,0:T(4,128)S(1)} %copy.163, f32[32,3,256]{2,1,0:T(4,128)S(1)} %copy.165), kind=kLoop, calls=%fused_computation.17.clone.1 | loop fusion | flops 8388608 | bytes 4341760 | tf_op jit(solution)/shard_map/while/body/eval_jaxpr/reduce_sum | solution.py:11
  81.8 2.4 %multiply_reduce_fusion.19 = f32[32,256]{1,0:T(8,128)S(1)} fusion(f32[32,256,128]{2,1,0:T(8,128)S(1)} %multiply_reduce_fusion.18, f32[32,128]{1,0:T(8,128)S(1)} %dynamic-slice_bitcast_fusion.10, f32[32,128]{1,0:T(8,128)S(1)} %fusion.42, f32[32,256]{1,0:T(8,128)S(1)} %fusion.43), kind=kLoop, calls=%fused_computation.18.clone.1 | loop fusion | flops 4186112 | bytes 4292608 | tf_op jit(solution)/shard_map/while/body/eval_jaxpr/reduce_sum | solution.py:27
  84.5 4.1 %multiply_reduce_fusion.18 = f32[32,256,128]{2,1,0:T(8,128)S(1)} fusion(f32[32,3,128]{2,1,0:T(4,128)S(1)} %copy.163, f32[32,3,256]{2,1,0:T(4,128)S(1)} %copy.165), kind=kLoop, calls=%fused_computation.17.clone.1 | loop fusion | flops 8388608 | bytes 4341760 | tf_op jit(solution)/shard_map/while/body/eval_jaxpr/reduce_sum | solution.py:11
  88.7 2.4 %multiply_reduce_fusion.19 = f32[32,256]{1,0:T(8,128)S(1)} fusion(f32[32,256,128]{2,1,0:T(8,128)S(1)} %multiply_reduce_fusion.18, f32[32,128]{1,0:T(8,128)S(1)} %dynamic-slice_bitcast_fusion.10, f32[32,128]{1,0:T(8,128)S(1)} %fusion.42, f32[32,256]{1,0:T(8,128)S(1)} %fusion.43), kind=kLoop, calls=%fused_computation.18.clone.1 | loop fusion | flops 4186112 | bytes 4292608 | tf_op jit(solution)/shard_map/while/body/eval_jaxpr/reduce_sum | solution.py:27
  91.8 3.4 %fusion.20 = f32[128,1,32]{2,1,0:T(1,128)S(1)} fusion(f32[128,128,1]{1,2,0:T(1,128)S(1)} %bitcast.182, f32[128,128,32]{1,2,0:T(8,128)S(1)} %copy-done), kind=kOutput, calls=%fused_computation.105 | convolution fusion | flops 6291456 | bytes 2179072 | tf_op jit(solution)/shard_map/cpr,cp->cr/dot_general | solution.py:112
  95.2 9.0 %psum.15 = f32[128,32]{1,0:T(8,128)S(1)} all-reduce(f32[128,32]{1,0:T(8,128)S(1)} %bitcast.215), channel_id=1, replica_groups=mesh['grp'=2,'clu'=4,'sub'=2,'rep'=2] {'sub'}, use_global_device_ids=true, to_apply=%region_24.25 | all-reduce | flops 4096 | bytes 32768 | tf_op jit(solution)/shard_map/psum | solution.py:113
  104.2 3.9 %copy.94 = f32[128,32,32]{2,1,0:T(8,128)} copy(f32[128,32,32]{0,2,1:T(8,128)} %param.28) | data formatting | bytes 1048576 | tf_op args[8]
  108.1 3.4 %fusion.21 = f32[128,1,32]{2,1,0:T(1,128)S(1)} fusion(f32[128,32,1]{1,2,0:T(1,128)S(1)} %bitcast.213, f32[128,32,32]{2,1,0:T(8,128)} %copy.94), kind=kOutput, calls=%fused_computation.106 | convolution fusion | flops 1572864 | bytes 557056 | tf_op jit(solution)/shard_map/crs,cr->cs/dot_general | solution.py:114
  111.6 13.9 %all_gather.7 = f32[64,32]{1,0:T(8,128)S(1)} all-gather(f32[16,32]{1,0:T(8,128)S(1)} %fusion.11), channel_id=1, replica_groups=mesh['grp'=2,'clu'=4,'sub'=2,'rep'=2] {'clu'}, dimensions={0}, use_global_device_ids=true | all-gather | bytes 10240 | tf_op jit(solution)/shard_map/all_gather | solution.py:120
  126.3 3.4 %fusion.22 = f32[16,1,32,1]{2,1,3,0:T(1,128)S(1)} fusion(f32[16,8,32,1]{2,3,1,0:T(1,128)S(1)} %bitcast.212, f32[16,8,32,32]{3,2,1,0:T(8,128)} %param.31), kind=kOutput, calls=%fused_computation.107 | convolution fusion | flops 1572864 | bytes 542720 | tf_op jit(solution)/shard_map/pkrs,pks->pr/dot_general | solution.py:121
  133.6 4.6 %all-to-all-start.1 = ((f32[4,1,10240]{2,1,0:T(1,128)}), f32[4,1,10240]{2,1,0:T(1,128)S(1)}, u32[]{:S(2)}, u32[]{:S(2)}) async-start(f32[4,1,10240]{2,1,0:T(1,128)} %all_to_all.20), calls=%async_computation.1 | async-start | bytes 327680 | tf_op jit(solution)/shard_map/all_to_all | solution.py:103
  139.7 2.1 all_to_all.21
  142.7 1.3 scatter_custom_fusion
  143.9 1.7 scatter_fusion
  145.8 5.1 %all-to-all-start.2 = ((f32[4,1,20480]{2,1,0:T(1,128)}), f32[4,1,20480]{2,1,0:T(1,128)S(1)}, u32[]{:S(2)}, u32[]{:S(2)}) async-start(f32[4,1,20480]{2,1,0:T(1,128)} %all_to_all.21), calls=%async_computation.3 | async-start | bytes 655360 | tf_op jit(solution)/shard_map/all_to_all | solution.py:92
  153.7 13.9 %while.44 = (s32[]{:T(128)}, f32[2,32,256]{2,1,0:T(8,128)S(1)}, f32[2,32,4,256]{3,2,1,0:T(4,128)S(1)}, f32[2,32,4,128]{3,2,1,0:T(4,128)S(1)}, f32[2,32,128]{2,1,0:T(8,128)}, /*index=5*/s32[]{:T(128)}) while((s32[]{:T(128)}, f32[2,32,256]{2,1,0:T(8,128)S(1)}, f32[2,32,4,256]{3,2,1,0:T(4,128)S(1)}, f32[2,32,4,128]{3,2,1,0:T(4,128)S(1)}, ...), condition=%wide.region_14.15_spmd, body=%wide.region_11.14_spmd.sunk | while | flops 12587010 | bytes 10338417 | solution.py:37
  154.0 4.1 %multiply_reduce_fusion.22 = f32[32,256,128]{2,1,0:T(8,128)S(1)} fusion(f32[32,3,128]{2,1,0:T(4,128)S(1)} %copy.171, f32[32,3,256]{2,1,0:T(4,128)S(1)} %copy.173), kind=kLoop, calls=%fused_computation.45.clone.1 | loop fusion | flops 8388608 | bytes 4341760 | tf_op jit(solution)/shard_map/while/body/eval_jaxpr/reduce_sum | solution.py:11
  158.2 2.4 %multiply_reduce_fusion.23 = f32[32,256]{1,0:T(8,128)S(1)} fusion(f32[32,256,128]{2,1,0:T(8,128)S(1)} %multiply_reduce_fusion.22, f32[32,128]{1,0:T(8,128)S(1)} %dynamic-slice_bitcast_fusion.13, f32[32,128]{1,0:T(8,128)S(1)} %fusion.46, f32[32,256]{1,0:T(8,128)S(1)} %fusion.47), kind=kLoop, calls=%fused_computation.46.clone.1 | loop fusion | flops 4186112 | bytes 4292608 | tf_op jit(solution)/shard_map/while/body/eval_jaxpr/reduce_sum | solution.py:27
  160.9 4.1 %multiply_reduce_fusion.22 = f32[32,256,128]{2,1,0:T(8,128)S(1)} fusion(f32[32,3,128]{2,1,0:T(4,128)S(1)} %copy.171, f32[32,3,256]{2,1,0:T(4,128)S(1)} %copy.173), kind=kLoop, calls=%fused_computation.45.clone.1 | loop fusion | flops 8388608 | bytes 4341760 | tf_op jit(solution)/shard_map/while/body/eval_jaxpr/reduce_sum | solution.py:11
  165.1 2.4 %multiply_reduce_fusion.23 = f32[32,256]{1,0:T(8,128)S(1)} fusion(f32[32,256,128]{2,1,0:T(8,128)S(1)} %multiply_reduce_fusion.22, f32[32,128]{1,0:T(8,128)S(1)} %dynamic-slice_bitcast_fusion.13, f32[32,128]{1,0:T(8,128)S(1)} %fusion.46, f32[32,256]{1,0:T(8,128)S(1)} %fusion.47), kind=kLoop, calls=%fused_computation.46.clone.1 | loop fusion | flops 4186112 | bytes 4292608 | tf_op jit(solution)/shard_map/while/body/eval_jaxpr/reduce_sum | solution.py:27
  170.7 8.4 %while.45 = (s32[]{:T(128)}, f32[2,32,128]{2,1,0:T(8,128)S(1)}, f32[2,32,4,128]{3,2,1,0:T(4,128)S(1)}, f32[2,32,4,256]{3,2,1,0:T(4,128)S(1)}, f32[2,32,256]{2,1,0:T(8,128)S(1)}, /*index=5*/s32[]{:T(128)}) while((s32[]{:T(128)}, f32[2,32,128]{2,1,0:T(8,128)S(1)}, f32[2,32,4,128]{3,2,1,0:T(4,128)S(1)}, f32[2,32,4,256]{3,2,1,0:T(4,128)S(1)}, ...), condition=%wide.region_21.22_spmd, body=%wide.region_18.21_spmd.sunk | while | flops 12591106 | bytes 10207317 | solution.py:37
  171.0 2.3 %multiply_reduce_fusion.24 = f32[32,128,256]{2,1,0:T(8,128)S(1)} fusion(f32[32,3,256]{2,1,0:T(4,128)S(1)} %copy.175, f32[32,3,128]{2,1,0:T(4,128)S(1)} %copy.177), kind=kLoop, calls=%fused_computation.57.clone.1 | loop fusion | flops 8388608 | bytes 4341760 | tf_op jit(solution)/shard_map/while/body/eval_jaxpr/reduce_sum | solution.py:11
  173.3 1.6 multiply_reduce_fusion.25
  175.2 2.3 %multiply_reduce_fusion.24 = f32[32,128,256]{2,1,0:T(8,128)S(1)} fusion(f32[32,3,256]{2,1,0:T(4,128)S(1)} %copy.175, f32[32,3,128]{2,1,0:T(4,128)S(1)} %copy.177), kind=kLoop, calls=%fused_computation.57.clone.1 | loop fusion | flops 8388608 | bytes 4341760 | tf_op jit(solution)/shard_map/while/body/eval_jaxpr/reduce_sum | solution.py:11
  177.5 1.6 multiply_reduce_fusion.25
  179.2 1.1 reduce-scatter.2.cloned.1.call-done
  180.3 2.9 %scatter_fusion.2 = f32[128,128]{1,0:T(8,128)} fusion(f32[128,128]{1,0:T(8,128)} %reduce-scatter.2.cloned.1.call-done, s32[128]{0:T(128)S(1)} %get-tuple-element.229, f32[128,128]{1,0:T(8,128)} %bitcast.50), kind=kCustom, calls=%fused_computation.15 | custom fusion | flops 16384 | bytes 197120 | tf_op jit(solution)/shard_map/scatter-add | solution.py:80
  183.2 2.3 %scatter_fusion.3 = f32[128,128]{1,0:T(8,128)} fusion(f32[128,128]{1,0:T(8,128)} %scatter_fusion.2, s32[64]{0:T(128)S(1)} %fusion.19, f32[64,128]{1,0:T(8,128)S(1)} %bitcast_multiply_fusion.1), kind=kCustom, calls=%fused_computation.16 | custom fusion | flops 8192 | bytes 98560 | tf_op jit(solution)/shard_map/scatter-add | solution.py:100
  185.5 1.8 fusion.23
  187.3 16.1 %all-reduce.2.cloned.1.call-done = f32[128,128]{1,0:T(8,128)} async-done(((f32[128,128]{1,0:T(8,128)}), f32[128,128]{1,0:T(8,128)}) %all-reduce.2.cloned.1.call-update) | async-done | bytes 65552 | tf_op jit(solution)/shard_map/psum | solution.py:111
  203.4 1.5 add_multiply_fusion
  (221 shorter events, 35.4 us)
Async XLA Ops:
  6.5 85.3 %copy-start = (f32[128,128,32]{1,2,0:T(8,128)S(1)}, f32[128,128,32]{1,2,0:T(8,128)}, u32[]{:S(2)}) copy-start(f32[128,128,32]{1,2,0:T(8,128)} %param.27) | copy-start | bytes 6291460
  8.0 123.4 %all-to-all-start = ((s32[4,2,16]{2,1,0:T(2,128)}), s32[4,2,16]{2,1,0:T(2,128)S(1)}, u32[]{:S(2)}, u32[]{:S(2)}) async-start(s32[4,2,16]{2,1,0:T(2,128)} %copy.82), calls=%async_computation | async-start | bytes 8192 | tf_op jit(solution)/shard_map/all_to_all | solution.py:91
  77.4 13.8 %copy-start.12 = (s32[1,4,16]{2,1,0:T(4,128)S(1)}, s32[1,4,16]{2,1,0:T(4,128)}, u32[]{:S(2)}) copy-start(s32[1,4,16]{2,1,0:T(4,128)} %param.24) | copy-start | bytes 772
  91.2 0.6 copy-start.7
  91.2 20.2 %copy-start.13 = (s32[128]{0:T(128)S(1)}, s32[128]{0:T(128)}, u32[]{:S(2)}) copy-start(s32[128]{0:T(128)} %param.29) | copy-start | bytes 1540
  91.2 34.2 %copy-start.10 = (s32[16,8]{0,1:T(8,128)S(1)}, s32[16,8]{0,1:T(8,128)}, u32[]{:S(2)}) copy-start(s32[16,8]{0,1:T(8,128)} %param.30) | copy-start | bytes 1540
  95.2 34.7 %copy-start.2 = (f32[128,4,256]{2,1,0:T(4,128)S(1)}, f32[128,4,256]{2,1,0:T(4,128)}, u32[]{:S(2)}) copy-start(f32[128,4,256]{2,1,0:T(4,128)} %param.22) | copy-start | bytes 1572868
  108.1 31.0 %copy-start.9 = (s32[1,4,16]{2,1,0:T(4,128)S(1)}, s32[1,4,16]{2,1,0:T(4,128)}, u32[]{:S(2)}) copy-start(s32[1,4,16]{2,1,0:T(4,128)} %param.25) | copy-start | bytes 772
  130.6 11.3 %copy-start.3 = (f32[128,32,32]{0,2,1:T(8,128)S(1)}, f32[128,32,32]{0,2,1:T(8,128)}, u32[]{:S(2)}) copy-start(f32[128,32,32]{0,2,1:T(8,128)} %param.28) | copy-start | bytes 1572868
  133.6 12.2 %all-to-all-start.1 = ((f32[4,1,10240]{2,1,0:T(1,128)}), f32[4,1,10240]{2,1,0:T(1,128)S(1)}, u32[]{:S(2)}, u32[]{:S(2)}) async-start(f32[4,1,10240]{2,1,0:T(1,128)} %all_to_all.20), calls=%async_computation.1 | async-start | bytes 327680 | tf_op jit(solution)/shard_map/all_to_all | solution.py:103
  145.8 23.6 %all-to-all-start.2 = ((f32[4,1,20480]{2,1,0:T(1,128)}), f32[4,1,20480]{2,1,0:T(1,128)S(1)}, u32[]{:S(2)}, u32[]{:S(2)}) async-start(f32[4,1,20480]{2,1,0:T(1,128)} %all_to_all.21), calls=%async_computation.3 | async-start | bytes 655360 | tf_op jit(solution)/shard_map/all_to_all | solution.py:92
  150.9 29.4 %reduce-scatter.2.cloned.1.call-start = ((), (), s32[]{:S(2)}) async-start(), calls=%async_computation.4 | async-start | bytes 196608 | tf_op jit(solution)/shard_map/reduce_scatter | solution.py:110
  153.7 13.9 %copy-start.11 = (f32[64]{0:T(128)S(1)}, f32[64]{0:T(128)}, u32[]{:S(2)}) copy-start(f32[64]{0:T(128)} %convert_element_type.26) | copy-start | bytes 772
  153.7 17.0 %copy-start.8 = (f32[2,32,128]{2,1,0:T(8,128)S(1)}, f32[2,32,128]{2,1,0:T(8,128)}, u32[]{:S(2)}) copy-start(f32[2,32,128]{2,1,0:T(8,128)} %custom-call.26) | copy-start | bytes 98308
  153.7 4.4 %copy-start.4 = (f32[2,32,128]{2,1,0:T(8,128)S(1)}, f32[2,32,128]{2,1,0:T(8,128)}, u32[]{:S(2)}) copy-start(f32[2,32,128]{2,1,0:T(8,128)} %get-tuple-element.429) | copy-start | bytes 98308 | tf_op jit(solution)/shard_map/while
  160.6 4.4 %copy-start.4 = (f32[2,32,128]{2,1,0:T(8,128)S(1)}, f32[2,32,128]{2,1,0:T(8,128)}, u32[]{:S(2)}) copy-start(f32[2,32,128]{2,1,0:T(8,128)} %get-tuple-element.429) | copy-start | bytes 98308 | tf_op jit(solution)/shard_map/while
  168.7 0.6 copy-start.1
  169.3 34.0 %all-reduce.2.cloned.1.call-start = ((), (), s32[]{:S(2)}) async-start(), calls=%async_computation.5 | async-start | bytes 131072 | tf_op jit(solution)/shard_map/psum | solution.py:111
  170.7 14.8 %copy-start.5 = (f32[128,32,1]{1,2,0:T(1,128)S(1)}, f32[128,32,1]{1,2,0:T(1,128)}, u32[]{:S(2)}) copy-start(f32[128,32,1]{1,2,0:T(1,128)} %copy.104) | copy-start | bytes 49156
  170.7 32.7 %copy-start.6 = (s32[128,128]{1,0:T(8,128)S(1)}, s32[128,128]{1,0:T(8,128)}, u32[]{:S(2)}) copy-start(s32[128,128]{1,0:T(8,128)} %param.21) | copy-start | bytes 196612
Sparse Core Ops, SparseCore 0:
  169.4 10.7 reduce-scatter.1
  185.6 17.6 all-reduce.1
where the time goes:
time: 213 us; the launch traced here: 212 us
  other arithmetic  81.8 us (38%)
  local copies, waits for them, and re-layouts  41.9 us (20%)
  blocking collectives  27.8 us (13%)
  waiting for transfers between devices  17.2 us (8%)
  starting transfers between devices  16 us (8%)
  between operations  13.7 us (6%)
  matrix products  12.2 us (6%)
    reduce_sum x10, other arithmetic, kernel_tile(): dist_sq = jnp.sum(delta * delta, axis=1)  37.7 us
    psum x1, waiting for transfers between devices, on_device(): near = lax.psum(near_rows + cols_acc, 'rep')  16.1 us
    reduce_sum x4, other arithmetic, single(): jnp.sum(tile * row_q[:, :, None], axis=1)  14.8 us
    all_gather x1, blocking collectives, on_device(): all_parents = lax.all_gather(parent_coeff, 'clu', axis=0, tiled=True)  13.9 us
    reduce_sum x6, other arithmetic, single(): jnp.sum(tile * col_q[:, None, :], axis=2)  12.8 us
    psum x1, blocking collectives, on_device(): leaf = lax.psum(leaf_part, 'sub')  8.96 us
    all_to_all x1, starting transfers between devices, on_device(): lax.all_to_all(ask_ints, 'clu', split_axis=0, concat_axis=0, tiled=True)  6.32 us
    all_to_all x1, starting transfers between devices, on_device(): lax.all_to_all(target_pack, 'clu', split_axis=0, concat_axis=0, tiled=True)  5.09 us
  transfers between devices with their start and end apart: 5, of which 2 were waited for; matrix products, arithmetic and copies ran while one was open for 58% of the time, Pallas kernels for 0%

commit v1 on v0

v1 whole, which is shorter than its diff:
```python
import functools

import jax
import jax.numpy as jnp
from jax import lax
from jax.experimental import pallas as pl
from jax.experimental.pallas import tpu as pltpu
from jax.sharding import PartitionSpec as P

F32 = jnp.float32
BF16 = jnp.bfloat16
HIGHEST = lax.Precision.HIGHEST
ROWS = 40
LANES = 128
PARAMS = pltpu.CompilerParams(vmem_limit_bytes=56 * 1024 * 1024)


def vmem():
    return pl.BlockSpec(memory_space=pltpu.VMEM)


def smem():
    return pl.BlockSpec(memory_space=pltpu.SMEM)


def whole(size):
    return -(-size // LANES) * LANES


def cut(v):
    return v.astype(BF16).astype(F32)


def powers(sign):
    lane = lax.broadcasted_iota(jnp.int32, (8, LANES), 1)
    out = jnp.full((8, LANES), 2.0 ** (-64 * sign), F32)
    for bit in range(7):
        out = out * jnp.where((lane >> bit) & 1 == 1, F32(2.0 ** (sign * 2**bit)), F32(1.0))
    return out


def frame(parts):
    low = [functools.reduce(jnp.minimum, [jnp.min(p[k]) for p in parts]) for k in range(3)]
    high = [functools.reduce(jnp.maximum, [jnp.max(p[k]) for p in parts]) for k in range(3)]
    width = functools.reduce(jnp.maximum, [jnp.max(jnp.abs(p[3])) for p in parts])
    for lo, hi in zip(low, high):
        width = jnp.maximum(width, 0.5 * (hi - lo))
    up, down = powers(1), powers(-1)
    size = jnp.min(jnp.where(up >= width, up, F32(2.0**63)))
    inv = jnp.max(jnp.where(up >= width, down, F32(2.0**-63)))
    magic = size * F32(1.5 * 2.0**20)
    centre = [(0.5 * (lo + hi) + magic) - magic for lo, hi in zip(low, high)]
    return centre, inv


def split_features(points, centre, inv):
    magic = F32(1.5 * 2.0**16)
    grid, rest = [], []
    for k in range(3):
        u = (points[k] - centre[k]) * inv
        h = (u + magic) - magic
        grid.append(h)
        rest.append(u - h)
    rad = points[3] * inv
    norm = grid[0] * grid[0] + grid[1] * grid[1] + grid[2] * grid[2]
    norm1 = cut(norm)
    norm2 = norm - norm1
    cross = grid[0] * rest[0] + grid[1] * rest[1] + grid[2] * rest[2]
    extra = 2.0 * cross + (rest[0] * rest[0] + rest[1] * rest[1] + rest[2] * rest[2]) + rad * rad
    extra1 = cut(extra)
    extra2 = cut(extra - extra1)
    extra3 = (extra - extra1) - extra2
    rest1 = [cut(v) for v in rest]
    rest2 = [v - w for v, w in zip(rest, rest1)]
    neg = lambda vs: [-2.0 * v for v in vs]
    one, zero = jnp.ones_like(rad), jnp.zeros_like(rad)
    left = grid + [norm1, norm2, one, one]
    right = neg(grid) + [one, one, norm1, norm2]
    left += [extra1, extra2, extra3, one, one, one]
    right += [one, one, one, extra1, extra2, extra3]
    left += grid + grid + rest1 + rest2 + rest1 + rest1 + rest2
    right += neg(rest1) + neg(rest2) + neg(grid) + neg(grid) + neg(rest1) + neg(rest2) + neg(rest1)
    left += [zero] * (ROWS - len(left))
    right += [zero] * (ROWS - len(right))
    return left, right, rad


def store_features(ref, rows):
    count = rows[0].shape[0]
    width = rows[0].shape[1]
    for k, row in enumerate(rows):
        for t, piece in enumerate(ref):
            piece[pl.ds(k, count, stride=ROWS), :] = row[:, t * LANES : min(width, (t + 1) * LANES)]


def load_features(ref, index):
    start = pl.multiple_of(index * ROWS, 8)
    return [piece[pl.ds(start, ROWS), :].astype(BF16) for piece in ref]


def contract(left, right):
    return lax.dot_general(left, right, (((0,), (0,)), ((), ())), preferred_element_type=F32)


def column(table, index):
    if table.shape[1] == LANES and table.shape[0] % 8 == 0:
        return jnp.take_along_axis(table, jnp.full(table.shape, index, jnp.int32), axis=1)
    lane = lax.broadcasted_iota(jnp.int32, table.shape, 1)
    picked = jnp.sum(jnp.where(lane == index, table, 0.0), axis=1, keepdims=True)
    return jnp.broadcast_to(picked, (table.shape[0], LANES))


def put_column(table_ref, first, value, second=None, other=None):
    lane = lax.broadcasted_iota(jnp.int32, table_ref.shape, 1)
    add = jnp.where(lane == first, value, 0.0)
    if second is not None:
        add = add + jnp.where(lane == second, other, 0.0)
    table_ref[...] += add


def pack_kernel(sizes, charges, mask, geo, targets, sources, live, masked, codes, *packs):
    C, S, L, slots = sizes
    me, sub = lax.axis_index("clu"), lax.axis_index("sub")
    masked[...] = charges[...] * mask[...].astype(F32)
    for shift in range(1, C):
        dest = lax.rem(me + shift, C)
        for j in range(slots):
            codes[shift - 1, j] = jnp.where(live[dest, j] > 0, sources[dest, j], -1)

    def fill(s):
        for shift in range(1, C):
            dest = lax.rem(me + shift, C)
            pack = packs[shift - 1]
            for j in range(slots):
                t = targets[dest, j]
                g = geo[t, :, s * L : (s + 1) * L]
                for k in range(4):
                    pack[k * slots + j : k * slots + j + 1, :] = g[k : k + 1]
                pack[4 * slots + j : 4 * slots + j + 1, :] = masked[pl.ds(t, 1), :]

    for s in range(S):
        pl.when(sub == s)(functools.partial(fill, s))


def local_kernel(sizes, geo, pairs, *rest):
    C, S, L, R, clusters, panels = sizes
    pieces = rest[:S]
    ups = rest[S : 2 * S]
    acc_out, up_sum = rest[2 * S : 2 * S + 2]
    q, qt, acc, acct, fa0, fa1, fb0, fb1, rads = rest[2 * S + 2 :]
    fa, fb = (fa0, fa1), (fb0, fb1)
    sub, rep = lax.axis_index("sub"), lax.axis_index("rep")
    total = ups[0][...]
    for u in ups[1:]:
        total = total + u[...]
    up_sum[...] = total

    def place(s):
        for shift in range(S):
            owner = (s - shift) % S
            q[:, owner * L : (owner + 1) * L] = pieces[shift][...]

    for s in range(S):
        pl.when(sub == s)(functools.partial(place, s))
    qt[...] = q[...].T
    acc[...] = jnp.zeros_like(acc)
    acct[...] = jnp.zeros_like(acct)
    points = [geo[:, k, :] for k in range(4)]
    centre, inv = frame([points])
    left, right, rad = split_features(points, centre, inv)
    store_features(fa, left)
    store_features(fb, right)
    rads[...] = rad

    half = panels // 2
    share = clusters // (S * R)
    first = (rep * S + sub) * share

    def self_tile(c):
        a = load_features(fa, c)
        b = load_features(fb, c)
        qrow = q[pl.ds(c, 1), :]
        radius = rads[pl.ds(c, 1), :]
        diag = lax.rsqrt(2.0 * (radius * radius))
        eye = lax.broadcasted_iota(jnp.int32, (half, half), 0) == lax.broadcasted_iota(
            jnp.int32, (half, half), 1
        )
        d00 = contract(a[0], b[0])
        d01 = contract(a[0], b[1])
        d11 = contract(a[1], b[1])
        g00 = jnp.where(eye, diag[:, :half], lax.rsqrt(d00))
        g11 = jnp.where(eye, diag[:, half:], lax.rsqrt(d11))
        g01 = lax.rsqrt(d01)
        qcol = column(qt[:half, :], c)
        top = jnp.sum(g00 * qrow[:, :half] + g01 * qrow[:, half:], axis=1, keepdims=True)
        bottom = jnp.sum(g11 * qrow[:, half:], axis=1, keepdims=True)
        back = jnp.sum(g01 * qcol, axis=0, keepdims=True)
        return top, bottom, jnp.concatenate([jnp.zeros_like(back), back], axis=1)

    def self_step(i, carry):
        c0 = first + 2 * i
        c1 = c0 + 1
        top0, bottom0, back0 = self_tile(c0)
        top1, bottom1, back1 = self_tile(c1)
        lane = lax.broadcasted_iota(jnp.int32, (half, clusters), 1)
        acct[:half, :] += jnp.where(lane == c0, top0, 0.0) + jnp.where(lane == c1, top1, 0.0)
        acct[half:, :] += jnp.where(lane == c0, bottom0, 0.0) + jnp.where(lane == c1, bottom1, 0.0)
        acc[pl.ds(c0, 1), :] += back0
        acc[pl.ds(c1, 1), :] += back1
        return carry

    lax.fori_loop(0, share // 2, self_step, 0)

    count = pairs.shape[1] // S
    begin = sub * count

    def pair_tile(p):
        ia, ib = pairs[0, p], pairs[1, p]
        a = load_features(fa, ia)
        b = load_features(fb, ib)
        left = jnp.concatenate(a, axis=1)
        g0 = lax.rsqrt(contract(left, b[0]))
        g1 = lax.rsqrt(contract(left, b[1]))
        qb = q[pl.ds(ib, 1), :]
        qcol = column(qt[...], ia)
        fwd = jnp.sum(g0 * qb[:, :LANES] + g1 * qb[:, LANES:], axis=1, keepdims=True)
        back = jnp.concatenate(
            [jnp.sum(g * qcol, axis=0, keepdims=True) for g in (g0, g1)], axis=1
        )
        return ia, ib, fwd, back

    def pair_step(i, carry):
        ia0, ib0, fwd0, back0 = pair_tile(begin + 2 * i)
        ia1, ib1, fwd1, back1 = pair_tile(begin + 2 * i + 1)
        put_column(acct, ia0, fwd0, ia1, fwd1)
        acc[pl.ds(ib0, 1), :] += back0
        acc[pl.ds(ib1, 1), :] += back1
        return carry

    lax.fori_loop(0, count // 2, pair_step, 0)
    acc_out[...] = (acc[...] + acct[...].T) * inv


def remote_kernel(sizes, geo, codes, acc_in, *rest):
    C, S, L, slots, clusters, panels = sizes
    pieces = rest[:S]
    packs = rest[S : S + C - 1]
    outs = rest[S + C - 1 : 2 * (S + C - 1)]
    parts, sends = outs[:S], outs[S:]
    q, tqt, acc, fwdt, sgeo, fa0, fb0, fb1, order = rest[2 * (S + C - 1) :]
    fa, fb = (fa0,), (fb0, fb1)
    sub = lax.axis_index("sub")
    n = (C - 1) * slots

    def place(s):
        for shift in range(S):
            owner = (s - shift) % S
            q[:, owner * L : (owner + 1) * L] = pieces[shift][...]

    for s in range(S):
        pl.when(sub == s)(functools.partial(place, s))
    acc[...] = jnp.zeros_like(acc)
    fwdt[...] = jnp.zeros_like(fwdt)
    found = jnp.int32(0)
    for shift in range(C - 1):
        for j in range(slots):
            code = codes[shift, j]
            order[found] = shift * slots + j
            found = found + (code >= 0).astype(jnp.int32)
            g = geo[jnp.maximum(code, 0)]
            for k in range(4):
                row = k * n + shift * slots + j
                sgeo[row : row + 1, :] = g[k : k + 1]
    tpoints = [
        jnp.concatenate([p[k * slots : (k + 1) * slots, :] for p in packs], axis=0) for k in range(5)
    ]
    spoints = [sgeo[k * n : (k + 1) * n, :] for k in range(4)]
    centre, inv = frame([tpoints, spoints])
    left, _, _ = split_features(tpoints, centre, inv)
    _, right, _ = split_features(spoints, centre, inv)
    store_features(fa, left)
    store_features(fb, right)
    wide = tqt.shape[1]
    tq = tpoints[4]
    if wide > n:
        tq = jnp.concatenate([tq, jnp.zeros((wide - n, L), F32)], axis=0)
    tqt[...] = tq.T

    def tile(i):
        ok = i < found
        slot = order[jnp.minimum(i, found - 1)]
        source = codes[slot // slots, lax.rem(slot, slots)]
        (a,) = load_features(fa, slot)
        b = load_features(fb, slot)
        g0 = lax.rsqrt(contract(a, b[0]))
        g1 = lax.rsqrt(contract(a, b[1]))
        qb = q[pl.ds(source, 1), :]
        qcol = column(tqt[...], slot)
        fwd = jnp.sum(g0 * qb[:, :LANES] + g1 * qb[:, LANES:], axis=1, keepdims=True)
        back = jnp.concatenate(
            [jnp.sum(g * qcol, axis=0, keepdims=True) for g in (g0, g1)], axis=1
        )
        return jnp.where(ok, slot, -1), source, fwd, jnp.where(ok, back, 0.0)

    def step(i, carry):
        slot0, source0, fwd0, back0 = tile(2 * i)
        slot1, source1, fwd1, back1 = tile(2 * i + 1)
        put_column(fwdt, slot0, fwd0, slot1, fwd1)
        acc[pl.ds(source0, 1), :] += back0
        acc[pl.ds(source1, 1), :] += back1
        return carry

    lax.fori_loop(0, (found + 1) // 2, step, 0)
    total = acc_in[...] + acc[...] * inv

    def give(s):
        for shift in range(S):
            other = (s + shift) % S
            parts[shift][...] = total[:, other * L : (other + 1) * L]

    for s in range(S):
        pl.when(sub == s)(functools.partial(give, s))
    fwd = (fwdt[...] * inv).T
    for shift in range(C - 1):
        sends[shift][...] = fwd[shift * slots : (shift + 1) * slots, :]


def up_kernel(basis, masked, transfer, parent, up):
    clusters = basis.shape[0]
    rank = basis.shape[1]
    lane = lax.broadcasted_iota(jnp.int32, (rank, clusters), 1)
    leaf = jnp.zeros((rank, clusters), F32)
    for c in range(clusters):
        part = jnp.sum(basis[c] * masked[c : c + 1, :], axis=1, keepdims=True)
        leaf = jnp.where(lane == c, part, leaf)
    lifted = jnp.zeros((rank, clusters), F32)
    for r in range(rank):
        lifted = lifted + transfer[r] * leaf[r : r + 1, :]
    which = lax.broadcasted_iota(jnp.int32, (up.shape[0], clusters), 0)
    onehot = (parent[...] == which).astype(F32)
    up[...] = lax.dot_general(
        onehot, lifted, (((1,), (1,)), ((), ())), precision=HIGHEST, preferred_element_type=F32
    )


def down_kernel(sizes, far_list, coupling, transfer, parent, basis, *rest):
    C = sizes
    ups = rest[:C]
    far, parents, leaf_field = rest[C:]
    me = lax.axis_index("clu")
    par_dev, far_n, rank = coupling.shape[0], coupling.shape[1], coupling.shape[2]
    clusters = basis.shape[0]
    for shift in range(C):
        owner = lax.rem(me + C - shift, C)
        parents[pl.ds(pl.multiple_of(owner * par_dev, 8), par_dev), :] = ups[shift][...]
    lane = lax.broadcasted_iota(jnp.int32, (rank, LANES), 1)
    field = jnp.zeros((rank, LANES), F32)
    for p in range(par_dev):
        part = jnp.zeros((rank, rank), F32)
        for k in range(far_n):
            part = part + coupling[p, k] * parents[pl.ds(far_list[p, k], 1), :]
        field = jnp.where(lane == p, jnp.sum(part, axis=1, keepdims=True), field)
    which = lax.broadcasted_iota(jnp.int32, (LANES, clusters), 0)
    onehot = (parent[...] == which).astype(F32)
    down = jnp.dot(field, onehot, precision=HIGHEST, preferred_element_type=F32)
    for r in range(rank):
        leaf_field[r : r + 1, :] = jnp.sum(transfer[r] * down, axis=0, keepdims=True)
    fields = leaf_field[...]
    for c in range(clusters):
        far[c : c + 1, :] = jnp.sum(basis[c] * fields[:, c : c + 1], axis=0, keepdims=True)


def final_kernel(sizes, *rest):
    C, S, R, slots = sizes
    lists = rest[:R]
    mask, far = rest[R : R + 2]
    near = rest[R + 2 : R + 2 + S * R]
    sums = rest[R + 2 + S * R : -1]
    out = rest[-1]
    me = lax.axis_index("clu")
    total = far[...]
    for part in near:
        total = total + part[...]
    out[...] = total
    for r in range(R):
        for shift in range(1, C):
            dest = lax.rem(me + shift, C)
            got = sums[r * (C - 1) + shift - 1]
            for j in range(slots):
                t = lists[r][dest, j]
                out[pl.ds(t, 1), :] += got[j : j + 1, :]
    out[...] = out[...] * mask[...].astype(F32)


def send(value, moves):
    names = tuple(name for name, _ in moves)
    steps = [step for _, step in moves]
    sizes = [lax.axis_size(name) for name in names]
    perm = []

    def flat(coords):
        index = 0
        for size, c in zip(sizes, coords):
            index = index * size + c
        return index

    total = 1
    for size in sizes:
        total *= size
    for index in range(total):
        coords, left = [], index
        for size in reversed(sizes):
            coords.append(left % size)
            left //= size
        coords.reverse()
        perm.append((index, flat([(c + s) % n for c, s, n in zip(coords, steps, sizes)])))
    return lax.ppermute(value, names if len(names) > 1 else names[0], perm)


def on_device(
    charges,
    panel_mask,
    geometry,
    remote_source,
    remote_target,
    remote_live,
    local_pairs,
    basis,
    transfer,
    parent_of,
    far_list,
    coupling,
):
    clusters, L = charges.shape
    panels = geometry.shape[2]
    C, S, R = lax.axis_size("clu"), lax.axis_size("sub"), lax.axis_size("rep")
    slots = remote_source.shape[2]
    par_dev, rank = far_list.shape[0], transfer.shape[1]
    n = (C - 1) * slots
    shape = jax.ShapeDtypeStruct
    targets = remote_target[0]
    basis_t = jnp.transpose(basis, (0, 2, 1))
    transfer_t = jnp.transpose(transfer, (1, 2, 0))
    parent = parent_of[None, :]

    made = pl.pallas_call(
        functools.partial(pack_kernel, (C, S, L, slots)),
        out_shape=[shape((clusters, L), F32), shape((C - 1, slots), jnp.int32)]
        + [shape((5 * slots, L), F32)] * (C - 1),
        in_specs=[vmem()] * 3 + [smem()] * 3,
        out_specs=[vmem(), smem()] + [vmem()] * (C - 1),
        compiler_params=PARAMS,
        name="packs",
    )(charges, panel_mask, geometry, targets, remote_source[0], remote_live[0])
    masked, codes, packs = made[0], made[1], made[2:]
    pieces = [masked] + [send(masked, (("sub", d),)) for d in range(1, S)]
    got_packs = [send(packs[d - 1], (("clu", d),)) for d in range(1, C)]
    got_codes = jnp.concatenate([send(codes[d - 1 : d], (("clu", d),)) for d in range(1, C)], axis=0)
    lists = [targets] + [send(targets, (("rep", d),)) for d in range(1, R)]

    up = pl.pallas_call(
        up_kernel,
        out_shape=shape((par_dev, rank), F32),
        in_specs=[vmem()] * 4,
        out_specs=vmem(),
        compiler_params=PARAMS,
        name="far_up",
    )(basis_t, masked, transfer_t, parent)
    ups = [up] + [send(up, (("sub", d),)) for d in range(1, S)]

    half = [pltpu.VMEM((clusters * ROWS, LANES), F32)] * 2
    acc, up_sum = pl.pallas_call(
        functools.partial(local_kernel, (C, S, L, R, clusters, panels)),
        out_shape=[shape((clusters, panels), F32), shape((par_dev, rank), F32)],
        in_specs=[vmem(), smem()] + [vmem()] * (2 * S),
        out_specs=[vmem(), vmem()],
        scratch_shapes=[
            pltpu.VMEM((clusters, panels), F32),
            pltpu.VMEM((panels, clusters), F32),
            pltpu.VMEM((clusters, panels), F32),
            pltpu.VMEM((panels, clusters), F32),
            *half,
            *half,
            pltpu.VMEM((clusters, panels), F32),
        ],
        compiler_params=PARAMS,
        name="near_local",
    )(geometry, local_pairs[0].T, *pieces, *ups)
    all_ups = [up_sum] + [send(up_sum, (("clu", d),)) for d in range(1, C)]

    made = pl.pallas_call(
        functools.partial(remote_kernel, (C, S, L, slots, clusters, panels)),
        out_shape=[shape((clusters, L), F32)] * S + [shape((slots, L), F32)] * (C - 1),
        in_specs=[vmem(), smem()] + [vmem()] * (1 + S + C - 1),
        out_specs=[vmem()] * (S + C - 1),
        scratch_shapes=[
            pltpu.VMEM((clusters, panels), F32),
            pltpu.VMEM((L, whole(n)), F32),
            pltpu.VMEM((clusters, panels), F32),
            pltpu.VMEM((L, whole(n)), F32),
            pltpu.VMEM((4 * n, panels), F32),
            pltpu.VMEM((n * ROWS, L), F32),
            pltpu.VMEM((n * ROWS, LANES), F32),
            pltpu.VMEM((n * ROWS, LANES), F32),
            pltpu.SMEM((n + 1,), jnp.int32),
        ],
        compiler_params=PARAMS,
        name="near_remote",
    )(geometry, got_codes, acc, *pieces, *got_packs)
    parts, sums = made[:S], made[S:]
    near = []
    for d in range(S):
        for e in range(R):
            near.append(send(parts[d], (("sub", d), ("rep", e))) if d or e else parts[0])
    back = []
    for e in range(R):
        for d in range(1, C):
            back.append(send(sums[d - 1], (("clu", C - d), ("rep", e))))

    far = pl.pallas_call(
        functools.partial(down_kernel, C),
        out_shape=shape((clusters, L), F32),
        in_specs=[smem()] + [vmem()] * (4 + C),
        out_specs=vmem(),
        scratch_shapes=[pltpu.VMEM((C * par_dev, rank), F32), pltpu.VMEM((rank, clusters), F32)],
        compiler_params=PARAMS,
        name="far_down",
    )(far_list, coupling, transfer_t, parent, basis_t, *all_ups)

    return pl.pallas_call(
        functools.partial(final_kernel, (C, S, R, slots)),
        out_shape=shape((clusters, L), F32),
        in_specs=[smem()] * R + [vmem()] * (2 + S * R + R * (C - 1)),
        out_specs=vmem(),
        compiler_params=PARAMS,
        name="combine",
    )(*lists, panel_mask, far, *near, *back)


def solution(mesh):
    placed = (
        P(("grp", "clu"), "sub"),
        P(("grp", "clu"), "sub"),
        P(("grp", "clu"), None, None),
        P(("grp", "clu"), None, "rep"),
        P(("grp", "clu"), None, "rep"),
        P(("grp", "clu"), None, "rep"),
        P(("grp", "clu"), "rep", None),
        P(("grp", "clu"), "sub", None),
        P(("grp", "clu"), None, None),
        P(("grp", "clu")),
        P(("grp", "clu"), None),
        P(("grp", "clu"), None, None, None),
    )
    return jax.shard_map(
        on_device, mesh=mesh, in_specs=placed, out_specs=P(("grp", "clu"), "sub"), check_vma=False
    )
```

time: 213 us -> 85.4 us (0.40)
  other arithmetic: 81.8 us -> 0.59 us
  Pallas kernels: 0 us -> 47.1 us
  local copies, waits for them, and re-layouts: 41.9 us -> 3.21 us
  blocking collectives: 27.8 us -> 0 us
  between operations: 13.7 us -> 0.23 us
  starting transfers between devices: 16 us -> 28.3 us
  matrix products: 12.2 us -> 0 us
  waiting for transfers between devices: 17.2 us -> 5.27 us
    reduce_sum x20 -> x0, other arithmetic: 65.3 us -> none  [the longest x10 37.7 us: kernel_tile(): dist_sq = jnp.sum(delta * delta, axis=1)]
    pallas_call x0 -> x6, Pallas kernels: none -> 47.1 us  [the longest x1 25.2 us: on_device(): pl.pallas_call(functools.partial(local_kernel, (C, S, L, R, clusters, pan...]
    ppermute x0 -> x21, starting transfers between devices: none -> 28.3 us  [send(): return lax.ppermute(value, names if len(names) > 1 else names[0], perm)]
    all_gather x2 -> x0, blocking collectives: 18.8 us -> none  [the longest x1 13.9 us: on_device(): all_parents = lax.all_gather(parent_coeff, 'clu', axis=0, tiled=True)]
    psum x1 -> x0, waiting for transfers between devices: 16.1 us -> none  [on_device(): near = lax.psum(near_rows + cols_acc, 'rep')]
    all_to_all x3 -> x0, starting transfers between devices: 16 us -> none  [the longest x1 6.32 us: on_device(): lax.all_to_all(ask_ints, 'clu', split_axis=0, concat_axis=0, tiled=True)]
    gather x12 -> x0, local copies, waits for them, and re-layouts: 12.3 us -> none  [the longest x1 1.94 us: on_device(): geometry[local_a]]
    dot_general x6 -> x0, matrix products: 12.2 us -> none  [the longest x1 3.39 us: on_device(): jnp.einsum('pkrs,pks->pr', coupling, all_parents[far_list], precision=hig...]
  transfers between devices with their start and end apart: 5 -> 21, of which waited for: 2 -> 6; matrix products, arithmetic and copies ran while one was open for 58% -> 1% of each run, Pallas kernels for 0% -> 39%
where the time goes in v1:
time: 85.4 us; the launch traced here: 84.7 us
  Pallas kernels  47.1 us (55%)
  starting transfers between devices  28.3 us (33%)
  waiting for transfers between devices  5.27 us (6%)
  local copies, waits for them, and re-layouts  3.21 us (4%)
    ppermute x21, starting transfers between devices, send(): return lax.ppermute(value, names if len(names) > 1 else names[0], perm)  28.3 us
    pallas_call x1, Pallas kernels, on_device(): pl.pallas_call(functools.partial(local_kernel, (C, S, L, R, clusters, pan...  25.2 us
    pallas_call x1, Pallas kernels, on_device(): pl.pallas_call(functools.partial(remote_kernel, (C, S, L, slots, clusters...  10.5 us
    ppermute x21, waiting for transfers between devices, send(): return lax.ppermute(value, names if len(names) > 1 else names[0], perm)  5.27 us
    pallas_call x1, Pallas kernels, on_device(): pl.pallas_call(functools.partial(down_kernel, C), out_shape=shape((cluste...  4.36 us
    unnamed x49, local copies, waits for them, and re-layouts  3.21 us
    pallas_call x1, Pallas kernels, on_device(): pl.pallas_call(up_kernel, out_shape=shape((par_dev, rank), F32), in_specs...  3.1 us
    pallas_call x1, Pallas kernels, on_device(): pl.pallas_call(functools.partial(pack_kernel, (C, S, L, slots)), out_shap...  2.02 us
  transfers between devices with their start and end apart: 21, of which 6 were waited for; matrix products, arithmetic and copies ran while one was open for 1% of the time, Pallas kernels for 39%

profile of v1, /device:TPU:0, one launch (start us, length us, event | category | flops | bytes accessed | tf_op | source)
XLA Modules:
  0.0 84.7 jit_solution(10014013179240110924)
XLA Ops:
  0.0 2.0 %packs.1 = (f32[128,128]{1,0:T(8,128)}, s32[3,16]{1,0:T(4,128)}, f32[80,128]{1,0:T(8,128)}, f32[80,128]{1,0:T(8,128)}, f32[80,128]{1,0:T(8,128)}) custom-call(f32[128,128]{1,0:T(8,128)} %charges.1, s32[128,128]{1,0:T(8,128)} %rest_2_.1, f32[128,4,256]{2,1,0:T(4,128)} %geo.5, s32[4,16]{1,0:T(4,128)} %bitcast.13, s32[4,16]{1,0:T(4,128)} %bitcast.16, ...), custom_call_target="tpu_custom_call" | custom-call | tf_op jit(solution)/shard_map/packs/pallas_call | solution.py:446
  2.1 3.0 %collective-permute-start.1 = (f32[128,128]{1,0:T(8,128)}, f32[128,128]{1,0:T(8,128)S(1)}, u32[]{:S(2)}, u32[]{:S(2)}) collective-permute-start(f32[128,128]{1,0:T(8,128)} %get-tuple-element.17.masked.rest_0_), channel_id=1, source_target_pairs={{0,2},{2,0},{1,3},{3,1},{4,6},{6,4},{5,7},{7,5},{8,10},{10,8},{9,1... | collective-permute-start | bytes 196616 | tf_op jit(solution)/shard_map/ppermute | solution.py:417
  5.1 3.1 %far_up.1.rest_2_ = f32[16,32]{1,0:T(8,128)} custom-call(f32[128,32,128]{2,1,0:T(8,128)} %bitcast.9, f32[128,128]{1,0:T(8,128)} %get-tuple-element.17.masked.rest_0_, f32[32,32,128]{2,1,0:T(8,128)} %bitcast.11, s32[1,128]{1,0:T(1,128)} %bitcast.18), custom_call_target="tpu_custom_call" | custom-call | tf_op jit(solution)/shard_map/far_up/pallas_call | solution.py:461
  8.2 0.0 collective-permute-start.2
  8.2 2.1 %collective-permute-start.6 = (s32[1,16]{1,0:T(1,128)S(1)}, s32[1,16]{1,0:T(1,128)S(1)}, u32[]{:S(2)}, u32[]{:S(2)}) collective-permute-start(s32[1,16]{1,0:T(1,128)S(1)} %get-tuple-element.29), channel_id=1, source_target_pairs={{0,4},{4,8},{8,12},{12,0},{1,5},{5,9},{9,13},{13,1},{2,6},{6,10},{... | collective-permute-start | bytes 200 | tf_op jit(solution)/shard_map/ppermute | solution.py:417
  10.3 2.6 %collective-permute-start.7 = (s32[1,16]{1,0:T(1,128)S(1)}, s32[1,16]{1,0:T(1,128)S(1)}, u32[]{:S(2)}, u32[]{:S(2)}) collective-permute-start(s32[1,16]{1,0:T(1,128)S(1)} %get-tuple-element.31), channel_id=1, source_target_pairs={{0,8},{4,12},{8,0},{12,4},{1,9},{5,13},{9,1},{13,5},{2,10},{6,14},... | collective-permute-start | bytes 200 | tf_op jit(solution)/shard_map/ppermute | solution.py:417
  12.9 1.3 %collective-permute-start.8 = (s32[1,16]{1,0:T(1,128)S(1)}, s32[1,16]{1,0:T(1,128)S(1)}, u32[]{:S(2)}, u32[]{:S(2)}) collective-permute-start(s32[1,16]{1,0:T(1,128)S(1)} %get-tuple-element.30), channel_id=1, source_target_pairs={{0,12},{4,0},{8,4},{12,8},{1,13},{5,1},{9,5},{13,9},{2,14},{6,2},{... | collective-permute-start | bytes 200 | tf_op jit(solution)/shard_map/ppermute | solution.py:417
  14.2 0.0 collective-permute-done.6
  14.2 0.6 collective-permute-start.10
  14.9 0.0 collective-permute-done.7
  14.9 2.4 %collective-permute-start.11 = (f32[80,128]{1,0:T(8,128)S(1)}, f32[80,128]{1,0:T(8,128)S(1)}, u32[]{:S(2)}, u32[]{:S(2)}) collective-permute-start(f32[80,128]{1,0:T(8,128)S(1)} %copy-done.22), channel_id=1, source_target_pairs={{0,12},{4,0},{8,4},{12,8},{1,13},{5,1},{9,5},{13,9},{2,14},{6,2},{... | collective-permute-start | bytes 122888 | tf_op jit(solution)/shard_map/ppermute | solution.py:417
  17.3 0.0 collective-permute-done.8
  17.3 0.6 pad_add_fusion.codes
  17.9 0.0 collective-permute-done.1.rest_1_
  17.9 0.6 copy-done.10
  18.5 0.0 copy-done
  18.5 25.2 %near_local.1 = (f32[128,256]{1,0:T(8,128)}, f32[16,32]{1,0:T(8,128)}) custom-call(f32[128,4,256]{2,1,0:T(4,128)} %geo.5, s32[2,128]{1,0:T(2,128)} %bitcast.20, f32[128,128]{1,0:T(8,128)} %get-tuple-element.17.masked.rest_0_, f32[128,128]{1,0:T(8,128)} %copy-done, f32[16,32]{1,0:T(8,128)} %far_up.1.rest_2_, f32[16,32]{1,0:T(8,128)} %copy-done.10), custom_call_target="tpu_custom_call" | custom-call | tf_op jit(solution)/shard_map/near_local/pallas_call | solution.py:472
  43.7 0.0 collective-permute-done.10.rest_3_
  43.7 0.0 collective-permute-done.9.rest_2_
  43.7 0.6 copy-done.4
  44.3 0.0 copy-done.5
  44.3 0.0 copy-done.6
  44.4 10.5 %near_remote.1 = (f32[128,128]{1,0:T(8,128)}, f32[128,128]{1,0:T(8,128)}, f32[16,128]{1,0:T(8,128)}, f32[16,128]{1,0:T(8,128)}, f32[16,128]{1,0:T(8,128)}) custom-call(f32[128,4,256]{2,1,0:T(4,128)} %geo.5, s32[3,16]{1,0:T(4,128)} %pad_add_fusion.codes, f32[128,256]{1,0:T(8,128)} %get-tuple-element.20.acc_in, f32[128,128]{1,0:T(8,128)} %get-tuple-element.17.masked.rest_0_, ...), custom_call_target="tpu_custom_call" | custom-call | tf_op jit(solution)/shard_map/near_remote/pallas_call | solution.py:491
  54.8 1.6 %collective-permute-start.13 = (f32[128,128]{1,0:T(8,128)}, f32[128,128]{1,0:T(8,128)S(1)}, u32[]{:S(2)}, u32[]{:S(2)}) collective-permute-start(f32[128,128]{1,0:T(8,128)} %get-tuple-element.25), channel_id=1, source_target_pairs={{0,2},{1,3},{2,0},{3,1},{4,6},{5,7},{6,4},{7,5},{8,10},{9,11},{10,... | collective-permute-start | bytes 196616 | tf_op jit(solution)/shard_map/ppermute | solution.py:417
  56.4 0.3 collective-permute-start.14
  56.7 1.2 %collective-permute-start.3 = (f32[16,32]{1,0:T(8,128)}, f32[16,32]{1,0:T(8,128)S(1)}, u32[]{:S(2)}, u32[]{:S(2)}) collective-permute-start(f32[16,32]{1,0:T(8,128)} %get-tuple-element.18.rest_0_), channel_id=1, source_target_pairs={{0,4},{4,8},{8,12},{12,0},{1,5},{5,9},{9,13},{13,1},{2,6},{6,10},{... | collective-permute-start | bytes 6152 | tf_op jit(solution)/shard_map/ppermute | solution.py:417
  57.8 0.1 collective-permute-start
  57.9 1.1 %collective-permute-done.rest_1_ = s32[4,16]{1,0:T(4,128)S(1)} collective-permute-done((s32[4,16]{1,0:T(4,128)S(1)}, s32[4,16]{1,0:T(4,128)S(1)}, u32[]{:S(2)}, u32[]{:S(2)}) %collective-permute-start) | collective-permute-done | bytes 288 | tf_op jit(solution)/shard_map/ppermute | solution.py:417
  59.0 3.2 %collective-permute-start.4 = (f32[16,32]{1,0:T(8,128)}, f32[16,32]{1,0:T(8,128)S(1)}, u32[]{:S(2)}, u32[]{:S(2)}) collective-permute-start(f32[16,32]{1,0:T(8,128)} %get-tuple-element.18.rest_0_), channel_id=1, source_target_pairs={{0,8},{4,12},{8,0},{12,4},{1,9},{5,13},{9,1},{13,5},{2,10},{6,14},... | collective-permute-start | bytes 6152 | tf_op jit(solution)/shard_map/ppermute | solution.py:417
  62.2 0.1 collective-permute-done.3.rest_1_
  62.3 2.0 %collective-permute-start.5 = (f32[16,32]{1,0:T(8,128)}, f32[16,32]{1,0:T(8,128)S(1)}, u32[]{:S(2)}, u32[]{:S(2)}) collective-permute-start(f32[16,32]{1,0:T(8,128)} %get-tuple-element.18.rest_0_), channel_id=1, source_target_pairs={{0,12},{4,0},{8,4},{12,8},{1,13},{5,1},{9,5},{13,9},{2,14},{6,2},{... | collective-permute-start | bytes 6152 | tf_op jit(solution)/shard_map/ppermute | solution.py:417
  64.4 2.1 %collective-permute-start.15 = (f32[16,128]{1,0:T(8,128)}, f32[16,128]{1,0:T(8,128)S(1)}, u32[]{:S(2)}, u32[]{:S(2)}) collective-permute-start(f32[16,128]{1,0:T(8,128)} %get-tuple-element.26), channel_id=1, source_target_pairs={{0,12},{1,13},{4,0},{5,1},{8,4},{9,5},{12,8},{13,9},{2,14},{3,15},... | collective-permute-start | bytes 24584 | tf_op jit(solution)/shard_map/ppermute | solution.py:417
  66.4 1.0 %collective-permute-start.16 = (f32[16,128]{1,0:T(8,128)}, f32[16,128]{1,0:T(8,128)S(1)}, u32[]{:S(2)}, u32[]{:S(2)}) collective-permute-start(f32[16,128]{1,0:T(8,128)} %get-tuple-element.27), channel_id=1, source_target_pairs={{0,8},{1,9},{4,12},{5,13},{8,0},{9,1},{12,4},{13,5},{2,10},{3,11},... | collective-permute-start | bytes 24584 | tf_op jit(solution)/shard_map/ppermute | solution.py:417
  67.5 0.8 collective-permute-done.15.rest_8_
  68.2 2.4 %collective-permute-start.17 = (f32[16,128]{1,0:T(8,128)}, f32[16,128]{1,0:T(8,128)S(1)}, u32[]{:S(2)}, u32[]{:S(2)}) collective-permute-start(f32[16,128]{1,0:T(8,128)} %get-tuple-element.28), channel_id=1, source_target_pairs={{0,4},{1,5},{4,8},{5,9},{8,12},{9,13},{12,0},{13,1},{2,6},{3,7},{6... | collective-permute-start | bytes 24584 | tf_op jit(solution)/shard_map/ppermute | solution.py:417
  70.6 0.6 collective-permute-done.16.rest_9_
  71.2 0.6 collective-permute-start.18
  71.8 2.1 %collective-permute-done.17.rest_10_ = f32[16,128]{1,0:T(8,128)S(1)} collective-permute-done((f32[16,128]{1,0:T(8,128)}, f32[16,128]{1,0:T(8,128)S(1)}, u32[]{:S(2)}, u32[]{:S(2)}) %collective-permute-start.17) | collective-permute-done | bytes 8224 | tf_op jit(solution)/shard_map/ppermute | solution.py:417
  73.9 0.5 collective-permute-done.18.rest_11_
  74.5 1.8 %collective-permute-start.20 = (f32[16,128]{1,0:T(8,128)}, f32[16,128]{1,0:T(8,128)S(1)}, u32[]{:S(2)}, u32[]{:S(2)}) collective-permute-start(f32[16,128]{1,0:T(8,128)} %get-tuple-element.28), channel_id=1, source_target_pairs={{0,5},{1,4},{4,9},{5,8},{8,13},{9,12},{12,1},{13,0},{2,7},{3,6},{6... | collective-permute-start | bytes 24584 | tf_op jit(solution)/shard_map/ppermute | solution.py:417
  76.2 0.7 copy.13.far_list
  76.9 4.4 %far_down.1.rest_3_ = f32[128,128]{1,0:T(8,128)} custom-call(s32[16,8]{1,0:T(8,128)} %copy.13.far_list, f32[16,8,32,32]{3,2,1,0:T(8,128)} %coupling.1, f32[32,32,128]{2,1,0:T(8,128)} %bitcast.12, s32[1,128]{1,0:T(1,128)} %bitcast.19, f32[128,32,128]{2,1,0:T(8,128)} %bitcast.10, f32[16,32]{1,0:T(8,128)} %get-tuple-element.18.rest_0_, f32[16,32]{1,0:T(8,128)} %copy-done.8, ...), custom_call_target="tpu_custom_call" | custom-call | tf_op jit(solution)/shard_map/far_down/pallas_call | solution.py:520
  81.4 0.5 copy-done.15
  81.9 0.0 copy-done.16
  81.9 0.1 copy-done.1
  82.0 0.0 copy-done.2
  82.0 0.6 copy-done.3
  82.7 2.0 %combine.1 = f32[128,128]{1,0:T(8,128)} custom-call(s32[4,16]{1,0:T(4,128)} %bitcast.14, s32[4,16]{1,0:T(4,128)} %copy-done.19, s32[128,128]{1,0:T(8,128)} %rest_2_.1, f32[128,128]{1,0:T(8,128)} %far_down.1.rest_3_, f32[128,128]{1,0:T(8,128)} %get-tuple-element.24.rest_4_, f32[128,128]{1,0:T(8,128)} %copy-done.1, f32[128,128]{1,0:T(8,128)} %copy-done.2, ...), custom_call_target="tpu_custom_call" | custom-call | tf_op jit(solution)/shard_map/combine/pallas_call | solution.py:530
  (51 shorter events, 0.1 us)
Async XLA Ops:
  2.0 6.2 %copy-start.20 = (s32[3,16]{1,0:T(4,128)S(1)}, s32[3,16]{1,0:T(4,128)}, u32[]{:S(2)}) copy-start(s32[3,16]{1,0:T(4,128)} %get-tuple-element.19) | copy-start | bytes 580
  2.0 12.2 %copy-start.23 = (f32[80,128]{1,0:T(8,128)S(1)}, f32[80,128]{1,0:T(8,128)}, u32[]{:S(2)}) copy-start(f32[80,128]{1,0:T(8,128)} %get-tuple-element.22) | copy-start | bytes 122884
  2.0 12.8 %copy-start.22 = (f32[80,128]{1,0:T(8,128)S(1)}, f32[80,128]{1,0:T(8,128)}, u32[]{:S(2)}) copy-start(f32[80,128]{1,0:T(8,128)} %get-tuple-element.23) | copy-start | bytes 122884
  2.1 15.2 %copy-start.21 = (f32[80,128]{1,0:T(8,128)S(1)}, f32[80,128]{1,0:T(8,128)}, u32[]{:S(2)}) copy-start(f32[80,128]{1,0:T(8,128)} %get-tuple-element.21) | copy-start | bytes 122884
  2.1 15.8 %collective-permute-start.1 = (f32[128,128]{1,0:T(8,128)}, f32[128,128]{1,0:T(8,128)S(1)}, u32[]{:S(2)}, u32[]{:S(2)}) collective-permute-start(f32[128,128]{1,0:T(8,128)} %get-tuple-element.17.masked.rest_0_), channel_id=1, source_target_pairs={{0,2},{2,0},{1,3},{3,1},{4,6},{6,4},{5,7},{7,5},{8,10},{10,8},{9,1... | collective-permute-start | bytes 196616 | tf_op jit(solution)/shard_map/ppermute | solution.py:417
  5.1 52.8 %copy-start.17 = (s32[1,4,16]{2,1,0:T(4,128)S(1)}, s32[1,4,16]{2,1,0:T(4,128)}, u32[]{:S(2)}) copy-start(s32[1,4,16]{2,1,0:T(4,128)} %param.16) | copy-start | bytes 772
  5.1 71.2 %copy-start.18 = (s32[16,8]{0,1:T(8,128)S(1)}, s32[16,8]{0,1:T(8,128)}, u32[]{:S(2)}) copy-start(s32[16,8]{0,1:T(8,128)} %param.22) | copy-start | bytes 1540
  8.2 9.7 %collective-permute-start.2 = (f32[16,32]{1,0:T(8,128)}, f32[16,32]{1,0:T(8,128)S(1)}, u32[]{:S(2)}, u32[]{:S(2)}) collective-permute-start(f32[16,32]{1,0:T(8,128)} %far_up.1.rest_2_), channel_id=1, source_target_pairs={{0,2},{2,0},{1,3},{3,1},{4,6},{6,4},{5,7},{7,5},{8,10},{10,8},{9,1... | collective-permute-start | bytes 6152 | tf_op jit(solution)/shard_map/ppermute | solution.py:417
  8.2 6.0 %collective-permute-start.6 = (s32[1,16]{1,0:T(1,128)S(1)}, s32[1,16]{1,0:T(1,128)S(1)}, u32[]{:S(2)}, u32[]{:S(2)}) collective-permute-start(s32[1,16]{1,0:T(1,128)S(1)} %get-tuple-element.29), channel_id=1, source_target_pairs={{0,4},{4,8},{8,12},{12,0},{1,5},{5,9},{9,13},{13,1},{2,6},{6,10},{... | collective-permute-start | bytes 200 | tf_op jit(solution)/shard_map/ppermute | solution.py:417
  10.3 4.6 %collective-permute-start.7 = (s32[1,16]{1,0:T(1,128)S(1)}, s32[1,16]{1,0:T(1,128)S(1)}, u32[]{:S(2)}, u32[]{:S(2)}) collective-permute-start(s32[1,16]{1,0:T(1,128)S(1)} %get-tuple-element.31), channel_id=1, source_target_pairs={{0,8},{4,12},{8,0},{12,4},{1,9},{5,13},{9,1},{13,5},{2,10},{6,14},... | collective-permute-start | bytes 200 | tf_op jit(solution)/shard_map/ppermute | solution.py:417
  12.9 4.4 %collective-permute-start.8 = (s32[1,16]{1,0:T(1,128)S(1)}, s32[1,16]{1,0:T(1,128)S(1)}, u32[]{:S(2)}, u32[]{:S(2)}) collective-permute-start(s32[1,16]{1,0:T(1,128)S(1)} %get-tuple-element.30), channel_id=1, source_target_pairs={{0,12},{4,0},{8,4},{12,8},{1,13},{5,1},{9,5},{13,9},{2,14},{6,2},{... | collective-permute-start | bytes 200 | tf_op jit(solution)/shard_map/ppermute | solution.py:417
  14.2 29.5 %collective-permute-start.10 = (f32[80,128]{1,0:T(8,128)S(1)}, f32[80,128]{1,0:T(8,128)S(1)}, u32[]{:S(2)}, u32[]{:S(2)}) collective-permute-start(f32[80,128]{1,0:T(8,128)S(1)} %copy-done.23), channel_id=1, source_target_pairs={{0,8},{4,12},{8,0},{12,4},{1,9},{5,13},{9,1},{13,5},{2,10},{6,14},... | collective-permute-start | bytes 122888 | tf_op jit(solution)/shard_map/ppermute | solution.py:417
  14.9 28.9 %collective-permute-start.11 = (f32[80,128]{1,0:T(8,128)S(1)}, f32[80,128]{1,0:T(8,128)S(1)}, u32[]{:S(2)}, u32[]{:S(2)}) collective-permute-start(f32[80,128]{1,0:T(8,128)S(1)} %copy-done.22), channel_id=1, source_target_pairs={{0,12},{4,0},{8,4},{12,8},{1,13},{5,1},{9,5},{13,9},{2,14},{6,2},{... | collective-permute-start | bytes 122888 | tf_op jit(solution)/shard_map/ppermute | solution.py:417
  17.3 26.4 %collective-permute-start.9 = (f32[80,128]{1,0:T(8,128)S(1)}, f32[80,128]{1,0:T(8,128)S(1)}, u32[]{:S(2)}, u32[]{:S(2)}) collective-permute-start(f32[80,128]{1,0:T(8,128)S(1)} %copy-done.21), channel_id=1, source_target_pairs={{0,4},{4,8},{8,12},{12,0},{1,5},{5,9},{9,13},{13,1},{2,6},{6,10},{... | collective-permute-start | bytes 122888 | tf_op jit(solution)/shard_map/ppermute | solution.py:417
  17.9 0.6 copy-start.10
  17.9 0.6 copy-start
  43.7 0.6 copy-start.4
  43.7 0.6 copy-start.5
  43.7 0.6 copy-start.6
  54.8 26.6 %collective-permute-start.12 = (f32[128,128]{1,0:T(8,128)}, f32[128,128]{1,0:T(8,128)S(1)}, u32[]{:S(2)}, u32[]{:S(2)}) collective-permute-start(f32[128,128]{1,0:T(8,128)} %get-tuple-element.24.rest_4_), channel_id=1, source_target_pairs={{0,1},{1,0},{2,3},{3,2},{4,5},{5,4},{6,7},{7,6},{8,9},{9,8},{10,11... | collective-permute-start | bytes 196616 | tf_op jit(solution)/shard_map/ppermute | solution.py:417
  54.8 26.6 %collective-permute-start.13 = (f32[128,128]{1,0:T(8,128)}, f32[128,128]{1,0:T(8,128)S(1)}, u32[]{:S(2)}, u32[]{:S(2)}) collective-permute-start(f32[128,128]{1,0:T(8,128)} %get-tuple-element.25), channel_id=1, source_target_pairs={{0,2},{1,3},{2,0},{3,1},{4,6},{5,7},{6,4},{7,5},{8,10},{9,11},{10,... | collective-permute-start | bytes 196616 | tf_op jit(solution)/shard_map/ppermute | solution.py:417
  56.4 25.0 %collective-permute-start.14 = (f32[128,128]{1,0:T(8,128)}, f32[128,128]{1,0:T(8,128)S(1)}, u32[]{:S(2)}, u32[]{:S(2)}) collective-permute-start(f32[128,128]{1,0:T(8,128)} %get-tuple-element.25), channel_id=1, source_target_pairs={{0,3},{1,2},{2,1},{3,0},{4,7},{5,6},{6,5},{7,4},{8,11},{9,10},{10,... | collective-permute-start | bytes 196616 | tf_op jit(solution)/shard_map/ppermute | solution.py:417
  56.7 5.7 %collective-permute-start.3 = (f32[16,32]{1,0:T(8,128)}, f32[16,32]{1,0:T(8,128)S(1)}, u32[]{:S(2)}, u32[]{:S(2)}) collective-permute-start(f32[16,32]{1,0:T(8,128)} %get-tuple-element.18.rest_0_), channel_id=1, source_target_pairs={{0,4},{4,8},{8,12},{12,0},{1,5},{5,9},{9,13},{13,1},{2,6},{6,10},{... | collective-permute-start | bytes 6152 | tf_op jit(solution)/shard_map/ppermute | solution.py:417
  57.8 1.2 %collective-permute-start = (s32[4,16]{1,0:T(4,128)S(1)}, s32[4,16]{1,0:T(4,128)S(1)}, u32[]{:S(2)}, u32[]{:S(2)}) collective-permute-start(s32[4,16]{1,0:T(4,128)S(1)} %bitcast.15), channel_id=1, source_target_pairs={{0,1},{1,0},{2,3},{3,2},{4,5},{5,4},{6,7},{7,6},{8,9},{9,8},{10,11... | collective-permute-start | bytes 776 | tf_op jit(solution)/shard_map/ppermute | solution.py:417
  59.0 22.4 %copy-start.19 = (s32[4,16]{1,0:T(4,128)}, s32[4,16]{1,0:T(4,128)S(1)}, u32[]{:S(2)}) copy-start(s32[4,16]{1,0:T(4,128)S(1)} %collective-permute-done.rest_1_) | copy-start | bytes 772
  59.0 5.4 %collective-permute-start.4 = (f32[16,32]{1,0:T(8,128)}, f32[16,32]{1,0:T(8,128)S(1)}, u32[]{:S(2)}, u32[]{:S(2)}) collective-permute-start(f32[16,32]{1,0:T(8,128)} %get-tuple-element.18.rest_0_), channel_id=1, source_target_pairs={{0,8},{4,12},{8,0},{12,4},{1,9},{5,13},{9,1},{13,5},{2,10},{6,14},... | collective-permute-start | bytes 6152 | tf_op jit(solution)/shard_map/ppermute | solution.py:417
  62.3 14.6 %copy-start.8 = (f32[16,32]{1,0:T(8,128)}, f32[16,32]{1,0:T(8,128)S(1)}, u32[]{:S(2)}) copy-start(f32[16,32]{1,0:T(8,128)S(1)} %collective-permute-done.3.rest_1_) | copy-start | bytes 6148
  62.3 4.1 %collective-permute-start.5 = (f32[16,32]{1,0:T(8,128)}, f32[16,32]{1,0:T(8,128)S(1)}, u32[]{:S(2)}, u32[]{:S(2)}) collective-permute-start(f32[16,32]{1,0:T(8,128)} %get-tuple-element.18.rest_0_), channel_id=1, source_target_pairs={{0,12},{4,0},{8,4},{12,8},{1,13},{5,1},{9,5},{13,9},{2,14},{6,2},{... | collective-permute-start | bytes 6152 | tf_op jit(solution)/shard_map/ppermute | solution.py:417
  64.4 12.6 %copy-start.11 = (f32[16,32]{1,0:T(8,128)}, f32[16,32]{1,0:T(8,128)S(1)}, u32[]{:S(2)}) copy-start(f32[16,32]{1,0:T(8,128)S(1)} %collective-permute-done.4.rest_2_) | copy-start | bytes 6148
  64.4 3.9 %collective-permute-start.15 = (f32[16,128]{1,0:T(8,128)}, f32[16,128]{1,0:T(8,128)S(1)}, u32[]{:S(2)}, u32[]{:S(2)}) collective-permute-start(f32[16,128]{1,0:T(8,128)} %get-tuple-element.26), channel_id=1, source_target_pairs={{0,12},{1,13},{4,0},{5,1},{8,4},{9,5},{12,8},{13,9},{2,14},{3,15},... | collective-permute-start | bytes 24584 | tf_op jit(solution)/shard_map/ppermute | solution.py:417
  66.4 10.5 %copy-start.13 = (f32[16,32]{1,0:T(8,128)}, f32[16,32]{1,0:T(8,128)S(1)}, u32[]{:S(2)}) copy-start(f32[16,32]{1,0:T(8,128)S(1)} %collective-permute-done.5.rest_3_) | copy-start | bytes 6148
  66.4 4.8 %collective-permute-start.16 = (f32[16,128]{1,0:T(8,128)}, f32[16,128]{1,0:T(8,128)S(1)}, u32[]{:S(2)}, u32[]{:S(2)}) collective-permute-start(f32[16,128]{1,0:T(8,128)} %get-tuple-element.27), channel_id=1, source_target_pairs={{0,8},{1,9},{4,12},{5,13},{8,0},{9,1},{12,4},{13,5},{2,10},{3,11},... | collective-permute-start | bytes 24584 | tf_op jit(solution)/shard_map/ppermute | solution.py:417
  68.2 13.1 %copy-start.7 = (f32[16,128]{1,0:T(8,128)}, f32[16,128]{1,0:T(8,128)S(1)}, u32[]{:S(2)}) copy-start(f32[16,128]{1,0:T(8,128)S(1)} %collective-permute-done.15.rest_8_) | copy-start | bytes 24580
  68.2 5.7 %collective-permute-start.17 = (f32[16,128]{1,0:T(8,128)}, f32[16,128]{1,0:T(8,128)S(1)}, u32[]{:S(2)}, u32[]{:S(2)}) collective-permute-start(f32[16,128]{1,0:T(8,128)} %get-tuple-element.28), channel_id=1, source_target_pairs={{0,4},{1,5},{4,8},{5,9},{8,12},{9,13},{12,0},{13,1},{2,6},{3,7},{6... | collective-permute-start | bytes 24584 | tf_op jit(solution)/shard_map/ppermute | solution.py:417
  71.2 10.1 %copy-start.9 = (f32[16,128]{1,0:T(8,128)}, f32[16,128]{1,0:T(8,128)S(1)}, u32[]{:S(2)}) copy-start(f32[16,128]{1,0:T(8,128)S(1)} %collective-permute-done.16.rest_9_) | copy-start | bytes 24580
  71.2 3.3 %collective-permute-start.18 = (f32[16,128]{1,0:T(8,128)}, f32[16,128]{1,0:T(8,128)S(1)}, u32[]{:S(2)}, u32[]{:S(2)}) collective-permute-start(f32[16,128]{1,0:T(8,128)} %get-tuple-element.26), channel_id=1, source_target_pairs={{0,13},{1,12},{4,1},{5,0},{8,5},{9,4},{12,9},{13,8},{2,15},{3,14},... | collective-permute-start | bytes 24584 | tf_op jit(solution)/shard_map/ppermute | solution.py:417
  73.9 7.4 %copy-start.12 = (f32[16,128]{1,0:T(8,128)}, f32[16,128]{1,0:T(8,128)S(1)}, u32[]{:S(2)}) copy-start(f32[16,128]{1,0:T(8,128)S(1)} %collective-permute-done.17.rest_10_) | copy-start | bytes 24580
  73.9 7.4 %collective-permute-start.19 = (f32[16,128]{1,0:T(8,128)}, f32[16,128]{1,0:T(8,128)S(1)}, u32[]{:S(2)}, u32[]{:S(2)}) collective-permute-start(f32[16,128]{1,0:T(8,128)} %get-tuple-element.27), channel_id=1, source_target_pairs={{0,9},{1,8},{4,13},{5,12},{8,1},{9,0},{12,5},{13,4},{2,11},{3,10},... | collective-permute-start | bytes 24584 | tf_op jit(solution)/shard_map/ppermute | solution.py:417
  74.5 6.8 %copy-start.14 = (f32[16,128]{1,0:T(8,128)}, f32[16,128]{1,0:T(8,128)S(1)}, u32[]{:S(2)}) copy-start(f32[16,128]{1,0:T(8,128)S(1)} %collective-permute-done.18.rest_11_) | copy-start | bytes 24580
  74.5 6.9 %collective-permute-start.20 = (f32[16,128]{1,0:T(8,128)}, f32[16,128]{1,0:T(8,128)S(1)}, u32[]{:S(2)}, u32[]{:S(2)}) collective-permute-start(f32[16,128]{1,0:T(8,128)} %get-tuple-element.28), channel_id=1, source_target_pairs={{0,5},{1,4},{4,9},{5,8},{8,13},{9,12},{12,1},{13,0},{2,7},{3,6},{6... | collective-permute-start | bytes 24584 | tf_op jit(solution)/shard_map/ppermute | solution.py:417
  81.3 0.6 copy-start.15
  81.3 0.6 copy-start.16
  81.4 0.6 copy-start.1
  81.4 0.6 copy-start.2
  82.0 0.6 copy-start.3

commit v2 on v1

v2 whole, which is shorter than its diff:
```python
import functools

import jax
import jax.numpy as jnp
from jax import lax
from jax.experimental import pallas as pl
from jax.experimental.pallas import tpu as pltpu
from jax.sharding import PartitionSpec as P

F32 = jnp.float32
BF16 = jnp.bfloat16
HIGHEST = lax.Precision.HIGHEST
ROWS = 40
USED = 34
LANES = 128
PARAMS = pltpu.CompilerParams(vmem_limit_bytes=56 * 1024 * 1024)


def vmem():
    return pl.BlockSpec(memory_space=pltpu.VMEM)


def smem():
    return pl.BlockSpec(memory_space=pltpu.SMEM)


def whole(size):
    return -(-size // LANES) * LANES


def cut(v):
    return v.astype(BF16).astype(F32)


def powers(sign):
    lane = lax.broadcasted_iota(jnp.int32, (8, LANES), 1)
    out = jnp.full((8, LANES), 2.0 ** (-64 * sign), F32)
    for bit in range(7):
        out = out * jnp.where((lane >> bit) & 1 == 1, F32(2.0 ** (sign * 2**bit)), F32(1.0))
    return out


def frame(parts):
    low = [functools.reduce(jnp.minimum, [jnp.min(p[k]) for p in parts]) for k in range(3)]
    high = [functools.reduce(jnp.maximum, [jnp.max(p[k]) for p in parts]) for k in range(3)]
    width = functools.reduce(jnp.maximum, [jnp.max(jnp.abs(p[3])) for p in parts])
    for lo, hi in zip(low, high):
        width = jnp.maximum(width, 0.5 * (hi - lo))
    up, down = powers(1), powers(-1)
    size = jnp.min(jnp.where(up >= width, up, F32(2.0**63)))
    inv = jnp.max(jnp.where(up >= width, down, F32(2.0**-63)))
    magic = size * F32(1.5 * 2.0**20)
    centre = [(0.5 * (lo + hi) + magic) - magic for lo, hi in zip(low, high)]
    return centre, inv


def split_features(points, centre, inv):
    magic = F32(1.5 * 2.0**16)
    grid, rest = [], []
    for k in range(3):
        u = (points[k] - centre[k]) * inv
        h = (u + magic) - magic
        grid.append(h)
        rest.append(u - h)
    rad = points[3] * inv
    norm = grid[0] * grid[0] + grid[1] * grid[1] + grid[2] * grid[2]
    norm1 = cut(norm)
    norm2 = norm - norm1
    cross = grid[0] * rest[0] + grid[1] * rest[1] + grid[2] * rest[2]
    extra = 2.0 * cross + (rest[0] * rest[0] + rest[1] * rest[1] + rest[2] * rest[2]) + rad * rad
    extra1 = cut(extra)
    extra2 = cut(extra - extra1)
    extra3 = (extra - extra1) - extra2
    rest1 = [cut(v) for v in rest]
    rest2 = [v - w for v, w in zip(rest, rest1)]
    neg = lambda vs: [-2.0 * v for v in vs]
    one = jnp.ones_like(rad)
    left = grid + [norm1, norm2, one, one]
    right = neg(grid) + [one, one, norm1, norm2]
    left += [extra1, extra2, extra3, one, one, one]
    right += [one, one, one, extra1, extra2, extra3]
    left += grid + grid + rest1 + rest2 + rest1 + rest1 + rest2
    right += neg(rest1) + neg(rest2) + neg(grid) + neg(grid) + neg(rest1) + neg(rest2) + neg(rest1)
    return left, right, rad


def store_features(ref, rows):
    count = rows[0].shape[0]
    width = rows[0].shape[1]
    for k, row in enumerate(rows):
        for t, piece in enumerate(ref):
            piece[pl.ds(k, count, stride=ROWS), :] = row[:, t * LANES : min(width, (t + 1) * LANES)]


def load_features(ref, index):
    start = pl.multiple_of(index * ROWS, 8)
    return [piece[pl.ds(start, USED), :].astype(BF16) for piece in ref]


def contract(left, right):
    return lax.dot_general(left, right, (((0,), (0,)), ((), ())), preferred_element_type=F32)


def column(table, index):
    if table.shape[1] == LANES and table.shape[0] % 8 == 0:
        return jnp.take_along_axis(table, jnp.full(table.shape, index, jnp.int32), axis=1)
    lane = lax.broadcasted_iota(jnp.int32, table.shape, 1)
    picked = jnp.sum(jnp.where(lane == index, table, 0.0), axis=1, keepdims=True)
    return jnp.broadcast_to(picked, (table.shape[0], LANES))


def put_column(table_ref, rows, index, value):
    lane = lax.broadcasted_iota(jnp.int32, (rows.stop - rows.start, table_ref.shape[1]), 1)
    table_ref[rows, :] += jnp.where(lane == index, value, 0.0)


def fold(v):
    return jnp.sum(v.reshape(v.shape[0] // 8, 8, v.shape[1]), axis=0)


def distances(left, right, out):
    whole_left = jnp.concatenate(left, axis=1) if len(left) > 1 else left[0]
    for t, r in enumerate(right):
        out[:, t * LANES : (t + 1) * LANES] = contract(whole_left, r)


def tile_sums(dist, qrow, qtable, slot, table_ref, index, step=64):
    height = dist.shape[0]
    step = min(step, height)
    q0, q1 = qrow[:, :LANES], qrow[:, LANES:]
    back0 = back1 = jnp.zeros((8, LANES), F32)
    for r in range(0, height, step):
        rows = slice(r, r + step)
        g0 = lax.rsqrt(dist[rows, :LANES])
        g1 = lax.rsqrt(dist[rows, LANES:])
        qcol = column(qtable[rows, :], slot)
        put_column(table_ref, rows, index, jnp.sum(g0 * q0 + g1 * q1, axis=1, keepdims=True))
        back0 = back0 + fold(g0 * qcol)
        back1 = back1 + fold(g1 * qcol)
    return jnp.concatenate(
        [jnp.sum(back0, axis=0, keepdims=True), jnp.sum(back1, axis=0, keepdims=True)], axis=1
    )


def assemble(sub, S, L, q, pieces):
    def place(s):
        for shift in range(S):
            owner = (s - shift) % S
            q[:, owner * L : (owner + 1) * L] = pieces[shift][...]

    for s in range(S):
        pl.when(sub == s)(functools.partial(place, s))


def pack_kernel(sizes, charges, mask, geo, targets, sources, live, masked, *packs):
    C, S, L, slots = sizes
    me, sub = lax.axis_index("clu"), lax.axis_index("sub")
    masked[...] = charges[...] * mask[...].astype(F32)
    lane = lax.broadcasted_iota(jnp.int32, (8, L), 1)
    for shift in range(1, C):
        dest = lax.rem(me + shift, C)
        codes = jnp.full((8, L), -1.0, F32)
        for j in range(slots):
            code = jnp.where(live[dest, j] > 0, sources[dest, j], -1)
            codes = jnp.where(lane == j, code.astype(F32), codes)
        packs[shift - 1][5 * slots :, :] = codes

    def fill(s):
        for shift in range(1, C):
            dest = lax.rem(me + shift, C)
            pack = packs[shift - 1]
            for j in range(slots):
                t = targets[dest, j]
                g = geo[t, :, s * L : (s + 1) * L]
                for k in range(4):
                    pack[k * slots + j : k * slots + j + 1, :] = g[k : k + 1]
                pack[4 * slots + j : 4 * slots + j + 1, :] = masked[pl.ds(t, 1), :]

    for s in range(S):
        pl.when(sub == s)(functools.partial(fill, s))


def remote_kernel(sizes, geo, codes, up, *rest):
    C, S, L, slots, clusters, panels = sizes
    pieces = rest[:S]
    packs = rest[S : S + C - 1]
    acc_out = rest[S + C - 1]
    sends = rest[S + C : S + C + C - 1]
    q, tqt, acc, fwdt, sgeo, fa0, fb0, fb1, dist0, dist1, order = rest[S + C + C - 1 :]
    fa, fb = (fa0,), (fb0, fb1)
    n = (C - 1) * slots
    assemble(lax.axis_index("sub"), S, L, q, pieces)
    acc[...] = jnp.zeros_like(acc)
    fwdt[...] = jnp.zeros_like(fwdt)
    found = jnp.int32(0)
    for shift in range(C - 1):
        for j in range(slots):
            code = codes[shift, j]
            order[found] = shift * slots + j
            found = found + (code >= 0).astype(jnp.int32)
            g = geo[jnp.maximum(code, 0)]
            for k in range(4):
                row = k * n + shift * slots + j
                sgeo[row : row + 1, :] = g[k : k + 1]
    tpoints = [
        jnp.concatenate([p[k * slots : (k + 1) * slots, :] for p in packs], axis=0) for k in range(5)
    ]
    spoints = [sgeo[k * n : (k + 1) * n, :] for k in range(4)]
    centre, inv = frame([tpoints, spoints])
    left, _, _ = split_features(tpoints, centre, inv)
    _, right, _ = split_features(spoints, centre, inv)
    store_features(fa, left)
    store_features(fb, right)
    wide = tqt.shape[1]
    tq = tpoints[4]
    if wide > n:
        tq = jnp.concatenate([tq, jnp.zeros((wide - n, L), F32)], axis=0)
    tqt[...] = tq.T

    def begin(i, dist):
        slot = order[jnp.minimum(i, jnp.maximum(found - 1, 0))]
        distances(load_features(fa, slot), load_features(fb, slot), dist)

    def finish(i, dist):
        ok = i < found
        slot = order[jnp.minimum(i, jnp.maximum(found - 1, 0))]
        source = jnp.maximum(codes[slot // slots, lax.rem(slot, slots)], 0)
        back = tile_sums(
            dist, q[pl.ds(source, 1), :], tqt, slot, fwdt, jnp.where(ok, slot, -1)
        )
        acc[pl.ds(source, 1), :] += jnp.where(ok, back, 0.0)

    def step(i, carry):
        begin(2 * i + 1, dist1)
        finish(2 * i, dist0)
        begin(2 * i + 2, dist0)
        finish(2 * i + 1, dist1)
        return carry

    begin(0, dist0)
    lax.fori_loop(0, (found + 1) // 2, step, 0)
    acc_out[...] = acc[...] * inv
    fwd = (fwdt[...] * inv).T
    rank = up.shape[1]
    for shift in range(C - 1):
        sends[shift][:slots, :] = fwd[shift * slots : (shift + 1) * slots, :]
        sends[shift][slots:, :] = jnp.zeros((up.shape[0], L), F32)
        sends[shift][slots:, :rank] = up[...]


def local_kernel(
    sizes, geo, pairs, targets, far_list, coupling, transfer, parent, up, acc_in, *rest
):
    C, S, L, R, slots, clusters, panels = sizes
    pieces = rest[:S]
    sums = rest[S : S + C - 1]
    parts = rest[S + C - 1 : 2 * S + C - 1]
    q, qt, acc, acct, fa0, fa1, fb0, fb1, rads, dist0, dist1, got, parents = rest[2 * S + C - 1 :]
    fa, fb = (fa0, fa1), (fb0, fb1)
    me, sub, rep = lax.axis_index("clu"), lax.axis_index("sub"), lax.axis_index("rep")
    assemble(sub, S, L, q, pieces)
    qt[...] = q[...].T
    acc[...] = jnp.zeros_like(acc)
    acct[...] = jnp.zeros_like(acct)
    points = [geo[:, k, :] for k in range(4)]
    centre, inv = frame([points])
    left, right, rad = split_features(points, centre, inv)
    store_features(fa, left)
    store_features(fb, right)
    rads[...] = rad

    half = panels // 2
    share = clusters // (S * R)
    first = (rep * S + sub) * share

    def begin_self(i, dist):
        c = first + jnp.minimum(i, share - 1)
        a = load_features(fa, c)
        b = load_features(fb, c)
        dist[:half, :half] = contract(a[0], b[0])
        dist[:half, half:] = contract(a[0], b[1])
        dist[half:, half:] = contract(a[1], b[1])

    def finish_self(i, dist):
        c = first + i
        qrow = q[pl.ds(c, 1), :]
        radius = rads[pl.ds(c, 1), :]
        diag = lax.rsqrt(2.0 * (radius * radius))
        back = jnp.zeros((8, LANES), F32)
        step = 64
        for r in range(0, panels, step):
            rows = slice(r, r + step)
            base = r % half
            eye = lax.broadcasted_iota(jnp.int32, (step, half), 0) + base == lax.broadcasted_iota(
                jnp.int32, (step, half), 1
            )
            if r < half:
                g0 = jnp.where(eye, diag[:, :half], lax.rsqrt(dist[rows, :half]))
                g1 = lax.rsqrt(dist[rows, half:])
                qcol = column(qt[rows, :], c)
                back = back + fold(g1 * qcol)
                part = g0 * qrow[:, :half] + g1 * qrow[:, half:]
            else:
                part = jnp.where(eye, diag[:, half:], lax.rsqrt(dist[rows, half:])) * qrow[:, half:]
            put_column(acct, rows, c, jnp.sum(part, axis=1, keepdims=True))
        back = jnp.sum(back, axis=0, keepdims=True)
        acc[pl.ds(c, 1), :] += jnp.concatenate([jnp.zeros_like(back), back], axis=1)

    def self_step(i, carry):
        begin_self(2 * i + 1, dist1)
        finish_self(2 * i, dist0)
        begin_self(2 * i + 2, dist0)
        finish_self(2 * i + 1, dist1)
        return carry

    begin_self(0, dist0)
    lax.fori_loop(0, share // 2, self_step, 0)

    count = pairs.shape[1] // S
    start = sub * count

    def begin(i, dist):
        p = start + jnp.minimum(i, count - 1)
        distances(load_features(fa, pairs[0, p]), load_features(fb, pairs[1, p]), dist)

    def finish(i, dist):
        ia, ib = pairs[0, start + i], pairs[1, start + i]
        acc[pl.ds(ib, 1), :] += tile_sums(dist, q[pl.ds(ib, 1), :], qt, ia, acct, ia)

    def pair_step(i, carry):
        begin(2 * i + 1, dist1)
        finish(2 * i, dist0)
        begin(2 * i + 2, dist0)
        finish(2 * i + 1, dist1)
        return carry

    begin(0, dist0)
    lax.fori_loop(0, count // 2, pair_step, 0)
    total = acc_in[...] + (acc[...] + acct[...].T) * inv

    got[...] = jnp.zeros_like(got)
    for shift in range(1, C):
        dest = lax.rem(me + shift, C)
        for j in range(slots):
            got[pl.ds(targets[dest, j], 1), :] += sums[shift - 1][j : j + 1, :]

    par_dev, far_n, rank = coupling.shape[0], coupling.shape[1], coupling.shape[2]
    parents[pl.ds(pl.multiple_of(me * par_dev, 8), par_dev), :] = up[...]
    for shift in range(1, C):
        owner = lax.rem(me + shift, C)
        parents[pl.ds(pl.multiple_of(owner * par_dev, 8), par_dev), :] = sums[shift - 1][slots:, :rank]
    lane = lax.broadcasted_iota(jnp.int32, (rank, LANES), 1)
    field = jnp.zeros((rank, LANES), F32)
    for p in range(par_dev):
        part = jnp.zeros((rank, rank), F32)
        for k in range(far_n):
            part = part + coupling[p, k] * parents[pl.ds(far_list[p, k], 1), :]
        field = jnp.where(lane == p, jnp.sum(part, axis=1, keepdims=True), field)
    which = lax.broadcasted_iota(jnp.int32, (LANES, clusters), 0)
    onehot = (parent[...] == which).astype(F32)
    down = jnp.dot(field, onehot, precision=HIGHEST, preferred_element_type=F32)
    fields = jnp.concatenate(
        [jnp.sum(transfer[r] * down, axis=0, keepdims=True) for r in range(rank)], axis=0
    )

    def give(s):
        for shift in range(S):
            other = (s + shift) % S
            part = total[:, other * L : (other + 1) * L]
            parts[shift][:clusters, :] = part + got[...] if shift == 0 else part
            for t in range(clusters // L):
                at = clusters + t * rank
                parts[shift][at : at + rank, :] = fields[:, t * L : (t + 1) * L]

    for s in range(S):
        pl.when(sub == s)(functools.partial(give, s))


def up_kernel(basis, masked, transfer, parent, up):
    clusters = basis.shape[0]
    rank = basis.shape[1]
    lane = lax.broadcasted_iota(jnp.int32, (rank, clusters), 1)
    leaf = jnp.zeros((rank, clusters), F32)
    for c in range(clusters):
        part = jnp.sum(basis[c] * masked[c : c + 1, :], axis=1, keepdims=True)
        leaf = jnp.where(lane == c, part, leaf)
    lifted = jnp.zeros((rank, clusters), F32)
    for r in range(rank):
        lifted = lifted + transfer[r] * leaf[r : r + 1, :]
    which = lax.broadcasted_iota(jnp.int32, (up.shape[0], clusters), 0)
    onehot = (parent[...] == which).astype(F32)
    up[...] = lax.dot_general(
        onehot, lifted, (((1,), (1,)), ((), ())), precision=HIGHEST, preferred_element_type=F32
    )


def final_kernel(sizes, mask, basis, *rest):
    S, R, L = sizes
    near, out = rest[: S * R], rest[-1]
    clusters, rank = basis.shape[0], basis.shape[1]
    fields = []
    for t in range(clusters // L):
        rows = slice(clusters + t * rank, clusters + (t + 1) * rank)
        fields.append(sum(near[d * R][rows, :] for d in range(1, S)) + near[0][rows, :])
    fields = jnp.concatenate(fields, axis=1) if len(fields) > 1 else fields[0]
    for c in range(clusters):
        out[c : c + 1, :] = jnp.sum(basis[c] * fields[:, c : c + 1], axis=0, keepdims=True)
    total = out[...]
    for part in near:
        total = total + part[:clusters, :]
    out[...] = total * mask[...].astype(F32)


def send(value, moves):
    names = tuple(name for name, _ in moves)
    steps = [step for _, step in moves]
    sizes = [lax.axis_size(name) for name in names]
    perm = []

    def flat(coords):
        index = 0
        for size, c in zip(sizes, coords):
            index = index * size + c
        return index

    total = 1
    for size in sizes:
        total *= size
    for index in range(total):
        coords, left = [], index
        for size in reversed(sizes):
            coords.append(left % size)
            left //= size
        coords.reverse()
        perm.append((index, flat([(c + s) % n for c, s, n in zip(coords, steps, sizes)])))
    return lax.ppermute(value, names if len(names) > 1 else names[0], perm)


def on_device(
    charges,
    panel_mask,
    geometry,
    remote_source,
    remote_target,
    remote_live,
    local_pairs,
    basis,
    transfer,
    parent_of,
    far_list,
    coupling,
):
    clusters, L = charges.shape
    panels = geometry.shape[2]
    C, S, R = lax.axis_size("clu"), lax.axis_size("sub"), lax.axis_size("rep")
    slots = remote_source.shape[2]
    par_dev, rank = far_list.shape[0], transfer.shape[1]
    n = (C - 1) * slots
    shape = jax.ShapeDtypeStruct
    targets = remote_target[0]
    basis_t = jnp.transpose(basis, (0, 2, 1))
    transfer_t = jnp.transpose(transfer, (1, 2, 0))
    parent = parent_of[None, :]

    made = pl.pallas_call(
        functools.partial(pack_kernel, (C, S, L, slots)),
        out_shape=[shape((clusters, L), F32)] + [shape((5 * slots + 8, L), F32)] * (C - 1),
        in_specs=[vmem()] * 3 + [smem()] * 3,
        out_specs=[vmem()] * C,
        compiler_params=PARAMS,
        name="packs",
    )(charges, panel_mask, geometry, targets, remote_source[0], remote_live[0])
    masked, packs = made[0], made[1:]
    pieces = [masked] + [send(masked, (("sub", d),)) for d in range(1, S)]
    packs = [send(packs[d - 1], (("clu", d),)) for d in range(1, C)]
    codes = jnp.stack([p[5 * slots, :slots] for p in packs]).astype(jnp.int32)

    up = pl.pallas_call(
        up_kernel,
        out_shape=shape((par_dev, rank), F32),
        in_specs=[vmem()] * 4,
        out_specs=vmem(),
        compiler_params=PARAMS,
        name="far_up",
    )(basis_t, masked, transfer_t, parent)

    made = pl.pallas_call(
        functools.partial(remote_kernel, (C, S, L, slots, clusters, panels)),
        out_shape=[shape((clusters, panels), F32)] + [shape((slots + par_dev, L), F32)] * (C - 1),
        in_specs=[vmem(), smem()] + [vmem()] * (1 + S + C - 1),
        out_specs=[vmem()] * C,
        scratch_shapes=[
            pltpu.VMEM((clusters, panels), F32),
            pltpu.VMEM((L, whole(n)), F32),
            pltpu.VMEM((clusters, panels), F32),
            pltpu.VMEM((L, whole(n)), F32),
            pltpu.VMEM((4 * n, panels), F32),
            pltpu.VMEM((n * ROWS, L), F32),
            pltpu.VMEM((n * ROWS, LANES), F32),
            pltpu.VMEM((n * ROWS, LANES), F32),
            pltpu.VMEM((L, panels), F32),
            pltpu.VMEM((L, panels), F32),
            pltpu.SMEM((n + 1,), jnp.int32),
        ],
        compiler_params=PARAMS,
        name="near_remote",
    )(geometry, codes, up, *pieces, *packs)
    acc, sums = made[0], [send(made[d], (("clu", C - d),)) for d in range(1, C)]

    half = [pltpu.VMEM((clusters * ROWS, LANES), F32)] * 2
    parts = pl.pallas_call(
        functools.partial(local_kernel, (C, S, L, R, slots, clusters, panels)),
        out_shape=[shape((clusters + clusters // L * rank, L), F32)] * S,
        in_specs=[vmem()] + [smem()] * 3 + [vmem()] * (5 + S + C - 1),
        out_specs=[vmem()] * S,
        scratch_shapes=[
            pltpu.VMEM((clusters, panels), F32),
            pltpu.VMEM((panels, clusters), F32),
            pltpu.VMEM((clusters, panels), F32),
            pltpu.VMEM((panels, clusters), F32),
            *half,
            *half,
            pltpu.VMEM((clusters, panels), F32),
            pltpu.VMEM((panels, panels), F32),
            pltpu.VMEM((panels, panels), F32),
            pltpu.VMEM((clusters, L), F32),
            pltpu.VMEM((C * par_dev, rank), F32),
        ],
        compiler_params=PARAMS,
        name="near_local",
    )(geometry, local_pairs[0].T, targets, far_list, coupling, transfer_t, parent, up, acc, *pieces, *sums)
    near = []
    for d in range(S):
        for e in range(R):
            near.append(send(parts[d], (("sub", d), ("rep", e))) if d or e else parts[0])

    return pl.pallas_call(
        functools.partial(final_kernel, (S, R, L)),
        out_shape=shape((clusters, L), F32),
        in_specs=[vmem()] * (2 + S * R),
        out_specs=vmem(),
        compiler_params=PARAMS,
        name="combine",
    )(panel_mask, basis_t, *near)


def solution(mesh):
    placed = (
        P(("grp", "clu"), "sub"),
        P(("grp", "clu"), "sub"),
        P(("grp", "clu"), None, None),
        P(("grp", "clu"), None, "rep"),
        P(("grp", "clu"), None, "rep"),
        P(("grp", "clu"), None, "rep"),
        P(("grp", "clu"), "rep", None),
        P(("grp", "clu"), "sub", None),
        P(("grp", "clu"), None, None),
        P(("grp", "clu")),
        P(("grp", "clu"), None),
        P(("grp", "clu"), None, None, None),
    )
    return jax.shard_map(
        on_device, mesh=mesh, in_specs=placed, out_specs=P(("grp", "clu"), "sub"), check_vma=False
    )
```

time: 85.4 us -> 72.5 us (0.85); the launches traced: 84.7 us -> 72.9 us
  starting transfers between devices: 28.3 us -> 12.7 us
  waiting for transfers between devices: 5.27 us -> 9.71 us
    ppermute x21 -> x10, starting transfers between devices: 28.3 us -> 12.7 us  [send(): return lax.ppermute(value, names if len(names) > 1 else names[0], perm)]
    ppermute x21 -> x10, waiting for transfers between devices: 5.27 us -> 9.71 us  [send(): return lax.ppermute(value, names if len(names) > 1 else names[0], perm)]
    unnamed x49 -> x23, local copies, waits for them, and re-layouts: 3.21 us -> 2.54 us
    pallas_call x3 -> x2, Pallas kernels: 31.5 us -> 31.6 us  [the longest x1 28.5 us: on_device(): pl.pallas_call(functools.partial(local_kernel, (C, S, L, R, slots, cluste...]
  transfers between devices with their start and end apart: 21 -> 10, of which waited for: 6 -> 5; matrix products, arithmetic and copies ran while one was open for 1% -> 2% of each run, Pallas kernels for 39% -> 4%
where the time goes in v2:
time: 72.5 us; the launch traced here: 72.9 us
  Pallas kernels  47.2 us (65%)
  starting transfers between devices  12.7 us (18%)
  waiting for transfers between devices  9.71 us (13%)
  local copies, waits for them, and re-layouts  2.55 us (4%)
    pallas_call x1, Pallas kernels, on_device(): pl.pallas_call(functools.partial(local_kernel, (C, S, L, R, slots, cluste...  28.5 us
    ppermute x10, starting transfers between devices, send(): return lax.ppermute(value, names if len(names) > 1 else names[0], perm)  12.7 us
    pallas_call x1, Pallas kernels, on_device(): pl.pallas_call(functools.partial(remote_kernel, (C, S, L, slots, clusters...  10.5 us
    ppermute x10, waiting for transfers between devices, send(): return lax.ppermute(value, names if len(names) > 1 else names[0], perm)  9.71 us
    pallas_call x1, Pallas kernels, on_device(): pl.pallas_call(functools.partial(final_kernel, (S, R, L)), out_shape=shap...  3.1 us
    pallas_call x1, Pallas kernels, on_device(): pl.pallas_call(up_kernel, out_shape=shape((par_dev, rank), F32), in_specs...  3.07 us
    unnamed x23, local copies, waits for them, and re-layouts  2.54 us
    pallas_call x1, Pallas kernels, on_device(): pl.pallas_call(functools.partial(pack_kernel, (C, S, L, slots)), out_shap...  2.02 us
  transfers between devices with their start and end apart: 10, of which 5 were waited for; matrix products, arithmetic and copies ran while one was open for 2% of the time, Pallas kernels for 4%

profile of v2, /device:TPU:0, one launch (start us, length us, event | category | flops | bytes accessed | tf_op | source)
XLA Modules:
  0.0 72.9 jit_solution(11273916331607277433)
XLA Ops:
  0.0 0.0 copy-start.10
  0.0 2.0 %packs.1 = (f32[128,128]{1,0:T(8,128)}, f32[88,128]{1,0:T(8,128)}, f32[88,128]{1,0:T(8,128)}, f32[88,128]{1,0:T(8,128)}) custom-call(f32[128,128]{1,0:T(8,128)} %charges.1, s32[128,128]{1,0:T(8,128)} %mask.3, f32[128,4,256]{2,1,0:T(4,128)} %geo.5, s32[4,16]{1,0:T(4,128)} %bitcast.13, s32[4,16]{1,0:T(4,128)} %bitcast.15, s32[4,16]{1,0:T(4,128)} %bitcast.16), custom_call_target="tpu_custom_call" | custom-call | tf_op jit(solution)/shard_map/packs/pallas_call | solution.py:465
  2.0 3.0 %collective-permute-start = (f32[88,128]{1,0:T(8,128)}, f32[88,128]{1,0:T(8,128)S(1)}, u32[]{:S(2)}, u32[]{:S(2)}) collective-permute-start(f32[88,128]{1,0:T(8,128)} %get-tuple-element.16), channel_id=1, source_target_pairs={{0,4},{4,8},{8,12},{12,0},{1,5},{5,9},{9,13},{13,1},{2,6},{6,10},{... | collective-permute-start | bytes 135176 | tf_op jit(solution)/shard_map/ppermute | solution.py:436
  5.0 2.6 %collective-permute-start.1 = (f32[88,128]{1,0:T(8,128)}, f32[88,128]{1,0:T(8,128)S(1)}, u32[]{:S(2)}, u32[]{:S(2)}) collective-permute-start(f32[88,128]{1,0:T(8,128)} %get-tuple-element.17), channel_id=1, source_target_pairs={{0,8},{4,12},{8,0},{12,4},{1,9},{5,13},{9,1},{13,5},{2,10},{6,14},... | collective-permute-start | bytes 135176 | tf_op jit(solution)/shard_map/ppermute | solution.py:436
  7.6 1.3 %collective-permute-start.2 = (f32[88,128]{1,0:T(8,128)}, f32[88,128]{1,0:T(8,128)S(1)}, u32[]{:S(2)}, u32[]{:S(2)}) collective-permute-start(f32[88,128]{1,0:T(8,128)} %get-tuple-element.18), channel_id=1, source_target_pairs={{0,12},{4,0},{8,4},{12,8},{1,13},{5,1},{9,5},{13,9},{2,14},{6,2},{... | collective-permute-start | bytes 135176 | tf_op jit(solution)/shard_map/ppermute | solution.py:436
  9.0 1.5 %collective-permute-start.3 = (f32[128,128]{1,0:T(8,128)}, f32[128,128]{1,0:T(8,128)S(1)}, u32[]{:S(2)}, u32[]{:S(2)}) collective-permute-start(f32[128,128]{1,0:T(8,128)} %get-tuple-element.15.masked.rest_0_), channel_id=1, source_target_pairs={{0,2},{2,0},{1,3},{3,1},{4,6},{6,4},{5,7},{7,5},{8,10},{10,8},{9,1... | collective-permute-start | bytes 196616 | tf_op jit(solution)/shard_map/ppermute | solution.py:436
  10.5 3.1 %far_up.1.up = f32[16,32]{1,0:T(8,128)} custom-call(f32[128,32,128]{2,1,0:T(8,128)} %bitcast.9, f32[128,128]{1,0:T(8,128)} %get-tuple-element.15.masked.rest_0_, f32[32,32,128]{2,1,0:T(8,128)} %bitcast.11, s32[1,128]{1,0:T(1,128)} %bitcast.17), custom_call_target="tpu_custom_call" | custom-call | tf_op jit(solution)/shard_map/far_up/pallas_call | solution.py:478
  13.6 0.0 collective-permute-done.rest_2_
  13.6 0.0 copy-start.4
  13.6 0.0 collective-permute-done.1.rest_3_
  13.6 0.0 copy-start.5
  13.6 0.0 collective-permute-done.2.rest_4_
  13.6 0.0 copy-start.6
  13.6 0.6 maximum_convert_fusion.codes
  14.2 0.0 collective-permute-done.3.rest_1_
  14.2 0.0 copy-done.4
  14.2 0.0 copy-done.5
  14.2 0.0 copy-done.6
  14.3 0.0 copy-start
  14.3 0.6 copy-done
  14.9 10.5 %near_remote.1 = (f32[128,256]{1,0:T(8,128)}, f32[32,128]{1,0:T(8,128)}, f32[32,128]{1,0:T(8,128)}, f32[32,128]{1,0:T(8,128)}) custom-call(f32[128,4,256]{2,1,0:T(4,128)} %geo.5, s32[3,16]{1,0:T(4,128)} %maximum_convert_fusion.codes, f32[16,32]{1,0:T(8,128)} %far_up.1.up, f32[128,128]{1,0:T(8,128)} %get-tuple-element.15.masked.rest_0_, f32[128,128]{1,0:T(8,128)} %copy-done, ...), custom_call_target="tpu_custom_call" | custom-call | tf_op jit(solution)/shard_map/near_remote/pallas_call | solution.py:487
  25.4 0.8 %collective-permute-start.4 = (f32[32,128]{1,0:T(8,128)}, f32[32,128]{1,0:T(8,128)S(1)}, u32[]{:S(2)}, u32[]{:S(2)}) collective-permute-start(f32[32,128]{1,0:T(8,128)} %get-tuple-element.20), channel_id=1, source_target_pairs={{0,12},{4,0},{8,4},{12,8},{1,13},{5,1},{9,5},{13,9},{2,14},{6,2},{... | collective-permute-start | bytes 49160 | tf_op jit(solution)/shard_map/ppermute | solution.py:436
  26.2 1.3 %collective-permute-start.5 = (f32[32,128]{1,0:T(8,128)}, f32[32,128]{1,0:T(8,128)S(1)}, u32[]{:S(2)}, u32[]{:S(2)}) collective-permute-start(f32[32,128]{1,0:T(8,128)} %get-tuple-element.21), channel_id=1, source_target_pairs={{0,8},{4,12},{8,0},{12,4},{1,9},{5,13},{9,1},{13,5},{2,10},{6,14},... | collective-permute-start | bytes 49160 | tf_op jit(solution)/shard_map/ppermute | solution.py:436
  27.5 0.0 collective-permute-start.6
  27.5 0.0 copy-done.10
  27.5 0.7 copy.13.far_list
  28.2 1.1 %collective-permute-done.4.rest_2_ = f32[32,128]{1,0:T(8,128)S(1)} collective-permute-done((f32[32,128]{1,0:T(8,128)}, f32[32,128]{1,0:T(8,128)S(1)}, u32[]{:S(2)}, u32[]{:S(2)}) %collective-permute-start.4) | collective-permute-done | bytes 16416 | tf_op jit(solution)/shard_map/ppermute | solution.py:436
  29.3 0.0 copy-start.7
  29.3 1.7 %collective-permute-done.5.rest_3_ = f32[32,128]{1,0:T(8,128)S(1)} collective-permute-done((f32[32,128]{1,0:T(8,128)}, f32[32,128]{1,0:T(8,128)S(1)}, u32[]{:S(2)}, u32[]{:S(2)}) %collective-permute-start.5) | collective-permute-done | bytes 16416 | tf_op jit(solution)/shard_map/ppermute | solution.py:436
  31.0 0.0 copy-start.8
  31.0 2.2 %collective-permute-done.6.rest_4_ = f32[32,128]{1,0:T(8,128)S(1)} collective-permute-done((f32[32,128]{1,0:T(8,128)}, f32[32,128]{1,0:T(8,128)S(1)}, u32[]{:S(2)}, u32[]{:S(2)}) %collective-permute-start.6) | collective-permute-done | bytes 16416 | tf_op jit(solution)/shard_map/ppermute | solution.py:436
  33.3 0.0 copy-start.9
  33.3 0.0 copy-done.7
  33.3 0.0 copy-done.8
  33.3 0.6 copy-done.9
  33.9 28.5 %near_local.1 = (f32[160,128]{1,0:T(8,128)}, f32[160,128]{1,0:T(8,128)}) custom-call(f32[128,4,256]{2,1,0:T(4,128)} %geo.5, s32[2,128]{1,0:T(2,128)} %bitcast.19, s32[4,16]{1,0:T(4,128)} %bitcast.14, s32[16,8]{1,0:T(8,128)} %copy.13.far_list, f32[16,8,32,32]{3,2,1,0:T(8,128)} %coupling.1, f32[32,32,128]{2,1,0:T(8,128)} %bitcast.12, s32[1,128]{1,0:T(1,128)} %bitcast.18, ...), custom_call_target="tpu_custom_call" | custom-call | tf_op jit(solution)/shard_map/near_local/pallas_call | solution.py:511
  62.3 0.0 collective-permute-start.7
  62.4 0.8 %collective-permute-start.9 = (f32[160,128]{1,0:T(8,128)}, f32[160,128]{1,0:T(8,128)S(1)}, u32[]{:S(2)}, u32[]{:S(2)}) collective-permute-start(f32[160,128]{1,0:T(8,128)} %get-tuple-element.24), channel_id=1, source_target_pairs={{0,3},{1,2},{2,1},{3,0},{4,7},{5,6},{6,5},{7,4},{8,11},{9,10},{10,... | collective-permute-start | bytes 245768 | tf_op jit(solution)/shard_map/ppermute | solution.py:436
  63.2 1.3 %collective-permute-start.8 = (f32[160,128]{1,0:T(8,128)}, f32[160,128]{1,0:T(8,128)S(1)}, u32[]{:S(2)}, u32[]{:S(2)}) collective-permute-start(f32[160,128]{1,0:T(8,128)} %get-tuple-element.24), channel_id=1, source_target_pairs={{0,2},{1,3},{2,0},{3,1},{4,6},{5,7},{6,4},{7,5},{8,10},{9,11},{10,... | collective-permute-start | bytes 245768 | tf_op jit(solution)/shard_map/ppermute | solution.py:436
  64.5 0.0 collective-permute-done.7.rest_1_
  64.5 0.0 copy-start.1
  64.5 2.3 %collective-permute-done.9.rest_3_ = f32[160,128]{1,0:T(8,128)S(1)} collective-permute-done((f32[160,128]{1,0:T(8,128)}, f32[160,128]{1,0:T(8,128)S(1)}, u32[]{:S(2)}, u32[]{:S(2)}) %collective-permute-start.9) | collective-permute-done | bytes 81952 | tf_op jit(solution)/shard_map/ppermute | solution.py:436
  66.8 0.0 copy-start.2
  66.8 2.3 %collective-permute-done.8.rest_2_ = f32[160,128]{1,0:T(8,128)S(1)} collective-permute-done((f32[160,128]{1,0:T(8,128)}, f32[160,128]{1,0:T(8,128)S(1)}, u32[]{:S(2)}, u32[]{:S(2)}) %collective-permute-start.8) | collective-permute-done | bytes 81952 | tf_op jit(solution)/shard_map/ppermute | solution.py:436
  69.1 0.0 copy-done.1
  69.1 0.0 copy-done.2
  69.1 0.6 copy-done.3
  69.8 3.1 %combine.1 = f32[128,128]{1,0:T(8,128)} custom-call(s32[128,128]{1,0:T(8,128)} %mask.3, f32[128,32,128]{2,1,0:T(8,128)} %bitcast.10, f32[160,128]{1,0:T(8,128)} %get-tuple-element.23.rest_0_, f32[160,128]{1,0:T(8,128)} %copy-done.1, f32[160,128]{1,0:T(8,128)} %copy-done.3, f32[160,128]{1,0:T(8,128)} %copy-done.2), custom_call_target="tpu_custom_call" | custom-call | tf_op jit(solution)/shard_map/combine/pallas_call | solution.py:537
  (4 shorter events, 0.0 us)
Async XLA Ops:
  0.0 27.5 %copy-start.10 = (s32[16,8]{0,1:T(8,128)S(1)}, s32[16,8]{0,1:T(8,128)}, u32[]{:S(2)}) copy-start(s32[16,8]{0,1:T(8,128)} %param.22) | copy-start | bytes 1540
  2.0 11.5 %collective-permute-start = (f32[88,128]{1,0:T(8,128)}, f32[88,128]{1,0:T(8,128)S(1)}, u32[]{:S(2)}, u32[]{:S(2)}) collective-permute-start(f32[88,128]{1,0:T(8,128)} %get-tuple-element.16), channel_id=1, source_target_pairs={{0,4},{4,8},{8,12},{12,0},{1,5},{5,9},{9,13},{13,1},{2,6},{6,10},{... | collective-permute-start | bytes 135176 | tf_op jit(solution)/shard_map/ppermute | solution.py:436
  5.0 8.5 %collective-permute-start.1 = (f32[88,128]{1,0:T(8,128)}, f32[88,128]{1,0:T(8,128)S(1)}, u32[]{:S(2)}, u32[]{:S(2)}) collective-permute-start(f32[88,128]{1,0:T(8,128)} %get-tuple-element.17), channel_id=1, source_target_pairs={{0,8},{4,12},{8,0},{12,4},{1,9},{5,13},{9,1},{13,5},{2,10},{6,14},... | collective-permute-start | bytes 135176 | tf_op jit(solution)/shard_map/ppermute | solution.py:436
  7.6 6.0 %collective-permute-start.2 = (f32[88,128]{1,0:T(8,128)}, f32[88,128]{1,0:T(8,128)S(1)}, u32[]{:S(2)}, u32[]{:S(2)}) collective-permute-start(f32[88,128]{1,0:T(8,128)} %get-tuple-element.18), channel_id=1, source_target_pairs={{0,12},{4,0},{8,4},{12,8},{1,13},{5,1},{9,5},{13,9},{2,14},{6,2},{... | collective-permute-start | bytes 135176 | tf_op jit(solution)/shard_map/ppermute | solution.py:436
  9.0 5.3 %collective-permute-start.3 = (f32[128,128]{1,0:T(8,128)}, f32[128,128]{1,0:T(8,128)S(1)}, u32[]{:S(2)}, u32[]{:S(2)}) collective-permute-start(f32[128,128]{1,0:T(8,128)} %get-tuple-element.15.masked.rest_0_), channel_id=1, source_target_pairs={{0,2},{2,0},{1,3},{3,1},{4,6},{6,4},{5,7},{7,5},{8,10},{10,8},{9,1... | collective-permute-start | bytes 196616 | tf_op jit(solution)/shard_map/ppermute | solution.py:436
  13.6 0.7 copy-start.4
  13.6 0.7 copy-start.5
  13.6 0.6 copy-start.6
  14.3 0.6 copy-start
  25.4 3.9 %collective-permute-start.4 = (f32[32,128]{1,0:T(8,128)}, f32[32,128]{1,0:T(8,128)S(1)}, u32[]{:S(2)}, u32[]{:S(2)}) collective-permute-start(f32[32,128]{1,0:T(8,128)} %get-tuple-element.20), channel_id=1, source_target_pairs={{0,12},{4,0},{8,4},{12,8},{1,13},{5,1},{9,5},{13,9},{2,14},{6,2},{... | collective-permute-start | bytes 49160 | tf_op jit(solution)/shard_map/ppermute | solution.py:436
  26.2 4.8 %collective-permute-start.5 = (f32[32,128]{1,0:T(8,128)}, f32[32,128]{1,0:T(8,128)S(1)}, u32[]{:S(2)}, u32[]{:S(2)}) collective-permute-start(f32[32,128]{1,0:T(8,128)} %get-tuple-element.21), channel_id=1, source_target_pairs={{0,8},{4,12},{8,0},{12,4},{1,9},{5,13},{9,1},{13,5},{2,10},{6,14},... | collective-permute-start | bytes 49160 | tf_op jit(solution)/shard_map/ppermute | solution.py:436
  27.5 5.7 %collective-permute-start.6 = (f32[32,128]{1,0:T(8,128)}, f32[32,128]{1,0:T(8,128)S(1)}, u32[]{:S(2)}, u32[]{:S(2)}) collective-permute-start(f32[32,128]{1,0:T(8,128)} %get-tuple-element.22), channel_id=1, source_target_pairs={{0,4},{4,8},{8,12},{12,0},{1,5},{5,9},{9,13},{13,1},{2,6},{6,10},{... | collective-permute-start | bytes 49160 | tf_op jit(solution)/shard_map/ppermute | solution.py:436
  29.3 3.9 %copy-start.7 = (f32[32,128]{1,0:T(8,128)}, f32[32,128]{1,0:T(8,128)S(1)}, u32[]{:S(2)}) copy-start(f32[32,128]{1,0:T(8,128)S(1)} %collective-permute-done.4.rest_2_) | copy-start | bytes 49156
  31.0 2.2 %copy-start.8 = (f32[32,128]{1,0:T(8,128)}, f32[32,128]{1,0:T(8,128)S(1)}, u32[]{:S(2)}) copy-start(f32[32,128]{1,0:T(8,128)S(1)} %collective-permute-done.5.rest_3_) | copy-start | bytes 49156
  33.3 0.6 copy-start.9
  62.3 2.1 %collective-permute-start.7 = (f32[160,128]{1,0:T(8,128)}, f32[160,128]{1,0:T(8,128)S(1)}, u32[]{:S(2)}, u32[]{:S(2)}) collective-permute-start(f32[160,128]{1,0:T(8,128)} %get-tuple-element.23.rest_0_), channel_id=1, source_target_pairs={{0,1},{1,0},{2,3},{3,2},{4,5},{5,4},{6,7},{7,6},{8,9},{9,8},{10,11... | collective-permute-start | bytes 245768 | tf_op jit(solution)/shard_map/ppermute | solution.py:436
  62.4 4.4 %collective-permute-start.9 = (f32[160,128]{1,0:T(8,128)}, f32[160,128]{1,0:T(8,128)S(1)}, u32[]{:S(2)}, u32[]{:S(2)}) collective-permute-start(f32[160,128]{1,0:T(8,128)} %get-tuple-element.24), channel_id=1, source_target_pairs={{0,3},{1,2},{2,1},{3,0},{4,7},{5,6},{6,5},{7,4},{8,11},{9,10},{10,... | collective-permute-start | bytes 245768 | tf_op jit(solution)/shard_map/ppermute | solution.py:436
  63.2 6.0 %collective-permute-start.8 = (f32[160,128]{1,0:T(8,128)}, f32[160,128]{1,0:T(8,128)S(1)}, u32[]{:S(2)}, u32[]{:S(2)}) collective-permute-start(f32[160,128]{1,0:T(8,128)} %get-tuple-element.24), channel_id=1, source_target_pairs={{0,2},{1,3},{2,0},{3,1},{4,6},{5,7},{6,4},{7,5},{8,10},{9,11},{10,... | collective-permute-start | bytes 245768 | tf_op jit(solution)/shard_map/ppermute | solution.py:436
  64.5 4.6 %copy-start.1 = (f32[160,128]{1,0:T(8,128)}, f32[160,128]{1,0:T(8,128)S(1)}, u32[]{:S(2)}) copy-start(f32[160,128]{1,0:T(8,128)S(1)} %collective-permute-done.7.rest_1_) | copy-start | bytes 245764
  66.8 2.3 %copy-start.2 = (f32[160,128]{1,0:T(8,128)}, f32[160,128]{1,0:T(8,128)S(1)}, u32[]{:S(2)}) copy-start(f32[160,128]{1,0:T(8,128)S(1)} %collective-permute-done.9.rest_3_) | copy-start | bytes 245764
  69.1 0.6 copy-start.3

commit v3 on v2

--- a/solution.py
+++ b/solution.py
@@ -11,7 +11,7 @@
 BF16 = jnp.bfloat16
 HIGHEST = lax.Precision.HIGHEST
 ROWS = 40
-USED = 34
+USED = 37
 LANES = 128
 PARAMS = pltpu.CompilerParams(vmem_limit_bytes=56 * 1024 * 1024)
 
@@ -54,7 +54,7 @@
     return centre, inv
 
 
-def split_features(points, centre, inv):
+def split_features(points, centre, inv, charge=None):
     magic = F32(1.5 * 2.0**16)
     grid, rest = [], []
     for k in range(3):
@@ -81,6 +81,11 @@
     right += [one, one, one, extra1, extra2, extra3]
     left += grid + grid + rest1 + rest2 + rest1 + rest1 + rest2
     right += neg(rest1) + neg(rest2) + neg(grid) + neg(grid) + neg(rest1) + neg(rest2) + neg(rest1)
+    if charge is not None:
+        charge1 = cut(charge)
+        charge2 = cut(charge - charge1)
+        left += [charge1, charge2, (charge - charge1) - charge2]
+    right += [jnp.zeros_like(rad)] * 3
     return left, right, rad
 
 
@@ -101,30 +106,40 @@
     return lax.dot_general(left, right, (((0,), (0,)), ((), ())), preferred_element_type=F32)
 
 
-def column(table, index):
-    if table.shape[1] == LANES and table.shape[0] % 8 == 0:
-        return jnp.take_along_axis(table, jnp.full(table.shape, index, jnp.int32), axis=1)
-    lane = lax.broadcasted_iota(jnp.int32, table.shape, 1)
-    picked = jnp.sum(jnp.where(lane == index, table, 0.0), axis=1, keepdims=True)
-    return jnp.broadcast_to(picked, (table.shape[0], LANES))
-
-
-def put_column(table_ref, rows, index, value):
-    lane = lax.broadcasted_iota(jnp.int32, (rows.stop - rows.start, table_ref.shape[1]), 1)
-    table_ref[rows, :] += jnp.where(lane == index, value, 0.0)
+def pick(rows, width, index):
+    lane = lax.broadcasted_iota(jnp.int32, (rows, width), 1)
+    return jnp.where(lane == index, 1.0, 0.0).astype(BF16)
 
 
 def fold(v):
     return jnp.sum(v.reshape(v.shape[0] // 8, 8, v.shape[1]), axis=0)
 
 
+def charge_rows():
+    row = lax.broadcasted_iota(jnp.int32, (USED, LANES), 0)
+    return jnp.where(row >= USED - 3, 1.0, 0.0).astype(BF16)
+
+
 def distances(left, right, out):
     whole_left = jnp.concatenate(left, axis=1) if len(left) > 1 else left[0]
-    for t, r in enumerate(right):
+    for t, r in enumerate(list(right) + [charge_rows()]):
         out[:, t * LANES : (t + 1) * LANES] = contract(whole_left, r)
 
 
-def tile_sums(dist, qrow, qtable, slot, table_ref, index, step=64):
+def keep(parts, rows, value):
+    high = value.astype(BF16)
+    parts[rows, :LANES] = high
+    parts[rows, LANES:] = (value - high.astype(F32)).astype(BF16)
+
+
+def add_columns(table, parts, indices):
+    width = table.shape[1]
+    left = jnp.concatenate([p[...] for p in parts], axis=1)
+    right = jnp.concatenate([pick(2 * LANES, width, i) for i in indices], axis=0)
+    table[...] += jnp.dot(left, right, preferred_element_type=F32)
+
+
+def tile_sums(dist, qrow, parts, step=64):
     height = dist.shape[0]
     step = min(step, height)
     q0, q1 = qrow[:, :LANES], qrow[:, LANES:]
@@ -132,9 +147,9 @@
     for r in range(0, height, step):
         rows = slice(r, r + step)
         g0 = lax.rsqrt(dist[rows, :LANES])
-        g1 = lax.rsqrt(dist[rows, LANES:])
-        qcol = column(qtable[rows, :], slot)
-        put_column(table_ref, rows, index, jnp.sum(g0 * q0 + g1 * q1, axis=1, keepdims=True))
+        g1 = lax.rsqrt(dist[rows, LANES : 2 * LANES])
+        qcol = dist[rows, 2 * LANES :]
+        keep(parts, rows, g0 * q0 + g1 * q1)
         back0 = back0 + fold(g0 * qcol)
         back1 = back1 + fold(g1 * qcol)
     return jnp.concatenate(
@@ -186,7 +201,7 @@
     packs = rest[S : S + C - 1]
     acc_out = rest[S + C - 1]
     sends = rest[S + C : S + C + C - 1]
-    q, tqt, acc, fwdt, sgeo, fa0, fb0, fb1, dist0, dist1, order = rest[S + C + C - 1 :]
+    q, acc, fwdt, sgeo, fa0, fb0, fb1, dist0, dist1, part0, part1, order = rest[S + C + C - 1 :]
     fa, fb = (fa0,), (fb0, fb1)
     n = (C - 1) * slots
     assemble(lax.axis_index("sub"), S, L, q, pieces)
@@ -207,34 +222,28 @@
     ]
     spoints = [sgeo[k * n : (k + 1) * n, :] for k in range(4)]
     centre, inv = frame([tpoints, spoints])
-    left, _, _ = split_features(tpoints, centre, inv)
+    left, _, _ = split_features(tpoints, centre, inv, tpoints[4])
     _, right, _ = split_features(spoints, centre, inv)
     store_features(fa, left)
     store_features(fb, right)
-    wide = tqt.shape[1]
-    tq = tpoints[4]
-    if wide > n:
-        tq = jnp.concatenate([tq, jnp.zeros((wide - n, L), F32)], axis=0)
-    tqt[...] = tq.T
-
     def begin(i, dist):
         slot = order[jnp.minimum(i, jnp.maximum(found - 1, 0))]
         distances(load_features(fa, slot), load_features(fb, slot), dist)
 
-    def finish(i, dist):
+    def finish(i, dist, part):
         ok = i < found
         slot = order[jnp.minimum(i, jnp.maximum(found - 1, 0))]
         source = jnp.maximum(codes[slot // slots, lax.rem(slot, slots)], 0)
-        back = tile_sums(
-            dist, q[pl.ds(source, 1), :], tqt, slot, fwdt, jnp.where(ok, slot, -1)
-        )
+        back = tile_sums(dist, q[pl.ds(source, 1), :], part)
         acc[pl.ds(source, 1), :] += jnp.where(ok, back, 0.0)
+        return jnp.where(ok, slot, -1)
 
     def step(i, carry):
         begin(2 * i + 1, dist1)
-        finish(2 * i, dist0)
+        slot0 = finish(2 * i, dist0, part0)
         begin(2 * i + 2, dist0)
-        finish(2 * i + 1, dist1)
+        slot1 = finish(2 * i + 1, dist1, part1)
+        add_columns(fwdt, (part0, part1), (slot0, slot1))
         return carry
 
     begin(0, dist0)
@@ -255,16 +264,15 @@
     pieces = rest[:S]
     sums = rest[S : S + C - 1]
     parts = rest[S + C - 1 : 2 * S + C - 1]
-    q, qt, acc, acct, fa0, fa1, fb0, fb1, rads, dist0, dist1, got, parents = rest[2 * S + C - 1 :]
+    q, acc, acct, fa0, fa1, fb0, fb1, rads, dist0, dist1, part0, part1, got, parents = rest[2 * S + C - 1 :]
     fa, fb = (fa0, fa1), (fb0, fb1)
     me, sub, rep = lax.axis_index("clu"), lax.axis_index("sub"), lax.axis_index("rep")
     assemble(sub, S, L, q, pieces)
-    qt[...] = q[...].T
     acc[...] = jnp.zeros_like(acc)
     acct[...] = jnp.zeros_like(acct)
     points = [geo[:, k, :] for k in range(4)]
     centre, inv = frame([points])
-    left, right, rad = split_features(points, centre, inv)
+    left, right, rad = split_features(points, centre, inv, q[...])
     store_features(fa, left)
     store_features(fb, right)
     rads[...] = rad
@@ -278,10 +286,11 @@
         a = load_features(fa, c)
         b = load_features(fb, c)
         dist[:half, :half] = contract(a[0], b[0])
-        dist[:half, half:] = contract(a[0], b[1])
-        dist[half:, half:] = contract(a[1], b[1])
-
-    def finish_self(i, dist):
+        dist[:half, half:panels] = contract(a[0], b[1])
+        dist[:half, panels:] = contract(a[0], charge_rows())
+        dist[half:, half:panels] = contract(a[1], b[1])
+
+    def finish_self(i, dist, parts):
         c = first + i
         qrow = q[pl.ds(c, 1), :]
         radius = rads[pl.ds(c, 1), :]
@@ -296,21 +305,23 @@
             )
             if r < half:
                 g0 = jnp.where(eye, diag[:, :half], lax.rsqrt(dist[rows, :half]))
-                g1 = lax.rsqrt(dist[rows, half:])
-                qcol = column(qt[rows, :], c)
+                g1 = lax.rsqrt(dist[rows, half:panels])
+                qcol = dist[rows, panels:]
                 back = back + fold(g1 * qcol)
                 part = g0 * qrow[:, :half] + g1 * qrow[:, half:]
             else:
-                part = jnp.where(eye, diag[:, half:], lax.rsqrt(dist[rows, half:])) * qrow[:, half:]
-            put_column(acct, rows, c, jnp.sum(part, axis=1, keepdims=True))
+                part = jnp.where(eye, diag[:, half:], lax.rsqrt(dist[rows, half:panels])) * qrow[:, half:]
+            keep(parts, rows, part)
         back = jnp.sum(back, axis=0, keepdims=True)
         acc[pl.ds(c, 1), :] += jnp.concatenate([jnp.zeros_like(back), back], axis=1)
+        return c
 
     def self_step(i, carry):
         begin_self(2 * i + 1, dist1)
-        finish_self(2 * i, dist0)
+        c0 = finish_self(2 * i, dist0, part0)
         begin_self(2 * i + 2, dist0)
-        finish_self(2 * i + 1, dist1)
+        c1 = finish_self(2 * i + 1, dist1, part1)
+        add_columns(acct, (part0, part1), (c0, c1))
         return carry
 
     begin_self(0, dist0)
@@ -323,15 +334,17 @@
         p = start + jnp.minimum(i, count - 1)
         distances(load_features(fa, pairs[0, p]), load_features(fb, pairs[1, p]), dist)
 
-    def finish(i, dist):
+    def finish(i, dist, part):
         ia, ib = pairs[0, start + i], pairs[1, start + i]
-        acc[pl.ds(ib, 1), :] += tile_sums(dist, q[pl.ds(ib, 1), :], qt, ia, acct, ia)
+        acc[pl.ds(ib, 1), :] += tile_sums(dist, q[pl.ds(ib, 1), :], part)
+        return ia
 
     def pair_step(i, carry):
         begin(2 * i + 1, dist1)
-        finish(2 * i, dist0)
+        ia0 = finish(2 * i, dist0, part0)
         begin(2 * i + 2, dist0)
-        finish(2 * i + 1, dist1)
+        ia1 = finish(2 * i + 1, dist1, part1)
+        add_columns(acct, (part0, part1), (ia0, ia1))
         return carry
 
     begin(0, dist0)
@@ -491,15 +504,16 @@
         out_specs=[vmem()] * C,
         scratch_shapes=[
             pltpu.VMEM((clusters, panels), F32),
-            pltpu.VMEM((L, whole(n)), F32),
             pltpu.VMEM((clusters, panels), F32),
             pltpu.VMEM((L, whole(n)), F32),
             pltpu.VMEM((4 * n, panels), F32),
             pltpu.VMEM((n * ROWS, L), F32),
             pltpu.VMEM((n * ROWS, LANES), F32),
             pltpu.VMEM((n * ROWS, LANES), F32),
-            pltpu.VMEM((L, panels), F32),
-            pltpu.VMEM((L, panels), F32),
+            pltpu.VMEM((L, panels + LANES), F32),
+            pltpu.VMEM((L, panels + LANES), F32),
+            pltpu.VMEM((L, 2 * LANES), BF16),
+            pltpu.VMEM((L, 2 * LANES), BF16),
             pltpu.SMEM((n + 1,), jnp.int32),
         ],
         compiler_params=PARAMS,
@@ -515,14 +529,15 @@
         out_specs=[vmem()] * S,
         scratch_shapes=[
             pltpu.VMEM((clusters, panels), F32),
-            pltpu.VMEM((panels, clusters), F32),
             pltpu.VMEM((clusters, panels), F32),
             pltpu.VMEM((panels, clusters), F32),
             *half,
             *half,
             pltpu.VMEM((clusters, panels), F32),
-            pltpu.VMEM((panels, panels), F32),
-            pltpu.VMEM((panels, panels), F32),
+            pltpu.VMEM((panels, panels + LANES), F32),
+            pltpu.VMEM((panels, panels + LANES), F32),
+            pltpu.VMEM((panels, 2 * LANES), BF16),
+            pltpu.VMEM((panels, 2 * LANES), BF16),
             pltpu.VMEM((clusters, L), F32),
             pltpu.VMEM((C * par_dev, rank), F32),
         ],

time: 72.5 us -> 74.4 us (1.026)
  Pallas kernels: 47.2 us -> 48.9 us
    pallas_call x1, Pallas kernels: 10.5 us -> 11.5 us  [on_device(): pl.pallas_call(functools.partial(remote_kernel, (C, S, L, slots, clusters...]
where the time goes in v3:
time: 74.4 us; the launch traced here: 74.6 us
  Pallas kernels  48.9 us (66%)
  starting transfers between devices  12.7 us (17%)
  waiting for transfers between devices  9.71 us (13%)
  local copies, waits for them, and re-layouts  2.55 us (3%)
    pallas_call x1, Pallas kernels, on_device(): pl.pallas_call(functools.partial(local_kernel, (C, S, L, R, slots, cluste...  29.2 us
    ppermute x10, starting transfers between devices, send(): return lax.ppermute(value, names if len(names) > 1 else names[0], perm)  12.7 us
    pallas_call x1, Pallas kernels, on_device(): pl.pallas_call(functools.partial(remote_kernel, (C, S, L, slots, clusters...  11.5 us
    ppermute x10, waiting for transfers between devices, send(): return lax.ppermute(value, names if len(names) > 1 else names[0], perm)  9.71 us
    pallas_call x1, Pallas kernels, on_device(): pl.pallas_call(functools.partial(final_kernel, (S, R, L)), out_shape=shap...  3.1 us
    pallas_call x1, Pallas kernels, on_device(): pl.pallas_call(up_kernel, out_shape=shape((par_dev, rank), F32), in_specs...  3.07 us
    unnamed x23, local copies, waits for them, and re-layouts  2.54 us
    pallas_call x1, Pallas kernels, on_device(): pl.pallas_call(functools.partial(pack_kernel, (C, S, L, slots)), out_shap...  2.02 us
  transfers between devices with their start and end apart: 10, of which 5 were waited for; matrix products, arithmetic and copies ran while one was open for 2% of the time, Pallas kernels for 4%

profile of v3, /device:TPU:0, one launch (start us, length us, event | category | flops | bytes accessed | tf_op | source)
XLA Modules:
  0.0 74.6 jit_solution(9063571485178384371)
XLA Ops:
  0.0 0.0 copy-start.10
  0.0 2.0 %packs.1 = (f32[128,128]{1,0:T(8,128)}, f32[88,128]{1,0:T(8,128)}, f32[88,128]{1,0:T(8,128)}, f32[88,128]{1,0:T(8,128)}) custom-call(f32[128,128]{1,0:T(8,128)} %charges.1, s32[128,128]{1,0:T(8,128)} %mask.3, f32[128,4,256]{2,1,0:T(4,128)} %geo.5, s32[4,16]{1,0:T(4,128)} %bitcast.13, s32[4,16]{1,0:T(4,128)} %bitcast.15, s32[4,16]{1,0:T(4,128)} %bitcast.16), custom_call_target="tpu_custom_call" | custom-call | tf_op jit(solution)/shard_map/packs/pallas_call | solution.py:478
  2.0 3.0 %collective-permute-start = (f32[88,128]{1,0:T(8,128)}, f32[88,128]{1,0:T(8,128)S(1)}, u32[]{:S(2)}, u32[]{:S(2)}) collective-permute-start(f32[88,128]{1,0:T(8,128)} %get-tuple-element.16), channel_id=1, source_target_pairs={{0,4},{4,8},{8,12},{12,0},{1,5},{5,9},{9,13},{13,1},{2,6},{6,10},{... | collective-permute-start | bytes 135176 | tf_op jit(solution)/shard_map/ppermute | solution.py:449
  5.0 2.6 %collective-permute-start.1 = (f32[88,128]{1,0:T(8,128)}, f32[88,128]{1,0:T(8,128)S(1)}, u32[]{:S(2)}, u32[]{:S(2)}) collective-permute-start(f32[88,128]{1,0:T(8,128)} %get-tuple-element.17), channel_id=1, source_target_pairs={{0,8},{4,12},{8,0},{12,4},{1,9},{5,13},{9,1},{13,5},{2,10},{6,14},... | collective-permute-start | bytes 135176 | tf_op jit(solution)/shard_map/ppermute | solution.py:449
  7.6 1.3 %collective-permute-start.2 = (f32[88,128]{1,0:T(8,128)}, f32[88,128]{1,0:T(8,128)S(1)}, u32[]{:S(2)}, u32[]{:S(2)}) collective-permute-start(f32[88,128]{1,0:T(8,128)} %get-tuple-element.18), channel_id=1, source_target_pairs={{0,12},{4,0},{8,4},{12,8},{1,13},{5,1},{9,5},{13,9},{2,14},{6,2},{... | collective-permute-start | bytes 135176 | tf_op jit(solution)/shard_map/ppermute | solution.py:449
  9.0 1.5 %collective-permute-start.3 = (f32[128,128]{1,0:T(8,128)}, f32[128,128]{1,0:T(8,128)S(1)}, u32[]{:S(2)}, u32[]{:S(2)}) collective-permute-start(f32[128,128]{1,0:T(8,128)} %get-tuple-element.15.masked.rest_0_), channel_id=1, source_target_pairs={{0,2},{2,0},{1,3},{3,1},{4,6},{6,4},{5,7},{7,5},{8,10},{10,8},{9,1... | collective-permute-start | bytes 196616 | tf_op jit(solution)/shard_map/ppermute | solution.py:449
  10.5 3.1 %far_up.1.up = f32[16,32]{1,0:T(8,128)} custom-call(f32[128,32,128]{2,1,0:T(8,128)} %bitcast.9, f32[128,128]{1,0:T(8,128)} %get-tuple-element.15.masked.rest_0_, f32[32,32,128]{2,1,0:T(8,128)} %bitcast.11, s32[1,128]{1,0:T(1,128)} %bitcast.17), custom_call_target="tpu_custom_call" | custom-call | tf_op jit(solution)/shard_map/far_up/pallas_call | solution.py:491
  13.6 0.0 collective-permute-done.rest_2_
  13.6 0.0 copy-start.4
  13.6 0.0 collective-permute-done.1.rest_3_
  13.6 0.0 copy-start.5
  13.6 0.0 collective-permute-done.2.rest_4_
  13.6 0.0 copy-start.6
  13.6 0.6 maximum_convert_fusion.codes
  14.2 0.0 collective-permute-done.3.rest_1_
  14.2 0.0 copy-done.4
  14.2 0.0 copy-done.5
  14.2 0.0 copy-done.6
  14.3 0.0 copy-start
  14.3 0.6 copy-done
  14.9 11.5 %near_remote.1 = (f32[128,256]{1,0:T(8,128)}, f32[32,128]{1,0:T(8,128)}, f32[32,128]{1,0:T(8,128)}, f32[32,128]{1,0:T(8,128)}) custom-call(f32[128,4,256]{2,1,0:T(4,128)} %geo.5, s32[3,16]{1,0:T(4,128)} %maximum_convert_fusion.codes, f32[16,32]{1,0:T(8,128)} %far_up.1.up, f32[128,128]{1,0:T(8,128)} %get-tuple-element.15.masked.rest_0_, f32[128,128]{1,0:T(8,128)} %copy-done, ...), custom_call_target="tpu_custom_call" | custom-call | tf_op jit(solution)/shard_map/near_remote/pallas_call | solution.py:500
  26.4 1.1 %collective-permute-start.4 = (f32[32,128]{1,0:T(8,128)}, f32[32,128]{1,0:T(8,128)S(1)}, u32[]{:S(2)}, u32[]{:S(2)}) collective-permute-start(f32[32,128]{1,0:T(8,128)} %get-tuple-element.20), channel_id=1, source_target_pairs={{0,12},{4,0},{8,4},{12,8},{1,13},{5,1},{9,5},{13,9},{2,14},{6,2},{... | collective-permute-start | bytes 49160 | tf_op jit(solution)/shard_map/ppermute | solution.py:449
  27.5 1.1 %collective-permute-start.5 = (f32[32,128]{1,0:T(8,128)}, f32[32,128]{1,0:T(8,128)S(1)}, u32[]{:S(2)}, u32[]{:S(2)}) collective-permute-start(f32[32,128]{1,0:T(8,128)} %get-tuple-element.21), channel_id=1, source_target_pairs={{0,8},{4,12},{8,0},{12,4},{1,9},{5,13},{9,1},{13,5},{2,10},{6,14},... | collective-permute-start | bytes 49160 | tf_op jit(solution)/shard_map/ppermute | solution.py:449
  28.5 0.0 collective-permute-start.6
  28.5 0.0 copy-done.10
  28.5 0.7 copy.13.far_list
  29.2 1.1 %collective-permute-done.4.rest_2_ = f32[32,128]{1,0:T(8,128)S(1)} collective-permute-done((f32[32,128]{1,0:T(8,128)}, f32[32,128]{1,0:T(8,128)S(1)}, u32[]{:S(2)}, u32[]{:S(2)}) %collective-permute-start.4) | collective-permute-done | bytes 16416 | tf_op jit(solution)/shard_map/ppermute | solution.py:449
  30.3 0.0 copy-start.7
  30.3 2.0 %collective-permute-done.5.rest_3_ = f32[32,128]{1,0:T(8,128)S(1)} collective-permute-done((f32[32,128]{1,0:T(8,128)}, f32[32,128]{1,0:T(8,128)S(1)}, u32[]{:S(2)}, u32[]{:S(2)}) %collective-permute-start.5) | collective-permute-done | bytes 16416 | tf_op jit(solution)/shard_map/ppermute | solution.py:449
  32.3 0.0 copy-start.8
  32.3 2.0 %collective-permute-done.6.rest_4_ = f32[32,128]{1,0:T(8,128)S(1)} collective-permute-done((f32[32,128]{1,0:T(8,128)}, f32[32,128]{1,0:T(8,128)S(1)}, u32[]{:S(2)}, u32[]{:S(2)}) %collective-permute-start.6) | collective-permute-done | bytes 16416 | tf_op jit(solution)/shard_map/ppermute | solution.py:449
  34.3 0.0 copy-start.9
  34.3 0.0 copy-done.7
  34.3 0.0 copy-done.8
  34.3 0.6 copy-done.9
  34.9 29.2 %near_local.1 = (f32[160,128]{1,0:T(8,128)}, f32[160,128]{1,0:T(8,128)}) custom-call(f32[128,4,256]{2,1,0:T(4,128)} %geo.5, s32[2,128]{1,0:T(2,128)} %bitcast.19, s32[4,16]{1,0:T(4,128)} %bitcast.14, s32[16,8]{1,0:T(8,128)} %copy.13.far_list, f32[16,8,32,32]{3,2,1,0:T(8,128)} %coupling.1, f32[32,32,128]{2,1,0:T(8,128)} %bitcast.12, s32[1,128]{1,0:T(1,128)} %bitcast.18, ...), custom_call_target="tpu_custom_call" | custom-call | tf_op jit(solution)/shard_map/near_local/pallas_call | solution.py:525
  64.0 0.0 collective-permute-start.7
  64.0 0.8 %collective-permute-start.9 = (f32[160,128]{1,0:T(8,128)}, f32[160,128]{1,0:T(8,128)S(1)}, u32[]{:S(2)}, u32[]{:S(2)}) collective-permute-start(f32[160,128]{1,0:T(8,128)} %get-tuple-element.24), channel_id=1, source_target_pairs={{0,3},{1,2},{2,1},{3,0},{4,7},{5,6},{6,5},{7,4},{8,11},{9,10},{10,... | collective-permute-start | bytes 245768 | tf_op jit(solution)/shard_map/ppermute | solution.py:449
  64.9 1.3 %collective-permute-start.8 = (f32[160,128]{1,0:T(8,128)}, f32[160,128]{1,0:T(8,128)S(1)}, u32[]{:S(2)}, u32[]{:S(2)}) collective-permute-start(f32[160,128]{1,0:T(8,128)} %get-tuple-element.24), channel_id=1, source_target_pairs={{0,2},{1,3},{2,0},{3,1},{4,6},{5,7},{6,4},{7,5},{8,10},{9,11},{10,... | collective-permute-start | bytes 245768 | tf_op jit(solution)/shard_map/ppermute | solution.py:449
  66.2 0.0 collective-permute-done.7.rest_1_
  66.2 0.0 copy-start.1
  66.2 2.3 %collective-permute-done.9.rest_3_ = f32[160,128]{1,0:T(8,128)S(1)} collective-permute-done((f32[160,128]{1,0:T(8,128)}, f32[160,128]{1,0:T(8,128)S(1)}, u32[]{:S(2)}, u32[]{:S(2)}) %collective-permute-start.9) | collective-permute-done | bytes 81952 | tf_op jit(solution)/shard_map/ppermute | solution.py:449
  68.5 0.0 copy-start.2
  68.5 2.3 %collective-permute-done.8.rest_2_ = f32[160,128]{1,0:T(8,128)S(1)} collective-permute-done((f32[160,128]{1,0:T(8,128)}, f32[160,128]{1,0:T(8,128)S(1)}, u32[]{:S(2)}, u32[]{:S(2)}) %collective-permute-start.8) | collective-permute-done | bytes 81952 | tf_op jit(solution)/shard_map/ppermute | solution.py:449
  70.8 0.0 copy-done.1
  70.8 0.0 copy-done.2
  70.8 0.6 copy-done.3
  71.5 3.1 %combine.1 = f32[128,128]{1,0:T(8,128)} custom-call(s32[128,128]{1,0:T(8,128)} %mask.3, f32[128,32,128]{2,1,0:T(8,128)} %bitcast.10, f32[160,128]{1,0:T(8,128)} %get-tuple-element.23.rest_0_, f32[160,128]{1,0:T(8,128)} %copy-done.1, f32[160,128]{1,0:T(8,128)} %copy-done.3, f32[160,128]{1,0:T(8,128)} %copy-done.2), custom_call_target="tpu_custom_call" | custom-call | tf_op jit(solution)/shard_map/combine/pallas_call | solution.py:552
  (4 shorter events, 0.0 us)
Async XLA Ops:
  0.0 28.5 %copy-start.10 = (s32[16,8]{0,1:T(8,128)S(1)}, s32[16,8]{0,1:T(8,128)}, u32[]{:S(2)}) copy-start(s32[16,8]{0,1:T(8,128)} %param.22) | copy-start | bytes 1540
  2.0 11.5 %collective-permute-start = (f32[88,128]{1,0:T(8,128)}, f32[88,128]{1,0:T(8,128)S(1)}, u32[]{:S(2)}, u32[]{:S(2)}) collective-permute-start(f32[88,128]{1,0:T(8,128)} %get-tuple-element.16), channel_id=1, source_target_pairs={{0,4},{4,8},{8,12},{12,0},{1,5},{5,9},{9,13},{13,1},{2,6},{6,10},{... | collective-permute-start | bytes 135176 | tf_op jit(solution)/shard_map/ppermute | solution.py:449
  5.0 8.5 %collective-permute-start.1 = (f32[88,128]{1,0:T(8,128)}, f32[88,128]{1,0:T(8,128)S(1)}, u32[]{:S(2)}, u32[]{:S(2)}) collective-permute-start(f32[88,128]{1,0:T(8,128)} %get-tuple-element.17), channel_id=1, source_target_pairs={{0,8},{4,12},{8,0},{12,4},{1,9},{5,13},{9,1},{13,5},{2,10},{6,14},... | collective-permute-start | bytes 135176 | tf_op jit(solution)/shard_map/ppermute | solution.py:449
  7.6 6.0 %collective-permute-start.2 = (f32[88,128]{1,0:T(8,128)}, f32[88,128]{1,0:T(8,128)S(1)}, u32[]{:S(2)}, u32[]{:S(2)}) collective-permute-start(f32[88,128]{1,0:T(8,128)} %get-tuple-element.18), channel_id=1, source_target_pairs={{0,12},{4,0},{8,4},{12,8},{1,13},{5,1},{9,5},{13,9},{2,14},{6,2},{... | collective-permute-start | bytes 135176 | tf_op jit(solution)/shard_map/ppermute | solution.py:449
  9.0 5.3 %collective-permute-start.3 = (f32[128,128]{1,0:T(8,128)}, f32[128,128]{1,0:T(8,128)S(1)}, u32[]{:S(2)}, u32[]{:S(2)}) collective-permute-start(f32[128,128]{1,0:T(8,128)} %get-tuple-element.15.masked.rest_0_), channel_id=1, source_target_pairs={{0,2},{2,0},{1,3},{3,1},{4,6},{6,4},{5,7},{7,5},{8,10},{10,8},{9,1... | collective-permute-start | bytes 196616 | tf_op jit(solution)/shard_map/ppermute | solution.py:449
  13.6 0.7 copy-start.4
  13.6 0.7 copy-start.5
  13.6 0.6 copy-start.6
  14.3 0.6 copy-start
  26.4 3.9 %collective-permute-start.4 = (f32[32,128]{1,0:T(8,128)}, f32[32,128]{1,0:T(8,128)S(1)}, u32[]{:S(2)}, u32[]{:S(2)}) collective-permute-start(f32[32,128]{1,0:T(8,128)} %get-tuple-element.20), channel_id=1, source_target_pairs={{0,12},{4,0},{8,4},{12,8},{1,13},{5,1},{9,5},{13,9},{2,14},{6,2},{... | collective-permute-start | bytes 49160 | tf_op jit(solution)/shard_map/ppermute | solution.py:449
  27.5 4.8 %collective-permute-start.5 = (f32[32,128]{1,0:T(8,128)}, f32[32,128]{1,0:T(8,128)S(1)}, u32[]{:S(2)}, u32[]{:S(2)}) collective-permute-start(f32[32,128]{1,0:T(8,128)} %get-tuple-element.21), channel_id=1, source_target_pairs={{0,8},{4,12},{8,0},{12,4},{1,9},{5,13},{9,1},{13,5},{2,10},{6,14},... | collective-permute-start | bytes 49160 | tf_op jit(solution)/shard_map/ppermute | solution.py:449
  28.5 5.7 %collective-permute-start.6 = (f32[32,128]{1,0:T(8,128)}, f32[32,128]{1,0:T(8,128)S(1)}, u32[]{:S(2)}, u32[]{:S(2)}) collective-permute-start(f32[32,128]{1,0:T(8,128)} %get-tuple-element.22), channel_id=1, source_target_pairs={{0,4},{4,8},{8,12},{12,0},{1,5},{5,9},{9,13},{13,1},{2,6},{6,10},{... | collective-permute-start | bytes 49160 | tf_op jit(solution)/shard_map/ppermute | solution.py:449
  30.3 3.9 %copy-start.7 = (f32[32,128]{1,0:T(8,128)}, f32[32,128]{1,0:T(8,128)S(1)}, u32[]{:S(2)}) copy-start(f32[32,128]{1,0:T(8,128)S(1)} %collective-permute-done.4.rest_2_) | copy-start | bytes 49156
  32.3 2.0 %copy-start.8 = (f32[32,128]{1,0:T(8,128)}, f32[32,128]{1,0:T(8,128)S(1)}, u32[]{:S(2)}) copy-start(f32[32,128]{1,0:T(8,128)S(1)} %collective-permute-done.5.rest_3_) | copy-start | bytes 49156
  34.3 0.6 copy-start.9
  64.0 2.1 %collective-permute-start.7 = (f32[160,128]{1,0:T(8,128)}, f32[160,128]{1,0:T(8,128)S(1)}, u32[]{:S(2)}, u32[]{:S(2)}) collective-permute-start(f32[160,128]{1,0:T(8,128)} %get-tuple-element.23.rest_0_), channel_id=1, source_target_pairs={{0,1},{1,0},{2,3},{3,2},{4,5},{5,4},{6,7},{7,6},{8,9},{9,8},{10,11... | collective-permute-start | bytes 245768 | tf_op jit(solution)/shard_map/ppermute | solution.py:449
  64.0 4.4 %collective-permute-start.9 = (f32[160,128]{1,0:T(8,128)}, f32[160,128]{1,0:T(8,128)S(1)}, u32[]{:S(2)}, u32[]{:S(2)}) collective-permute-start(f32[160,128]{1,0:T(8,128)} %get-tuple-element.24), channel_id=1, source_target_pairs={{0,3},{1,2},{2,1},{3,0},{4,7},{5,6},{6,5},{7,4},{8,11},{9,10},{10,... | collective-permute-start | bytes 245768 | tf_op jit(solution)/shard_map/ppermute | solution.py:449
  64.9 6.0 %collective-permute-start.8 = (f32[160,128]{1,0:T(8,128)}, f32[160,128]{1,0:T(8,128)S(1)}, u32[]{:S(2)}, u32[]{:S(2)}) collective-permute-start(f32[160,128]{1,0:T(8,128)} %get-tuple-element.24), channel_id=1, source_target_pairs={{0,2},{1,3},{2,0},{3,1},{4,6},{5,7},{6,4},{7,5},{8,10},{9,11},{10,... | collective-permute-start | bytes 245768 | tf_op jit(solution)/shard_map/ppermute | solution.py:449
  66.2 4.6 %copy-start.1 = (f32[160,128]{1,0:T(8,128)}, f32[160,128]{1,0:T(8,128)S(1)}, u32[]{:S(2)}) copy-start(f32[160,128]{1,0:T(8,128)S(1)} %collective-permute-done.7.rest_1_) | copy-start | bytes 245764
  68.5 2.3 %copy-start.2 = (f32[160,128]{1,0:T(8,128)}, f32[160,128]{1,0:T(8,128)S(1)}, u32[]{:S(2)}) copy-start(f32[160,128]{1,0:T(8,128)S(1)} %collective-permute-done.9.rest_3_) | copy-start | bytes 245764
  70.8 0.6 copy-start.3

commit v4 on v3

--- a/solution.py
+++ b/solution.py
@@ -111,6 +111,11 @@
     return jnp.where(lane == index, 1.0, 0.0).astype(BF16)
 
 
+def twice_rsqrt(d):
+    y = lax.rsqrt(d.astype(BF16)).astype(F32)
+    return y * (3.0 - (d * y) * y)
+
+
 def fold(v):
     return jnp.sum(v.reshape(v.shape[0] // 8, 8, v.shape[1]), axis=0)
 
@@ -146,8 +151,8 @@
     back0 = back1 = jnp.zeros((8, LANES), F32)
     for r in range(0, height, step):
         rows = slice(r, r + step)
-        g0 = lax.rsqrt(dist[rows, :LANES])
-        g1 = lax.rsqrt(dist[rows, LANES : 2 * LANES])
+        g0 = twice_rsqrt(dist[rows, :LANES])
+        g1 = twice_rsqrt(dist[rows, LANES : 2 * LANES])
         qcol = dist[rows, 2 * LANES :]
         keep(parts, rows, g0 * q0 + g1 * q1)
         back0 = back0 + fold(g0 * qcol)
@@ -248,8 +253,8 @@
 
     begin(0, dist0)
     lax.fori_loop(0, (found + 1) // 2, step, 0)
-    acc_out[...] = acc[...] * inv
-    fwd = (fwdt[...] * inv).T
+    acc_out[...] = acc[...] * (0.5 * inv)
+    fwd = (fwdt[...] * (0.5 * inv)).T
     rank = up.shape[1]
     for shift in range(C - 1):
         sends[shift][:slots, :] = fwd[shift * slots : (shift + 1) * slots, :]
@@ -294,7 +299,7 @@
         c = first + i
         qrow = q[pl.ds(c, 1), :]
         radius = rads[pl.ds(c, 1), :]
-        diag = lax.rsqrt(2.0 * (radius * radius))
+        diag = 2.0 * lax.rsqrt(2.0 * (radius * radius))
         back = jnp.zeros((8, LANES), F32)
         step = 64
         for r in range(0, panels, step):
@@ -304,13 +309,13 @@
                 jnp.int32, (step, half), 1
             )
             if r < half:
-                g0 = jnp.where(eye, diag[:, :half], lax.rsqrt(dist[rows, :half]))
-                g1 = lax.rsqrt(dist[rows, half:panels])
+                g0 = jnp.where(eye, diag[:, :half], twice_rsqrt(dist[rows, :half]))
+                g1 = twice_rsqrt(dist[rows, half:panels])
                 qcol = dist[rows, panels:]
                 back = back + fold(g1 * qcol)
                 part = g0 * qrow[:, :half] + g1 * qrow[:, half:]
             else:
-                part = jnp.where(eye, diag[:, half:], lax.rsqrt(dist[rows, half:panels])) * qrow[:, half:]
+                part = jnp.where(eye, diag[:, half:], twice_rsqrt(dist[rows, half:panels])) * qrow[:, half:]
             keep(parts, rows, part)
         back = jnp.sum(back, axis=0, keepdims=True)
         acc[pl.ds(c, 1), :] += jnp.concatenate([jnp.zeros_like(back), back], axis=1)
@@ -349,7 +354,7 @@
 
     begin(0, dist0)
     lax.fori_loop(0, count // 2, pair_step, 0)
-    total = acc_in[...] + (acc[...] + acct[...].T) * inv
+    total = acc_in[...] + (acc[...] + acct[...].T) * (0.5 * inv)
 
     got[...] = jnp.zeros_like(got)
     for shift in range(1, C):

time: 74.4 us -> 80.1 us (1.077)
  Pallas kernels: 48.9 us -> 54.6 us
  waiting for transfers between devices: 9.71 us -> 8.78 us
    pallas_call x1, Pallas kernels: 29.2 us -> 34.3 us  [on_device(): pl.pallas_call(functools.partial(local_kernel, (C, S, L, R, slots, cluste...]
    ppermute x10, waiting for transfers between devices: 9.71 us -> 8.78 us  [send(): return lax.ppermute(value, names if len(names) > 1 else names[0], perm)]
where the time goes in v4:
time: 80.1 us; the launch traced here: 79.5 us
  Pallas kernels  54.6 us (68%)
  starting transfers between devices  13 us (16%)
  waiting for transfers between devices  8.78 us (11%)
  local copies, waits for them, and re-layouts  2.55 us (3%)
    pallas_call x1, Pallas kernels, on_device(): pl.pallas_call(functools.partial(local_kernel, (C, S, L, R, slots, cluste...  34.3 us
    ppermute x10, starting transfers between devices, send(): return lax.ppermute(value, names if len(names) > 1 else names[0], perm)  13 us
    pallas_call x1, Pallas kernels, on_device(): pl.pallas_call(functools.partial(remote_kernel, (C, S, L, slots, clusters...  12.1 us
    ppermute x10, waiting for transfers between devices, send(): return lax.ppermute(value, names if len(names) > 1 else names[0], perm)  8.78 us
    pallas_call x1, Pallas kernels, on_device(): pl.pallas_call(functools.partial(final_kernel, (S, R, L)), out_shape=shap...  3.1 us
    pallas_call x1, Pallas kernels, on_device(): pl.pallas_call(up_kernel, out_shape=shape((par_dev, rank), F32), in_specs...  3.07 us
    unnamed x23, local copies, waits for them, and re-layouts  2.54 us
    pallas_call x1, Pallas kernels, on_device(): pl.pallas_call(functools.partial(pack_kernel, (C, S, L, slots)), out_shap...  2.02 us
  transfers between devices with their start and end apart: 10, of which 5 were waited for; matrix products, arithmetic and copies ran while one was open for 2% of the time, Pallas kernels for 4%

profile of v4, /device:TPU:0, one launch (start us, length us, event | category | flops | bytes accessed | tf_op | source)
XLA Modules:
  0.0 79.5 jit_solution(7981827650375840234)
XLA Ops:
  0.0 0.0 copy-start.10
  0.0 2.0 %packs.1 = (f32[128,128]{1,0:T(8,128)}, f32[88,128]{1,0:T(8,128)}, f32[88,128]{1,0:T(8,128)}, f32[88,128]{1,0:T(8,128)}) custom-call(f32[128,128]{1,0:T(8,128)} %charges.1, s32[128,128]{1,0:T(8,128)} %mask.3, f32[128,4,256]{2,1,0:T(4,128)} %geo.5, s32[4,16]{1,0:T(4,128)} %bitcast.13, s32[4,16]{1,0:T(4,128)} %bitcast.15, s32[4,16]{1,0:T(4,128)} %bitcast.16), custom_call_target="tpu_custom_call" | custom-call | tf_op jit(solution)/shard_map/packs/pallas_call | solution.py:483
  2.0 3.0 %collective-permute-start = (f32[88,128]{1,0:T(8,128)}, f32[88,128]{1,0:T(8,128)S(1)}, u32[]{:S(2)}, u32[]{:S(2)}) collective-permute-start(f32[88,128]{1,0:T(8,128)} %get-tuple-element.16), channel_id=1, source_target_pairs={{0,4},{4,8},{8,12},{12,0},{1,5},{5,9},{9,13},{13,1},{2,6},{6,10},{... | collective-permute-start | bytes 135176 | tf_op jit(solution)/shard_map/ppermute | solution.py:454
  5.0 2.6 %collective-permute-start.1 = (f32[88,128]{1,0:T(8,128)}, f32[88,128]{1,0:T(8,128)S(1)}, u32[]{:S(2)}, u32[]{:S(2)}) collective-permute-start(f32[88,128]{1,0:T(8,128)} %get-tuple-element.17), channel_id=1, source_target_pairs={{0,8},{4,12},{8,0},{12,4},{1,9},{5,13},{9,1},{13,5},{2,10},{6,14},... | collective-permute-start | bytes 135176 | tf_op jit(solution)/shard_map/ppermute | solution.py:454
  7.6 1.3 %collective-permute-start.2 = (f32[88,128]{1,0:T(8,128)}, f32[88,128]{1,0:T(8,128)S(1)}, u32[]{:S(2)}, u32[]{:S(2)}) collective-permute-start(f32[88,128]{1,0:T(8,128)} %get-tuple-element.18), channel_id=1, source_target_pairs={{0,12},{4,0},{8,4},{12,8},{1,13},{5,1},{9,5},{13,9},{2,14},{6,2},{... | collective-permute-start | bytes 135176 | tf_op jit(solution)/shard_map/ppermute | solution.py:454
  9.0 1.5 %collective-permute-start.3 = (f32[128,128]{1,0:T(8,128)}, f32[128,128]{1,0:T(8,128)S(1)}, u32[]{:S(2)}, u32[]{:S(2)}) collective-permute-start(f32[128,128]{1,0:T(8,128)} %get-tuple-element.15.masked.rest_0_), channel_id=1, source_target_pairs={{0,2},{2,0},{1,3},{3,1},{4,6},{6,4},{5,7},{7,5},{8,10},{10,8},{9,1... | collective-permute-start | bytes 196616 | tf_op jit(solution)/shard_map/ppermute | solution.py:454
  10.5 3.1 %far_up.1.up = f32[16,32]{1,0:T(8,128)} custom-call(f32[128,32,128]{2,1,0:T(8,128)} %bitcast.9, f32[128,128]{1,0:T(8,128)} %get-tuple-element.15.masked.rest_0_, f32[32,32,128]{2,1,0:T(8,128)} %bitcast.11, s32[1,128]{1,0:T(1,128)} %bitcast.17), custom_call_target="tpu_custom_call" | custom-call | tf_op jit(solution)/shard_map/far_up/pallas_call | solution.py:496
  13.6 0.0 collective-permute-done.rest_2_
  13.6 0.0 copy-start.4
  13.6 0.0 collective-permute-done.1.rest_3_
  13.6 0.0 copy-start.5
  13.6 0.0 collective-permute-done.2.rest_4_
  13.6 0.0 copy-start.6
  13.6 0.6 maximum_convert_fusion.codes
  14.2 0.0 collective-permute-done.3.rest_1_
  14.2 0.0 copy-done.4
  14.2 0.0 copy-done.5
  14.2 0.0 copy-done.6
  14.3 0.0 copy-start
  14.3 0.6 copy-done
  14.9 12.1 %near_remote.1 = (f32[128,256]{1,0:T(8,128)}, f32[32,128]{1,0:T(8,128)}, f32[32,128]{1,0:T(8,128)}, f32[32,128]{1,0:T(8,128)}) custom-call(f32[128,4,256]{2,1,0:T(4,128)} %geo.5, s32[3,16]{1,0:T(4,128)} %maximum_convert_fusion.codes, f32[16,32]{1,0:T(8,128)} %far_up.1.up, f32[128,128]{1,0:T(8,128)} %get-tuple-element.15.masked.rest_0_, f32[128,128]{1,0:T(8,128)} %copy-done, ...), custom_call_target="tpu_custom_call" | custom-call | tf_op jit(solution)/shard_map/near_remote/pallas_call | solution.py:505
  26.9 1.4 %collective-permute-start.4 = (f32[32,128]{1,0:T(8,128)}, f32[32,128]{1,0:T(8,128)S(1)}, u32[]{:S(2)}, u32[]{:S(2)}) collective-permute-start(f32[32,128]{1,0:T(8,128)} %get-tuple-element.20), channel_id=1, source_target_pairs={{0,12},{4,0},{8,4},{12,8},{1,13},{5,1},{9,5},{13,9},{2,14},{6,2},{... | collective-permute-start | bytes 49160 | tf_op jit(solution)/shard_map/ppermute | solution.py:454
  28.4 0.0 collective-permute-start.5
  28.4 0.9 %collective-permute-start.6 = (f32[32,128]{1,0:T(8,128)}, f32[32,128]{1,0:T(8,128)S(1)}, u32[]{:S(2)}, u32[]{:S(2)}) collective-permute-start(f32[32,128]{1,0:T(8,128)} %get-tuple-element.22), channel_id=1, source_target_pairs={{0,4},{4,8},{8,12},{12,0},{1,5},{5,9},{9,13},{13,1},{2,6},{6,10},{... | collective-permute-start | bytes 49160 | tf_op jit(solution)/shard_map/ppermute | solution.py:454
  29.3 0.0 copy-done.10
  29.3 0.7 copy.13.far_list
  30.0 0.9 %collective-permute-done.4.rest_2_ = f32[32,128]{1,0:T(8,128)S(1)} collective-permute-done((f32[32,128]{1,0:T(8,128)}, f32[32,128]{1,0:T(8,128)S(1)}, u32[]{:S(2)}, u32[]{:S(2)}) %collective-permute-start.4) | collective-permute-done | bytes 16416 | tf_op jit(solution)/shard_map/ppermute | solution.py:454
  30.9 0.0 copy-start.7
  30.9 2.5 %collective-permute-done.5.rest_3_ = f32[32,128]{1,0:T(8,128)S(1)} collective-permute-done((f32[32,128]{1,0:T(8,128)}, f32[32,128]{1,0:T(8,128)S(1)}, u32[]{:S(2)}, u32[]{:S(2)}) %collective-permute-start.5) | collective-permute-done | bytes 16416 | tf_op jit(solution)/shard_map/ppermute | solution.py:454
  33.4 0.0 copy-start.8
  33.4 0.7 collective-permute-done.6.rest_4_
  34.1 0.0 copy-start.9
  34.1 0.0 copy-done.7
  34.1 0.0 copy-done.8
  34.1 0.6 copy-done.9
  34.7 34.3 %near_local.1 = (f32[160,128]{1,0:T(8,128)}, f32[160,128]{1,0:T(8,128)}) custom-call(f32[128,4,256]{2,1,0:T(4,128)} %geo.5, s32[2,128]{1,0:T(2,128)} %bitcast.19, s32[4,16]{1,0:T(4,128)} %bitcast.14, s32[16,8]{1,0:T(8,128)} %copy.13.far_list, f32[16,8,32,32]{3,2,1,0:T(8,128)} %coupling.1, f32[32,32,128]{2,1,0:T(8,128)} %bitcast.12, s32[1,128]{1,0:T(1,128)} %bitcast.18, ...), custom_call_target="tpu_custom_call" | custom-call | tf_op jit(solution)/shard_map/near_local/pallas_call | solution.py:530
  69.0 0.0 collective-permute-start.7
  69.0 1.6 %collective-permute-start.9 = (f32[160,128]{1,0:T(8,128)}, f32[160,128]{1,0:T(8,128)S(1)}, u32[]{:S(2)}, u32[]{:S(2)}) collective-permute-start(f32[160,128]{1,0:T(8,128)} %get-tuple-element.24), channel_id=1, source_target_pairs={{0,3},{1,2},{2,1},{3,0},{4,7},{5,6},{6,5},{7,4},{8,11},{9,10},{10,... | collective-permute-start | bytes 245768 | tf_op jit(solution)/shard_map/ppermute | solution.py:454
  70.7 0.5 collective-permute-start.8
  71.2 0.0 collective-permute-done.7.rest_1_
  71.2 0.0 copy-start.1
  71.2 2.6 %collective-permute-done.9.rest_3_ = f32[160,128]{1,0:T(8,128)S(1)} collective-permute-done((f32[160,128]{1,0:T(8,128)}, f32[160,128]{1,0:T(8,128)S(1)}, u32[]{:S(2)}, u32[]{:S(2)}) %collective-permute-start.9) | collective-permute-done | bytes 81952 | tf_op jit(solution)/shard_map/ppermute | solution.py:454
  73.8 0.0 copy-start.2
  73.8 2.0 %collective-permute-done.8.rest_2_ = f32[160,128]{1,0:T(8,128)S(1)} collective-permute-done((f32[160,128]{1,0:T(8,128)}, f32[160,128]{1,0:T(8,128)S(1)}, u32[]{:S(2)}, u32[]{:S(2)}) %collective-permute-start.8) | collective-permute-done | bytes 81952 | tf_op jit(solution)/shard_map/ppermute | solution.py:454
  75.8 0.0 copy-done.1
  75.8 0.0 copy-done.2
  75.8 0.6 copy-done.3
  76.5 3.1 %combine.1 = f32[128,128]{1,0:T(8,128)} custom-call(s32[128,128]{1,0:T(8,128)} %mask.3, f32[128,32,128]{2,1,0:T(8,128)} %bitcast.10, f32[160,128]{1,0:T(8,128)} %get-tuple-element.23.rest_0_, f32[160,128]{1,0:T(8,128)} %copy-done.1, f32[160,128]{1,0:T(8,128)} %copy-done.3, f32[160,128]{1,0:T(8,128)} %copy-done.2), custom_call_target="tpu_custom_call" | custom-call | tf_op jit(solution)/shard_map/combine/pallas_call | solution.py:557
  (4 shorter events, 0.0 us)
Async XLA Ops:
  0.0 29.3 %copy-start.10 = (s32[16,8]{0,1:T(8,128)S(1)}, s32[16,8]{0,1:T(8,128)}, u32[]{:S(2)}) copy-start(s32[16,8]{0,1:T(8,128)} %param.22) | copy-start | bytes 1540
  2.0 11.5 %collective-permute-start = (f32[88,128]{1,0:T(8,128)}, f32[88,128]{1,0:T(8,128)S(1)}, u32[]{:S(2)}, u32[]{:S(2)}) collective-permute-start(f32[88,128]{1,0:T(8,128)} %get-tuple-element.16), channel_id=1, source_target_pairs={{0,4},{4,8},{8,12},{12,0},{1,5},{5,9},{9,13},{13,1},{2,6},{6,10},{... | collective-permute-start | bytes 135176 | tf_op jit(solution)/shard_map/ppermute | solution.py:454
  5.0 8.5 %collective-permute-start.1 = (f32[88,128]{1,0:T(8,128)}, f32[88,128]{1,0:T(8,128)S(1)}, u32[]{:S(2)}, u32[]{:S(2)}) collective-permute-start(f32[88,128]{1,0:T(8,128)} %get-tuple-element.17), channel_id=1, source_target_pairs={{0,8},{4,12},{8,0},{12,4},{1,9},{5,13},{9,1},{13,5},{2,10},{6,14},... | collective-permute-start | bytes 135176 | tf_op jit(solution)/shard_map/ppermute | solution.py:454
  7.6 6.0 %collective-permute-start.2 = (f32[88,128]{1,0:T(8,128)}, f32[88,128]{1,0:T(8,128)S(1)}, u32[]{:S(2)}, u32[]{:S(2)}) collective-permute-start(f32[88,128]{1,0:T(8,128)} %get-tuple-element.18), channel_id=1, source_target_pairs={{0,12},{4,0},{8,4},{12,8},{1,13},{5,1},{9,5},{13,9},{2,14},{6,2},{... | collective-permute-start | bytes 135176 | tf_op jit(solution)/shard_map/ppermute | solution.py:454
  9.0 5.3 %collective-permute-start.3 = (f32[128,128]{1,0:T(8,128)}, f32[128,128]{1,0:T(8,128)S(1)}, u32[]{:S(2)}, u32[]{:S(2)}) collective-permute-start(f32[128,128]{1,0:T(8,128)} %get-tuple-element.15.masked.rest_0_), channel_id=1, source_target_pairs={{0,2},{2,0},{1,3},{3,1},{4,6},{6,4},{5,7},{7,5},{8,10},{10,8},{9,1... | collective-permute-start | bytes 196616 | tf_op jit(solution)/shard_map/ppermute | solution.py:454
  13.6 0.7 copy-start.4
  13.6 0.7 copy-start.5
  13.6 0.6 copy-start.6
  14.3 0.6 copy-start
  26.9 3.9 %collective-permute-start.4 = (f32[32,128]{1,0:T(8,128)}, f32[32,128]{1,0:T(8,128)S(1)}, u32[]{:S(2)}, u32[]{:S(2)}) collective-permute-start(f32[32,128]{1,0:T(8,128)} %get-tuple-element.20), channel_id=1, source_target_pairs={{0,12},{4,0},{8,4},{12,8},{1,13},{5,1},{9,5},{13,9},{2,14},{6,2},{... | collective-permute-start | bytes 49160 | tf_op jit(solution)/shard_map/ppermute | solution.py:454
  28.4 5.0 %collective-permute-start.5 = (f32[32,128]{1,0:T(8,128)}, f32[32,128]{1,0:T(8,128)S(1)}, u32[]{:S(2)}, u32[]{:S(2)}) collective-permute-start(f32[32,128]{1,0:T(8,128)} %get-tuple-element.21), channel_id=1, source_target_pairs={{0,8},{4,12},{8,0},{12,4},{1,9},{5,13},{9,1},{13,5},{2,10},{6,14},... | collective-permute-start | bytes 49160 | tf_op jit(solution)/shard_map/ppermute | solution.py:454
  28.4 5.7 %collective-permute-start.6 = (f32[32,128]{1,0:T(8,128)}, f32[32,128]{1,0:T(8,128)S(1)}, u32[]{:S(2)}, u32[]{:S(2)}) collective-permute-start(f32[32,128]{1,0:T(8,128)} %get-tuple-element.22), channel_id=1, source_target_pairs={{0,4},{4,8},{8,12},{12,0},{1,5},{5,9},{9,13},{13,1},{2,6},{6,10},{... | collective-permute-start | bytes 49160 | tf_op jit(solution)/shard_map/ppermute | solution.py:454
  30.9 3.2 %copy-start.7 = (f32[32,128]{1,0:T(8,128)}, f32[32,128]{1,0:T(8,128)S(1)}, u32[]{:S(2)}) copy-start(f32[32,128]{1,0:T(8,128)S(1)} %collective-permute-done.4.rest_2_) | copy-start | bytes 49156
  33.4 0.7 copy-start.8
  34.1 0.6 copy-start.9
  69.0 2.1 %collective-permute-start.7 = (f32[160,128]{1,0:T(8,128)}, f32[160,128]{1,0:T(8,128)S(1)}, u32[]{:S(2)}, u32[]{:S(2)}) collective-permute-start(f32[160,128]{1,0:T(8,128)} %get-tuple-element.23.rest_0_), channel_id=1, source_target_pairs={{0,1},{1,0},{2,3},{3,2},{4,5},{5,4},{6,7},{7,6},{8,9},{9,8},{10,11... | collective-permute-start | bytes 245768 | tf_op jit(solution)/shard_map/ppermute | solution.py:454
  69.0 4.7 %collective-permute-start.9 = (f32[160,128]{1,0:T(8,128)}, f32[160,128]{1,0:T(8,128)S(1)}, u32[]{:S(2)}, u32[]{:S(2)}) collective-permute-start(f32[160,128]{1,0:T(8,128)} %get-tuple-element.24), channel_id=1, source_target_pairs={{0,3},{1,2},{2,1},{3,0},{4,7},{5,6},{6,5},{7,4},{8,11},{9,10},{10,... | collective-permute-start | bytes 245768 | tf_op jit(solution)/shard_map/ppermute | solution.py:454
  70.7 5.2 %collective-permute-start.8 = (f32[160,128]{1,0:T(8,128)}, f32[160,128]{1,0:T(8,128)S(1)}, u32[]{:S(2)}, u32[]{:S(2)}) collective-permute-start(f32[160,128]{1,0:T(8,128)} %get-tuple-element.24), channel_id=1, source_target_pairs={{0,2},{1,3},{2,0},{3,1},{4,6},{5,7},{6,4},{7,5},{8,10},{9,11},{10,... | collective-permute-start | bytes 245768 | tf_op jit(solution)/shard_map/ppermute | solution.py:454
  71.2 4.6 %copy-start.1 = (f32[160,128]{1,0:T(8,128)}, f32[160,128]{1,0:T(8,128)S(1)}, u32[]{:S(2)}) copy-start(f32[160,128]{1,0:T(8,128)S(1)} %collective-permute-done.7.rest_1_) | copy-start | bytes 245764
  73.8 2.1 %copy-start.2 = (f32[160,128]{1,0:T(8,128)}, f32[160,128]{1,0:T(8,128)S(1)}, u32[]{:S(2)}) copy-start(f32[160,128]{1,0:T(8,128)S(1)} %collective-permute-done.9.rest_3_) | copy-start | bytes 245764
  75.8 0.6 copy-start.3

commit v5 on v3

--- a/solution.py
+++ b/solution.py
@@ -103,7 +103,7 @@
 
 
 def contract(left, right):
-    return lax.dot_general(left, right, (((0,), (0,)), ((), ())), preferred_element_type=F32)
+    return jnp.dot(left, right, preferred_element_type=F32)
 
 
 def pick(rows, width, index):
@@ -122,8 +122,8 @@
 
 def distances(left, right, out):
     whole_left = jnp.concatenate(left, axis=1) if len(left) > 1 else left[0]
-    for t, r in enumerate(list(right) + [charge_rows()]):
-        out[:, t * LANES : (t + 1) * LANES] = contract(whole_left, r)
+    whole_right = jnp.concatenate(list(right) + [charge_rows()], axis=1)
+    out[...] = contract(whole_left.T, whole_right)
 
 
 def keep(parts, rows, value):
@@ -285,10 +285,8 @@
         c = first + jnp.minimum(i, share - 1)
         a = load_features(fa, c)
         b = load_features(fb, c)
-        dist[:half, :half] = contract(a[0], b[0])
-        dist[:half, half:panels] = contract(a[0], b[1])
-        dist[:half, panels:] = contract(a[0], charge_rows())
-        dist[half:, half:panels] = contract(a[1], b[1])
+        dist[:half, :] = contract(a[0].T, jnp.concatenate([b[0], b[1], charge_rows()], axis=1))
+        dist[half:, half:panels] = contract(a[1].T, b[1])
 
     def finish_self(i, dist, parts):
         c = first + i

time: 74.4 us -> 75.7 us (1.017)
  Pallas kernels: 48.9 us -> 49.8 us
where the time goes in v5:
time: 75.7 us; the launch traced here: 75.5 us
  Pallas kernels  49.8 us (66%)
  starting transfers between devices  12.9 us (17%)
  waiting for transfers between devices  9.49 us (13%)
  local copies, waits for them, and re-layouts  2.55 us (3%)
    pallas_call x1, Pallas kernels, on_device(): pl.pallas_call(functools.partial(local_kernel, (C, S, L, R, slots, cluste...  29.8 us
    ppermute x10, starting transfers between devices, send(): return lax.ppermute(value, names if len(names) > 1 else names[0], perm)  12.9 us
    pallas_call x1, Pallas kernels, on_device(): pl.pallas_call(functools.partial(remote_kernel, (C, S, L, slots, clusters...  11.7 us
    ppermute x10, waiting for transfers between devices, send(): return lax.ppermute(value, names if len(names) > 1 else names[0], perm)  9.49 us
    pallas_call x1, Pallas kernels, on_device(): pl.pallas_call(functools.partial(final_kernel, (S, R, L)), out_shape=shap...  3.1 us
    pallas_call x1, Pallas kernels, on_device(): pl.pallas_call(up_kernel, out_shape=shape((par_dev, rank), F32), in_specs...  3.07 us
    unnamed x23, local copies, waits for them, and re-layouts  2.54 us
    pallas_call x1, Pallas kernels, on_device(): pl.pallas_call(functools.partial(pack_kernel, (C, S, L, slots)), out_shap...  2.02 us
  transfers between devices with their start and end apart: 10, of which 5 were waited for; matrix products, arithmetic and copies ran while one was open for 2% of the time, Pallas kernels for 4%

profile of v5, /device:TPU:0, one launch (start us, length us, event | category | flops | bytes accessed | tf_op | source)
XLA Modules:
  0.0 75.5 jit_solution(4543041286747473211)
XLA Ops:
  0.0 0.0 copy-start.10
  0.0 2.0 %packs.1 = (f32[128,128]{1,0:T(8,128)}, f32[88,128]{1,0:T(8,128)}, f32[88,128]{1,0:T(8,128)}, f32[88,128]{1,0:T(8,128)}) custom-call(f32[128,128]{1,0:T(8,128)} %charges.1, s32[128,128]{1,0:T(8,128)} %mask.3, f32[128,4,256]{2,1,0:T(4,128)} %geo.5, s32[4,16]{1,0:T(4,128)} %bitcast.13, s32[4,16]{1,0:T(4,128)} %bitcast.15, s32[4,16]{1,0:T(4,128)} %bitcast.16), custom_call_target="tpu_custom_call" | custom-call | tf_op jit(solution)/shard_map/packs/pallas_call | solution.py:476
  2.0 3.0 %collective-permute-start = (f32[88,128]{1,0:T(8,128)}, f32[88,128]{1,0:T(8,128)S(1)}, u32[]{:S(2)}, u32[]{:S(2)}) collective-permute-start(f32[88,128]{1,0:T(8,128)} %get-tuple-element.16), channel_id=1, source_target_pairs={{0,4},{4,8},{8,12},{12,0},{1,5},{5,9},{9,13},{13,1},{2,6},{6,10},{... | collective-permute-start | bytes 135176 | tf_op jit(solution)/shard_map/ppermute | solution.py:447
  5.0 2.6 %collective-permute-start.1 = (f32[88,128]{1,0:T(8,128)}, f32[88,128]{1,0:T(8,128)S(1)}, u32[]{:S(2)}, u32[]{:S(2)}) collective-permute-start(f32[88,128]{1,0:T(8,128)} %get-tuple-element.17), channel_id=1, source_target_pairs={{0,8},{4,12},{8,0},{12,4},{1,9},{5,13},{9,1},{13,5},{2,10},{6,14},... | collective-permute-start | bytes 135176 | tf_op jit(solution)/shard_map/ppermute | solution.py:447
  7.6 1.3 %collective-permute-start.2 = (f32[88,128]{1,0:T(8,128)}, f32[88,128]{1,0:T(8,128)S(1)}, u32[]{:S(2)}, u32[]{:S(2)}) collective-permute-start(f32[88,128]{1,0:T(8,128)} %get-tuple-element.18), channel_id=1, source_target_pairs={{0,12},{4,0},{8,4},{12,8},{1,13},{5,1},{9,5},{13,9},{2,14},{6,2},{... | collective-permute-start | bytes 135176 | tf_op jit(solution)/shard_map/ppermute | solution.py:447
  9.0 1.5 %collective-permute-start.3 = (f32[128,128]{1,0:T(8,128)}, f32[128,128]{1,0:T(8,128)S(1)}, u32[]{:S(2)}, u32[]{:S(2)}) collective-permute-start(f32[128,128]{1,0:T(8,128)} %get-tuple-element.15.masked.rest_0_), channel_id=1, source_target_pairs={{0,2},{2,0},{1,3},{3,1},{4,6},{6,4},{5,7},{7,5},{8,10},{10,8},{9,1... | collective-permute-start | bytes 196616 | tf_op jit(solution)/shard_map/ppermute | solution.py:447
  10.5 3.1 %far_up.1.up = f32[16,32]{1,0:T(8,128)} custom-call(f32[128,32,128]{2,1,0:T(8,128)} %bitcast.9, f32[128,128]{1,0:T(8,128)} %get-tuple-element.15.masked.rest_0_, f32[32,32,128]{2,1,0:T(8,128)} %bitcast.11, s32[1,128]{1,0:T(1,128)} %bitcast.17), custom_call_target="tpu_custom_call" | custom-call | tf_op jit(solution)/shard_map/far_up/pallas_call | solution.py:489
  13.6 0.0 collective-permute-done.rest_2_
  13.6 0.0 copy-start.4
  13.6 0.0 collective-permute-done.1.rest_3_
  13.6 0.0 copy-start.5
  13.6 0.0 collective-permute-done.2.rest_4_
  13.6 0.0 copy-start.6
  13.6 0.6 maximum_convert_fusion.codes
  14.2 0.0 collective-permute-done.3.rest_1_
  14.2 0.0 copy-done.4
  14.2 0.0 copy-done.5
  14.2 0.0 copy-done.6
  14.3 0.0 copy-start
  14.3 0.6 copy-done
  14.9 11.7 %near_remote.1 = (f32[128,256]{1,0:T(8,128)}, f32[32,128]{1,0:T(8,128)}, f32[32,128]{1,0:T(8,128)}, f32[32,128]{1,0:T(8,128)}) custom-call(f32[128,4,256]{2,1,0:T(4,128)} %geo.5, s32[3,16]{1,0:T(4,128)} %maximum_convert_fusion.codes, f32[16,32]{1,0:T(8,128)} %far_up.1.up, f32[128,128]{1,0:T(8,128)} %get-tuple-element.15.masked.rest_0_, f32[128,128]{1,0:T(8,128)} %copy-done, ...), custom_call_target="tpu_custom_call" | custom-call | tf_op jit(solution)/shard_map/near_remote/pallas_call | solution.py:498
  26.6 0.7 collective-permute-start.4
  27.3 1.4 %collective-permute-start.5 = (f32[32,128]{1,0:T(8,128)}, f32[32,128]{1,0:T(8,128)S(1)}, u32[]{:S(2)}, u32[]{:S(2)}) collective-permute-start(f32[32,128]{1,0:T(8,128)} %get-tuple-element.21), channel_id=1, source_target_pairs={{0,8},{4,12},{8,0},{12,4},{1,9},{5,13},{9,1},{13,5},{2,10},{6,14},... | collective-permute-start | bytes 49160 | tf_op jit(solution)/shard_map/ppermute | solution.py:447
  28.8 0.2 collective-permute-start.6
  29.0 0.0 copy-done.10
  29.0 0.7 copy.13.far_list
  29.6 0.9 %collective-permute-done.4.rest_2_ = f32[32,128]{1,0:T(8,128)S(1)} collective-permute-done((f32[32,128]{1,0:T(8,128)}, f32[32,128]{1,0:T(8,128)S(1)}, u32[]{:S(2)}, u32[]{:S(2)}) %collective-permute-start.4) | collective-permute-done | bytes 16416 | tf_op jit(solution)/shard_map/ppermute | solution.py:447
  30.6 0.0 copy-start.7
  30.6 1.6 %collective-permute-done.5.rest_3_ = f32[32,128]{1,0:T(8,128)S(1)} collective-permute-done((f32[32,128]{1,0:T(8,128)}, f32[32,128]{1,0:T(8,128)S(1)}, u32[]{:S(2)}, u32[]{:S(2)}) %collective-permute-start.5) | collective-permute-done | bytes 16416 | tf_op jit(solution)/shard_map/ppermute | solution.py:447
  32.2 0.0 copy-start.8
  32.2 2.3 %collective-permute-done.6.rest_4_ = f32[32,128]{1,0:T(8,128)S(1)} collective-permute-done((f32[32,128]{1,0:T(8,128)}, f32[32,128]{1,0:T(8,128)S(1)}, u32[]{:S(2)}, u32[]{:S(2)}) %collective-permute-start.6) | collective-permute-done | bytes 16416 | tf_op jit(solution)/shard_map/ppermute | solution.py:447
  34.5 0.0 copy-start.9
  34.5 0.0 copy-done.7
  34.5 0.0 copy-done.8
  34.5 0.6 copy-done.9
  35.1 29.8 %near_local.1 = (f32[160,128]{1,0:T(8,128)}, f32[160,128]{1,0:T(8,128)}) custom-call(f32[128,4,256]{2,1,0:T(4,128)} %geo.5, s32[2,128]{1,0:T(2,128)} %bitcast.19, s32[4,16]{1,0:T(4,128)} %bitcast.14, s32[16,8]{1,0:T(8,128)} %copy.13.far_list, f32[16,8,32,32]{3,2,1,0:T(8,128)} %coupling.1, f32[32,32,128]{2,1,0:T(8,128)} %bitcast.12, s32[1,128]{1,0:T(1,128)} %bitcast.18, ...), custom_call_target="tpu_custom_call" | custom-call | tf_op jit(solution)/shard_map/near_local/pallas_call | solution.py:523
  64.9 0.0 collective-permute-start.7
  64.9 0.8 %collective-permute-start.9 = (f32[160,128]{1,0:T(8,128)}, f32[160,128]{1,0:T(8,128)S(1)}, u32[]{:S(2)}, u32[]{:S(2)}) collective-permute-start(f32[160,128]{1,0:T(8,128)} %get-tuple-element.24), channel_id=1, source_target_pairs={{0,3},{1,2},{2,1},{3,0},{4,7},{5,6},{6,5},{7,4},{8,11},{9,10},{10,... | collective-permute-start | bytes 245768 | tf_op jit(solution)/shard_map/ppermute | solution.py:447
  65.7 1.3 %collective-permute-start.8 = (f32[160,128]{1,0:T(8,128)}, f32[160,128]{1,0:T(8,128)S(1)}, u32[]{:S(2)}, u32[]{:S(2)}) collective-permute-start(f32[160,128]{1,0:T(8,128)} %get-tuple-element.24), channel_id=1, source_target_pairs={{0,2},{1,3},{2,0},{3,1},{4,6},{5,7},{6,4},{7,5},{8,10},{9,11},{10,... | collective-permute-start | bytes 245768 | tf_op jit(solution)/shard_map/ppermute | solution.py:447
  67.1 0.0 collective-permute-done.7.rest_1_
  67.1 0.0 copy-start.1
  67.1 2.3 %collective-permute-done.9.rest_3_ = f32[160,128]{1,0:T(8,128)S(1)} collective-permute-done((f32[160,128]{1,0:T(8,128)}, f32[160,128]{1,0:T(8,128)S(1)}, u32[]{:S(2)}, u32[]{:S(2)}) %collective-permute-start.9) | collective-permute-done | bytes 81952 | tf_op jit(solution)/shard_map/ppermute | solution.py:447
  69.4 0.0 copy-start.2
  69.4 2.3 %collective-permute-done.8.rest_2_ = f32[160,128]{1,0:T(8,128)S(1)} collective-permute-done((f32[160,128]{1,0:T(8,128)}, f32[160,128]{1,0:T(8,128)S(1)}, u32[]{:S(2)}, u32[]{:S(2)}) %collective-permute-start.8) | collective-permute-done | bytes 81952 | tf_op jit(solution)/shard_map/ppermute | solution.py:447
  71.7 0.0 copy-done.1
  71.7 0.0 copy-done.2
  71.7 0.6 copy-done.3
  72.4 3.1 %combine.1 = f32[128,128]{1,0:T(8,128)} custom-call(s32[128,128]{1,0:T(8,128)} %mask.3, f32[128,32,128]{2,1,0:T(8,128)} %bitcast.10, f32[160,128]{1,0:T(8,128)} %get-tuple-element.23.rest_0_, f32[160,128]{1,0:T(8,128)} %copy-done.1, f32[160,128]{1,0:T(8,128)} %copy-done.3, f32[160,128]{1,0:T(8,128)} %copy-done.2), custom_call_target="tpu_custom_call" | custom-call | tf_op jit(solution)/shard_map/combine/pallas_call | solution.py:550
  (4 shorter events, 0.0 us)
Async XLA Ops:
  0.0 29.0 %copy-start.10 = (s32[16,8]{0,1:T(8,128)S(1)}, s32[16,8]{0,1:T(8,128)}, u32[]{:S(2)}) copy-start(s32[16,8]{0,1:T(8,128)} %param.22) | copy-start | bytes 1540
  2.0 11.5 %collective-permute-start = (f32[88,128]{1,0:T(8,128)}, f32[88,128]{1,0:T(8,128)S(1)}, u32[]{:S(2)}, u32[]{:S(2)}) collective-permute-start(f32[88,128]{1,0:T(8,128)} %get-tuple-element.16), channel_id=1, source_target_pairs={{0,4},{4,8},{8,12},{12,0},{1,5},{5,9},{9,13},{13,1},{2,6},{6,10},{... | collective-permute-start | bytes 135176 | tf_op jit(solution)/shard_map/ppermute | solution.py:447
  5.0 8.5 %collective-permute-start.1 = (f32[88,128]{1,0:T(8,128)}, f32[88,128]{1,0:T(8,128)S(1)}, u32[]{:S(2)}, u32[]{:S(2)}) collective-permute-start(f32[88,128]{1,0:T(8,128)} %get-tuple-element.17), channel_id=1, source_target_pairs={{0,8},{4,12},{8,0},{12,4},{1,9},{5,13},{9,1},{13,5},{2,10},{6,14},... | collective-permute-start | bytes 135176 | tf_op jit(solution)/shard_map/ppermute | solution.py:447
  7.6 6.0 %collective-permute-start.2 = (f32[88,128]{1,0:T(8,128)}, f32[88,128]{1,0:T(8,128)S(1)}, u32[]{:S(2)}, u32[]{:S(2)}) collective-permute-start(f32[88,128]{1,0:T(8,128)} %get-tuple-element.18), channel_id=1, source_target_pairs={{0,12},{4,0},{8,4},{12,8},{1,13},{5,1},{9,5},{13,9},{2,14},{6,2},{... | collective-permute-start | bytes 135176 | tf_op jit(solution)/shard_map/ppermute | solution.py:447
  9.0 5.3 %collective-permute-start.3 = (f32[128,128]{1,0:T(8,128)}, f32[128,128]{1,0:T(8,128)S(1)}, u32[]{:S(2)}, u32[]{:S(2)}) collective-permute-start(f32[128,128]{1,0:T(8,128)} %get-tuple-element.15.masked.rest_0_), channel_id=1, source_target_pairs={{0,2},{2,0},{1,3},{3,1},{4,6},{6,4},{5,7},{7,5},{8,10},{10,8},{9,1... | collective-permute-start | bytes 196616 | tf_op jit(solution)/shard_map/ppermute | solution.py:447
  13.6 0.7 copy-start.4
  13.6 0.7 copy-start.5
  13.6 0.6 copy-start.6
  14.3 0.6 copy-start
  26.6 3.9 %collective-permute-start.4 = (f32[32,128]{1,0:T(8,128)}, f32[32,128]{1,0:T(8,128)S(1)}, u32[]{:S(2)}, u32[]{:S(2)}) collective-permute-start(f32[32,128]{1,0:T(8,128)} %get-tuple-element.20), channel_id=1, source_target_pairs={{0,12},{4,0},{8,4},{12,8},{1,13},{5,1},{9,5},{13,9},{2,14},{6,2},{... | collective-permute-start | bytes 49160 | tf_op jit(solution)/shard_map/ppermute | solution.py:447
  27.3 4.8 %collective-permute-start.5 = (f32[32,128]{1,0:T(8,128)}, f32[32,128]{1,0:T(8,128)S(1)}, u32[]{:S(2)}, u32[]{:S(2)}) collective-permute-start(f32[32,128]{1,0:T(8,128)} %get-tuple-element.21), channel_id=1, source_target_pairs={{0,8},{4,12},{8,0},{12,4},{1,9},{5,13},{9,1},{13,5},{2,10},{6,14},... | collective-permute-start | bytes 49160 | tf_op jit(solution)/shard_map/ppermute | solution.py:447
  28.8 5.7 %collective-permute-start.6 = (f32[32,128]{1,0:T(8,128)}, f32[32,128]{1,0:T(8,128)S(1)}, u32[]{:S(2)}, u32[]{:S(2)}) collective-permute-start(f32[32,128]{1,0:T(8,128)} %get-tuple-element.22), channel_id=1, source_target_pairs={{0,4},{4,8},{8,12},{12,0},{1,5},{5,9},{9,13},{13,1},{2,6},{6,10},{... | collective-permute-start | bytes 49160 | tf_op jit(solution)/shard_map/ppermute | solution.py:447
  30.6 3.9 %copy-start.7 = (f32[32,128]{1,0:T(8,128)}, f32[32,128]{1,0:T(8,128)S(1)}, u32[]{:S(2)}) copy-start(f32[32,128]{1,0:T(8,128)S(1)} %collective-permute-done.4.rest_2_) | copy-start | bytes 49156
  32.2 2.3 %copy-start.8 = (f32[32,128]{1,0:T(8,128)}, f32[32,128]{1,0:T(8,128)S(1)}, u32[]{:S(2)}) copy-start(f32[32,128]{1,0:T(8,128)S(1)} %collective-permute-done.5.rest_3_) | copy-start | bytes 49156
  34.5 0.6 copy-start.9
  64.9 2.1 %collective-permute-start.7 = (f32[160,128]{1,0:T(8,128)}, f32[160,128]{1,0:T(8,128)S(1)}, u32[]{:S(2)}, u32[]{:S(2)}) collective-permute-start(f32[160,128]{1,0:T(8,128)} %get-tuple-element.23.rest_0_), channel_id=1, source_target_pairs={{0,1},{1,0},{2,3},{3,2},{4,5},{5,4},{6,7},{7,6},{8,9},{9,8},{10,11... | collective-permute-start | bytes 245768 | tf_op jit(solution)/shard_map/ppermute | solution.py:447
  64.9 4.4 %collective-permute-start.9 = (f32[160,128]{1,0:T(8,128)}, f32[160,128]{1,0:T(8,128)S(1)}, u32[]{:S(2)}, u32[]{:S(2)}) collective-permute-start(f32[160,128]{1,0:T(8,128)} %get-tuple-element.24), channel_id=1, source_target_pairs={{0,3},{1,2},{2,1},{3,0},{4,7},{5,6},{6,5},{7,4},{8,11},{9,10},{10,... | collective-permute-start | bytes 245768 | tf_op jit(solution)/shard_map/ppermute | solution.py:447
  65.7 6.0 %collective-permute-start.8 = (f32[160,128]{1,0:T(8,128)}, f32[160,128]{1,0:T(8,128)S(1)}, u32[]{:S(2)}, u32[]{:S(2)}) collective-permute-start(f32[160,128]{1,0:T(8,128)} %get-tuple-element.24), channel_id=1, source_target_pairs={{0,2},{1,3},{2,0},{3,1},{4,6},{5,7},{6,4},{7,5},{8,10},{9,11},{10,... | collective-permute-start | bytes 245768 | tf_op jit(solution)/shard_map/ppermute | solution.py:447
  67.1 4.6 %copy-start.1 = (f32[160,128]{1,0:T(8,128)}, f32[160,128]{1,0:T(8,128)S(1)}, u32[]{:S(2)}) copy-start(f32[160,128]{1,0:T(8,128)S(1)} %collective-permute-done.7.rest_1_) | copy-start | bytes 245764
  69.4 2.3 %copy-start.2 = (f32[160,128]{1,0:T(8,128)}, f32[160,128]{1,0:T(8,128)S(1)}, u32[]{:S(2)}) copy-start(f32[160,128]{1,0:T(8,128)S(1)} %collective-permute-done.9.rest_3_) | copy-start | bytes 245764
  71.7 0.6 copy-start.3

commit v6 on v2

--- a/solution.py
+++ b/solution.py
@@ -109,9 +109,14 @@
     return jnp.broadcast_to(picked, (table.shape[0], LANES))
 
 
-def put_column(table_ref, rows, index, value):
-    lane = lax.broadcasted_iota(jnp.int32, (rows.stop - rows.start, table_ref.shape[1]), 1)
-    table_ref[rows, :] += jnp.where(lane == index, value, 0.0)
+def put_column(table, rows, index, value):
+    shape = (rows.stop - rows.start, table.shape[1])
+    lane = lax.broadcasted_iota(jnp.int32, shape, 1)
+    pltpu.store(table.at[rows, :], jnp.broadcast_to(value, shape), mask=lane == index)
+
+
+def inverse_root(d):
+    return lax.exp2(-0.5 * lax.log2(d))
 
 
 def fold(v):
@@ -131,8 +136,8 @@
     back0 = back1 = jnp.zeros((8, LANES), F32)
     for r in range(0, height, step):
         rows = slice(r, r + step)
-        g0 = lax.rsqrt(dist[rows, :LANES])
-        g1 = lax.rsqrt(dist[rows, LANES:])
+        g0 = inverse_root(dist[rows, :LANES])
+        g1 = inverse_root(dist[rows, LANES:])
         qcol = column(qtable[rows, :], slot)
         put_column(table_ref, rows, index, jnp.sum(g0 * q0 + g1 * q1, axis=1, keepdims=True))
         back0 = back0 + fold(g0 * qcol)
@@ -255,7 +260,7 @@
     pieces = rest[:S]
     sums = rest[S : S + C - 1]
     parts = rest[S + C - 1 : 2 * S + C - 1]
-    q, qt, acc, acct, fa0, fa1, fb0, fb1, rads, dist0, dist1, got, parents = rest[2 * S + C - 1 :]
+    q, qt, acc, acct, fa0, fa1, fb0, fb1, rads, dist0, dist1, got, parents, rows = rest[2 * S + C - 1 :]
     fa, fb = (fa0, fa1), (fb0, fb1)
     me, sub, rep = lax.axis_index("clu"), lax.axis_index("sub"), lax.axis_index("rep")
     assemble(sub, S, L, q, pieces)
@@ -289,20 +294,20 @@
         back = jnp.zeros((8, LANES), F32)
         step = 64
         for r in range(0, panels, step):
-            rows = slice(r, r + step)
+            span = slice(r, r + step)
             base = r % half
             eye = lax.broadcasted_iota(jnp.int32, (step, half), 0) + base == lax.broadcasted_iota(
                 jnp.int32, (step, half), 1
             )
             if r < half:
-                g0 = jnp.where(eye, diag[:, :half], lax.rsqrt(dist[rows, :half]))
-                g1 = lax.rsqrt(dist[rows, half:])
-                qcol = column(qt[rows, :], c)
+                g0 = jnp.where(eye, diag[:, :half], inverse_root(dist[span, :half]))
+                g1 = inverse_root(dist[span, half:])
+                qcol = column(qt[span, :], c)
                 back = back + fold(g1 * qcol)
                 part = g0 * qrow[:, :half] + g1 * qrow[:, half:]
             else:
-                part = jnp.where(eye, diag[:, half:], lax.rsqrt(dist[rows, half:])) * qrow[:, half:]
-            put_column(acct, rows, c, jnp.sum(part, axis=1, keepdims=True))
+                part = jnp.where(eye, diag[:, half:], inverse_root(dist[span, half:])) * qrow[:, half:]
+            put_column(acct, span, i, jnp.sum(part, axis=1, keepdims=True))
         back = jnp.sum(back, axis=0, keepdims=True)
         acc[pl.ds(c, 1), :] += jnp.concatenate([jnp.zeros_like(back), back], axis=1)
 
@@ -325,7 +330,7 @@
 
     def finish(i, dist):
         ia, ib = pairs[0, start + i], pairs[1, start + i]
-        acc[pl.ds(ib, 1), :] += tile_sums(dist, q[pl.ds(ib, 1), :], qt, ia, acct, ia)
+        acc[pl.ds(ib, 1), :] += tile_sums(dist, q[pl.ds(ib, 1), :], qt, ia, acct, share + i)
 
     def pair_step(i, carry):
         begin(2 * i + 1, dist1)
@@ -336,7 +341,12 @@
 
     begin(0, dist0)
     lax.fori_loop(0, count // 2, pair_step, 0)
-    total = acc_in[...] + (acc[...] + acct[...].T) * inv
+    rows[...] = acct[...].T
+    for i in range(share):
+        acc[pl.ds(first + i, 1), :] += rows[i : i + 1, :]
+    for i in range(count):
+        acc[pl.ds(pairs[0, start + i], 1), :] += rows[share + i : share + i + 1, :]
+    total = acc_in[...] + acc[...] * inv
 
     got[...] = jnp.zeros_like(got)
     for shift in range(1, C):
@@ -507,6 +517,7 @@
     )(geometry, codes, up, *pieces, *packs)
     acc, sums = made[0], [send(made[d], (("clu", C - d),)) for d in range(1, C)]
 
+    columns = whole(clusters // (S * R) + local_pairs.shape[1] // S)
     half = [pltpu.VMEM((clusters * ROWS, LANES), F32)] * 2
     parts = pl.pallas_call(
         functools.partial(local_kernel, (C, S, L, R, slots, clusters, panels)),
@@ -517,7 +528,7 @@
             pltpu.VMEM((clusters, panels), F32),
             pltpu.VMEM((panels, clusters), F32),
             pltpu.VMEM((clusters, panels), F32),
-            pltpu.VMEM((panels, clusters), F32),
+            pltpu.VMEM((panels, columns), F32),
             *half,
             *half,
             pltpu.VMEM((clusters, panels), F32),
@@ -525,6 +536,7 @@
             pltpu.VMEM((panels, panels), F32),
             pltpu.VMEM((clusters, L), F32),
             pltpu.VMEM((C * par_dev, rank), F32),
+            pltpu.VMEM((columns, panels), F32),
         ],
         compiler_params=PARAMS,
         name="near_local",

time: 72.5 us -> 74.6 us (1.029)
  Pallas kernels: 47.2 us -> 48.7 us
    pallas_call x1, Pallas kernels: 28.5 us -> 29.6 us  [on_device(): pl.pallas_call(functools.partial(local_kernel, (C, S, L, R, slots, cluste...]
where the time goes in v6:
time: 74.6 us; the launch traced here: 74.4 us
  Pallas kernels  48.7 us (65%)
  starting transfers between devices  13 us (17%)
  waiting for transfers between devices  9.49 us (13%)
  local copies, waits for them, and re-layouts  2.55 us (3%)
    pallas_call x1, Pallas kernels, on_device(): pl.pallas_call(functools.partial(local_kernel, (C, S, L, R, slots, cluste...  29.6 us
    ppermute x10, starting transfers between devices, send(): return lax.ppermute(value, names if len(names) > 1 else names[0], perm)  13 us
    pallas_call x1, Pallas kernels, on_device(): pl.pallas_call(functools.partial(remote_kernel, (C, S, L, slots, clusters...  10.9 us
    ppermute x10, waiting for transfers between devices, send(): return lax.ppermute(value, names if len(names) > 1 else names[0], perm)  9.49 us
    pallas_call x1, Pallas kernels, on_device(): pl.pallas_call(functools.partial(final_kernel, (S, R, L)), out_shape=shap...  3.1 us
    pallas_call x1, Pallas kernels, on_device(): pl.pallas_call(up_kernel, out_shape=shape((par_dev, rank), F32), in_specs...  3.07 us
    unnamed x23, local copies, waits for them, and re-layouts  2.54 us
    pallas_call x1, Pallas kernels, on_device(): pl.pallas_call(functools.partial(pack_kernel, (C, S, L, slots)), out_shap...  2.02 us
  transfers between devices with their start and end apart: 10, of which 5 were waited for; matrix products, arithmetic and copies ran while one was open for 2% of the time, Pallas kernels for 4%

profile of v6, /device:TPU:0, one launch (start us, length us, event | category | flops | bytes accessed | tf_op | source)
XLA Modules:
  0.0 74.4 jit_solution(1486302005125663519)
XLA Ops:
  0.0 0.0 copy-start.10
  0.0 2.0 %packs.1 = (f32[128,128]{1,0:T(8,128)}, f32[88,128]{1,0:T(8,128)}, f32[88,128]{1,0:T(8,128)}, f32[88,128]{1,0:T(8,128)}) custom-call(f32[128,128]{1,0:T(8,128)} %charges.1, s32[128,128]{1,0:T(8,128)} %mask.3, f32[128,4,256]{2,1,0:T(4,128)} %geo.5, s32[4,16]{1,0:T(4,128)} %bitcast.13, s32[4,16]{1,0:T(4,128)} %bitcast.15, s32[4,16]{1,0:T(4,128)} %bitcast.16), custom_call_target="tpu_custom_call" | custom-call | tf_op jit(solution)/shard_map/packs/pallas_call | solution.py:475
  2.0 3.0 %collective-permute-start = (f32[88,128]{1,0:T(8,128)}, f32[88,128]{1,0:T(8,128)S(1)}, u32[]{:S(2)}, u32[]{:S(2)}) collective-permute-start(f32[88,128]{1,0:T(8,128)} %get-tuple-element.16), channel_id=1, source_target_pairs={{0,4},{4,8},{8,12},{12,0},{1,5},{5,9},{9,13},{13,1},{2,6},{6,10},{... | collective-permute-start | bytes 135176 | tf_op jit(solution)/shard_map/ppermute | solution.py:446
  5.0 2.6 %collective-permute-start.1 = (f32[88,128]{1,0:T(8,128)}, f32[88,128]{1,0:T(8,128)S(1)}, u32[]{:S(2)}, u32[]{:S(2)}) collective-permute-start(f32[88,128]{1,0:T(8,128)} %get-tuple-element.17), channel_id=1, source_target_pairs={{0,8},{4,12},{8,0},{12,4},{1,9},{5,13},{9,1},{13,5},{2,10},{6,14},... | collective-permute-start | bytes 135176 | tf_op jit(solution)/shard_map/ppermute | solution.py:446
  7.6 1.3 %collective-permute-start.2 = (f32[88,128]{1,0:T(8,128)}, f32[88,128]{1,0:T(8,128)S(1)}, u32[]{:S(2)}, u32[]{:S(2)}) collective-permute-start(f32[88,128]{1,0:T(8,128)} %get-tuple-element.18), channel_id=1, source_target_pairs={{0,12},{4,0},{8,4},{12,8},{1,13},{5,1},{9,5},{13,9},{2,14},{6,2},{... | collective-permute-start | bytes 135176 | tf_op jit(solution)/shard_map/ppermute | solution.py:446
  9.0 1.5 %collective-permute-start.3 = (f32[128,128]{1,0:T(8,128)}, f32[128,128]{1,0:T(8,128)S(1)}, u32[]{:S(2)}, u32[]{:S(2)}) collective-permute-start(f32[128,128]{1,0:T(8,128)} %get-tuple-element.15.masked.rest_0_), channel_id=1, source_target_pairs={{0,2},{2,0},{1,3},{3,1},{4,6},{6,4},{5,7},{7,5},{8,10},{10,8},{9,1... | collective-permute-start | bytes 196616 | tf_op jit(solution)/shard_map/ppermute | solution.py:446
  10.5 3.1 %far_up.1.up = f32[16,32]{1,0:T(8,128)} custom-call(f32[128,32,128]{2,1,0:T(8,128)} %bitcast.9, f32[128,128]{1,0:T(8,128)} %get-tuple-element.15.masked.rest_0_, f32[32,32,128]{2,1,0:T(8,128)} %bitcast.11, s32[1,128]{1,0:T(1,128)} %bitcast.17), custom_call_target="tpu_custom_call" | custom-call | tf_op jit(solution)/shard_map/far_up/pallas_call | solution.py:488
  13.6 0.0 collective-permute-done.rest_2_
  13.6 0.0 copy-start.4
  13.6 0.0 collective-permute-done.1.rest_3_
  13.6 0.0 copy-start.5
  13.6 0.0 collective-permute-done.2.rest_4_
  13.6 0.0 copy-start.6
  13.6 0.6 maximum_convert_fusion.codes
  14.2 0.0 collective-permute-done.3.rest_1_
  14.2 0.0 copy-done.4
  14.2 0.0 copy-done.5
  14.2 0.0 copy-done.6
  14.3 0.0 copy-start
  14.3 0.6 copy-done
  14.9 10.9 %near_remote.1 = (f32[128,256]{1,0:T(8,128)}, f32[32,128]{1,0:T(8,128)}, f32[32,128]{1,0:T(8,128)}, f32[32,128]{1,0:T(8,128)}) custom-call(f32[128,4,256]{2,1,0:T(4,128)} %geo.5, s32[3,16]{1,0:T(4,128)} %maximum_convert_fusion.codes, f32[16,32]{1,0:T(8,128)} %far_up.1.up, f32[128,128]{1,0:T(8,128)} %get-tuple-element.15.masked.rest_0_, f32[128,128]{1,0:T(8,128)} %copy-done, ...), custom_call_target="tpu_custom_call" | custom-call | tf_op jit(solution)/shard_map/near_remote/pallas_call | solution.py:497
  25.8 1.4 %collective-permute-start.4 = (f32[32,128]{1,0:T(8,128)}, f32[32,128]{1,0:T(8,128)S(1)}, u32[]{:S(2)}, u32[]{:S(2)}) collective-permute-start(f32[32,128]{1,0:T(8,128)} %get-tuple-element.20), channel_id=1, source_target_pairs={{0,12},{4,0},{8,4},{12,8},{1,13},{5,1},{9,5},{13,9},{2,14},{6,2},{... | collective-permute-start | bytes 49160 | tf_op jit(solution)/shard_map/ppermute | solution.py:446
  27.2 0.7 collective-permute-start.5
  27.9 0.2 collective-permute-start.6
  28.2 0.0 copy-done.10
  28.2 0.7 copy.13.far_list
  28.8 0.9 %collective-permute-done.4.rest_2_ = f32[32,128]{1,0:T(8,128)S(1)} collective-permute-done((f32[32,128]{1,0:T(8,128)}, f32[32,128]{1,0:T(8,128)S(1)}, u32[]{:S(2)}, u32[]{:S(2)}) %collective-permute-start.4) | collective-permute-done | bytes 16416 | tf_op jit(solution)/shard_map/ppermute | solution.py:446
  29.8 0.0 copy-start.7
  29.8 2.5 %collective-permute-done.5.rest_3_ = f32[32,128]{1,0:T(8,128)S(1)} collective-permute-done((f32[32,128]{1,0:T(8,128)}, f32[32,128]{1,0:T(8,128)S(1)}, u32[]{:S(2)}, u32[]{:S(2)}) %collective-permute-start.5) | collective-permute-done | bytes 16416 | tf_op jit(solution)/shard_map/ppermute | solution.py:446
  32.3 0.0 copy-start.8
  32.3 1.4 %collective-permute-done.6.rest_4_ = f32[32,128]{1,0:T(8,128)S(1)} collective-permute-done((f32[32,128]{1,0:T(8,128)}, f32[32,128]{1,0:T(8,128)S(1)}, u32[]{:S(2)}, u32[]{:S(2)}) %collective-permute-start.6) | collective-permute-done | bytes 16416 | tf_op jit(solution)/shard_map/ppermute | solution.py:446
  33.7 0.0 copy-start.9
  33.7 0.0 copy-done.7
  33.7 0.0 copy-done.8
  33.7 0.6 copy-done.9
  34.3 29.6 %near_local.1 = (f32[160,128]{1,0:T(8,128)}, f32[160,128]{1,0:T(8,128)}) custom-call(f32[128,4,256]{2,1,0:T(4,128)} %geo.5, s32[2,128]{1,0:T(2,128)} %bitcast.19, s32[4,16]{1,0:T(4,128)} %bitcast.14, s32[16,8]{1,0:T(8,128)} %copy.13.far_list, f32[16,8,32,32]{3,2,1,0:T(8,128)} %coupling.1, f32[32,32,128]{2,1,0:T(8,128)} %bitcast.12, s32[1,128]{1,0:T(1,128)} %bitcast.18, ...), custom_call_target="tpu_custom_call" | custom-call | tf_op jit(solution)/shard_map/near_local/pallas_call | solution.py:522
  63.9 0.0 collective-permute-start.7
  63.9 0.9 %collective-permute-start.9 = (f32[160,128]{1,0:T(8,128)}, f32[160,128]{1,0:T(8,128)S(1)}, u32[]{:S(2)}, u32[]{:S(2)}) collective-permute-start(f32[160,128]{1,0:T(8,128)} %get-tuple-element.24), channel_id=1, source_target_pairs={{0,3},{1,2},{2,1},{3,0},{4,7},{5,6},{6,5},{7,4},{8,11},{9,10},{10,... | collective-permute-start | bytes 245768 | tf_op jit(solution)/shard_map/ppermute | solution.py:446
  64.8 1.3 %collective-permute-start.8 = (f32[160,128]{1,0:T(8,128)}, f32[160,128]{1,0:T(8,128)S(1)}, u32[]{:S(2)}, u32[]{:S(2)}) collective-permute-start(f32[160,128]{1,0:T(8,128)} %get-tuple-element.24), channel_id=1, source_target_pairs={{0,2},{1,3},{2,0},{3,1},{4,6},{5,7},{6,4},{7,5},{8,10},{9,11},{10,... | collective-permute-start | bytes 245768 | tf_op jit(solution)/shard_map/ppermute | solution.py:446
  66.1 0.0 collective-permute-done.7.rest_1_
  66.1 0.0 copy-start.1
  66.1 2.3 %collective-permute-done.9.rest_3_ = f32[160,128]{1,0:T(8,128)S(1)} collective-permute-done((f32[160,128]{1,0:T(8,128)}, f32[160,128]{1,0:T(8,128)S(1)}, u32[]{:S(2)}, u32[]{:S(2)}) %collective-permute-start.9) | collective-permute-done | bytes 81952 | tf_op jit(solution)/shard_map/ppermute | solution.py:446
  68.4 0.0 copy-start.2
  68.4 2.3 %collective-permute-done.8.rest_2_ = f32[160,128]{1,0:T(8,128)S(1)} collective-permute-done((f32[160,128]{1,0:T(8,128)}, f32[160,128]{1,0:T(8,128)S(1)}, u32[]{:S(2)}, u32[]{:S(2)}) %collective-permute-start.8) | collective-permute-done | bytes 81952 | tf_op jit(solution)/shard_map/ppermute | solution.py:446
  70.7 0.0 copy-done.1
  70.7 0.0 copy-done.2
  70.7 0.6 copy-done.3
  71.3 3.1 %combine.1 = f32[128,128]{1,0:T(8,128)} custom-call(s32[128,128]{1,0:T(8,128)} %mask.3, f32[128,32,128]{2,1,0:T(8,128)} %bitcast.10, f32[160,128]{1,0:T(8,128)} %get-tuple-element.23.rest_0_, f32[160,128]{1,0:T(8,128)} %copy-done.1, f32[160,128]{1,0:T(8,128)} %copy-done.3, f32[160,128]{1,0:T(8,128)} %copy-done.2), custom_call_target="tpu_custom_call" | custom-call | tf_op jit(solution)/shard_map/combine/pallas_call | solution.py:549
  (4 shorter events, 0.0 us)
Async XLA Ops:
  0.0 28.2 %copy-start.10 = (s32[16,8]{0,1:T(8,128)S(1)}, s32[16,8]{0,1:T(8,128)}, u32[]{:S(2)}) copy-start(s32[16,8]{0,1:T(8,128)} %param.22) | copy-start | bytes 1540
  2.0 11.5 %collective-permute-start = (f32[88,128]{1,0:T(8,128)}, f32[88,128]{1,0:T(8,128)S(1)}, u32[]{:S(2)}, u32[]{:S(2)}) collective-permute-start(f32[88,128]{1,0:T(8,128)} %get-tuple-element.16), channel_id=1, source_target_pairs={{0,4},{4,8},{8,12},{12,0},{1,5},{5,9},{9,13},{13,1},{2,6},{6,10},{... | collective-permute-start | bytes 135176 | tf_op jit(solution)/shard_map/ppermute | solution.py:446
  5.0 8.5 %collective-permute-start.1 = (f32[88,128]{1,0:T(8,128)}, f32[88,128]{1,0:T(8,128)S(1)}, u32[]{:S(2)}, u32[]{:S(2)}) collective-permute-start(f32[88,128]{1,0:T(8,128)} %get-tuple-element.17), channel_id=1, source_target_pairs={{0,8},{4,12},{8,0},{12,4},{1,9},{5,13},{9,1},{13,5},{2,10},{6,14},... | collective-permute-start | bytes 135176 | tf_op jit(solution)/shard_map/ppermute | solution.py:446
  7.6 6.0 %collective-permute-start.2 = (f32[88,128]{1,0:T(8,128)}, f32[88,128]{1,0:T(8,128)S(1)}, u32[]{:S(2)}, u32[]{:S(2)}) collective-permute-start(f32[88,128]{1,0:T(8,128)} %get-tuple-element.18), channel_id=1, source_target_pairs={{0,12},{4,0},{8,4},{12,8},{1,13},{5,1},{9,5},{13,9},{2,14},{6,2},{... | collective-permute-start | bytes 135176 | tf_op jit(solution)/shard_map/ppermute | solution.py:446
  9.0 5.3 %collective-permute-start.3 = (f32[128,128]{1,0:T(8,128)}, f32[128,128]{1,0:T(8,128)S(1)}, u32[]{:S(2)}, u32[]{:S(2)}) collective-permute-start(f32[128,128]{1,0:T(8,128)} %get-tuple-element.15.masked.rest_0_), channel_id=1, source_target_pairs={{0,2},{2,0},{1,3},{3,1},{4,6},{6,4},{5,7},{7,5},{8,10},{10,8},{9,1... | collective-permute-start | bytes 196616 | tf_op jit(solution)/shard_map/ppermute | solution.py:446
  13.6 0.7 copy-start.4
  13.6 0.7 copy-start.5
  13.6 0.6 copy-start.6
  14.3 0.6 copy-start
  25.8 3.9 %collective-permute-start.4 = (f32[32,128]{1,0:T(8,128)}, f32[32,128]{1,0:T(8,128)S(1)}, u32[]{:S(2)}, u32[]{:S(2)}) collective-permute-start(f32[32,128]{1,0:T(8,128)} %get-tuple-element.20), channel_id=1, source_target_pairs={{0,12},{4,0},{8,4},{12,8},{1,13},{5,1},{9,5},{13,9},{2,14},{6,2},{... | collective-permute-start | bytes 49160 | tf_op jit(solution)/shard_map/ppermute | solution.py:446
  27.2 5.0 %collective-permute-start.5 = (f32[32,128]{1,0:T(8,128)}, f32[32,128]{1,0:T(8,128)S(1)}, u32[]{:S(2)}, u32[]{:S(2)}) collective-permute-start(f32[32,128]{1,0:T(8,128)} %get-tuple-element.21), channel_id=1, source_target_pairs={{0,8},{4,12},{8,0},{12,4},{1,9},{5,13},{9,1},{13,5},{2,10},{6,14},... | collective-permute-start | bytes 49160 | tf_op jit(solution)/shard_map/ppermute | solution.py:446
  27.9 5.7 %collective-permute-start.6 = (f32[32,128]{1,0:T(8,128)}, f32[32,128]{1,0:T(8,128)S(1)}, u32[]{:S(2)}, u32[]{:S(2)}) collective-permute-start(f32[32,128]{1,0:T(8,128)} %get-tuple-element.22), channel_id=1, source_target_pairs={{0,4},{4,8},{8,12},{12,0},{1,5},{5,9},{9,13},{13,1},{2,6},{6,10},{... | collective-permute-start | bytes 49160 | tf_op jit(solution)/shard_map/ppermute | solution.py:446
  29.8 3.9 %copy-start.7 = (f32[32,128]{1,0:T(8,128)}, f32[32,128]{1,0:T(8,128)S(1)}, u32[]{:S(2)}) copy-start(f32[32,128]{1,0:T(8,128)S(1)} %collective-permute-done.4.rest_2_) | copy-start | bytes 49156
  32.3 1.4 %copy-start.8 = (f32[32,128]{1,0:T(8,128)}, f32[32,128]{1,0:T(8,128)S(1)}, u32[]{:S(2)}) copy-start(f32[32,128]{1,0:T(8,128)S(1)} %collective-permute-done.5.rest_3_) | copy-start | bytes 49156
  33.7 0.6 copy-start.9
  63.9 2.1 %collective-permute-start.7 = (f32[160,128]{1,0:T(8,128)}, f32[160,128]{1,0:T(8,128)S(1)}, u32[]{:S(2)}, u32[]{:S(2)}) collective-permute-start(f32[160,128]{1,0:T(8,128)} %get-tuple-element.23.rest_0_), channel_id=1, source_target_pairs={{0,1},{1,0},{2,3},{3,2},{4,5},{5,4},{6,7},{7,6},{8,9},{9,8},{10,11... | collective-permute-start | bytes 245768 | tf_op jit(solution)/shard_map/ppermute | solution.py:446
  63.9 4.4 %collective-permute-start.9 = (f32[160,128]{1,0:T(8,128)}, f32[160,128]{1,0:T(8,128)S(1)}, u32[]{:S(2)}, u32[]{:S(2)}) collective-permute-start(f32[160,128]{1,0:T(8,128)} %get-tuple-element.24), channel_id=1, source_target_pairs={{0,3},{1,2},{2,1},{3,0},{4,7},{5,6},{6,5},{7,4},{8,11},{9,10},{10,... | collective-permute-start | bytes 245768 | tf_op jit(solution)/shard_map/ppermute | solution.py:446
  64.8 5.9 %collective-permute-start.8 = (f32[160,128]{1,0:T(8,128)}, f32[160,128]{1,0:T(8,128)S(1)}, u32[]{:S(2)}, u32[]{:S(2)}) collective-permute-start(f32[160,128]{1,0:T(8,128)} %get-tuple-element.24), channel_id=1, source_target_pairs={{0,2},{1,3},{2,0},{3,1},{4,6},{5,7},{6,4},{7,5},{8,10},{9,11},{10,... | collective-permute-start | bytes 245768 | tf_op jit(solution)/shard_map/ppermute | solution.py:446
  66.1 4.6 %copy-start.1 = (f32[160,128]{1,0:T(8,128)}, f32[160,128]{1,0:T(8,128)S(1)}, u32[]{:S(2)}) copy-start(f32[160,128]{1,0:T(8,128)S(1)} %collective-permute-done.7.rest_1_) | copy-start | bytes 245764
  68.4 2.3 %copy-start.2 = (f32[160,128]{1,0:T(8,128)}, f32[160,128]{1,0:T(8,128)S(1)}, u32[]{:S(2)}) copy-start(f32[160,128]{1,0:T(8,128)S(1)} %collective-permute-done.9.rest_3_) | copy-start | bytes 245764
  70.7 0.6 copy-start.3

commit v7 on v6

--- a/solution.py
+++ b/solution.py
@@ -147,6 +147,25 @@
     )
 
 
+def pipeline(total, begin, finish, ring):
+    size = len(ring)
+    ahead = min(2, size - 1)
+
+    def body(i, carry):
+        for k in range(size):
+            begin(i * size + k + ahead, ring[(k + ahead) % size])
+            finish(i * size + k, ring[k])
+        return carry
+
+    for k in range(ahead):
+        begin(k, ring[k])
+    lax.fori_loop(0, (total + size - 1) // size, body, 0)
+
+
+def ring_size(total):
+    return next(size for size in (8, 4, 2, 1) if total % size == 0)
+
+
 def assemble(sub, S, L, q, pieces):
     def place(s):
         for shift in range(S):
@@ -191,7 +210,7 @@
     packs = rest[S : S + C - 1]
     acc_out = rest[S + C - 1]
     sends = rest[S + C : S + C + C - 1]
-    q, tqt, acc, fwdt, sgeo, fa0, fb0, fb1, dist0, dist1, order = rest[S + C + C - 1 :]
+    q, tqt, acc, fwdt, sgeo, fa0, fb0, fb1, order, *ring = rest[S + C + C - 1 :]
     fa, fb = (fa0,), (fb0, fb1)
     n = (C - 1) * slots
     assemble(lax.axis_index("sub"), S, L, q, pieces)
@@ -235,15 +254,7 @@
         )
         acc[pl.ds(source, 1), :] += jnp.where(ok, back, 0.0)
 
-    def step(i, carry):
-        begin(2 * i + 1, dist1)
-        finish(2 * i, dist0)
-        begin(2 * i + 2, dist0)
-        finish(2 * i + 1, dist1)
-        return carry
-
-    begin(0, dist0)
-    lax.fori_loop(0, (found + 1) // 2, step, 0)
+    pipeline(found, begin, finish, ring)
     acc_out[...] = acc[...] * inv
     fwd = (fwdt[...] * inv).T
     rank = up.shape[1]
@@ -260,7 +271,7 @@
     pieces = rest[:S]
     sums = rest[S : S + C - 1]
     parts = rest[S + C - 1 : 2 * S + C - 1]
-    q, qt, acc, acct, fa0, fa1, fb0, fb1, rads, dist0, dist1, got, parents, rows = rest[2 * S + C - 1 :]
+    q, qt, acc, acct, fa0, fa1, fb0, fb1, rads, got, parents, rows, *ring = rest[2 * S + C - 1 :]
     fa, fb = (fa0, fa1), (fb0, fb1)
     me, sub, rep = lax.axis_index("clu"), lax.axis_index("sub"), lax.axis_index("rep")
     assemble(sub, S, L, q, pieces)
@@ -311,15 +322,7 @@
         back = jnp.sum(back, axis=0, keepdims=True)
         acc[pl.ds(c, 1), :] += jnp.concatenate([jnp.zeros_like(back), back], axis=1)
 
-    def self_step(i, carry):
-        begin_self(2 * i + 1, dist1)
-        finish_self(2 * i, dist0)
-        begin_self(2 * i + 2, dist0)
-        finish_self(2 * i + 1, dist1)
-        return carry
-
-    begin_self(0, dist0)
-    lax.fori_loop(0, share // 2, self_step, 0)
+    pipeline(share, begin_self, finish_self, ring[: ring_size(share)])
 
     count = pairs.shape[1] // S
     start = sub * count
@@ -332,15 +335,7 @@
         ia, ib = pairs[0, start + i], pairs[1, start + i]
         acc[pl.ds(ib, 1), :] += tile_sums(dist, q[pl.ds(ib, 1), :], qt, ia, acct, share + i)
 
-    def pair_step(i, carry):
-        begin(2 * i + 1, dist1)
-        finish(2 * i, dist0)
-        begin(2 * i + 2, dist0)
-        finish(2 * i + 1, dist1)
-        return carry
-
-    begin(0, dist0)
-    lax.fori_loop(0, count // 2, pair_step, 0)
+    pipeline(count, begin, finish, ring[: ring_size(count)])
     rows[...] = acct[...].T
     for i in range(share):
         acc[pl.ds(first + i, 1), :] += rows[i : i + 1, :]
@@ -508,10 +503,9 @@
             pltpu.VMEM((n * ROWS, L), F32),
             pltpu.VMEM((n * ROWS, LANES), F32),
             pltpu.VMEM((n * ROWS, LANES), F32),
-            pltpu.VMEM((L, panels), F32),
-            pltpu.VMEM((L, panels), F32),
             pltpu.SMEM((n + 1,), jnp.int32),
-        ],
+        ]
+        + [pltpu.VMEM((L, panels), F32)] * 4,
         compiler_params=PARAMS,
         name="near_remote",
     )(geometry, codes, up, *pieces, *packs)
@@ -532,12 +526,11 @@
             *half,
             *half,
             pltpu.VMEM((clusters, panels), F32),
-            pltpu.VMEM((panels, panels), F32),
-            pltpu.VMEM((panels, panels), F32),
             pltpu.VMEM((clusters, L), F32),
             pltpu.VMEM((C * par_dev, rank), F32),
             pltpu.VMEM((columns, panels), F32),
-        ],
+        ]
+        + [pltpu.VMEM((panels, panels), F32)] * 8,
         compiler_params=PARAMS,
         name="near_local",
     )(geometry, local_pairs[0].T, targets, far_list, coupling, transfer_t, parent, up, acc, *pieces, *sums)

time: 74.6 us -> 70.5 us (0.945)
  Pallas kernels: 48.7 us -> 45.1 us
    pallas_call x1, Pallas kernels: 29.6 us -> 27.7 us  [on_device(): pl.pallas_call(functools.partial(local_kernel, (C, S, L, R, slots, cluste...]
    pallas_call x1, Pallas kernels: 10.9 us -> 9.15 us  [on_device(): pl.pallas_call(functools.partial(remote_kernel, (C, S, L, slots, clusters...]
where the time goes in v7:
time: 70.5 us; the launch traced here: 70.2 us
  Pallas kernels  45.1 us (64%)
  starting transfers between devices  13 us (18%)
  waiting for transfers between devices  8.97 us (13%)
  local copies, waits for them, and re-layouts  2.55 us (4%)
    pallas_call x1, Pallas kernels, on_device(): pl.pallas_call(functools.partial(local_kernel, (C, S, L, R, slots, cluste...  27.7 us
    ppermute x10, starting transfers between devices, send(): return lax.ppermute(value, names if len(names) > 1 else names[0], perm)  13 us
    pallas_call x1, Pallas kernels, on_device(): pl.pallas_call(functools.partial(remote_kernel, (C, S, L, slots, clusters...  9.15 us
    ppermute x10, waiting for transfers between devices, send(): return lax.ppermute(value, names if len(names) > 1 else names[0], perm)  8.97 us
    pallas_call x1, Pallas kernels, on_device(): pl.pallas_call(functools.partial(final_kernel, (S, R, L)), out_shape=shap...  3.1 us
    pallas_call x1, Pallas kernels, on_device(): pl.pallas_call(up_kernel, out_shape=shape((par_dev, rank), F32), in_specs...  3.07 us
    unnamed x23, local copies, waits for them, and re-layouts  2.54 us
    pallas_call x1, Pallas kernels, on_device(): pl.pallas_call(functools.partial(pack_kernel, (C, S, L, slots)), out_shap...  2.02 us
  transfers between devices with their start and end apart: 10, of which 5 were waited for; matrix products, arithmetic and copies ran while one was open for 2% of the time, Pallas kernels for 4%

profile of v7, /device:TPU:0, one launch (start us, length us, event | category | flops | bytes accessed | tf_op | source)
XLA Modules:
  0.0 70.2 jit_solution(16418472004711075917)
XLA Ops:
  0.0 0.0 copy-start.10
  0.0 2.0 %packs.1 = (f32[128,128]{1,0:T(8,128)}, f32[88,128]{1,0:T(8,128)}, f32[88,128]{1,0:T(8,128)}, f32[88,128]{1,0:T(8,128)}) custom-call(f32[128,128]{1,0:T(8,128)} %charges.1, s32[128,128]{1,0:T(8,128)} %mask.3, f32[128,4,256]{2,1,0:T(4,128)} %geo.5, s32[4,16]{1,0:T(4,128)} %bitcast.13, s32[4,16]{1,0:T(4,128)} %bitcast.15, s32[4,16]{1,0:T(4,128)} %bitcast.16), custom_call_target="tpu_custom_call" | custom-call | tf_op jit(solution)/shard_map/packs/pallas_call | solution.py:470
  2.0 3.0 %collective-permute-start = (f32[88,128]{1,0:T(8,128)}, f32[88,128]{1,0:T(8,128)S(1)}, u32[]{:S(2)}, u32[]{:S(2)}) collective-permute-start(f32[88,128]{1,0:T(8,128)} %get-tuple-element.16), channel_id=1, source_target_pairs={{0,4},{4,8},{8,12},{12,0},{1,5},{5,9},{9,13},{13,1},{2,6},{6,10},{... | collective-permute-start | bytes 135176 | tf_op jit(solution)/shard_map/ppermute | solution.py:441
  5.0 2.6 %collective-permute-start.1 = (f32[88,128]{1,0:T(8,128)}, f32[88,128]{1,0:T(8,128)S(1)}, u32[]{:S(2)}, u32[]{:S(2)}) collective-permute-start(f32[88,128]{1,0:T(8,128)} %get-tuple-element.17), channel_id=1, source_target_pairs={{0,8},{4,12},{8,0},{12,4},{1,9},{5,13},{9,1},{13,5},{2,10},{6,14},... | collective-permute-start | bytes 135176 | tf_op jit(solution)/shard_map/ppermute | solution.py:441
  7.6 1.3 %collective-permute-start.2 = (f32[88,128]{1,0:T(8,128)}, f32[88,128]{1,0:T(8,128)S(1)}, u32[]{:S(2)}, u32[]{:S(2)}) collective-permute-start(f32[88,128]{1,0:T(8,128)} %get-tuple-element.18), channel_id=1, source_target_pairs={{0,12},{4,0},{8,4},{12,8},{1,13},{5,1},{9,5},{13,9},{2,14},{6,2},{... | collective-permute-start | bytes 135176 | tf_op jit(solution)/shard_map/ppermute | solution.py:441
  9.0 1.5 %collective-permute-start.3 = (f32[128,128]{1,0:T(8,128)}, f32[128,128]{1,0:T(8,128)S(1)}, u32[]{:S(2)}, u32[]{:S(2)}) collective-permute-start(f32[128,128]{1,0:T(8,128)} %get-tuple-element.15.masked.rest_0_), channel_id=1, source_target_pairs={{0,2},{2,0},{1,3},{3,1},{4,6},{6,4},{5,7},{7,5},{8,10},{10,8},{9,1... | collective-permute-start | bytes 196616 | tf_op jit(solution)/shard_map/ppermute | solution.py:441
  10.5 3.1 %far_up.1.up = f32[16,32]{1,0:T(8,128)} custom-call(f32[128,32,128]{2,1,0:T(8,128)} %bitcast.9, f32[128,128]{1,0:T(8,128)} %get-tuple-element.15.masked.rest_0_, f32[32,32,128]{2,1,0:T(8,128)} %bitcast.11, s32[1,128]{1,0:T(1,128)} %bitcast.17), custom_call_target="tpu_custom_call" | custom-call | tf_op jit(solution)/shard_map/far_up/pallas_call | solution.py:483
  13.6 0.0 collective-permute-done.rest_2_
  13.6 0.0 copy-start.4
  13.6 0.0 collective-permute-done.1.rest_3_
  13.6 0.0 copy-start.5
  13.6 0.0 collective-permute-done.2.rest_4_
  13.6 0.0 copy-start.6
  13.6 0.6 maximum_convert_fusion.codes
  14.2 0.0 collective-permute-done.3.rest_1_
  14.2 0.0 copy-done.4
  14.2 0.0 copy-done.5
  14.2 0.0 copy-done.6
  14.3 0.0 copy-start
  14.3 0.6 copy-done
  14.9 9.1 %near_remote.1 = (f32[128,256]{1,0:T(8,128)}, f32[32,128]{1,0:T(8,128)}, f32[32,128]{1,0:T(8,128)}, f32[32,128]{1,0:T(8,128)}) custom-call(f32[128,4,256]{2,1,0:T(4,128)} %geo.5, s32[3,16]{1,0:T(4,128)} %maximum_convert_fusion.codes, f32[16,32]{1,0:T(8,128)} %far_up.1.up, f32[128,128]{1,0:T(8,128)} %get-tuple-element.15.masked.rest_0_, f32[128,128]{1,0:T(8,128)} %copy-done, ...), custom_call_target="tpu_custom_call" | custom-call | tf_op jit(solution)/shard_map/near_remote/pallas_call | solution.py:492
  24.0 1.4 %collective-permute-start.4 = (f32[32,128]{1,0:T(8,128)}, f32[32,128]{1,0:T(8,128)S(1)}, u32[]{:S(2)}, u32[]{:S(2)}) collective-permute-start(f32[32,128]{1,0:T(8,128)} %get-tuple-element.20), channel_id=1, source_target_pairs={{0,12},{4,0},{8,4},{12,8},{1,13},{5,1},{9,5},{13,9},{2,14},{6,2},{... | collective-permute-start | bytes 49160 | tf_op jit(solution)/shard_map/ppermute | solution.py:441
  25.5 0.2 collective-permute-start.5
  25.6 0.7 %collective-permute-start.6 = (f32[32,128]{1,0:T(8,128)}, f32[32,128]{1,0:T(8,128)S(1)}, u32[]{:S(2)}, u32[]{:S(2)}) collective-permute-start(f32[32,128]{1,0:T(8,128)} %get-tuple-element.22), channel_id=1, source_target_pairs={{0,4},{4,8},{8,12},{12,0},{1,5},{5,9},{9,13},{13,1},{2,6},{6,10},{... | collective-permute-start | bytes 49160 | tf_op jit(solution)/shard_map/ppermute | solution.py:441
  26.4 0.0 copy-done.10
  26.4 0.7 copy.13.far_list
  27.1 1.0 %collective-permute-done.4.rest_2_ = f32[32,128]{1,0:T(8,128)S(1)} collective-permute-done((f32[32,128]{1,0:T(8,128)}, f32[32,128]{1,0:T(8,128)S(1)}, u32[]{:S(2)}, u32[]{:S(2)}) %collective-permute-start.4) | collective-permute-done | bytes 16416 | tf_op jit(solution)/shard_map/ppermute | solution.py:441
  28.0 0.0 copy-start.7
  28.0 2.4 %collective-permute-done.5.rest_3_ = f32[32,128]{1,0:T(8,128)S(1)} collective-permute-done((f32[32,128]{1,0:T(8,128)}, f32[32,128]{1,0:T(8,128)S(1)}, u32[]{:S(2)}, u32[]{:S(2)}) %collective-permute-start.5) | collective-permute-done | bytes 16416 | tf_op jit(solution)/shard_map/ppermute | solution.py:441
  30.5 0.0 copy-start.8
  30.5 0.9 %collective-permute-done.6.rest_4_ = f32[32,128]{1,0:T(8,128)S(1)} collective-permute-done((f32[32,128]{1,0:T(8,128)}, f32[32,128]{1,0:T(8,128)S(1)}, u32[]{:S(2)}, u32[]{:S(2)}) %collective-permute-start.6) | collective-permute-done | bytes 16416 | tf_op jit(solution)/shard_map/ppermute | solution.py:441
  31.4 0.0 copy-start.9
  31.4 0.0 copy-done.7
  31.4 0.0 copy-done.8
  31.4 0.6 copy-done.9
  32.0 27.7 %near_local.1 = (f32[160,128]{1,0:T(8,128)}, f32[160,128]{1,0:T(8,128)}) custom-call(f32[128,4,256]{2,1,0:T(4,128)} %geo.5, s32[2,128]{1,0:T(2,128)} %bitcast.19, s32[4,16]{1,0:T(4,128)} %bitcast.14, s32[16,8]{1,0:T(8,128)} %copy.13.far_list, f32[16,8,32,32]{3,2,1,0:T(8,128)} %coupling.1, f32[32,32,128]{2,1,0:T(8,128)} %bitcast.12, s32[1,128]{1,0:T(1,128)} %bitcast.18, ...), custom_call_target="tpu_custom_call" | custom-call | tf_op jit(solution)/shard_map/near_local/pallas_call | solution.py:516
  59.7 0.0 collective-permute-start.7
  59.7 1.4 %collective-permute-start.9 = (f32[160,128]{1,0:T(8,128)}, f32[160,128]{1,0:T(8,128)S(1)}, u32[]{:S(2)}, u32[]{:S(2)}) collective-permute-start(f32[160,128]{1,0:T(8,128)} %get-tuple-element.24), channel_id=1, source_target_pairs={{0,3},{1,2},{2,1},{3,0},{4,7},{5,6},{6,5},{7,4},{8,11},{9,10},{10,... | collective-permute-start | bytes 245768 | tf_op jit(solution)/shard_map/ppermute | solution.py:441
  61.2 0.7 collective-permute-start.8
  61.9 0.0 collective-permute-done.7.rest_1_
  61.9 0.0 copy-start.1
  61.9 2.4 %collective-permute-done.9.rest_3_ = f32[160,128]{1,0:T(8,128)S(1)} collective-permute-done((f32[160,128]{1,0:T(8,128)}, f32[160,128]{1,0:T(8,128)S(1)}, u32[]{:S(2)}, u32[]{:S(2)}) %collective-permute-start.9) | collective-permute-done | bytes 81952 | tf_op jit(solution)/shard_map/ppermute | solution.py:441
  64.3 0.0 copy-start.2
  64.3 2.2 %collective-permute-done.8.rest_2_ = f32[160,128]{1,0:T(8,128)S(1)} collective-permute-done((f32[160,128]{1,0:T(8,128)}, f32[160,128]{1,0:T(8,128)S(1)}, u32[]{:S(2)}, u32[]{:S(2)}) %collective-permute-start.8) | collective-permute-done | bytes 81952 | tf_op jit(solution)/shard_map/ppermute | solution.py:441
  66.5 0.0 copy-done.1
  66.5 0.0 copy-done.2
  66.5 0.6 copy-done.3
  67.1 3.1 %combine.1 = f32[128,128]{1,0:T(8,128)} custom-call(s32[128,128]{1,0:T(8,128)} %mask.3, f32[128,32,128]{2,1,0:T(8,128)} %bitcast.10, f32[160,128]{1,0:T(8,128)} %get-tuple-element.23.rest_0_, f32[160,128]{1,0:T(8,128)} %copy-done.1, f32[160,128]{1,0:T(8,128)} %copy-done.3, f32[160,128]{1,0:T(8,128)} %copy-done.2), custom_call_target="tpu_custom_call" | custom-call | tf_op jit(solution)/shard_map/combine/pallas_call | solution.py:542
  (4 shorter events, 0.0 us)
Async XLA Ops:
  0.0 26.4 %copy-start.10 = (s32[16,8]{0,1:T(8,128)S(1)}, s32[16,8]{0,1:T(8,128)}, u32[]{:S(2)}) copy-start(s32[16,8]{0,1:T(8,128)} %param.22) | copy-start | bytes 1540
  2.0 11.5 %collective-permute-start = (f32[88,128]{1,0:T(8,128)}, f32[88,128]{1,0:T(8,128)S(1)}, u32[]{:S(2)}, u32[]{:S(2)}) collective-permute-start(f32[88,128]{1,0:T(8,128)} %get-tuple-element.16), channel_id=1, source_target_pairs={{0,4},{4,8},{8,12},{12,0},{1,5},{5,9},{9,13},{13,1},{2,6},{6,10},{... | collective-permute-start | bytes 135176 | tf_op jit(solution)/shard_map/ppermute | solution.py:441
  5.0 8.5 %collective-permute-start.1 = (f32[88,128]{1,0:T(8,128)}, f32[88,128]{1,0:T(8,128)S(1)}, u32[]{:S(2)}, u32[]{:S(2)}) collective-permute-start(f32[88,128]{1,0:T(8,128)} %get-tuple-element.17), channel_id=1, source_target_pairs={{0,8},{4,12},{8,0},{12,4},{1,9},{5,13},{9,1},{13,5},{2,10},{6,14},... | collective-permute-start | bytes 135176 | tf_op jit(solution)/shard_map/ppermute | solution.py:441
  7.6 6.0 %collective-permute-start.2 = (f32[88,128]{1,0:T(8,128)}, f32[88,128]{1,0:T(8,128)S(1)}, u32[]{:S(2)}, u32[]{:S(2)}) collective-permute-start(f32[88,128]{1,0:T(8,128)} %get-tuple-element.18), channel_id=1, source_target_pairs={{0,12},{4,0},{8,4},{12,8},{1,13},{5,1},{9,5},{13,9},{2,14},{6,2},{... | collective-permute-start | bytes 135176 | tf_op jit(solution)/shard_map/ppermute | solution.py:441
  9.0 5.3 %collective-permute-start.3 = (f32[128,128]{1,0:T(8,128)}, f32[128,128]{1,0:T(8,128)S(1)}, u32[]{:S(2)}, u32[]{:S(2)}) collective-permute-start(f32[128,128]{1,0:T(8,128)} %get-tuple-element.15.masked.rest_0_), channel_id=1, source_target_pairs={{0,2},{2,0},{1,3},{3,1},{4,6},{6,4},{5,7},{7,5},{8,10},{10,8},{9,1... | collective-permute-start | bytes 196616 | tf_op jit(solution)/shard_map/ppermute | solution.py:441
  13.6 0.7 copy-start.4
  13.6 0.7 copy-start.5
  13.6 0.6 copy-start.6
  14.3 0.6 copy-start
  24.0 4.0 %collective-permute-start.4 = (f32[32,128]{1,0:T(8,128)}, f32[32,128]{1,0:T(8,128)S(1)}, u32[]{:S(2)}, u32[]{:S(2)}) collective-permute-start(f32[32,128]{1,0:T(8,128)} %get-tuple-element.20), channel_id=1, source_target_pairs={{0,12},{4,0},{8,4},{12,8},{1,13},{5,1},{9,5},{13,9},{2,14},{6,2},{... | collective-permute-start | bytes 49160 | tf_op jit(solution)/shard_map/ppermute | solution.py:441
  25.5 5.0 %collective-permute-start.5 = (f32[32,128]{1,0:T(8,128)}, f32[32,128]{1,0:T(8,128)S(1)}, u32[]{:S(2)}, u32[]{:S(2)}) collective-permute-start(f32[32,128]{1,0:T(8,128)} %get-tuple-element.21), channel_id=1, source_target_pairs={{0,8},{4,12},{8,0},{12,4},{1,9},{5,13},{9,1},{13,5},{2,10},{6,14},... | collective-permute-start | bytes 49160 | tf_op jit(solution)/shard_map/ppermute | solution.py:441
  25.6 5.7 %collective-permute-start.6 = (f32[32,128]{1,0:T(8,128)}, f32[32,128]{1,0:T(8,128)S(1)}, u32[]{:S(2)}, u32[]{:S(2)}) collective-permute-start(f32[32,128]{1,0:T(8,128)} %get-tuple-element.22), channel_id=1, source_target_pairs={{0,4},{4,8},{8,12},{12,0},{1,5},{5,9},{9,13},{13,1},{2,6},{6,10},{... | collective-permute-start | bytes 49160 | tf_op jit(solution)/shard_map/ppermute | solution.py:441
  28.0 3.4 %copy-start.7 = (f32[32,128]{1,0:T(8,128)}, f32[32,128]{1,0:T(8,128)S(1)}, u32[]{:S(2)}) copy-start(f32[32,128]{1,0:T(8,128)S(1)} %collective-permute-done.4.rest_2_) | copy-start | bytes 49156
  30.5 0.9 %copy-start.8 = (f32[32,128]{1,0:T(8,128)}, f32[32,128]{1,0:T(8,128)S(1)}, u32[]{:S(2)}) copy-start(f32[32,128]{1,0:T(8,128)S(1)} %collective-permute-done.5.rest_3_) | copy-start | bytes 49156
  31.4 0.6 copy-start.9
  59.7 2.1 %collective-permute-start.7 = (f32[160,128]{1,0:T(8,128)}, f32[160,128]{1,0:T(8,128)S(1)}, u32[]{:S(2)}, u32[]{:S(2)}) collective-permute-start(f32[160,128]{1,0:T(8,128)} %get-tuple-element.23.rest_0_), channel_id=1, source_target_pairs={{0,1},{1,0},{2,3},{3,2},{4,5},{5,4},{6,7},{7,6},{8,9},{9,8},{10,11... | collective-permute-start | bytes 245768 | tf_op jit(solution)/shard_map/ppermute | solution.py:441
  59.7 4.5 %collective-permute-start.9 = (f32[160,128]{1,0:T(8,128)}, f32[160,128]{1,0:T(8,128)S(1)}, u32[]{:S(2)}, u32[]{:S(2)}) collective-permute-start(f32[160,128]{1,0:T(8,128)} %get-tuple-element.24), channel_id=1, source_target_pairs={{0,3},{1,2},{2,1},{3,0},{4,7},{5,6},{6,5},{7,4},{8,11},{9,10},{10,... | collective-permute-start | bytes 245768 | tf_op jit(solution)/shard_map/ppermute | solution.py:441
  61.2 5.3 %collective-permute-start.8 = (f32[160,128]{1,0:T(8,128)}, f32[160,128]{1,0:T(8,128)S(1)}, u32[]{:S(2)}, u32[]{:S(2)}) collective-permute-start(f32[160,128]{1,0:T(8,128)} %get-tuple-element.24), channel_id=1, source_target_pairs={{0,2},{1,3},{2,0},{3,1},{4,6},{5,7},{6,4},{7,5},{8,10},{9,11},{10,... | collective-permute-start | bytes 245768 | tf_op jit(solution)/shard_map/ppermute | solution.py:441
  61.9 4.6 %copy-start.1 = (f32[160,128]{1,0:T(8,128)}, f32[160,128]{1,0:T(8,128)S(1)}, u32[]{:S(2)}) copy-start(f32[160,128]{1,0:T(8,128)S(1)} %collective-permute-done.7.rest_1_) | copy-start | bytes 245764
  64.3 2.2 %copy-start.2 = (f32[160,128]{1,0:T(8,128)}, f32[160,128]{1,0:T(8,128)S(1)}, u32[]{:S(2)}) copy-start(f32[160,128]{1,0:T(8,128)S(1)} %collective-permute-done.9.rest_3_) | copy-start | bytes 245764
  66.5 0.6 copy-start.3

commit v8 on v7

--- a/solution.py
+++ b/solution.py
@@ -116,7 +116,7 @@
 
 
 def inverse_root(d):
-    return lax.exp2(-0.5 * lax.log2(d))
+    return lax.rsqrt(d)
 
 
 def fold(v):
@@ -129,22 +129,44 @@
         out[:, t * LANES : (t + 1) * LANES] = contract(whole_left, r)
 
 
-def tile_sums(dist, qrow, qtable, slot, table_ref, index, step=64):
-    height = dist.shape[0]
+def staged(spans, *stages):
+    held = {}
+    for t in range(len(spans) + len(stages) - 1):
+        for depth in reversed(range(len(stages))):
+            k = t - depth
+            if 0 <= k < len(spans):
+                held[k] = stages[depth](spans[k], held.get(k))
+                if depth == len(stages) - 1:
+                    del held[k]
+
+
+def spans_of(height, step=16):
     step = min(step, height)
+    return [slice(r, r + step) for r in range(0, height, step)]
+
+
+def tile_sums(dist, qrow, qtable, slot, table, index):
     q0, q1 = qrow[:, :LANES], qrow[:, LANES:]
-    back0 = back1 = jnp.zeros((8, LANES), F32)
-    for r in range(0, height, step):
-        rows = slice(r, r + step)
-        g0 = inverse_root(dist[rows, :LANES])
-        g1 = inverse_root(dist[rows, LANES:])
-        qcol = column(qtable[rows, :], slot)
-        put_column(table_ref, rows, index, jnp.sum(g0 * q0 + g1 * q1, axis=1, keepdims=True))
-        back0 = back0 + fold(g0 * qcol)
-        back1 = back1 + fold(g1 * qcol)
-    return jnp.concatenate(
-        [jnp.sum(back0, axis=0, keepdims=True), jnp.sum(back1, axis=0, keepdims=True)], axis=1
-    )
+    back = [jnp.zeros((8, LANES), F32), jnp.zeros((8, LANES), F32)]
+
+    def root(rows, _):
+        return (
+            inverse_root(dist[rows, :LANES]),
+            inverse_root(dist[rows, LANES:]),
+            column(qtable[rows, :], slot),
+        )
+
+    def sums(rows, held):
+        g0, g1, qcol = held
+        back[0] = back[0] + fold(g0 * qcol)
+        back[1] = back[1] + fold(g1 * qcol)
+        return jnp.sum(g0 * q0 + g1 * q1, axis=1, keepdims=True)
+
+    def store(rows, held):
+        put_column(table, rows, index, held)
+
+    staged(spans_of(dist.shape[0]), root, sums, store)
+    return jnp.concatenate([jnp.sum(b, axis=0, keepdims=True) for b in back], axis=1)
 
 
 def pipeline(total, begin, finish, ring):
@@ -302,24 +324,36 @@
         qrow = q[pl.ds(c, 1), :]
         radius = rads[pl.ds(c, 1), :]
         diag = lax.rsqrt(2.0 * (radius * radius))
-        back = jnp.zeros((8, LANES), F32)
-        step = 64
-        for r in range(0, panels, step):
-            span = slice(r, r + step)
-            base = r % half
-            eye = lax.broadcasted_iota(jnp.int32, (step, half), 0) + base == lax.broadcasted_iota(
-                jnp.int32, (step, half), 1
-            )
-            if r < half:
-                g0 = jnp.where(eye, diag[:, :half], inverse_root(dist[span, :half]))
-                g1 = inverse_root(dist[span, half:])
-                qcol = column(qt[span, :], c)
-                back = back + fold(g1 * qcol)
+        back = [jnp.zeros((8, LANES), F32)]
+
+        def eye(span):
+            shape = (span.stop - span.start, half)
+            row = lax.broadcasted_iota(jnp.int32, shape, 0) + span.start % half
+            return row == lax.broadcasted_iota(jnp.int32, shape, 1)
+
+        def root(span, _):
+            if span.start < half:
+                return (
+                    jnp.where(eye(span), diag[:, :half], inverse_root(dist[span, :half])),
+                    inverse_root(dist[span, half:]),
+                    column(qt[span, :], c),
+                )
+            return (jnp.where(eye(span), diag[:, half:], inverse_root(dist[span, half:])),)
+
+        def sums(span, held):
+            if span.start < half:
+                g0, g1, qcol = held
+                back[0] = back[0] + fold(g1 * qcol)
                 part = g0 * qrow[:, :half] + g1 * qrow[:, half:]
             else:
-                part = jnp.where(eye, diag[:, half:], inverse_root(dist[span, half:])) * qrow[:, half:]
-            put_column(acct, span, i, jnp.sum(part, axis=1, keepdims=True))
-        back = jnp.sum(back, axis=0, keepdims=True)
+                part = held[0] * qrow[:, half:]
+            return jnp.sum(part, axis=1, keepdims=True)
+
+        def store(span, held):
+            put_column(acct, span, i, held)
+
+        staged(spans_of(panels), root, sums, store)
+        back = jnp.sum(back[0], axis=0, keepdims=True)
         acc[pl.ds(c, 1), :] += jnp.concatenate([jnp.zeros_like(back), back], axis=1)
 
     pipeline(share, begin_self, finish_self, ring[: ring_size(share)])

time: 70.5 us -> 72.5 us (1.028)
  Pallas kernels: 45.1 us -> 46.6 us
    pallas_call x1, Pallas kernels: 9.15 us -> 10 us  [on_device(): pl.pallas_call(functools.partial(remote_kernel, (C, S, L, slots, clusters...]
where the time goes in v8:
time: 72.5 us; the launch traced here: 72.3 us
  Pallas kernels  46.6 us (64%)
  starting transfers between devices  13 us (18%)
  waiting for transfers between devices  9.49 us (13%)
  local copies, waits for them, and re-layouts  2.55 us (4%)
    pallas_call x1, Pallas kernels, on_device(): pl.pallas_call(functools.partial(local_kernel, (C, S, L, R, slots, cluste...  28.4 us
    ppermute x10, starting transfers between devices, send(): return lax.ppermute(value, names if len(names) > 1 else names[0], perm)  13 us
    pallas_call x1, Pallas kernels, on_device(): pl.pallas_call(functools.partial(remote_kernel, (C, S, L, slots, clusters...  10 us
    ppermute x10, waiting for transfers between devices, send(): return lax.ppermute(value, names if len(names) > 1 else names[0], perm)  9.49 us
    pallas_call x1, Pallas kernels, on_device(): pl.pallas_call(functools.partial(final_kernel, (S, R, L)), out_shape=shap...  3.1 us
    pallas_call x1, Pallas kernels, on_device(): pl.pallas_call(up_kernel, out_shape=shape((par_dev, rank), F32), in_specs...  3.07 us
    unnamed x23, local copies, waits for them, and re-layouts  2.54 us
    pallas_call x1, Pallas kernels, on_device(): pl.pallas_call(functools.partial(pack_kernel, (C, S, L, slots)), out_shap...  2.02 us
  transfers between devices with their start and end apart: 10, of which 5 were waited for; matrix products, arithmetic and copies ran while one was open for 2% of the time, Pallas kernels for 4%

profile of v8, /device:TPU:0, one launch (start us, length us, event | category | flops | bytes accessed | tf_op | source)
XLA Modules:
  0.0 72.3 jit_solution(17954275898997043269)
XLA Ops:
  0.0 0.0 copy-start.10
  0.0 2.0 %packs.1 = (f32[128,128]{1,0:T(8,128)}, f32[88,128]{1,0:T(8,128)}, f32[88,128]{1,0:T(8,128)}, f32[88,128]{1,0:T(8,128)}) custom-call(f32[128,128]{1,0:T(8,128)} %charges.1, s32[128,128]{1,0:T(8,128)} %mask.3, f32[128,4,256]{2,1,0:T(4,128)} %geo.5, s32[4,16]{1,0:T(4,128)} %bitcast.13, s32[4,16]{1,0:T(4,128)} %bitcast.15, s32[4,16]{1,0:T(4,128)} %bitcast.16), custom_call_target="tpu_custom_call" | custom-call | tf_op jit(solution)/shard_map/packs/pallas_call | solution.py:504
  2.0 3.0 %collective-permute-start = (f32[88,128]{1,0:T(8,128)}, f32[88,128]{1,0:T(8,128)S(1)}, u32[]{:S(2)}, u32[]{:S(2)}) collective-permute-start(f32[88,128]{1,0:T(8,128)} %get-tuple-element.16), channel_id=1, source_target_pairs={{0,4},{4,8},{8,12},{12,0},{1,5},{5,9},{9,13},{13,1},{2,6},{6,10},{... | collective-permute-start | bytes 135176 | tf_op jit(solution)/shard_map/ppermute | solution.py:475
  5.0 2.6 %collective-permute-start.1 = (f32[88,128]{1,0:T(8,128)}, f32[88,128]{1,0:T(8,128)S(1)}, u32[]{:S(2)}, u32[]{:S(2)}) collective-permute-start(f32[88,128]{1,0:T(8,128)} %get-tuple-element.17), channel_id=1, source_target_pairs={{0,8},{4,12},{8,0},{12,4},{1,9},{5,13},{9,1},{13,5},{2,10},{6,14},... | collective-permute-start | bytes 135176 | tf_op jit(solution)/shard_map/ppermute | solution.py:475
  7.6 1.3 %collective-permute-start.2 = (f32[88,128]{1,0:T(8,128)}, f32[88,128]{1,0:T(8,128)S(1)}, u32[]{:S(2)}, u32[]{:S(2)}) collective-permute-start(f32[88,128]{1,0:T(8,128)} %get-tuple-element.18), channel_id=1, source_target_pairs={{0,12},{4,0},{8,4},{12,8},{1,13},{5,1},{9,5},{13,9},{2,14},{6,2},{... | collective-permute-start | bytes 135176 | tf_op jit(solution)/shard_map/ppermute | solution.py:475
  9.0 1.5 %collective-permute-start.3 = (f32[128,128]{1,0:T(8,128)}, f32[128,128]{1,0:T(8,128)S(1)}, u32[]{:S(2)}, u32[]{:S(2)}) collective-permute-start(f32[128,128]{1,0:T(8,128)} %get-tuple-element.15.masked.rest_0_), channel_id=1, source_target_pairs={{0,2},{2,0},{1,3},{3,1},{4,6},{6,4},{5,7},{7,5},{8,10},{10,8},{9,1... | collective-permute-start | bytes 196616 | tf_op jit(solution)/shard_map/ppermute | solution.py:475
  10.5 3.1 %far_up.1.up = f32[16,32]{1,0:T(8,128)} custom-call(f32[128,32,128]{2,1,0:T(8,128)} %bitcast.9, f32[128,128]{1,0:T(8,128)} %get-tuple-element.15.masked.rest_0_, f32[32,32,128]{2,1,0:T(8,128)} %bitcast.11, s32[1,128]{1,0:T(1,128)} %bitcast.17), custom_call_target="tpu_custom_call" | custom-call | tf_op jit(solution)/shard_map/far_up/pallas_call | solution.py:517
  13.6 0.0 collective-permute-done.rest_2_
  13.6 0.0 copy-start.4
  13.6 0.0 collective-permute-done.1.rest_3_
  13.6 0.0 copy-start.5
  13.6 0.0 collective-permute-done.2.rest_4_
  13.6 0.0 copy-start.6
  13.6 0.6 maximum_convert_fusion.codes
  14.2 0.0 collective-permute-done.3.rest_1_
  14.2 0.0 copy-done.4
  14.2 0.0 copy-done.5
  14.2 0.0 copy-done.6
  14.3 0.0 copy-start
  14.3 0.6 copy-done
  14.9 10.0 %near_remote.1 = (f32[128,256]{1,0:T(8,128)}, f32[32,128]{1,0:T(8,128)}, f32[32,128]{1,0:T(8,128)}, f32[32,128]{1,0:T(8,128)}) custom-call(f32[128,4,256]{2,1,0:T(4,128)} %geo.5, s32[3,16]{1,0:T(4,128)} %maximum_convert_fusion.codes, f32[16,32]{1,0:T(8,128)} %far_up.1.up, f32[128,128]{1,0:T(8,128)} %get-tuple-element.15.masked.rest_0_, f32[128,128]{1,0:T(8,128)} %copy-done, ...), custom_call_target="tpu_custom_call" | custom-call | tf_op jit(solution)/shard_map/near_remote/pallas_call | solution.py:526
  24.9 1.4 %collective-permute-start.4 = (f32[32,128]{1,0:T(8,128)}, f32[32,128]{1,0:T(8,128)S(1)}, u32[]{:S(2)}, u32[]{:S(2)}) collective-permute-start(f32[32,128]{1,0:T(8,128)} %get-tuple-element.20), channel_id=1, source_target_pairs={{0,12},{4,0},{8,4},{12,8},{1,13},{5,1},{9,5},{13,9},{2,14},{6,2},{... | collective-permute-start | bytes 49160 | tf_op jit(solution)/shard_map/ppermute | solution.py:475
  26.3 0.7 collective-permute-start.5
  27.0 0.2 collective-permute-start.6
  27.3 0.0 copy-done.10
  27.3 0.7 copy.13.far_list
  27.9 0.9 %collective-permute-done.4.rest_2_ = f32[32,128]{1,0:T(8,128)S(1)} collective-permute-done((f32[32,128]{1,0:T(8,128)}, f32[32,128]{1,0:T(8,128)S(1)}, u32[]{:S(2)}, u32[]{:S(2)}) %collective-permute-start.4) | collective-permute-done | bytes 16416 | tf_op jit(solution)/shard_map/ppermute | solution.py:475
  28.8 0.0 copy-start.7
  28.8 2.5 %collective-permute-done.5.rest_3_ = f32[32,128]{1,0:T(8,128)S(1)} collective-permute-done((f32[32,128]{1,0:T(8,128)}, f32[32,128]{1,0:T(8,128)S(1)}, u32[]{:S(2)}, u32[]{:S(2)}) %collective-permute-start.5) | collective-permute-done | bytes 16416 | tf_op jit(solution)/shard_map/ppermute | solution.py:475
  31.4 0.0 copy-start.8
  31.4 1.4 %collective-permute-done.6.rest_4_ = f32[32,128]{1,0:T(8,128)S(1)} collective-permute-done((f32[32,128]{1,0:T(8,128)}, f32[32,128]{1,0:T(8,128)S(1)}, u32[]{:S(2)}, u32[]{:S(2)}) %collective-permute-start.6) | collective-permute-done | bytes 16416 | tf_op jit(solution)/shard_map/ppermute | solution.py:475
  32.8 0.0 copy-start.9
  32.8 0.0 copy-done.7
  32.8 0.0 copy-done.8
  32.8 0.6 copy-done.9
  33.4 28.4 %near_local.1 = (f32[160,128]{1,0:T(8,128)}, f32[160,128]{1,0:T(8,128)}) custom-call(f32[128,4,256]{2,1,0:T(4,128)} %geo.5, s32[2,128]{1,0:T(2,128)} %bitcast.19, s32[4,16]{1,0:T(4,128)} %bitcast.14, s32[16,8]{1,0:T(8,128)} %copy.13.far_list, f32[16,8,32,32]{3,2,1,0:T(8,128)} %coupling.1, f32[32,32,128]{2,1,0:T(8,128)} %bitcast.12, s32[1,128]{1,0:T(1,128)} %bitcast.18, ...), custom_call_target="tpu_custom_call" | custom-call | tf_op jit(solution)/shard_map/near_local/pallas_call | solution.py:550
  61.8 0.0 collective-permute-start.7
  61.8 0.9 %collective-permute-start.9 = (f32[160,128]{1,0:T(8,128)}, f32[160,128]{1,0:T(8,128)S(1)}, u32[]{:S(2)}, u32[]{:S(2)}) collective-permute-start(f32[160,128]{1,0:T(8,128)} %get-tuple-element.24), channel_id=1, source_target_pairs={{0,3},{1,2},{2,1},{3,0},{4,7},{5,6},{6,5},{7,4},{8,11},{9,10},{10,... | collective-permute-start | bytes 245768 | tf_op jit(solution)/shard_map/ppermute | solution.py:475
  62.7 1.2 %collective-permute-start.8 = (f32[160,128]{1,0:T(8,128)}, f32[160,128]{1,0:T(8,128)S(1)}, u32[]{:S(2)}, u32[]{:S(2)}) collective-permute-start(f32[160,128]{1,0:T(8,128)} %get-tuple-element.24), channel_id=1, source_target_pairs={{0,2},{1,3},{2,0},{3,1},{4,6},{5,7},{6,4},{7,5},{8,10},{9,11},{10,... | collective-permute-start | bytes 245768 | tf_op jit(solution)/shard_map/ppermute | solution.py:475
  63.9 0.0 collective-permute-done.7.rest_1_
  63.9 0.0 copy-start.1
  63.9 2.3 %collective-permute-done.9.rest_3_ = f32[160,128]{1,0:T(8,128)S(1)} collective-permute-done((f32[160,128]{1,0:T(8,128)}, f32[160,128]{1,0:T(8,128)S(1)}, u32[]{:S(2)}, u32[]{:S(2)}) %collective-permute-start.9) | collective-permute-done | bytes 81952 | tf_op jit(solution)/shard_map/ppermute | solution.py:475
  66.2 0.0 copy-start.2
  66.2 2.3 %collective-permute-done.8.rest_2_ = f32[160,128]{1,0:T(8,128)S(1)} collective-permute-done((f32[160,128]{1,0:T(8,128)}, f32[160,128]{1,0:T(8,128)S(1)}, u32[]{:S(2)}, u32[]{:S(2)}) %collective-permute-start.8) | collective-permute-done | bytes 81952 | tf_op jit(solution)/shard_map/ppermute | solution.py:475
  68.6 0.0 copy-done.1
  68.6 0.0 copy-done.2
  68.6 0.6 copy-done.3
  69.2 3.1 %combine.1 = f32[128,128]{1,0:T(8,128)} custom-call(s32[128,128]{1,0:T(8,128)} %mask.3, f32[128,32,128]{2,1,0:T(8,128)} %bitcast.10, f32[160,128]{1,0:T(8,128)} %get-tuple-element.23.rest_0_, f32[160,128]{1,0:T(8,128)} %copy-done.1, f32[160,128]{1,0:T(8,128)} %copy-done.3, f32[160,128]{1,0:T(8,128)} %copy-done.2), custom_call_target="tpu_custom_call" | custom-call | tf_op jit(solution)/shard_map/combine/pallas_call | solution.py:576
  (4 shorter events, 0.0 us)
Async XLA Ops:
  0.0 27.3 %copy-start.10 = (s32[16,8]{0,1:T(8,128)S(1)}, s32[16,8]{0,1:T(8,128)}, u32[]{:S(2)}) copy-start(s32[16,8]{0,1:T(8,128)} %param.22) | copy-start | bytes 1540
  2.0 11.5 %collective-permute-start = (f32[88,128]{1,0:T(8,128)}, f32[88,128]{1,0:T(8,128)S(1)}, u32[]{:S(2)}, u32[]{:S(2)}) collective-permute-start(f32[88,128]{1,0:T(8,128)} %get-tuple-element.16), channel_id=1, source_target_pairs={{0,4},{4,8},{8,12},{12,0},{1,5},{5,9},{9,13},{13,1},{2,6},{6,10},{... | collective-permute-start | bytes 135176 | tf_op jit(solution)/shard_map/ppermute | solution.py:475
  5.0 8.5 %collective-permute-start.1 = (f32[88,128]{1,0:T(8,128)}, f32[88,128]{1,0:T(8,128)S(1)}, u32[]{:S(2)}, u32[]{:S(2)}) collective-permute-start(f32[88,128]{1,0:T(8,128)} %get-tuple-element.17), channel_id=1, source_target_pairs={{0,8},{4,12},{8,0},{12,4},{1,9},{5,13},{9,1},{13,5},{2,10},{6,14},... | collective-permute-start | bytes 135176 | tf_op jit(solution)/shard_map/ppermute | solution.py:475
  7.6 6.0 %collective-permute-start.2 = (f32[88,128]{1,0:T(8,128)}, f32[88,128]{1,0:T(8,128)S(1)}, u32[]{:S(2)}, u32[]{:S(2)}) collective-permute-start(f32[88,128]{1,0:T(8,128)} %get-tuple-element.18), channel_id=1, source_target_pairs={{0,12},{4,0},{8,4},{12,8},{1,13},{5,1},{9,5},{13,9},{2,14},{6,2},{... | collective-permute-start | bytes 135176 | tf_op jit(solution)/shard_map/ppermute | solution.py:475
  9.0 5.3 %collective-permute-start.3 = (f32[128,128]{1,0:T(8,128)}, f32[128,128]{1,0:T(8,128)S(1)}, u32[]{:S(2)}, u32[]{:S(2)}) collective-permute-start(f32[128,128]{1,0:T(8,128)} %get-tuple-element.15.masked.rest_0_), channel_id=1, source_target_pairs={{0,2},{2,0},{1,3},{3,1},{4,6},{6,4},{5,7},{7,5},{8,10},{10,8},{9,1... | collective-permute-start | bytes 196616 | tf_op jit(solution)/shard_map/ppermute | solution.py:475
  13.6 0.7 copy-start.4
  13.6 0.7 copy-start.5
  13.6 0.6 copy-start.6
  14.3 0.6 copy-start
  24.9 3.9 %collective-permute-start.4 = (f32[32,128]{1,0:T(8,128)}, f32[32,128]{1,0:T(8,128)S(1)}, u32[]{:S(2)}, u32[]{:S(2)}) collective-permute-start(f32[32,128]{1,0:T(8,128)} %get-tuple-element.20), channel_id=1, source_target_pairs={{0,12},{4,0},{8,4},{12,8},{1,13},{5,1},{9,5},{13,9},{2,14},{6,2},{... | collective-permute-start | bytes 49160 | tf_op jit(solution)/shard_map/ppermute | solution.py:475
  26.3 5.0 %collective-permute-start.5 = (f32[32,128]{1,0:T(8,128)}, f32[32,128]{1,0:T(8,128)S(1)}, u32[]{:S(2)}, u32[]{:S(2)}) collective-permute-start(f32[32,128]{1,0:T(8,128)} %get-tuple-element.21), channel_id=1, source_target_pairs={{0,8},{4,12},{8,0},{12,4},{1,9},{5,13},{9,1},{13,5},{2,10},{6,14},... | collective-permute-start | bytes 49160 | tf_op jit(solution)/shard_map/ppermute | solution.py:475
  27.0 5.7 %collective-permute-start.6 = (f32[32,128]{1,0:T(8,128)}, f32[32,128]{1,0:T(8,128)S(1)}, u32[]{:S(2)}, u32[]{:S(2)}) collective-permute-start(f32[32,128]{1,0:T(8,128)} %get-tuple-element.22), channel_id=1, source_target_pairs={{0,4},{4,8},{8,12},{12,0},{1,5},{5,9},{9,13},{13,1},{2,6},{6,10},{... | collective-permute-start | bytes 49160 | tf_op jit(solution)/shard_map/ppermute | solution.py:475
  28.8 3.9 %copy-start.7 = (f32[32,128]{1,0:T(8,128)}, f32[32,128]{1,0:T(8,128)S(1)}, u32[]{:S(2)}) copy-start(f32[32,128]{1,0:T(8,128)S(1)} %collective-permute-done.4.rest_2_) | copy-start | bytes 49156
  31.4 1.4 %copy-start.8 = (f32[32,128]{1,0:T(8,128)}, f32[32,128]{1,0:T(8,128)S(1)}, u32[]{:S(2)}) copy-start(f32[32,128]{1,0:T(8,128)S(1)} %collective-permute-done.5.rest_3_) | copy-start | bytes 49156
  32.8 0.6 copy-start.9
  61.8 2.1 %collective-permute-start.7 = (f32[160,128]{1,0:T(8,128)}, f32[160,128]{1,0:T(8,128)S(1)}, u32[]{:S(2)}, u32[]{:S(2)}) collective-permute-start(f32[160,128]{1,0:T(8,128)} %get-tuple-element.23.rest_0_), channel_id=1, source_target_pairs={{0,1},{1,0},{2,3},{3,2},{4,5},{5,4},{6,7},{7,6},{8,9},{9,8},{10,11... | collective-permute-start | bytes 245768 | tf_op jit(solution)/shard_map/ppermute | solution.py:475
  61.8 4.4 %collective-permute-start.9 = (f32[160,128]{1,0:T(8,128)}, f32[160,128]{1,0:T(8,128)S(1)}, u32[]{:S(2)}, u32[]{:S(2)}) collective-permute-start(f32[160,128]{1,0:T(8,128)} %get-tuple-element.24), channel_id=1, source_target_pairs={{0,3},{1,2},{2,1},{3,0},{4,7},{5,6},{6,5},{7,4},{8,11},{9,10},{10,... | collective-permute-start | bytes 245768 | tf_op jit(solution)/shard_map/ppermute | solution.py:475
  62.7 5.8 %collective-permute-start.8 = (f32[160,128]{1,0:T(8,128)}, f32[160,128]{1,0:T(8,128)S(1)}, u32[]{:S(2)}, u32[]{:S(2)}) collective-permute-start(f32[160,128]{1,0:T(8,128)} %get-tuple-element.24), channel_id=1, source_target_pairs={{0,2},{1,3},{2,0},{3,1},{4,6},{5,7},{6,4},{7,5},{8,10},{9,11},{10,... | collective-permute-start | bytes 245768 | tf_op jit(solution)/shard_map/ppermute | solution.py:475
  63.9 4.6 %copy-start.1 = (f32[160,128]{1,0:T(8,128)}, f32[160,128]{1,0:T(8,128)S(1)}, u32[]{:S(2)}) copy-start(f32[160,128]{1,0:T(8,128)S(1)} %collective-permute-done.7.rest_1_) | copy-start | bytes 245764
  66.2 2.3 %copy-start.2 = (f32[160,128]{1,0:T(8,128)}, f32[160,128]{1,0:T(8,128)S(1)}, u32[]{:S(2)}) copy-start(f32[160,128]{1,0:T(8,128)S(1)} %collective-permute-done.9.rest_3_) | copy-start | bytes 245764
  68.6 0.6 copy-start.3

commit v9 on v8

--- a/solution.py
+++ b/solution.py
@@ -8,10 +8,7 @@
 from jax.sharding import PartitionSpec as P
 
 F32 = jnp.float32
-BF16 = jnp.bfloat16
 HIGHEST = lax.Precision.HIGHEST
-ROWS = 40
-USED = 34
 LANES = 128
 PARAMS = pltpu.CompilerParams(vmem_limit_bytes=56 * 1024 * 1024)
 
@@ -26,79 +23,6 @@
 
 def whole(size):
     return -(-size // LANES) * LANES
-
-
-def cut(v):
-    return v.astype(BF16).astype(F32)
-
-
-def powers(sign):
-    lane = lax.broadcasted_iota(jnp.int32, (8, LANES), 1)
-    out = jnp.full((8, LANES), 2.0 ** (-64 * sign), F32)
-    for bit in range(7):
-        out = out * jnp.where((lane >> bit) & 1 == 1, F32(2.0 ** (sign * 2**bit)), F32(1.0))
-    return out
-
-
-def frame(parts):
-    low = [functools.reduce(jnp.minimum, [jnp.min(p[k]) for p in parts]) for k in range(3)]
-    high = [functools.reduce(jnp.maximum, [jnp.max(p[k]) for p in parts]) for k in range(3)]
-    width = functools.reduce(jnp.maximum, [jnp.max(jnp.abs(p[3])) for p in parts])
-    for lo, hi in zip(low, high):
-        width = jnp.maximum(width, 0.5 * (hi - lo))
-    up, down = powers(1), powers(-1)
-    size = jnp.min(jnp.where(up >= width, up, F32(2.0**63)))
-    inv = jnp.max(jnp.where(up >= width, down, F32(2.0**-63)))
-    magic = size * F32(1.5 * 2.0**20)
-    centre = [(0.5 * (lo + hi) + magic) - magic for lo, hi in zip(low, high)]
-    return centre, inv
-
-
-def split_features(points, centre, inv):
-    magic = F32(1.5 * 2.0**16)
-    grid, rest = [], []
-    for k in range(3):
-        u = (points[k] - centre[k]) * inv
-        h = (u + magic) - magic
-        grid.append(h)
-        rest.append(u - h)
-    rad = points[3] * inv
-    norm = grid[0] * grid[0] + grid[1] * grid[1] + grid[2] * grid[2]
-    norm1 = cut(norm)
-    norm2 = norm - norm1
-    cross = grid[0] * rest[0] + grid[1] * rest[1] + grid[2] * rest[2]
-    extra = 2.0 * cross + (rest[0] * rest[0] + rest[1] * rest[1] + rest[2] * rest[2]) + rad * rad
-    extra1 = cut(extra)
-    extra2 = cut(extra - extra1)
-    extra3 = (extra - extra1) - extra2
-    rest1 = [cut(v) for v in rest]
-    rest2 = [v - w for v, w in zip(rest, rest1)]
-    neg = lambda vs: [-2.0 * v for v in vs]
-    one = jnp.ones_like(rad)
-    left = grid + [norm1, norm2, one, one]
-    right = neg(grid) + [one, one, norm1, norm2]
-    left += [extra1, extra2, extra3, one, one, one]
-    right += [one, one, one, extra1, extra2, extra3]
-    left += grid + grid + rest1 + rest2 + rest1 + rest1 + rest2
-    right += neg(rest1) + neg(rest2) + neg(grid) + neg(grid) + neg(rest1) + neg(rest2) + neg(rest1)
-    return left, right, rad
-
-
-def store_features(ref, rows):
-    count = rows[0].shape[0]
-    width = rows[0].shape[1]
-    for k, row in enumerate(rows):
-        for t, piece in enumerate(ref):
-            piece[pl.ds(k, count, stride=ROWS), :] = row[:, t * LANES : min(width, (t + 1) * LANES)]
-
-
-def load_features(ref, index):
-    start = pl.multiple_of(index * ROWS, 8)
-    return [piece[pl.ds(start, USED), :].astype(BF16) for piece in ref]
-
-
-def contract(left, right):
-    return lax.dot_general(left, right, (((0,), (0,)), ((), ())), preferred_element_type=F32)
 
 
 def column(table, index):
@@ -121,12 +45,6 @@
 
 def fold(v):
     return jnp.sum(v.reshape(v.shape[0] // 8, 8, v.shape[1]), axis=0)
-
-
-def distances(left, right, out):
-    whole_left = jnp.concatenate(left, axis=1) if len(left) > 1 else left[0]
-    for t, r in enumerate(right):
-        out[:, t * LANES : (t + 1) * LANES] = contract(whole_left, r)
 
 
 def staged(spans, *stages):
@@ -145,47 +63,50 @@
     return [slice(r, r + step) for r in range(0, height, step)]
 
 
-def tile_sums(dist, qrow, qtable, slot, table, index):
-    q0, q1 = qrow[:, :LANES], qrow[:, LANES:]
+def kernel_values(columns, row):
+    x, y, z, rr = columns
+    dx, dy, dz = x - row[0], y - row[1], z - row[2]
+    return lax.rsqrt((dx * dx + dy * dy + dz * dz) + (rr + row[3]))
+
+
+def panel_rows(points):
+    rows = [points[0:1, :], points[1:2, :], points[2:3, :], points[3:4, :] * points[3:4, :]]
+    return [[r[:, t : t + LANES] for r in rows] for t in range(0, points.shape[1], LANES)]
+
+
+def tile_sums(tables, slot, points, qrow, table, index):
+    blocks = panel_rows(points)
+    q = [qrow[:, :LANES], qrow[:, LANES:]]
     back = [jnp.zeros((8, LANES), F32), jnp.zeros((8, LANES), F32)]
 
     def root(rows, _):
-        return (
-            inverse_root(dist[rows, :LANES]),
-            inverse_root(dist[rows, LANES:]),
-            column(qtable[rows, :], slot),
-        )
+        *place, qcol = [column(t[rows, :], slot) for t in tables]
+        return [kernel_values(place, b) for b in blocks] + [qcol]
 
     def sums(rows, held):
         g0, g1, qcol = held
         back[0] = back[0] + fold(g0 * qcol)
         back[1] = back[1] + fold(g1 * qcol)
-        return jnp.sum(g0 * q0 + g1 * q1, axis=1, keepdims=True)
+        return jnp.sum(g0 * q[0] + g1 * q[1], axis=1, keepdims=True)
 
     def store(rows, held):
         put_column(table, rows, index, held)
 
-    staged(spans_of(dist.shape[0]), root, sums, store)
+    staged(spans_of(tables[0].shape[0]), root, sums, store)
     return jnp.concatenate([jnp.sum(b, axis=0, keepdims=True) for b in back], axis=1)
 
 
-def pipeline(total, begin, finish, ring):
-    size = len(ring)
-    ahead = min(2, size - 1)
-
+def pipeline(total, tile, size):
     def body(i, carry):
         for k in range(size):
-            begin(i * size + k + ahead, ring[(k + ahead) % size])
-            finish(i * size + k, ring[k])
+            tile(i * size + k)
         return carry
 
-    for k in range(ahead):
-        begin(k, ring[k])
     lax.fori_loop(0, (total + size - 1) // size, body, 0)
 
 
 def ring_size(total):
-    return next(size for size in (8, 4, 2, 1) if total % size == 0)
+    return next(size for size in (4, 2, 1) if total % size == 0)
 
 
 def assemble(sub, S, L, q, pieces):
@@ -232,8 +153,7 @@
     packs = rest[S : S + C - 1]
     acc_out = rest[S + C - 1]
     sends = rest[S + C : S + C + C - 1]
-    q, tqt, acc, fwdt, sgeo, fa0, fb0, fb1, order, *ring = rest[S + C + C - 1 :]
-    fa, fb = (fa0,), (fb0, fb1)
+    q, acc, fwdt, order, *tables = rest[S + C + C - 1 :]
     n = (C - 1) * slots
     assemble(lax.axis_index("sub"), S, L, q, pieces)
     acc[...] = jnp.zeros_like(acc)
@@ -241,44 +161,28 @@
     found = jnp.int32(0)
     for shift in range(C - 1):
         for j in range(slots):
-            code = codes[shift, j]
             order[found] = shift * slots + j
-            found = found + (code >= 0).astype(jnp.int32)
-            g = geo[jnp.maximum(code, 0)]
-            for k in range(4):
-                row = k * n + shift * slots + j
-                sgeo[row : row + 1, :] = g[k : k + 1]
-    tpoints = [
-        jnp.concatenate([p[k * slots : (k + 1) * slots, :] for p in packs], axis=0) for k in range(5)
-    ]
-    spoints = [sgeo[k * n : (k + 1) * n, :] for k in range(4)]
-    centre, inv = frame([tpoints, spoints])
-    left, _, _ = split_features(tpoints, centre, inv)
-    _, right, _ = split_features(spoints, centre, inv)
-    store_features(fa, left)
-    store_features(fb, right)
-    wide = tqt.shape[1]
-    tq = tpoints[4]
-    if wide > n:
-        tq = jnp.concatenate([tq, jnp.zeros((wide - n, L), F32)], axis=0)
-    tqt[...] = tq.T
-
-    def begin(i, dist):
-        slot = order[jnp.minimum(i, jnp.maximum(found - 1, 0))]
-        distances(load_features(fa, slot), load_features(fb, slot), dist)
-
-    def finish(i, dist):
+            found = found + (codes[shift, j] >= 0).astype(jnp.int32)
+    wide = fwdt.shape[1]
+    for k in range(5):
+        rows = [p[k * slots : (k + 1) * slots, :] for p in packs]
+        if wide > n:
+            rows.append(jnp.zeros((wide - n, L), F32))
+        value = jnp.concatenate(rows, axis=0).T
+        tables[k][...] = value * value if k == 3 else value
+
+    def tile(i):
         ok = i < found
         slot = order[jnp.minimum(i, jnp.maximum(found - 1, 0))]
         source = jnp.maximum(codes[slot // slots, lax.rem(slot, slots)], 0)
         back = tile_sums(
-            dist, q[pl.ds(source, 1), :], tqt, slot, fwdt, jnp.where(ok, slot, -1)
+            tables, slot, geo[source], q[pl.ds(source, 1), :], fwdt, jnp.where(ok, slot, -1)
         )
         acc[pl.ds(source, 1), :] += jnp.where(ok, back, 0.0)
 
-    pipeline(found, begin, finish, ring)
-    acc_out[...] = acc[...] * inv
-    fwd = (fwdt[...] * inv).T
+    pipeline(found, tile, 4)
+    acc_out[...] = acc[...]
+    fwd = fwdt[...].T
     rank = up.shape[1]
     for shift in range(C - 1):
         sends[shift][:slots, :] = fwd[shift * slots : (shift + 1) * slots, :]
@@ -293,52 +197,31 @@
     pieces = rest[:S]
     sums = rest[S : S + C - 1]
     parts = rest[S + C - 1 : 2 * S + C - 1]
-    q, qt, acc, acct, fa0, fa1, fb0, fb1, rads, got, parents, rows, *ring = rest[2 * S + C - 1 :]
-    fa, fb = (fa0, fa1), (fb0, fb1)
+    q, acc, acct, got, parents, rows, *tables = rest[2 * S + C - 1 :]
     me, sub, rep = lax.axis_index("clu"), lax.axis_index("sub"), lax.axis_index("rep")
     assemble(sub, S, L, q, pieces)
-    qt[...] = q[...].T
     acc[...] = jnp.zeros_like(acc)
     acct[...] = jnp.zeros_like(acct)
-    points = [geo[:, k, :] for k in range(4)]
-    centre, inv = frame([points])
-    left, right, rad = split_features(points, centre, inv)
-    store_features(fa, left)
-    store_features(fb, right)
-    rads[...] = rad
+    for k in range(4):
+        value = geo[:, k, :].T
+        tables[k][...] = value * value if k == 3 else value
+    tables[4][...] = q[...].T
 
     half = panels // 2
     share = clusters // (S * R)
     first = (rep * S + sub) * share
 
-    def begin_self(i, dist):
-        c = first + jnp.minimum(i, share - 1)
-        a = load_features(fa, c)
-        b = load_features(fb, c)
-        dist[:half, :half] = contract(a[0], b[0])
-        dist[:half, half:] = contract(a[0], b[1])
-        dist[half:, half:] = contract(a[1], b[1])
-
-    def finish_self(i, dist):
+    def self_tile(i):
         c = first + i
+        blocks = panel_rows(geo[c])
         qrow = q[pl.ds(c, 1), :]
-        radius = rads[pl.ds(c, 1), :]
-        diag = lax.rsqrt(2.0 * (radius * radius))
         back = [jnp.zeros((8, LANES), F32)]
 
-        def eye(span):
-            shape = (span.stop - span.start, half)
-            row = lax.broadcasted_iota(jnp.int32, shape, 0) + span.start % half
-            return row == lax.broadcasted_iota(jnp.int32, shape, 1)
-
         def root(span, _):
+            *place, qcol = [column(t[span, :], c) for t in tables]
             if span.start < half:
-                return (
-                    jnp.where(eye(span), diag[:, :half], inverse_root(dist[span, :half])),
-                    inverse_root(dist[span, half:]),
-                    column(qt[span, :], c),
-                )
-            return (jnp.where(eye(span), diag[:, half:], inverse_root(dist[span, half:])),)
+                return [kernel_values(place, b) for b in blocks] + [qcol]
+            return [kernel_values(place, blocks[1])]
 
         def sums(span, held):
             if span.start < half:
@@ -353,29 +236,27 @@
             put_column(acct, span, i, held)
 
         staged(spans_of(panels), root, sums, store)
-        back = jnp.sum(back[0], axis=0, keepdims=True)
-        acc[pl.ds(c, 1), :] += jnp.concatenate([jnp.zeros_like(back), back], axis=1)
-
-    pipeline(share, begin_self, finish_self, ring[: ring_size(share)])
+        total = jnp.sum(back[0], axis=0, keepdims=True)
+        acc[pl.ds(c, 1), :] += jnp.concatenate([jnp.zeros_like(total), total], axis=1)
+
+    pipeline(share, self_tile, ring_size(share))
 
     count = pairs.shape[1] // S
     start = sub * count
 
-    def begin(i, dist):
-        p = start + jnp.minimum(i, count - 1)
-        distances(load_features(fa, pairs[0, p]), load_features(fb, pairs[1, p]), dist)
-
-    def finish(i, dist):
+    def pair_tile(i):
         ia, ib = pairs[0, start + i], pairs[1, start + i]
-        acc[pl.ds(ib, 1), :] += tile_sums(dist, q[pl.ds(ib, 1), :], qt, ia, acct, share + i)
-
-    pipeline(count, begin, finish, ring[: ring_size(count)])
+        acc[pl.ds(ib, 1), :] += tile_sums(
+            tables, ia, geo[ib], q[pl.ds(ib, 1), :], acct, share + i
+        )
+
+    pipeline(count, pair_tile, ring_size(count))
     rows[...] = acct[...].T
     for i in range(share):
         acc[pl.ds(first + i, 1), :] += rows[i : i + 1, :]
     for i in range(count):
         acc[pl.ds(pairs[0, start + i], 1), :] += rows[share + i : share + i + 1, :]
-    total = acc_in[...] + acc[...] * inv
+    total = acc_in[...] + acc[...]
 
     got[...] = jnp.zeros_like(got)
     for shift in range(1, C):
@@ -530,23 +411,17 @@
         out_specs=[vmem()] * C,
         scratch_shapes=[
             pltpu.VMEM((clusters, panels), F32),
-            pltpu.VMEM((L, whole(n)), F32),
             pltpu.VMEM((clusters, panels), F32),
             pltpu.VMEM((L, whole(n)), F32),
-            pltpu.VMEM((4 * n, panels), F32),
-            pltpu.VMEM((n * ROWS, L), F32),
-            pltpu.VMEM((n * ROWS, LANES), F32),
-            pltpu.VMEM((n * ROWS, LANES), F32),
             pltpu.SMEM((n + 1,), jnp.int32),
         ]
-        + [pltpu.VMEM((L, panels), F32)] * 4,
+        + [pltpu.VMEM((L, whole(n)), F32)] * 5,
         compiler_params=PARAMS,
         name="near_remote",
     )(geometry, codes, up, *pieces, *packs)
     acc, sums = made[0], [send(made[d], (("clu", C - d),)) for d in range(1, C)]
 
     columns = whole(clusters // (S * R) + local_pairs.shape[1] // S)
-    half = [pltpu.VMEM((clusters * ROWS, LANES), F32)] * 2
     parts = pl.pallas_call(
         functools.partial(local_kernel, (C, S, L, R, slots, clusters, panels)),
         out_shape=[shape((clusters + clusters // L * rank, L), F32)] * S,
@@ -554,17 +429,13 @@
         out_specs=[vmem()] * S,
         scratch_shapes=[
             pltpu.VMEM((clusters, panels), F32),
-            pltpu.VMEM((panels, clusters), F32),
             pltpu.VMEM((clusters, panels), F32),
             pltpu.VMEM((panels, columns), F32),
-            *half,
-            *half,
-            pltpu.VMEM((clusters, panels), F32),
             pltpu.VMEM((clusters, L), F32),
             pltpu.VMEM((C * par_dev, rank), F32),
             pltpu.VMEM((columns, panels), F32),
         ]
-        + [pltpu.VMEM((panels, panels), F32)] * 8,
+        + [pltpu.VMEM((panels, clusters), F32)] * 5,
         compiler_params=PARAMS,
         name="near_local",
     )(geometry, local_pairs[0].T, targets, far_list, coupling, transfer_t, parent, up, acc, *pieces, *sums)

time: 72.5 us -> 221 us (3.05)
  Pallas kernels: 46.6 us -> 192 us
  starting transfers between devices: 13 us -> 15.7 us
    pallas_call x1, Pallas kernels: 28.4 us -> 149 us  [on_device(): pl.pallas_call(functools.partial(local_kernel, (C, S, L, R, slots, cluste...]
    pallas_call x1, Pallas kernels: 10 us -> 35 us  [on_device(): pl.pallas_call(functools.partial(remote_kernel, (C, S, L, slots, clusters...]
    ppermute x10, starting transfers between devices: 13 us -> 15.7 us  [send(): return lax.ppermute(value, names if len(names) > 1 else names[0], perm)]
  transfers between devices with their start and end apart: 10 -> 10, of which waited for: 5 -> 5; matrix products, arithmetic and copies ran while one was open for 2% -> 1% of each run, Pallas kernels for 4% -> 1%
where the time goes in v9:
time: 221 us
  Pallas kernels  192 us (87%)
  starting transfers between devices  15.7 us (7%)
  waiting for transfers between devices  9.71 us (4%)
  local copies, waits for them, and re-layouts  2.55 us (1%)
    pallas_call x1, Pallas kernels, on_device(): pl.pallas_call(functools.partial(local_kernel, (C, S, L, R, slots, cluste...  149 us
    pallas_call x1, Pallas kernels, on_device(): pl.pallas_call(functools.partial(remote_kernel, (C, S, L, slots, clusters...  35 us
    ppermute x10, starting transfers between devices, send(): return lax.ppermute(value, names if len(names) > 1 else names[0], perm)  15.7 us
    ppermute x10, waiting for transfers between devices, send(): return lax.ppermute(value, names if len(names) > 1 else names[0], perm)  9.71 us
  transfers between devices with their start and end apart: 10, of which 5 were waited for; matrix products, arithmetic and copies ran while one was open for 1% of the time, Pallas kernels for 1%

profile of v9, /device:TPU:0, one launch (start us, length us, event | category | flops | bytes accessed | tf_op | source)
XLA Modules:
  0.0 221.2 jit_solution(7728674383844480067)
XLA Ops:
  0.0 0.0 copy-start.10
  0.0 2.0 packs.1
  2.0 3.0 %collective-permute-start = (f32[88,128]{1,0:T(8,128)}, f32[88,128]{1,0:T(8,128)S(1)}, u32[]{:S(2)}, u32[]{:S(2)}) collective-permute-start(f32[88,128]{1,0:T(8,128)} %get-tuple-element.16), channel_id=1, source_target_pairs={{0,4},{4,8},{8,12},{12,0},{1,5},{5,9},{9,13},{13,1},{2,6},{6,10},{... | collective-permute-start | bytes 135176 | tf_op jit(solution)/shard_map/ppermute | solution.py:356
  5.0 2.6 %collective-permute-start.1 = (f32[88,128]{1,0:T(8,128)}, f32[88,128]{1,0:T(8,128)S(1)}, u32[]{:S(2)}, u32[]{:S(2)}) collective-permute-start(f32[88,128]{1,0:T(8,128)} %get-tuple-element.17), channel_id=1, source_target_pairs={{0,8},{4,12},{8,0},{12,4},{1,9},{5,13},{9,1},{13,5},{2,10},{6,14},... | collective-permute-start | bytes 135176 | tf_op jit(solution)/shard_map/ppermute | solution.py:356
  7.6 1.3 collective-permute-start.2
  9.0 1.5 collective-permute-start.3
  10.5 3.1 %far_up.1.up = f32[16,32]{1,0:T(8,128)} custom-call(f32[128,32,128]{2,1,0:T(8,128)} %bitcast.9, f32[128,128]{1,0:T(8,128)} %get-tuple-element.15.masked.rest_0_, f32[32,32,128]{2,1,0:T(8,128)} %bitcast.11, s32[1,128]{1,0:T(1,128)} %bitcast.17), custom_call_target="tpu_custom_call" | custom-call | tf_op jit(solution)/shard_map/far_up/pallas_call | solution.py:398
  13.6 0.0 collective-permute-done.rest_2_
  13.6 0.0 copy-start.4
  13.6 0.0 collective-permute-done.1.rest_3_
  13.6 0.0 copy-start.5
  13.6 0.0 collective-permute-done.2.rest_4_
  13.6 0.0 copy-start.6
  13.6 0.6 maximum_convert_fusion.codes
  14.2 0.0 collective-permute-done.3.rest_1_
  14.2 0.0 copy-done.4
  14.2 0.0 copy-done.5
  14.2 0.0 copy-done.6
  14.3 0.0 copy-start
  14.3 0.6 copy-done
  14.9 35.0 %near_remote.1 = (f32[128,256]{1,0:T(8,128)}, f32[32,128]{1,0:T(8,128)}, f32[32,128]{1,0:T(8,128)}, f32[32,128]{1,0:T(8,128)}) custom-call(f32[128,4,256]{2,1,0:T(4,128)} %geo.5, s32[3,16]{1,0:T(4,128)} %maximum_convert_fusion.codes, f32[16,32]{1,0:T(8,128)} %far_up.1.up, f32[128,128]{1,0:T(8,128)} %get-tuple-element.15.masked.rest_0_, f32[128,128]{1,0:T(8,128)} %copy-done, ...), custom_call_target="tpu_custom_call" | custom-call | tf_op jit(solution)/shard_map/near_remote/pallas_call | solution.py:407
  49.9 4.4 %collective-permute-start.4 = (f32[32,128]{1,0:T(8,128)}, f32[32,128]{1,0:T(8,128)S(1)}, u32[]{:S(2)}, u32[]{:S(2)}) collective-permute-start(f32[32,128]{1,0:T(8,128)} %get-tuple-element.20), channel_id=1, source_target_pairs={{0,12},{4,0},{8,4},{12,8},{1,13},{5,1},{9,5},{13,9},{2,14},{6,2},{... | collective-permute-start | bytes 49160 | tf_op jit(solution)/shard_map/ppermute | solution.py:356
  54.3 0.7 collective-permute-start.5
  55.0 0.0 collective-permute-start.6
  55.0 0.0 copy-done.10
  55.0 0.7 copy.13.far_list
  55.7 0.3 collective-permute-done.4.rest_2_
  56.0 0.0 copy-start.7
  56.0 3.2 %collective-permute-done.5.rest_3_ = f32[32,128]{1,0:T(8,128)S(1)} collective-permute-done((f32[32,128]{1,0:T(8,128)}, f32[32,128]{1,0:T(8,128)S(1)}, u32[]{:S(2)}, u32[]{:S(2)}) %collective-permute-start.5) | collective-permute-done | bytes 16416 | tf_op jit(solution)/shard_map/ppermute | solution.py:356
  59.2 0.0 copy-start.8
  59.2 1.6 collective-permute-done.6.rest_4_
  60.8 0.0 copy-start.9
  60.8 0.0 copy-done.7
  60.8 0.0 copy-done.8
  60.8 0.6 copy-done.9
  61.4 149.3 %near_local.1 = (f32[160,128]{1,0:T(8,128)}, f32[160,128]{1,0:T(8,128)}) custom-call(f32[128,4,256]{2,1,0:T(4,128)} %geo.5, s32[2,128]{1,0:T(2,128)} %bitcast.19, s32[4,16]{1,0:T(4,128)} %bitcast.14, s32[16,8]{1,0:T(8,128)} %copy.13.far_list, f32[16,8,32,32]{3,2,1,0:T(8,128)} %coupling.1, f32[32,32,128]{2,1,0:T(8,128)} %bitcast.12, s32[1,128]{1,0:T(1,128)} %bitcast.18, ...), custom_call_target="tpu_custom_call" | custom-call | tf_op jit(solution)/shard_map/near_local/pallas_call | solution.py:425
  210.7 0.0 collective-permute-start.7
  210.7 0.9 collective-permute-start.9
  211.6 1.2 collective-permute-start.8
  212.8 0.0 collective-permute-done.7.rest_1_
  212.8 0.0 copy-start.1
  212.8 2.3 %collective-permute-done.9.rest_3_ = f32[160,128]{1,0:T(8,128)S(1)} collective-permute-done((f32[160,128]{1,0:T(8,128)}, f32[160,128]{1,0:T(8,128)S(1)}, u32[]{:S(2)}, u32[]{:S(2)}) %collective-permute-start.9) | collective-permute-done | bytes 81952 | tf_op jit(solution)/shard_map/ppermute | solution.py:356
  215.1 2.3 %collective-permute-done.8.rest_2_ = f32[160,128]{1,0:T(8,128)S(1)} collective-permute-done((f32[160,128]{1,0:T(8,128)}, f32[160,128]{1,0:T(8,128)S(1)}, u32[]{:S(2)}, u32[]{:S(2)}) %collective-permute-start.8) | collective-permute-done | bytes 81952 | tf_op jit(solution)/shard_map/ppermute | solution.py:356
  217.4 0.0 copy-done.1
  217.4 0.0 copy-done.2
  217.4 0.0 copy-start.3
  217.4 0.6 copy-done.3
  218.1 3.1 %combine.1 = f32[128,128]{1,0:T(8,128)} custom-call(s32[128,128]{1,0:T(8,128)} %mask.3, f32[128,32,128]{2,1,0:T(8,128)} %bitcast.10, f32[160,128]{1,0:T(8,128)} %get-tuple-element.23.rest_0_, f32[160,128]{1,0:T(8,128)} %copy-done.1, f32[160,128]{1,0:T(8,128)} %copy-done.3, f32[160,128]{1,0:T(8,128)} %copy-done.2), custom_call_target="tpu_custom_call" | custom-call | tf_op jit(solution)/shard_map/combine/pallas_call | solution.py:447
  (4 shorter events, 0.0 us)
Async XLA Ops:
  0.0 55.0 %copy-start.10 = (s32[16,8]{0,1:T(8,128)S(1)}, s32[16,8]{0,1:T(8,128)}, u32[]{:S(2)}) copy-start(s32[16,8]{0,1:T(8,128)} %param.22) | copy-start | bytes 1540
  2.0 11.5 %collective-permute-start = (f32[88,128]{1,0:T(8,128)}, f32[88,128]{1,0:T(8,128)S(1)}, u32[]{:S(2)}, u32[]{:S(2)}) collective-permute-start(f32[88,128]{1,0:T(8,128)} %get-tuple-element.16), channel_id=1, source_target_pairs={{0,4},{4,8},{8,12},{12,0},{1,5},{5,9},{9,13},{13,1},{2,6},{6,10},{... | collective-permute-start | bytes 135176 | tf_op jit(solution)/shard_map/ppermute | solution.py:356
  5.0 8.5 %collective-permute-start.1 = (f32[88,128]{1,0:T(8,128)}, f32[88,128]{1,0:T(8,128)S(1)}, u32[]{:S(2)}, u32[]{:S(2)}) collective-permute-start(f32[88,128]{1,0:T(8,128)} %get-tuple-element.17), channel_id=1, source_target_pairs={{0,8},{4,12},{8,0},{12,4},{1,9},{5,13},{9,1},{13,5},{2,10},{6,14},... | collective-permute-start | bytes 135176 | tf_op jit(solution)/shard_map/ppermute | solution.py:356
  7.6 6.0 %collective-permute-start.2 = (f32[88,128]{1,0:T(8,128)}, f32[88,128]{1,0:T(8,128)S(1)}, u32[]{:S(2)}, u32[]{:S(2)}) collective-permute-start(f32[88,128]{1,0:T(8,128)} %get-tuple-element.18), channel_id=1, source_target_pairs={{0,12},{4,0},{8,4},{12,8},{1,13},{5,1},{9,5},{13,9},{2,14},{6,2},{... | collective-permute-start | bytes 135176 | tf_op jit(solution)/shard_map/ppermute | solution.py:356
  9.0 5.3 %collective-permute-start.3 = (f32[128,128]{1,0:T(8,128)}, f32[128,128]{1,0:T(8,128)S(1)}, u32[]{:S(2)}, u32[]{:S(2)}) collective-permute-start(f32[128,128]{1,0:T(8,128)} %get-tuple-element.15.masked.rest_0_), channel_id=1, source_target_pairs={{0,2},{2,0},{1,3},{3,1},{4,6},{6,4},{5,7},{7,5},{8,10},{10,8},{9,1... | collective-permute-start | bytes 196616 | tf_op jit(solution)/shard_map/ppermute | solution.py:356
  13.6 0.7 copy-start.4
  13.6 0.7 copy-start.5
  13.6 0.6 copy-start.6
  14.3 0.6 copy-start
  49.9 6.1 %collective-permute-start.4 = (f32[32,128]{1,0:T(8,128)}, f32[32,128]{1,0:T(8,128)S(1)}, u32[]{:S(2)}, u32[]{:S(2)}) collective-permute-start(f32[32,128]{1,0:T(8,128)} %get-tuple-element.20), channel_id=1, source_target_pairs={{0,12},{4,0},{8,4},{12,8},{1,13},{5,1},{9,5},{13,9},{2,14},{6,2},{... | collective-permute-start | bytes 49160 | tf_op jit(solution)/shard_map/ppermute | solution.py:356
  54.3 4.8 %collective-permute-start.5 = (f32[32,128]{1,0:T(8,128)}, f32[32,128]{1,0:T(8,128)S(1)}, u32[]{:S(2)}, u32[]{:S(2)}) collective-permute-start(f32[32,128]{1,0:T(8,128)} %get-tuple-element.21), channel_id=1, source_target_pairs={{0,8},{4,12},{8,0},{12,4},{1,9},{5,13},{9,1},{13,5},{2,10},{6,14},... | collective-permute-start | bytes 49160 | tf_op jit(solution)/shard_map/ppermute | solution.py:356
  55.0 5.7 %collective-permute-start.6 = (f32[32,128]{1,0:T(8,128)}, f32[32,128]{1,0:T(8,128)S(1)}, u32[]{:S(2)}, u32[]{:S(2)}) collective-permute-start(f32[32,128]{1,0:T(8,128)} %get-tuple-element.22), channel_id=1, source_target_pairs={{0,4},{4,8},{8,12},{12,0},{1,5},{5,9},{9,13},{13,1},{2,6},{6,10},{... | collective-permute-start | bytes 49160 | tf_op jit(solution)/shard_map/ppermute | solution.py:356
  56.0 4.8 %copy-start.7 = (f32[32,128]{1,0:T(8,128)}, f32[32,128]{1,0:T(8,128)S(1)}, u32[]{:S(2)}) copy-start(f32[32,128]{1,0:T(8,128)S(1)} %collective-permute-done.4.rest_2_) | copy-start | bytes 49156
  59.2 1.6 copy-start.8
  60.8 0.6 copy-start.9
  210.7 2.1 collective-permute-start.7
  210.7 4.4 %collective-permute-start.9 = (f32[160,128]{1,0:T(8,128)}, f32[160,128]{1,0:T(8,128)S(1)}, u32[]{:S(2)}, u32[]{:S(2)}) collective-permute-start(f32[160,128]{1,0:T(8,128)} %get-tuple-element.24), channel_id=1, source_target_pairs={{0,3},{1,2},{2,1},{3,0},{4,7},{5,6},{6,5},{7,4},{8,11},{9,10},{10,... | collective-permute-start | bytes 245768 | tf_op jit(solution)/shard_map/ppermute | solution.py:356
  211.6 5.9 %collective-permute-start.8 = (f32[160,128]{1,0:T(8,128)}, f32[160,128]{1,0:T(8,128)S(1)}, u32[]{:S(2)}, u32[]{:S(2)}) collective-permute-start(f32[160,128]{1,0:T(8,128)} %get-tuple-element.24), channel_id=1, source_target_pairs={{0,2},{1,3},{2,0},{3,1},{4,6},{5,7},{6,4},{7,5},{8,10},{9,11},{10,... | collective-permute-start | bytes 245768 | tf_op jit(solution)/shard_map/ppermute | solution.py:356
  212.8 4.6 %copy-start.1 = (f32[160,128]{1,0:T(8,128)}, f32[160,128]{1,0:T(8,128)S(1)}, u32[]{:S(2)}) copy-start(f32[160,128]{1,0:T(8,128)S(1)} %collective-permute-done.7.rest_1_) | copy-start | bytes 245764
  215.1 2.3 %copy-start.2 = (f32[160,128]{1,0:T(8,128)}, f32[160,128]{1,0:T(8,128)S(1)}, u32[]{:S(2)}) copy-start(f32[160,128]{1,0:T(8,128)S(1)} %collective-permute-done.9.rest_3_) | copy-start | bytes 245764
  217.4 0.6 copy-start.3

commit v10 on v8

--- a/solution.py
+++ b/solution.py
@@ -98,15 +98,11 @@
 
 
 def contract(left, right):
-    return lax.dot_general(left, right, (((0,), (0,)), ((), ())), preferred_element_type=F32)
-
-
-def column(table, index):
-    if table.shape[1] == LANES and table.shape[0] % 8 == 0:
-        return jnp.take_along_axis(table, jnp.full(table.shape, index, jnp.int32), axis=1)
-    lane = lax.broadcasted_iota(jnp.int32, table.shape, 1)
-    picked = jnp.sum(jnp.where(lane == index, table, 0.0), axis=1, keepdims=True)
-    return jnp.broadcast_to(picked, (table.shape[0], LANES))
+    return jnp.dot(left, right, preferred_element_type=F32)
+
+
+def upright(row):
+    return jnp.broadcast_to(row, (8, row.shape[1])).T[:, :1]
 
 
 def put_column(table, rows, index, value):
@@ -125,8 +121,7 @@
 
 def distances(left, right, out):
     whole_left = jnp.concatenate(left, axis=1) if len(left) > 1 else left[0]
-    for t, r in enumerate(right):
-        out[:, t * LANES : (t + 1) * LANES] = contract(whole_left, r)
+    out[...] = contract(whole_left.T, jnp.concatenate(right, axis=1))
 
 
 def staged(spans, *stages):
@@ -140,26 +135,26 @@
                     del held[k]
 
 
-def spans_of(height, step=16):
+def spans_of(height, step=32):
     step = min(step, height)
     return [slice(r, r + step) for r in range(0, height, step)]
 
 
-def tile_sums(dist, qrow, qtable, slot, table, index):
+def tile_sums(dist, qrow, qleft, table, index):
     q0, q1 = qrow[:, :LANES], qrow[:, LANES:]
+    qcol = upright(qleft)
     back = [jnp.zeros((8, LANES), F32), jnp.zeros((8, LANES), F32)]
 
     def root(rows, _):
         return (
             inverse_root(dist[rows, :LANES]),
             inverse_root(dist[rows, LANES:]),
-            column(qtable[rows, :], slot),
         )
 
     def sums(rows, held):
-        g0, g1, qcol = held
-        back[0] = back[0] + fold(g0 * qcol)
-        back[1] = back[1] + fold(g1 * qcol)
+        g0, g1 = held
+        back[0] = back[0] + fold(g0 * qcol[rows, :])
+        back[1] = back[1] + fold(g1 * qcol[rows, :])
         return jnp.sum(g0 * q0 + g1 * q1, axis=1, keepdims=True)
 
     def store(rows, held):
@@ -232,7 +227,7 @@
     packs = rest[S : S + C - 1]
     acc_out = rest[S + C - 1]
     sends = rest[S + C : S + C + C - 1]
-    q, tqt, acc, fwdt, sgeo, fa0, fb0, fb1, order, *ring = rest[S + C + C - 1 :]
+    q, tq, acc, fwdt, sgeo, fa0, fb0, fb1, order, *ring = rest[S + C + C - 1 :]
     fa, fb = (fa0,), (fb0, fb1)
     n = (C - 1) * slots
     assemble(lax.axis_index("sub"), S, L, q, pieces)
@@ -257,11 +252,7 @@
     _, right, _ = split_features(spoints, centre, inv)
     store_features(fa, left)
     store_features(fb, right)
-    wide = tqt.shape[1]
-    tq = tpoints[4]
-    if wide > n:
-        tq = jnp.concatenate([tq, jnp.zeros((wide - n, L), F32)], axis=0)
-    tqt[...] = tq.T
+    tq[...] = tpoints[4]
 
     def begin(i, dist):
         slot = order[jnp.minimum(i, jnp.maximum(found - 1, 0))]
@@ -272,7 +263,7 @@
         slot = order[jnp.minimum(i, jnp.maximum(found - 1, 0))]
         source = jnp.maximum(codes[slot // slots, lax.rem(slot, slots)], 0)
         back = tile_sums(
-            dist, q[pl.ds(source, 1), :], tqt, slot, fwdt, jnp.where(ok, slot, -1)
+            dist, q[pl.ds(source, 1), :], tq[pl.ds(slot, 1), :], fwdt, jnp.where(ok, slot, -1)
         )
         acc[pl.ds(source, 1), :] += jnp.where(ok, back, 0.0)
 
@@ -293,11 +284,10 @@
     pieces = rest[:S]
     sums = rest[S : S + C - 1]
     parts = rest[S + C - 1 : 2 * S + C - 1]
-    q, qt, acc, acct, fa0, fa1, fb0, fb1, rads, got, parents, rows, *ring = rest[2 * S + C - 1 :]
+    q, acc, acct, fa0, fa1, fb0, fb1, rads, got, parents, rows, *ring = rest[2 * S + C - 1 :]
     fa, fb = (fa0, fa1), (fb0, fb1)
     me, sub, rep = lax.axis_index("clu"), lax.axis_index("sub"), lax.axis_index("rep")
     assemble(sub, S, L, q, pieces)
-    qt[...] = q[...].T
     acc[...] = jnp.zeros_like(acc)
     acct[...] = jnp.zeros_like(acct)
     points = [geo[:, k, :] for k in range(4)]
@@ -315,13 +305,13 @@
         c = first + jnp.minimum(i, share - 1)
         a = load_features(fa, c)
         b = load_features(fb, c)
-        dist[:half, :half] = contract(a[0], b[0])
-        dist[:half, half:] = contract(a[0], b[1])
-        dist[half:, half:] = contract(a[1], b[1])
+        dist[:half, :] = contract(a[0].T, jnp.concatenate(b, axis=1))
+        dist[half:, half:] = contract(a[1].T, b[1])
 
     def finish_self(i, dist):
         c = first + i
         qrow = q[pl.ds(c, 1), :]
+        qcol = upright(qrow[:, :half])
         radius = rads[pl.ds(c, 1), :]
         diag = lax.rsqrt(2.0 * (radius * radius))
         back = [jnp.zeros((8, LANES), F32)]
@@ -336,14 +326,13 @@
                 return (
                     jnp.where(eye(span), diag[:, :half], inverse_root(dist[span, :half])),
                     inverse_root(dist[span, half:]),
-                    column(qt[span, :], c),
                 )
             return (jnp.where(eye(span), diag[:, half:], inverse_root(dist[span, half:])),)
 
         def sums(span, held):
             if span.start < half:
-                g0, g1, qcol = held
-                back[0] = back[0] + fold(g1 * qcol)
+                g0, g1 = held
+                back[0] = back[0] + fold(g1 * qcol[span, :])
                 part = g0 * qrow[:, :half] + g1 * qrow[:, half:]
             else:
                 part = held[0] * qrow[:, half:]
@@ -367,7 +356,9 @@
 
     def finish(i, dist):
         ia, ib = pairs[0, start + i], pairs[1, start + i]
-        acc[pl.ds(ib, 1), :] += tile_sums(dist, q[pl.ds(ib, 1), :], qt, ia, acct, share + i)
+        acc[pl.ds(ib, 1), :] += tile_sums(
+            dist, q[pl.ds(ib, 1), :], q[pl.ds(ia, 1), :], acct, share + i
+        )
 
     pipeline(count, begin, finish, ring[: ring_size(count)])
     rows[...] = acct[...].T
@@ -530,7 +521,7 @@
         out_specs=[vmem()] * C,
         scratch_shapes=[
             pltpu.VMEM((clusters, panels), F32),
-            pltpu.VMEM((L, whole(n)), F32),
+            pltpu.VMEM((n, L), F32),
             pltpu.VMEM((clusters, panels), F32),
             pltpu.VMEM((L, whole(n)), F32),
             pltpu.VMEM((4 * n, panels), F32),
@@ -554,7 +545,6 @@
         out_specs=[vmem()] * S,
         scratch_shapes=[
             pltpu.VMEM((clusters, panels), F32),
-            pltpu.VMEM((panels, clusters), F32),
             pltpu.VMEM((clusters, panels), F32),
             pltpu.VMEM((panels, columns), F32),
             *half,

time: 72.5 us -> 65.7 us (0.906)
  Pallas kernels: 46.6 us -> 40.2 us
    pallas_call x1, Pallas kernels: 28.4 us -> 23.3 us  [on_device(): pl.pallas_call(functools.partial(local_kernel, (C, S, L, R, slots, cluste...]
    pallas_call x1, Pallas kernels: 10 us -> 8.69 us  [on_device(): pl.pallas_call(functools.partial(remote_kernel, (C, S, L, slots, clusters...]
  transfers between devices with their start and end apart: 10 -> 10, of which waited for: 5 -> 5; matrix products, arithmetic and copies ran while one was open for 2% -> 2% of each run, Pallas kernels for 4% -> 5%
where the time goes in v10:
time: 65.7 us; the launch traced here: 65.9 us
  Pallas kernels  40.2 us (61%)
  starting transfers between devices  13 us (20%)
  waiting for transfers between devices  9.49 us (14%)
  local copies, waits for them, and re-layouts  2.55 us (4%)
    pallas_call x1, Pallas kernels, on_device(): pl.pallas_call(functools.partial(local_kernel, (C, S, L, R, slots, cluste...  23.3 us
    ppermute x10, starting transfers between devices, send(): return lax.ppermute(value, names if len(names) > 1 else names[0], perm)  13 us
    ppermute x10, waiting for transfers between devices, send(): return lax.ppermute(value, names if len(names) > 1 else names[0], perm)  9.49 us
    pallas_call x1, Pallas kernels, on_device(): pl.pallas_call(functools.partial(remote_kernel, (C, S, L, slots, clusters...  8.69 us
    pallas_call x1, Pallas kernels, on_device(): pl.pallas_call(functools.partial(final_kernel, (S, R, L)), out_shape=shap...  3.1 us
    pallas_call x1, Pallas kernels, on_device(): pl.pallas_call(up_kernel, out_shape=shape((par_dev, rank), F32), in_specs...  3.07 us
    unnamed x23, local copies, waits for them, and re-layouts  2.54 us
    pallas_call x1, Pallas kernels, on_device(): pl.pallas_call(functools.partial(pack_kernel, (C, S, L, slots)), out_shap...  2.02 us
  transfers between devices with their start and end apart: 10, of which 5 were waited for; matrix products, arithmetic and copies ran while one was open for 2% of the time, Pallas kernels for 5%

profile of v10, /device:TPU:0, one launch (start us, length us, event | category | flops | bytes accessed | tf_op | source)
XLA Modules:
  0.0 65.9 jit_solution(17654798001085368233)
XLA Ops:
  0.0 0.0 copy-start.10
  0.0 2.0 %packs.1 = (f32[128,128]{1,0:T(8,128)}, f32[88,128]{1,0:T(8,128)}, f32[88,128]{1,0:T(8,128)}, f32[88,128]{1,0:T(8,128)}) custom-call(f32[128,128]{1,0:T(8,128)} %charges.1, s32[128,128]{1,0:T(8,128)} %mask.3, f32[128,4,256]{2,1,0:T(4,128)} %geo.5, s32[4,16]{1,0:T(4,128)} %bitcast.13, s32[4,16]{1,0:T(4,128)} %bitcast.15, s32[4,16]{1,0:T(4,128)} %bitcast.16), custom_call_target="tpu_custom_call" | custom-call | tf_op jit(solution)/shard_map/packs/pallas_call | solution.py:495
  2.0 3.0 %collective-permute-start = (f32[88,128]{1,0:T(8,128)}, f32[88,128]{1,0:T(8,128)S(1)}, u32[]{:S(2)}, u32[]{:S(2)}) collective-permute-start(f32[88,128]{1,0:T(8,128)} %get-tuple-element.16), channel_id=1, source_target_pairs={{0,4},{4,8},{8,12},{12,0},{1,5},{5,9},{9,13},{13,1},{2,6},{6,10},{... | collective-permute-start | bytes 135176 | tf_op jit(solution)/shard_map/ppermute | solution.py:466
  5.0 2.6 %collective-permute-start.1 = (f32[88,128]{1,0:T(8,128)}, f32[88,128]{1,0:T(8,128)S(1)}, u32[]{:S(2)}, u32[]{:S(2)}) collective-permute-start(f32[88,128]{1,0:T(8,128)} %get-tuple-element.17), channel_id=1, source_target_pairs={{0,8},{4,12},{8,0},{12,4},{1,9},{5,13},{9,1},{13,5},{2,10},{6,14},... | collective-permute-start | bytes 135176 | tf_op jit(solution)/shard_map/ppermute | solution.py:466
  7.6 1.3 %collective-permute-start.2 = (f32[88,128]{1,0:T(8,128)}, f32[88,128]{1,0:T(8,128)S(1)}, u32[]{:S(2)}, u32[]{:S(2)}) collective-permute-start(f32[88,128]{1,0:T(8,128)} %get-tuple-element.18), channel_id=1, source_target_pairs={{0,12},{4,0},{8,4},{12,8},{1,13},{5,1},{9,5},{13,9},{2,14},{6,2},{... | collective-permute-start | bytes 135176 | tf_op jit(solution)/shard_map/ppermute | solution.py:466
  9.0 1.5 %collective-permute-start.3 = (f32[128,128]{1,0:T(8,128)}, f32[128,128]{1,0:T(8,128)S(1)}, u32[]{:S(2)}, u32[]{:S(2)}) collective-permute-start(f32[128,128]{1,0:T(8,128)} %get-tuple-element.15.masked.rest_0_), channel_id=1, source_target_pairs={{0,2},{2,0},{1,3},{3,1},{4,6},{6,4},{5,7},{7,5},{8,10},{10,8},{9,1... | collective-permute-start | bytes 196616 | tf_op jit(solution)/shard_map/ppermute | solution.py:466
  10.5 3.1 %far_up.1.up = f32[16,32]{1,0:T(8,128)} custom-call(f32[128,32,128]{2,1,0:T(8,128)} %bitcast.9, f32[128,128]{1,0:T(8,128)} %get-tuple-element.15.masked.rest_0_, f32[32,32,128]{2,1,0:T(8,128)} %bitcast.11, s32[1,128]{1,0:T(1,128)} %bitcast.17), custom_call_target="tpu_custom_call" | custom-call | tf_op jit(solution)/shard_map/far_up/pallas_call | solution.py:508
  13.6 0.0 collective-permute-done.rest_2_
  13.6 0.0 copy-start.4
  13.6 0.0 collective-permute-done.1.rest_3_
  13.6 0.0 copy-start.5
  13.6 0.0 collective-permute-done.2.rest_4_
  13.6 0.0 copy-start.6
  13.6 0.6 maximum_convert_fusion.codes
  14.2 0.0 collective-permute-done.3.rest_1_
  14.2 0.0 copy-done.4
  14.2 0.0 copy-done.5
  14.2 0.0 copy-done.6
  14.3 0.0 copy-start
  14.3 0.6 copy-done
  14.9 8.7 %near_remote.1 = (f32[128,256]{1,0:T(8,128)}, f32[32,128]{1,0:T(8,128)}, f32[32,128]{1,0:T(8,128)}, f32[32,128]{1,0:T(8,128)}) custom-call(f32[128,4,256]{2,1,0:T(4,128)} %geo.5, s32[3,16]{1,0:T(4,128)} %maximum_convert_fusion.codes, f32[16,32]{1,0:T(8,128)} %far_up.1.up, f32[128,128]{1,0:T(8,128)} %get-tuple-element.15.masked.rest_0_, f32[128,128]{1,0:T(8,128)} %copy-done, ...), custom_call_target="tpu_custom_call" | custom-call | tf_op jit(solution)/shard_map/near_remote/pallas_call | solution.py:517
  23.6 1.4 %collective-permute-start.4 = (f32[32,128]{1,0:T(8,128)}, f32[32,128]{1,0:T(8,128)S(1)}, u32[]{:S(2)}, u32[]{:S(2)}) collective-permute-start(f32[32,128]{1,0:T(8,128)} %get-tuple-element.20), channel_id=1, source_target_pairs={{0,12},{4,0},{8,4},{12,8},{1,13},{5,1},{9,5},{13,9},{2,14},{6,2},{... | collective-permute-start | bytes 49160 | tf_op jit(solution)/shard_map/ppermute | solution.py:466
  25.0 0.7 %collective-permute-start.5 = (f32[32,128]{1,0:T(8,128)}, f32[32,128]{1,0:T(8,128)S(1)}, u32[]{:S(2)}, u32[]{:S(2)}) collective-permute-start(f32[32,128]{1,0:T(8,128)} %get-tuple-element.21), channel_id=1, source_target_pairs={{0,8},{4,12},{8,0},{12,4},{1,9},{5,13},{9,1},{13,5},{2,10},{6,14},... | collective-permute-start | bytes 49160 | tf_op jit(solution)/shard_map/ppermute | solution.py:466
  25.7 0.2 collective-permute-start.6
  25.9 0.0 copy-done.10
  25.9 0.7 %copy.13.far_list = s32[16,8]{1,0:T(8,128)} copy(s32[16,8]{0,1:T(8,128)S(1)} %copy-done.10) | data formatting | bytes 1024 | tf_op args[10]
  26.6 0.9 %collective-permute-done.4.rest_2_ = f32[32,128]{1,0:T(8,128)S(1)} collective-permute-done((f32[32,128]{1,0:T(8,128)}, f32[32,128]{1,0:T(8,128)S(1)}, u32[]{:S(2)}, u32[]{:S(2)}) %collective-permute-start.4) | collective-permute-done | bytes 16416 | tf_op jit(solution)/shard_map/ppermute | solution.py:466
  27.5 0.0 copy-start.7
  27.5 2.5 %collective-permute-done.5.rest_3_ = f32[32,128]{1,0:T(8,128)S(1)} collective-permute-done((f32[32,128]{1,0:T(8,128)}, f32[32,128]{1,0:T(8,128)S(1)}, u32[]{:S(2)}, u32[]{:S(2)}) %collective-permute-start.5) | collective-permute-done | bytes 16416 | tf_op jit(solution)/shard_map/ppermute | solution.py:466
  30.0 0.0 copy-start.8
  30.0 1.4 %collective-permute-done.6.rest_4_ = f32[32,128]{1,0:T(8,128)S(1)} collective-permute-done((f32[32,128]{1,0:T(8,128)}, f32[32,128]{1,0:T(8,128)S(1)}, u32[]{:S(2)}, u32[]{:S(2)}) %collective-permute-start.6) | collective-permute-done | bytes 16416 | tf_op jit(solution)/shard_map/ppermute | solution.py:466
  31.5 0.0 copy-start.9
  31.5 0.0 copy-done.7
  31.5 0.0 copy-done.8
  31.5 0.6 copy-done.9
  32.1 23.3 %near_local.1 = (f32[160,128]{1,0:T(8,128)}, f32[160,128]{1,0:T(8,128)}) custom-call(f32[128,4,256]{2,1,0:T(4,128)} %geo.5, s32[2,128]{1,0:T(2,128)} %bitcast.19, s32[4,16]{1,0:T(4,128)} %bitcast.14, s32[16,8]{1,0:T(8,128)} %copy.13.far_list, f32[16,8,32,32]{3,2,1,0:T(8,128)} %coupling.1, f32[32,32,128]{2,1,0:T(8,128)} %bitcast.12, s32[1,128]{1,0:T(1,128)} %bitcast.18, ...), custom_call_target="tpu_custom_call" | custom-call | tf_op jit(solution)/shard_map/near_local/pallas_call | solution.py:541
  55.4 0.0 collective-permute-start.7
  55.4 0.9 %collective-permute-start.9 = (f32[160,128]{1,0:T(8,128)}, f32[160,128]{1,0:T(8,128)S(1)}, u32[]{:S(2)}, u32[]{:S(2)}) collective-permute-start(f32[160,128]{1,0:T(8,128)} %get-tuple-element.24), channel_id=1, source_target_pairs={{0,3},{1,2},{2,1},{3,0},{4,7},{5,6},{6,5},{7,4},{8,11},{9,10},{10,... | collective-permute-start | bytes 245768 | tf_op jit(solution)/shard_map/ppermute | solution.py:466
  56.3 1.2 %collective-permute-start.8 = (f32[160,128]{1,0:T(8,128)}, f32[160,128]{1,0:T(8,128)S(1)}, u32[]{:S(2)}, u32[]{:S(2)}) collective-permute-start(f32[160,128]{1,0:T(8,128)} %get-tuple-element.24), channel_id=1, source_target_pairs={{0,2},{1,3},{2,0},{3,1},{4,6},{5,7},{6,4},{7,5},{8,10},{9,11},{10,... | collective-permute-start | bytes 245768 | tf_op jit(solution)/shard_map/ppermute | solution.py:466
  57.5 0.0 collective-permute-done.7.rest_1_
  57.5 0.0 copy-start.1
  57.5 2.3 %collective-permute-done.9.rest_3_ = f32[160,128]{1,0:T(8,128)S(1)} collective-permute-done((f32[160,128]{1,0:T(8,128)}, f32[160,128]{1,0:T(8,128)S(1)}, u32[]{:S(2)}, u32[]{:S(2)}) %collective-permute-start.9) | collective-permute-done | bytes 81952 | tf_op jit(solution)/shard_map/ppermute | solution.py:466
  59.8 0.0 copy-start.2
  59.8 2.3 %collective-permute-done.8.rest_2_ = f32[160,128]{1,0:T(8,128)S(1)} collective-permute-done((f32[160,128]{1,0:T(8,128)}, f32[160,128]{1,0:T(8,128)S(1)}, u32[]{:S(2)}, u32[]{:S(2)}) %collective-permute-start.8) | collective-permute-done | bytes 81952 | tf_op jit(solution)/shard_map/ppermute | solution.py:466
  62.1 0.0 copy-done.1
  62.1 0.0 copy-done.2
  62.1 0.6 copy-done.3
  62.8 3.1 %combine.1 = f32[128,128]{1,0:T(8,128)} custom-call(s32[128,128]{1,0:T(8,128)} %mask.3, f32[128,32,128]{2,1,0:T(8,128)} %bitcast.10, f32[160,128]{1,0:T(8,128)} %get-tuple-element.23.rest_0_, f32[160,128]{1,0:T(8,128)} %copy-done.1, f32[160,128]{1,0:T(8,128)} %copy-done.3, f32[160,128]{1,0:T(8,128)} %copy-done.2), custom_call_target="tpu_custom_call" | custom-call | tf_op jit(solution)/shard_map/combine/pallas_call | solution.py:566
  (4 shorter events, 0.0 us)
Async XLA Ops:
  0.0 25.9 %copy-start.10 = (s32[16,8]{0,1:T(8,128)S(1)}, s32[16,8]{0,1:T(8,128)}, u32[]{:S(2)}) copy-start(s32[16,8]{0,1:T(8,128)} %param.22) | copy-start | bytes 1540
  2.0 11.5 %collective-permute-start = (f32[88,128]{1,0:T(8,128)}, f32[88,128]{1,0:T(8,128)S(1)}, u32[]{:S(2)}, u32[]{:S(2)}) collective-permute-start(f32[88,128]{1,0:T(8,128)} %get-tuple-element.16), channel_id=1, source_target_pairs={{0,4},{4,8},{8,12},{12,0},{1,5},{5,9},{9,13},{13,1},{2,6},{6,10},{... | collective-permute-start | bytes 135176 | tf_op jit(solution)/shard_map/ppermute | solution.py:466
  5.0 8.5 %collective-permute-start.1 = (f32[88,128]{1,0:T(8,128)}, f32[88,128]{1,0:T(8,128)S(1)}, u32[]{:S(2)}, u32[]{:S(2)}) collective-permute-start(f32[88,128]{1,0:T(8,128)} %get-tuple-element.17), channel_id=1, source_target_pairs={{0,8},{4,12},{8,0},{12,4},{1,9},{5,13},{9,1},{13,5},{2,10},{6,14},... | collective-permute-start | bytes 135176 | tf_op jit(solution)/shard_map/ppermute | solution.py:466
  7.6 6.0 %collective-permute-start.2 = (f32[88,128]{1,0:T(8,128)}, f32[88,128]{1,0:T(8,128)S(1)}, u32[]{:S(2)}, u32[]{:S(2)}) collective-permute-start(f32[88,128]{1,0:T(8,128)} %get-tuple-element.18), channel_id=1, source_target_pairs={{0,12},{4,0},{8,4},{12,8},{1,13},{5,1},{9,5},{13,9},{2,14},{6,2},{... | collective-permute-start | bytes 135176 | tf_op jit(solution)/shard_map/ppermute | solution.py:466
  9.0 5.3 %collective-permute-start.3 = (f32[128,128]{1,0:T(8,128)}, f32[128,128]{1,0:T(8,128)S(1)}, u32[]{:S(2)}, u32[]{:S(2)}) collective-permute-start(f32[128,128]{1,0:T(8,128)} %get-tuple-element.15.masked.rest_0_), channel_id=1, source_target_pairs={{0,2},{2,0},{1,3},{3,1},{4,6},{6,4},{5,7},{7,5},{8,10},{10,8},{9,1... | collective-permute-start | bytes 196616 | tf_op jit(solution)/shard_map/ppermute | solution.py:466
  13.6 0.7 %copy-start.4 = (f32[88,128]{1,0:T(8,128)}, f32[88,128]{1,0:T(8,128)S(1)}, u32[]{:S(2)}) copy-start(f32[88,128]{1,0:T(8,128)S(1)} %collective-permute-done.rest_2_) | copy-start | bytes 135172
  13.6 0.7 %copy-start.5 = (f32[88,128]{1,0:T(8,128)}, f32[88,128]{1,0:T(8,128)S(1)}, u32[]{:S(2)}) copy-start(f32[88,128]{1,0:T(8,128)S(1)} %collective-permute-done.1.rest_3_) | copy-start | bytes 135172
  13.6 0.6 copy-start.6
  14.3 0.6 copy-start
  23.6 4.0 %collective-permute-start.4 = (f32[32,128]{1,0:T(8,128)}, f32[32,128]{1,0:T(8,128)S(1)}, u32[]{:S(2)}, u32[]{:S(2)}) collective-permute-start(f32[32,128]{1,0:T(8,128)} %get-tuple-element.20), channel_id=1, source_target_pairs={{0,12},{4,0},{8,4},{12,8},{1,13},{5,1},{9,5},{13,9},{2,14},{6,2},{... | collective-permute-start | bytes 49160 | tf_op jit(solution)/shard_map/ppermute | solution.py:466
  25.0 5.0 %collective-permute-start.5 = (f32[32,128]{1,0:T(8,128)}, f32[32,128]{1,0:T(8,128)S(1)}, u32[]{:S(2)}, u32[]{:S(2)}) collective-permute-start(f32[32,128]{1,0:T(8,128)} %get-tuple-element.21), channel_id=1, source_target_pairs={{0,8},{4,12},{8,0},{12,4},{1,9},{5,13},{9,1},{13,5},{2,10},{6,14},... | collective-permute-start | bytes 49160 | tf_op jit(solution)/shard_map/ppermute | solution.py:466
  25.7 5.7 %collective-permute-start.6 = (f32[32,128]{1,0:T(8,128)}, f32[32,128]{1,0:T(8,128)S(1)}, u32[]{:S(2)}, u32[]{:S(2)}) collective-permute-start(f32[32,128]{1,0:T(8,128)} %get-tuple-element.22), channel_id=1, source_target_pairs={{0,4},{4,8},{8,12},{12,0},{1,5},{5,9},{9,13},{13,1},{2,6},{6,10},{... | collective-permute-start | bytes 49160 | tf_op jit(solution)/shard_map/ppermute | solution.py:466
  27.5 3.9 %copy-start.7 = (f32[32,128]{1,0:T(8,128)}, f32[32,128]{1,0:T(8,128)S(1)}, u32[]{:S(2)}) copy-start(f32[32,128]{1,0:T(8,128)S(1)} %collective-permute-done.4.rest_2_) | copy-start | bytes 49156
  30.0 1.4 %copy-start.8 = (f32[32,128]{1,0:T(8,128)}, f32[32,128]{1,0:T(8,128)S(1)}, u32[]{:S(2)}) copy-start(f32[32,128]{1,0:T(8,128)S(1)} %collective-permute-done.5.rest_3_) | copy-start | bytes 49156
  31.5 0.6 copy-start.9
  55.4 2.1 %collective-permute-start.7 = (f32[160,128]{1,0:T(8,128)}, f32[160,128]{1,0:T(8,128)S(1)}, u32[]{:S(2)}, u32[]{:S(2)}) collective-permute-start(f32[160,128]{1,0:T(8,128)} %get-tuple-element.23.rest_0_), channel_id=1, source_target_pairs={{0,1},{1,0},{2,3},{3,2},{4,5},{5,4},{6,7},{7,6},{8,9},{9,8},{10,11... | collective-permute-start | bytes 245768 | tf_op jit(solution)/shard_map/ppermute | solution.py:466
  55.4 4.4 %collective-permute-start.9 = (f32[160,128]{1,0:T(8,128)}, f32[160,128]{1,0:T(8,128)S(1)}, u32[]{:S(2)}, u32[]{:S(2)}) collective-permute-start(f32[160,128]{1,0:T(8,128)} %get-tuple-element.24), channel_id=1, source_target_pairs={{0,3},{1,2},{2,1},{3,0},{4,7},{5,6},{6,5},{7,4},{8,11},{9,10},{10,... | collective-permute-start | bytes 245768 | tf_op jit(solution)/shard_map/ppermute | solution.py:466
  56.3 5.9 %collective-permute-start.8 = (f32[160,128]{1,0:T(8,128)}, f32[160,128]{1,0:T(8,128)S(1)}, u32[]{:S(2)}, u32[]{:S(2)}) collective-permute-start(f32[160,128]{1,0:T(8,128)} %get-tuple-element.24), channel_id=1, source_target_pairs={{0,2},{1,3},{2,0},{3,1},{4,6},{5,7},{6,4},{7,5},{8,10},{9,11},{10,... | collective-permute-start | bytes 245768 | tf_op jit(solution)/shard_map/ppermute | solution.py:466
  57.5 4.6 %copy-start.1 = (f32[160,128]{1,0:T(8,128)}, f32[160,128]{1,0:T(8,128)S(1)}, u32[]{:S(2)}) copy-start(f32[160,128]{1,0:T(8,128)S(1)} %collective-permute-done.7.rest_1_) | copy-start | bytes 245764
  59.8 2.3 %copy-start.2 = (f32[160,128]{1,0:T(8,128)}, f32[160,128]{1,0:T(8,128)S(1)}, u32[]{:S(2)}) copy-start(f32[160,128]{1,0:T(8,128)S(1)} %collective-permute-done.9.rest_3_) | copy-start | bytes 245764
  62.1 0.6 copy-start.3

commit v11 on v10

--- a/solution.py
+++ b/solution.py
@@ -180,7 +180,7 @@
 
 
 def ring_size(total):
-    return next(size for size in (8, 4, 2, 1) if total % size == 0)
+    return next(size for size in (4, 2, 1) if total % size == 0)
 
 
 def assemble(sub, S, L, q, pieces):
@@ -198,24 +198,22 @@
     me, sub = lax.axis_index("clu"), lax.axis_index("sub")
     masked[...] = charges[...] * mask[...].astype(F32)
     lane = lax.broadcasted_iota(jnp.int32, (8, L), 1)
-    for shift in range(1, C):
-        dest = lax.rem(me + shift, C)
-        codes = jnp.full((8, L), -1.0, F32)
-        for j in range(slots):
-            code = jnp.where(live[dest, j] > 0, sources[dest, j], -1)
-            codes = jnp.where(lane == j, code.astype(F32), codes)
-        packs[shift - 1][5 * slots :, :] = codes
 
     def fill(s):
         for shift in range(1, C):
             dest = lax.rem(me + shift, C)
             pack = packs[shift - 1]
-            for j in range(slots):
+
+            def slot(j, codes):
                 t = targets[dest, j]
                 g = geo[t, :, s * L : (s + 1) * L]
                 for k in range(4):
-                    pack[k * slots + j : k * slots + j + 1, :] = g[k : k + 1]
-                pack[4 * slots + j : 4 * slots + j + 1, :] = masked[pl.ds(t, 1), :]
+                    pack[pl.ds(k * slots + j, 1), :] = g[k : k + 1]
+                pack[pl.ds(4 * slots + j, 1), :] = masked[pl.ds(t, 1), :]
+                code = jnp.where(live[dest, j] > 0, sources[dest, j], -1)
+                return jnp.where(lane == j, code.astype(F32), codes)
+
+            pack[5 * slots :, :] = lax.fori_loop(0, slots, slot, jnp.full((8, L), -1.0, F32))
 
     for s in range(S):
         pl.when(sub == s)(functools.partial(fill, s))
@@ -406,14 +404,22 @@
         pl.when(sub == s)(functools.partial(give, s))
 
 
-def up_kernel(basis, masked, transfer, parent, up):
+def up_kernel(basis, masked, transfer, parent, up, groups):
     clusters = basis.shape[0]
     rank = basis.shape[1]
-    lane = lax.broadcasted_iota(jnp.int32, (rank, clusters), 1)
-    leaf = jnp.zeros((rank, clusters), F32)
-    for c in range(clusters):
-        part = jnp.sum(basis[c] * masked[c : c + 1, :], axis=1, keepdims=True)
-        leaf = jnp.where(lane == c, part, leaf)
+    lane = lax.broadcasted_iota(jnp.int32, (rank, LANES), 1)
+
+    def group(g, carry):
+        rows = masked[pl.ds(pl.multiple_of(g * 8, 8), 8), :]
+        leaf = jnp.zeros((rank, LANES), F32)
+        for j in range(8):
+            part = jnp.sum(basis[g * 8 + j] * rows[j : j + 1, :], axis=1, keepdims=True)
+            leaf = jnp.where(lane == j, part, leaf)
+        groups[g] = leaf
+        return carry
+
+    lax.fori_loop(0, clusters // 8, group, 0)
+    leaf = jnp.concatenate([groups[g][:, :8] for g in range(clusters // 8)], axis=1)
     lifted = jnp.zeros((rank, clusters), F32)
     for r in range(rank):
         lifted = lifted + transfer[r] * leaf[r : r + 1, :]
@@ -426,19 +432,30 @@
 
 def final_kernel(sizes, mask, basis, *rest):
     S, R, L = sizes
-    near, out = rest[: S * R], rest[-1]
+    near, out, groups = rest[: S * R], rest[-2], rest[-1]
     clusters, rank = basis.shape[0], basis.shape[1]
     fields = []
     for t in range(clusters // L):
         rows = slice(clusters + t * rank, clusters + (t + 1) * rank)
         fields.append(sum(near[d * R][rows, :] for d in range(1, S)) + near[0][rows, :])
     fields = jnp.concatenate(fields, axis=1) if len(fields) > 1 else fields[0]
-    for c in range(clusters):
-        out[c : c + 1, :] = jnp.sum(basis[c] * fields[:, c : c + 1], axis=0, keepdims=True)
-    total = out[...]
-    for part in near:
-        total = total + part[:clusters, :]
-    out[...] = total * mask[...].astype(F32)
+    for g in range(clusters // 8):
+        groups[g, :, :8] = fields[:, g * 8 : (g + 1) * 8]
+
+    def group(g, carry):
+        span = pl.ds(pl.multiple_of(g * 8, 8), 8)
+        field = groups[g]
+        far = [
+            jnp.sum(basis[g * 8 + j] * field[:, j : j + 1], axis=0, keepdims=True)
+            for j in range(8)
+        ]
+        total = jnp.concatenate(far, axis=0)
+        for part in near:
+            total = total + part[span, :]
+        out[span, :] = total * mask[span, :].astype(F32)
+        return carry
+
+    lax.fori_loop(0, clusters // 8, group, 0)
 
 
 def send(value, moves):
@@ -510,6 +527,7 @@
         out_shape=shape((par_dev, rank), F32),
         in_specs=[vmem()] * 4,
         out_specs=vmem(),
+        scratch_shapes=[pltpu.VMEM((clusters // 8, rank, LANES), F32)],
         compiler_params=PARAMS,
         name="far_up",
     )(basis_t, masked, transfer_t, parent)
@@ -554,7 +572,7 @@
             pltpu.VMEM((C * par_dev, rank), F32),
             pltpu.VMEM((columns, panels), F32),
         ]
-        + [pltpu.VMEM((panels, panels), F32)] * 8,
+        + [pltpu.VMEM((panels, panels), F32)] * 4,
         compiler_params=PARAMS,
         name="near_local",
     )(geometry, local_pairs[0].T, targets, far_list, coupling, transfer_t, parent, up, acc, *pieces, *sums)
@@ -568,6 +586,7 @@
         out_shape=shape((clusters, L), F32),
         in_specs=[vmem()] * (2 + S * R),
         out_specs=vmem(),
+        scratch_shapes=[pltpu.VMEM((clusters // 8, rank, LANES), F32)],
         compiler_params=PARAMS,
         name="combine",
     )(panel_mask, basis_t, *near)

time: 65.7 us -> 70.5 us (1.073)
  Pallas kernels: 40.2 us -> 44.8 us
    pallas_call x1, Pallas kernels: 23.3 us -> 24.9 us  [on_device(): pl.pallas_call(functools.partial(local_kernel, (C, S, L, R, slots, cluste...]
    pallas_call x1, Pallas kernels: 3.1 us -> 4.53 us  [on_device(): pl.pallas_call(functools.partial(final_kernel, (S, R, L)), out_shape=shap...]
    pallas_call x1, Pallas kernels: 3.07 us -> 4.37 us  [on_device(): pl.pallas_call(up_kernel, out_shape=shape((par_dev, rank), F32), in_specs...]
  transfers between devices with their start and end apart: 10 -> 10, of which waited for: 5 -> 5; matrix products, arithmetic and copies ran while one was open for 2% -> 2% of each run, Pallas kernels for 5% -> 6%
where the time goes in v11:
time: 70.5 us
  Pallas kernels  44.8 us (64%)
  starting transfers between devices  13 us (18%)
  waiting for transfers between devices  9.49 us (13%)
  local copies, waits for them, and re-layouts  2.55 us (4%)
    pallas_call x1, Pallas kernels, on_device(): pl.pallas_call(functools.partial(local_kernel, (C, S, L, R, slots, cluste...  24.9 us
    ppermute x10, starting transfers between devices, send(): return lax.ppermute(value, names if len(names) > 1 else names[0], perm)  13 us
    ppermute x10, waiting for transfers between devices, send(): return lax.ppermute(value, names if len(names) > 1 else names[0], perm)  9.49 us
    pallas_call x1, Pallas kernels, on_device(): pl.pallas_call(functools.partial(remote_kernel, (C, S, L, slots, clusters...  8.68 us
    pallas_call x1, Pallas kernels, on_device(): pl.pallas_call(functools.partial(final_kernel, (S, R, L)), out_shape=shap...  4.53 us
    pallas_call x1, Pallas kernels, on_device(): pl.pallas_call(up_kernel, out_shape=shape((par_dev, rank), F32), in_specs...  4.37 us
    unnamed x23, local copies, waits for them, and re-layouts  2.54 us
    pallas_call x1, Pallas kernels, on_device(): pl.pallas_call(functools.partial(pack_kernel, (C, S, L, slots)), out_shap...  2.33 us
  transfers between devices with their start and end apart: 10, of which 5 were waited for; matrix products, arithmetic and copies ran while one was open for 2% of the time, Pallas kernels for 6%

profile of v11, /device:TPU:0, one launch (start us, length us, event | category | flops | bytes accessed | tf_op | source)
XLA Modules:
  0.0 70.5 jit_solution(12408146551201650318)
XLA Ops:
  0.0 0.0 copy-start.10
  0.0 2.3 %packs.1 = (f32[128,128]{1,0:T(8,128)}, f32[88,128]{1,0:T(8,128)}, f32[88,128]{1,0:T(8,128)}, f32[88,128]{1,0:T(8,128)}) custom-call(f32[128,128]{1,0:T(8,128)} %charges.1, s32[128,128]{1,0:T(8,128)} %mask.3, f32[128,4,256]{2,1,0:T(4,128)} %geo.5, s32[4,16]{1,0:T(4,128)} %bitcast.13, s32[4,16]{1,0:T(4,128)} %bitcast.15, s32[4,16]{1,0:T(4,128)} %bitcast.16), custom_call_target="tpu_custom_call" | custom-call | tf_op jit(solution)/shard_map/packs/pallas_call | solution.py:512
  2.3 3.0 %collective-permute-start = (f32[88,128]{1,0:T(8,128)}, f32[88,128]{1,0:T(8,128)S(1)}, u32[]{:S(2)}, u32[]{:S(2)}) collective-permute-start(f32[88,128]{1,0:T(8,128)} %get-tuple-element.16), channel_id=1, source_target_pairs={{0,4},{4,8},{8,12},{12,0},{1,5},{5,9},{9,13},{13,1},{2,6},{6,10},{... | collective-permute-start | bytes 135176 | tf_op jit(solution)/shard_map/ppermute | solution.py:483
  5.4 2.6 %collective-permute-start.1 = (f32[88,128]{1,0:T(8,128)}, f32[88,128]{1,0:T(8,128)S(1)}, u32[]{:S(2)}, u32[]{:S(2)}) collective-permute-start(f32[88,128]{1,0:T(8,128)} %get-tuple-element.17), channel_id=1, source_target_pairs={{0,8},{4,12},{8,0},{12,4},{1,9},{5,13},{9,1},{13,5},{2,10},{6,14},... | collective-permute-start | bytes 135176 | tf_op jit(solution)/shard_map/ppermute | solution.py:483
  7.9 1.3 %collective-permute-start.2 = (f32[88,128]{1,0:T(8,128)}, f32[88,128]{1,0:T(8,128)S(1)}, u32[]{:S(2)}, u32[]{:S(2)}) collective-permute-start(f32[88,128]{1,0:T(8,128)} %get-tuple-element.18), channel_id=1, source_target_pairs={{0,12},{4,0},{8,4},{12,8},{1,13},{5,1},{9,5},{13,9},{2,14},{6,2},{... | collective-permute-start | bytes 135176 | tf_op jit(solution)/shard_map/ppermute | solution.py:483
  9.3 1.5 %collective-permute-start.3 = (f32[128,128]{1,0:T(8,128)}, f32[128,128]{1,0:T(8,128)S(1)}, u32[]{:S(2)}, u32[]{:S(2)}) collective-permute-start(f32[128,128]{1,0:T(8,128)} %get-tuple-element.15.masked.rest_0_), channel_id=1, source_target_pairs={{0,2},{2,0},{1,3},{3,1},{4,6},{6,4},{5,7},{7,5},{8,10},{10,8},{9,1... | collective-permute-start | bytes 196616 | tf_op jit(solution)/shard_map/ppermute | solution.py:483
  10.8 4.4 %far_up.1.up = f32[16,32]{1,0:T(8,128)} custom-call(f32[128,32,128]{2,1,0:T(8,128)} %bitcast.9, f32[128,128]{1,0:T(8,128)} %get-tuple-element.15.masked.rest_0_, f32[32,32,128]{2,1,0:T(8,128)} %bitcast.11, s32[1,128]{1,0:T(1,128)} %bitcast.17), custom_call_target="tpu_custom_call" | custom-call | tf_op jit(solution)/shard_map/far_up/pallas_call | solution.py:525
  15.2 0.0 collective-permute-done.rest_2_
  15.2 0.0 copy-start.4
  15.2 0.0 collective-permute-done.1.rest_3_
  15.2 0.0 copy-start.5
  15.2 0.0 collective-permute-done.2.rest_4_
  15.2 0.0 copy-start.6
  15.2 0.6 maximum_convert_fusion.codes
  15.8 0.0 collective-permute-done.3.rest_1_
  15.8 0.0 copy-done.4
  15.8 0.0 copy-done.5
  15.9 0.0 copy-done.6
  15.9 0.0 copy-start
  15.9 0.6 copy-done
  16.5 8.7 %near_remote.1 = (f32[128,256]{1,0:T(8,128)}, f32[32,128]{1,0:T(8,128)}, f32[32,128]{1,0:T(8,128)}, f32[32,128]{1,0:T(8,128)}) custom-call(f32[128,4,256]{2,1,0:T(4,128)} %geo.5, s32[3,16]{1,0:T(4,128)} %maximum_convert_fusion.codes, f32[16,32]{1,0:T(8,128)} %far_up.1.up, f32[128,128]{1,0:T(8,128)} %get-tuple-element.15.masked.rest_0_, f32[128,128]{1,0:T(8,128)} %copy-done, ...), custom_call_target="tpu_custom_call" | custom-call | tf_op jit(solution)/shard_map/near_remote/pallas_call | solution.py:535
  25.2 0.5 collective-permute-start.4
  25.6 1.7 %collective-permute-start.5 = (f32[32,128]{1,0:T(8,128)}, f32[32,128]{1,0:T(8,128)S(1)}, u32[]{:S(2)}, u32[]{:S(2)}) collective-permute-start(f32[32,128]{1,0:T(8,128)} %get-tuple-element.21), channel_id=1, source_target_pairs={{0,8},{4,12},{8,0},{12,4},{1,9},{5,13},{9,1},{13,5},{2,10},{6,14},... | collective-permute-start | bytes 49160 | tf_op jit(solution)/shard_map/ppermute | solution.py:483
  27.3 0.2 collective-permute-start.6
  27.5 0.0 copy-done.10
  27.5 0.7 copy.13.far_list
  28.2 0.9 %collective-permute-done.4.rest_2_ = f32[32,128]{1,0:T(8,128)S(1)} collective-permute-done((f32[32,128]{1,0:T(8,128)}, f32[32,128]{1,0:T(8,128)S(1)}, u32[]{:S(2)}, u32[]{:S(2)}) %collective-permute-start.4) | collective-permute-done | bytes 16416 | tf_op jit(solution)/shard_map/ppermute | solution.py:483
  29.1 0.0 copy-start.7
  29.1 1.3 %collective-permute-done.5.rest_3_ = f32[32,128]{1,0:T(8,128)S(1)} collective-permute-done((f32[32,128]{1,0:T(8,128)}, f32[32,128]{1,0:T(8,128)S(1)}, u32[]{:S(2)}, u32[]{:S(2)}) %collective-permute-start.5) | collective-permute-done | bytes 16416 | tf_op jit(solution)/shard_map/ppermute | solution.py:483
  30.5 0.0 copy-start.8
  30.5 2.6 %collective-permute-done.6.rest_4_ = f32[32,128]{1,0:T(8,128)S(1)} collective-permute-done((f32[32,128]{1,0:T(8,128)}, f32[32,128]{1,0:T(8,128)S(1)}, u32[]{:S(2)}, u32[]{:S(2)}) %collective-permute-start.6) | collective-permute-done | bytes 16416 | tf_op jit(solution)/shard_map/ppermute | solution.py:483
  33.1 0.0 copy-start.9
  33.1 0.0 copy-done.7
  33.1 0.0 copy-done.8
  33.1 0.6 copy-done.9
  33.7 24.9 %near_local.1 = (f32[160,128]{1,0:T(8,128)}, f32[160,128]{1,0:T(8,128)}) custom-call(f32[128,4,256]{2,1,0:T(4,128)} %geo.5, s32[2,128]{1,0:T(2,128)} %bitcast.19, s32[4,16]{1,0:T(4,128)} %bitcast.14, s32[16,8]{1,0:T(8,128)} %copy.13.far_list, f32[16,8,32,32]{3,2,1,0:T(8,128)} %coupling.1, f32[32,32,128]{2,1,0:T(8,128)} %bitcast.12, s32[1,128]{1,0:T(1,128)} %bitcast.18, ...), custom_call_target="tpu_custom_call" | custom-call | tf_op jit(solution)/shard_map/near_local/pallas_call | solution.py:559
  58.6 0.0 collective-permute-start.7
  58.6 0.6 collective-permute-start.9
  59.2 1.5 %collective-permute-start.8 = (f32[160,128]{1,0:T(8,128)}, f32[160,128]{1,0:T(8,128)S(1)}, u32[]{:S(2)}, u32[]{:S(2)}) collective-permute-start(f32[160,128]{1,0:T(8,128)} %get-tuple-element.24), channel_id=1, source_target_pairs={{0,2},{1,3},{2,0},{3,1},{4,6},{5,7},{6,4},{7,5},{8,10},{9,11},{10,... | collective-permute-start | bytes 245768 | tf_op jit(solution)/shard_map/ppermute | solution.py:483
  60.7 0.0 collective-permute-done.7.rest_1_
  60.7 0.0 copy-start.1
  60.7 2.3 %collective-permute-done.9.rest_3_ = f32[160,128]{1,0:T(8,128)S(1)} collective-permute-done((f32[160,128]{1,0:T(8,128)}, f32[160,128]{1,0:T(8,128)S(1)}, u32[]{:S(2)}, u32[]{:S(2)}) %collective-permute-start.9) | collective-permute-done | bytes 81952 | tf_op jit(solution)/shard_map/ppermute | solution.py:483
  63.0 2.3 %collective-permute-done.8.rest_2_ = f32[160,128]{1,0:T(8,128)S(1)} collective-permute-done((f32[160,128]{1,0:T(8,128)}, f32[160,128]{1,0:T(8,128)S(1)}, u32[]{:S(2)}, u32[]{:S(2)}) %collective-permute-start.8) | collective-permute-done | bytes 81952 | tf_op jit(solution)/shard_map/ppermute | solution.py:483
  65.4 0.0 copy-done.1
  65.4 0.0 copy-done.2
  65.4 0.0 copy-start.3
  65.4 0.6 copy-done.3
  66.0 4.5 %combine.1 = f32[128,128]{1,0:T(8,128)} custom-call(s32[128,128]{1,0:T(8,128)} %mask.3, f32[128,32,128]{2,1,0:T(8,128)} %bitcast.10, f32[160,128]{1,0:T(8,128)} %get-tuple-element.23.rest_0_, f32[160,128]{1,0:T(8,128)} %copy-done.1, f32[160,128]{1,0:T(8,128)} %copy-done.3, f32[160,128]{1,0:T(8,128)} %copy-done.2), custom_call_target="tpu_custom_call" | custom-call | tf_op jit(solution)/shard_map/combine/pallas_call | solution.py:584
  (4 shorter events, 0.0 us)
Async XLA Ops:
  0.0 27.5 %copy-start.10 = (s32[16,8]{0,1:T(8,128)S(1)}, s32[16,8]{0,1:T(8,128)}, u32[]{:S(2)}) copy-start(s32[16,8]{0,1:T(8,128)} %param.22) | copy-start | bytes 1540
  2.3 12.8 %collective-permute-start = (f32[88,128]{1,0:T(8,128)}, f32[88,128]{1,0:T(8,128)S(1)}, u32[]{:S(2)}, u32[]{:S(2)}) collective-permute-start(f32[88,128]{1,0:T(8,128)} %get-tuple-element.16), channel_id=1, source_target_pairs={{0,4},{4,8},{8,12},{12,0},{1,5},{5,9},{9,13},{13,1},{2,6},{6,10},{... | collective-permute-start | bytes 135176 | tf_op jit(solution)/shard_map/ppermute | solution.py:483
  5.4 9.8 %collective-permute-start.1 = (f32[88,128]{1,0:T(8,128)}, f32[88,128]{1,0:T(8,128)S(1)}, u32[]{:S(2)}, u32[]{:S(2)}) collective-permute-start(f32[88,128]{1,0:T(8,128)} %get-tuple-element.17), channel_id=1, source_target_pairs={{0,8},{4,12},{8,0},{12,4},{1,9},{5,13},{9,1},{13,5},{2,10},{6,14},... | collective-permute-start | bytes 135176 | tf_op jit(solution)/shard_map/ppermute | solution.py:483
  7.9 7.3 %collective-permute-start.2 = (f32[88,128]{1,0:T(8,128)}, f32[88,128]{1,0:T(8,128)S(1)}, u32[]{:S(2)}, u32[]{:S(2)}) collective-permute-start(f32[88,128]{1,0:T(8,128)} %get-tuple-element.18), channel_id=1, source_target_pairs={{0,12},{4,0},{8,4},{12,8},{1,13},{5,1},{9,5},{13,9},{2,14},{6,2},{... | collective-permute-start | bytes 135176 | tf_op jit(solution)/shard_map/ppermute | solution.py:483
  9.3 6.5 %collective-permute-start.3 = (f32[128,128]{1,0:T(8,128)}, f32[128,128]{1,0:T(8,128)S(1)}, u32[]{:S(2)}, u32[]{:S(2)}) collective-permute-start(f32[128,128]{1,0:T(8,128)} %get-tuple-element.15.masked.rest_0_), channel_id=1, source_target_pairs={{0,2},{2,0},{1,3},{3,1},{4,6},{6,4},{5,7},{7,5},{8,10},{10,8},{9,1... | collective-permute-start | bytes 196616 | tf_op jit(solution)/shard_map/ppermute | solution.py:483
  15.2 0.7 copy-start.4
  15.2 0.7 copy-start.5
  15.2 0.6 copy-start.6
  15.9 0.6 copy-start
  25.2 4.0 %collective-permute-start.4 = (f32[32,128]{1,0:T(8,128)}, f32[32,128]{1,0:T(8,128)S(1)}, u32[]{:S(2)}, u32[]{:S(2)}) collective-permute-start(f32[32,128]{1,0:T(8,128)} %get-tuple-element.20), channel_id=1, source_target_pairs={{0,12},{4,0},{8,4},{12,8},{1,13},{5,1},{9,5},{13,9},{2,14},{6,2},{... | collective-permute-start | bytes 49160 | tf_op jit(solution)/shard_map/ppermute | solution.py:483
  25.6 4.8 %collective-permute-start.5 = (f32[32,128]{1,0:T(8,128)}, f32[32,128]{1,0:T(8,128)S(1)}, u32[]{:S(2)}, u32[]{:S(2)}) collective-permute-start(f32[32,128]{1,0:T(8,128)} %get-tuple-element.21), channel_id=1, source_target_pairs={{0,8},{4,12},{8,0},{12,4},{1,9},{5,13},{9,1},{13,5},{2,10},{6,14},... | collective-permute-start | bytes 49160 | tf_op jit(solution)/shard_map/ppermute | solution.py:483
  27.3 5.7 %collective-permute-start.6 = (f32[32,128]{1,0:T(8,128)}, f32[32,128]{1,0:T(8,128)S(1)}, u32[]{:S(2)}, u32[]{:S(2)}) collective-permute-start(f32[32,128]{1,0:T(8,128)} %get-tuple-element.22), channel_id=1, source_target_pairs={{0,4},{4,8},{8,12},{12,0},{1,5},{5,9},{9,13},{13,1},{2,6},{6,10},{... | collective-permute-start | bytes 49160 | tf_op jit(solution)/shard_map/ppermute | solution.py:483
  29.1 3.9 %copy-start.7 = (f32[32,128]{1,0:T(8,128)}, f32[32,128]{1,0:T(8,128)S(1)}, u32[]{:S(2)}) copy-start(f32[32,128]{1,0:T(8,128)S(1)} %collective-permute-done.4.rest_2_) | copy-start | bytes 49156
  30.5 2.6 %copy-start.8 = (f32[32,128]{1,0:T(8,128)}, f32[32,128]{1,0:T(8,128)S(1)}, u32[]{:S(2)}) copy-start(f32[32,128]{1,0:T(8,128)S(1)} %collective-permute-done.5.rest_3_) | copy-start | bytes 49156
  33.1 0.6 copy-start.9
  58.6 2.1 %collective-permute-start.7 = (f32[160,128]{1,0:T(8,128)}, f32[160,128]{1,0:T(8,128)S(1)}, u32[]{:S(2)}, u32[]{:S(2)}) collective-permute-start(f32[160,128]{1,0:T(8,128)} %get-tuple-element.23.rest_0_), channel_id=1, source_target_pairs={{0,1},{1,0},{2,3},{3,2},{4,5},{5,4},{6,7},{7,6},{8,9},{9,8},{10,11... | collective-permute-start | bytes 245768 | tf_op jit(solution)/shard_map/ppermute | solution.py:483
  58.6 4.4 %collective-permute-start.9 = (f32[160,128]{1,0:T(8,128)}, f32[160,128]{1,0:T(8,128)S(1)}, u32[]{:S(2)}, u32[]{:S(2)}) collective-permute-start(f32[160,128]{1,0:T(8,128)} %get-tuple-element.24), channel_id=1, source_target_pairs={{0,3},{1,2},{2,1},{3,0},{4,7},{5,6},{6,5},{7,4},{8,11},{9,10},{10,... | collective-permute-start | bytes 245768 | tf_op jit(solution)/shard_map/ppermute | solution.py:483
  59.2 6.1 %collective-permute-start.8 = (f32[160,128]{1,0:T(8,128)}, f32[160,128]{1,0:T(8,128)S(1)}, u32[]{:S(2)}, u32[]{:S(2)}) collective-permute-start(f32[160,128]{1,0:T(8,128)} %get-tuple-element.24), channel_id=1, source_target_pairs={{0,2},{1,3},{2,0},{3,1},{4,6},{5,7},{6,4},{7,5},{8,10},{9,11},{10,... | collective-permute-start | bytes 245768 | tf_op jit(solution)/shard_map/ppermute | solution.py:483
  60.7 4.6 %copy-start.1 = (f32[160,128]{1,0:T(8,128)}, f32[160,128]{1,0:T(8,128)S(1)}, u32[]{:S(2)}) copy-start(f32[160,128]{1,0:T(8,128)S(1)} %collective-permute-done.7.rest_1_) | copy-start | bytes 245764
  63.0 2.3 %copy-start.2 = (f32[160,128]{1,0:T(8,128)}, f32[160,128]{1,0:T(8,128)S(1)}, u32[]{:S(2)}) copy-start(f32[160,128]{1,0:T(8,128)S(1)} %collective-permute-done.9.rest_3_) | copy-start | bytes 245764
  65.4 0.6 copy-start.3

commit v12 on v10

--- a/solution.py
+++ b/solution.py
@@ -13,11 +13,15 @@
 ROWS = 40
 USED = 34
 LANES = 128
-PARAMS = pltpu.CompilerParams(vmem_limit_bytes=56 * 1024 * 1024)
+PARAMS = pltpu.CompilerParams(vmem_limit_bytes=44 * 1024 * 1024)
 
 
 def vmem():
     return pl.BlockSpec(memory_space=pltpu.VMEM)
+
+
+def near_by(*arrays):
+    return [pltpu.with_memory_space_constraint(x, pltpu.VMEM) for x in arrays]
 
 
 def smem():
@@ -180,7 +184,7 @@
 
 
 def ring_size(total):
-    return next(size for size in (8, 4, 2, 1) if total % size == 0)
+    return next(size for size in (16, 8, 4, 2, 1) if total % size == 0)
 
 
 def assemble(sub, S, L, q, pieces):
@@ -221,22 +225,31 @@
         pl.when(sub == s)(functools.partial(fill, s))
 
 
-def remote_kernel(sizes, geo, codes, up, *rest):
+def remote_kernel(sizes, geo, up, *rest):
     C, S, L, slots, clusters, panels = sizes
     pieces = rest[:S]
     packs = rest[S : S + C - 1]
     acc_out = rest[S + C - 1]
     sends = rest[S + C : S + C + C - 1]
-    q, tq, acc, fwdt, sgeo, fa0, fb0, fb1, order, *ring = rest[S + C + C - 1 :]
+    q, tq, acc, fwdt, sgeo, fa0, fb0, fb1, order, codes, sems, *ring = rest[S + C + C - 1 :]
     fa, fb = (fa0,), (fb0, fb1)
     n = (C - 1) * slots
+    copies = [
+        pltpu.make_async_copy(packs[k].at[pl.ds(5 * slots, 8), :], codes.at[k], sems.at[k])
+        for k in range(C - 1)
+    ]
+    for copy in copies:
+        copy.start()
     assemble(lax.axis_index("sub"), S, L, q, pieces)
     acc[...] = jnp.zeros_like(acc)
     fwdt[...] = jnp.zeros_like(fwdt)
+    for copy in copies:
+        copy.wait()
     found = jnp.int32(0)
     for shift in range(C - 1):
         for j in range(slots):
-            code = codes[shift, j]
+            code = codes[shift, 0, j].astype(jnp.int32)
+            order[n + 1 + shift * slots + j] = jnp.maximum(code, 0)
             order[found] = shift * slots + j
             found = found + (code >= 0).astype(jnp.int32)
             g = geo[jnp.maximum(code, 0)]
@@ -261,7 +274,7 @@
     def finish(i, dist):
         ok = i < found
         slot = order[jnp.minimum(i, jnp.maximum(found - 1, 0))]
-        source = jnp.maximum(codes[slot // slots, lax.rem(slot, slots)], 0)
+        source = order[n + 1 + slot]
         back = tile_sums(
             dist, q[pl.ds(source, 1), :], tq[pl.ds(slot, 1), :], fwdt, jnp.where(ok, slot, -1)
         )
@@ -384,7 +397,7 @@
     for p in range(par_dev):
         part = jnp.zeros((rank, rank), F32)
         for k in range(far_n):
-            part = part + coupling[p, k] * parents[pl.ds(far_list[p, k], 1), :]
+            part = part + coupling[p, k] * parents[pl.ds(far_list[k, p], 1), :]
         field = jnp.where(lane == p, jnp.sum(part, axis=1, keepdims=True), field)
     which = lax.broadcasted_iota(jnp.int32, (LANES, clusters), 0)
     onehot = (parent[...] == which).astype(F32)
@@ -494,30 +507,30 @@
 
     made = pl.pallas_call(
         functools.partial(pack_kernel, (C, S, L, slots)),
-        out_shape=[shape((clusters, L), F32)] + [shape((5 * slots + 8, L), F32)] * (C - 1),
+        out_shape=[pltpu.VMEM((clusters, L), F32)] + [pltpu.VMEM((5 * slots + 8, L), F32)] * (C - 1),
         in_specs=[vmem()] * 3 + [smem()] * 3,
         out_specs=[vmem()] * C,
         compiler_params=PARAMS,
         name="packs",
-    )(charges, panel_mask, geometry, targets, remote_source[0], remote_live[0])
+    )(*near_by(charges, panel_mask, geometry), targets, remote_source[0], remote_live[0])
     masked, packs = made[0], made[1:]
     pieces = [masked] + [send(masked, (("sub", d),)) for d in range(1, S)]
     packs = [send(packs[d - 1], (("clu", d),)) for d in range(1, C)]
-    codes = jnp.stack([p[5 * slots, :slots] for p in packs]).astype(jnp.int32)
 
     up = pl.pallas_call(
         up_kernel,
-        out_shape=shape((par_dev, rank), F32),
+        out_shape=pltpu.VMEM((par_dev, rank), F32),
         in_specs=[vmem()] * 4,
         out_specs=vmem(),
         compiler_params=PARAMS,
         name="far_up",
-    )(basis_t, masked, transfer_t, parent)
+    )(*near_by(basis_t, masked, transfer_t, parent))
 
     made = pl.pallas_call(
         functools.partial(remote_kernel, (C, S, L, slots, clusters, panels)),
-        out_shape=[shape((clusters, panels), F32)] + [shape((slots + par_dev, L), F32)] * (C - 1),
-        in_specs=[vmem(), smem()] + [vmem()] * (1 + S + C - 1),
+        out_shape=[pltpu.VMEM((clusters, panels), F32)]
+        + [pltpu.VMEM((slots + par_dev, L), F32)] * (C - 1),
+        in_specs=[vmem()] * (2 + S + C - 1),
         out_specs=[vmem()] * C,
         scratch_shapes=[
             pltpu.VMEM((clusters, panels), F32),
@@ -528,19 +541,21 @@
             pltpu.VMEM((n * ROWS, L), F32),
             pltpu.VMEM((n * ROWS, LANES), F32),
             pltpu.VMEM((n * ROWS, LANES), F32),
-            pltpu.SMEM((n + 1,), jnp.int32),
+            pltpu.SMEM((2 * n + 1,), jnp.int32),
+            pltpu.SMEM((C - 1, 8, L), F32),
+            pltpu.SemaphoreType.DMA((C - 1,)),
         ]
-        + [pltpu.VMEM((L, panels), F32)] * 4,
+        + [pltpu.VMEM((L, panels), F32)] * 8,
         compiler_params=PARAMS,
         name="near_remote",
-    )(geometry, codes, up, *pieces, *packs)
+    )(*near_by(geometry, up, *pieces, *packs))
     acc, sums = made[0], [send(made[d], (("clu", C - d),)) for d in range(1, C)]
 
     columns = whole(clusters // (S * R) + local_pairs.shape[1] // S)
     half = [pltpu.VMEM((clusters * ROWS, LANES), F32)] * 2
     parts = pl.pallas_call(
         functools.partial(local_kernel, (C, S, L, R, slots, clusters, panels)),
-        out_shape=[shape((clusters + clusters // L * rank, L), F32)] * S,
+        out_shape=[pltpu.VMEM((clusters + clusters // L * rank, L), F32)] * S,
         in_specs=[vmem()] + [smem()] * 3 + [vmem()] * (5 + S + C - 1),
         out_specs=[vmem()] * S,
         scratch_shapes=[
@@ -554,10 +569,16 @@
             pltpu.VMEM((C * par_dev, rank), F32),
             pltpu.VMEM((columns, panels), F32),
         ]
-        + [pltpu.VMEM((panels, panels), F32)] * 8,
+        + [pltpu.VMEM((panels, panels), F32)] * 16,
         compiler_params=PARAMS,
         name="near_local",
-    )(geometry, local_pairs[0].T, targets, far_list, coupling, transfer_t, parent, up, acc, *pieces, *sums)
+    )(
+        *near_by(geometry),
+        local_pairs[0].T,
+        targets,
+        far_list.T,
+        *near_by(coupling, transfer_t, parent, up, acc, *pieces, *sums),
+    )
     near = []
     for d in range(S):
         for e in range(R):
@@ -570,7 +591,7 @@
         out_specs=vmem(),
         compiler_params=PARAMS,
         name="combine",
-    )(panel_mask, basis_t, *near)
+    )(*near_by(panel_mask, basis_t, *near))
 
 
 def solution(mesh):

time: 65.7 us -> 61.6 us (0.938)
  Pallas kernels: 40.2 us -> 30.1 us
  local copies, waits for them, and re-layouts: 2.55 us -> 8.1 us
    unnamed x23 -> x32, local copies, waits for them, and re-layouts: 2.54 us -> 8.1 us
    pallas_call x1, Pallas kernels: 8.69 us -> 6.16 us  [on_device(): pl.pallas_call(functools.partial(remote_kernel, (C, S, L, slots, clusters...]
    pallas_call x1, Pallas kernels: 23.3 us -> 20.9 us  [on_device(): pl.pallas_call(functools.partial(local_kernel, (C, S, L, R, slots, cluste...]
    pallas_call x1, Pallas kernels: 3.07 us -> 0.76 us  [on_device(): pl.pallas_call(up_kernel, out_shape=pltpu.VMEM((par_dev, rank), F32), in_...]
    pallas_call x1, Pallas kernels: 3.1 us -> 1.49 us  [on_device(): pl.pallas_call(functools.partial(final_kernel, (S, R, L)), out_shape=shap...]
    pallas_call x1, Pallas kernels: 2.02 us -> 0.83 us  [on_device(): pl.pallas_call(functools.partial(pack_kernel, (C, S, L, slots)), out_shap...]
  transfers between devices with their start and end apart: 10 -> 10, of which waited for: 5 -> 5; matrix products, arithmetic and copies ran while one was open for 2% -> 0% of each run, Pallas kernels for 5% -> 1%
where the time goes in v12:
time: 61.6 us; the launch traced here: 61.2 us
  Pallas kernels  30.1 us (49%)
  starting transfers between devices  13.1 us (21%)
  waiting for transfers between devices  9.76 us (16%)
  local copies, waits for them, and re-layouts  8.1 us (13%)
    pallas_call x1, Pallas kernels, on_device(): pl.pallas_call(functools.partial(local_kernel, (C, S, L, R, slots, cluste...  20.9 us
    ppermute x10, starting transfers between devices, send(): return lax.ppermute(value, names if len(names) > 1 else names[0], perm)  13.1 us
    ppermute x10, waiting for transfers between devices, send(): return lax.ppermute(value, names if len(names) > 1 else names[0], perm)  9.76 us
    unnamed x32, local copies, waits for them, and re-layouts  8.1 us
    pallas_call x1, Pallas kernels, on_device(): pl.pallas_call(functools.partial(remote_kernel, (C, S, L, slots, clusters...  6.16 us
    pallas_call x1, Pallas kernels, on_device(): pl.pallas_call(functools.partial(final_kernel, (S, R, L)), out_shape=shap...  1.49 us
  transfers between devices with their start and end apart: 10, of which 5 were waited for; matrix products, arithmetic and copies ran while one was open for 0% of the time, Pallas kernels for 1%

profile of v12, /device:TPU:0, one launch (start us, length us, event | category | flops | bytes accessed | tf_op | source)
XLA Modules:
  0.0 61.2 jit_solution(16981762533301793831)
XLA Ops:
  0.0 0.0 copy-start.10
  0.0 0.0 copy-start.15
  0.0 0.0 copy-start.2
  0.0 1.1 %copy-done.2 = f32[128,4,256]{2,1,0:T(4,128)S(1)} copy-done((f32[128,4,256]{2,1,0:T(4,128)S(1)}, f32[128,4,256]{2,1,0:T(4,128)}, u32[]{:S(2)}) %copy-start.2) | copy-done | bytes 524312
  1.1 0.0 copy-start.6
  1.1 0.8 %copy-done.6 = s32[128,128]{1,0:T(8,128)S(1)} copy-done((s32[128,128]{1,0:T(8,128)S(1)}, s32[128,128]{1,0:T(8,128)}, u32[]{:S(2)}) %copy-start.6) | copy-done | bytes 65560
  1.9 0.0 copy-start.8
  1.9 0.8 %copy-done.8 = f32[128,128]{1,0:T(8,128)S(1)} copy-done((f32[128,128]{1,0:T(8,128)S(1)}, f32[128,128]{1,0:T(8,128)}, u32[]{:S(2)}) %copy-start.8) | copy-done | bytes 65560
  2.8 0.0 copy-start.9
  2.8 0.7 %copy-done.9 = s32[1,4,16]{2,1,0:T(4,128)S(1)} copy-done((s32[1,4,16]{2,1,0:T(4,128)S(1)}, s32[1,4,16]{2,1,0:T(4,128)}, u32[]{:S(2)}) %copy-start.9) | copy-done | bytes 280
  3.4 0.0 copy-start.12
  3.4 0.7 %copy-done.12 = s32[1,4,16]{2,1,0:T(4,128)S(1)} copy-done((s32[1,4,16]{2,1,0:T(4,128)S(1)}, s32[1,4,16]{2,1,0:T(4,128)}, u32[]{:S(2)}) %copy-start.12) | copy-done | bytes 280
  4.1 0.7 %copy-done.13 = s32[1,4,16]{2,1,0:T(4,128)S(1)} copy-done((s32[1,4,16]{2,1,0:T(4,128)S(1)}, s32[1,4,16]{2,1,0:T(4,128)}, u32[]{:S(2)}) %copy-start.13) | copy-done | bytes 280
  4.8 0.8 %packs.1 = (f32[128,128]{1,0:T(8,128)S(1)}, f32[88,128]{1,0:T(8,128)S(1)}, f32[88,128]{1,0:T(8,128)S(1)}, f32[88,128]{1,0:T(8,128)S(1)}) custom-call(f32[128,128]{1,0:T(8,128)S(1)} %copy-done.8, s32[128,128]{1,0:T(8,128)S(1)} %copy-done.6, f32[128,4,256]{2,1,0:T(4,128)S(1)} %copy-done.2, s32[4,16]{1,0:T(4,128)S(1)} %bitcast.14, s32[4,16]{1,0:T(4,128)S(1)} %bitcast.17, ...), custom_call_target="tpu_custom_call" | custom-call | tf_op jit(solution)/shard_map/packs/pallas_call | solution.py:508
  5.6 3.0 %collective-permute-start = (f32[128,128]{1,0:T(8,128)S(1)}, f32[128,128]{1,0:T(8,128)S(1)}, u32[]{:S(2)}, u32[]{:S(2)}) collective-permute-start(f32[128,128]{1,0:T(8,128)S(1)} %get-tuple-element.15.masked.rest_0_), channel_id=1, source_target_pairs={{0,2},{2,0},{1,3},{3,1},{4,6},{6,4},{5,7},{7,5},{8,10},{10,8},{9,1... | collective-permute-start | bytes 196616 | tf_op jit(solution)/shard_map/ppermute | solution.py:479
  8.6 1.6 %collective-permute-start.1 = (f32[88,128]{1,0:T(8,128)S(1)}, f32[88,128]{1,0:T(8,128)S(1)}, u32[]{:S(2)}, u32[]{:S(2)}) collective-permute-start(f32[88,128]{1,0:T(8,128)S(1)} %get-tuple-element.16), channel_id=1, source_target_pairs={{0,4},{4,8},{8,12},{12,0},{1,5},{5,9},{9,13},{13,1},{2,6},{6,10},{... | collective-permute-start | bytes 135176 | tf_op jit(solution)/shard_map/ppermute | solution.py:479
  10.2 2.6 %collective-permute-start.2 = (f32[88,128]{1,0:T(8,128)S(1)}, f32[88,128]{1,0:T(8,128)S(1)}, u32[]{:S(2)}, u32[]{:S(2)}) collective-permute-start(f32[88,128]{1,0:T(8,128)S(1)} %get-tuple-element.17), channel_id=1, source_target_pairs={{0,8},{4,12},{8,0},{12,4},{1,9},{5,13},{9,1},{13,5},{2,10},{6,14},... | collective-permute-start | bytes 135176 | tf_op jit(solution)/shard_map/ppermute | solution.py:479
  12.8 1.3 %collective-permute-start.3 = (f32[88,128]{1,0:T(8,128)S(1)}, f32[88,128]{1,0:T(8,128)S(1)}, u32[]{:S(2)}, u32[]{:S(2)}) collective-permute-start(f32[88,128]{1,0:T(8,128)S(1)} %get-tuple-element.18), channel_id=1, source_target_pairs={{0,12},{4,0},{8,4},{12,8},{1,13},{5,1},{9,5},{13,9},{2,14},{6,2},{... | collective-permute-start | bytes 135176 | tf_op jit(solution)/shard_map/ppermute | solution.py:479
  14.2 1.6 %copy-done = f32[128,128,32]{1,2,0:T(8,128)S(1)} copy-done((f32[128,128,32]{1,2,0:T(8,128)S(1)}, f32[128,128,32]{1,2,0:T(8,128)}, u32[]{:S(2)}) %copy-start) | copy-done | bytes 2097176
  15.8 1.0 %copy-done.5 = f32[128,32,32]{0,2,1:T(8,128)S(1)} copy-done((f32[128,32,32]{0,2,1:T(8,128)S(1)}, f32[128,32,32]{0,2,1:T(8,128)}, u32[]{:S(2)}) %copy-start.5) | copy-done | bytes 524312
  16.8 0.7 %copy-done.14 = s32[128]{0:T(128)S(1)} copy-done((s32[128]{0:T(128)S(1)}, s32[128]{0:T(128)}, u32[]{:S(2)}) %copy-start.14) | copy-done | bytes 536
  17.5 0.8 %far_up.1.up = f32[16,32]{1,0:T(8,128)S(1)} custom-call(f32[128,32,128]{2,1,0:T(8,128)S(1)} %bitcast.10, f32[128,128]{1,0:T(8,128)S(1)} %get-tuple-element.15.masked.rest_0_, f32[32,32,128]{2,1,0:T(8,128)S(1)} %bitcast.12, s32[1,128]{1,0:T(1,128)S(1)} %bitcast.19), custom_call_target="tpu_custom_call" | custom-call | tf_op jit(solution)/shard_map/far_up/pallas_call | solution.py:520
  18.2 0.0 collective-permute-done.1.rest_2_
  18.2 0.0 collective-permute-done.2.rest_3_
  18.2 0.0 collective-permute-done.3.rest_4_
  18.3 0.0 collective-permute-done.rest_1_
  18.3 0.0 copy-done.3
  18.3 6.2 %near_remote.1 = (f32[128,256]{1,0:T(8,128)S(1)}, f32[32,128]{1,0:T(8,128)S(1)}, f32[32,128]{1,0:T(8,128)S(1)}, f32[32,128]{1,0:T(8,128)S(1)}) custom-call(f32[128,4,256]{2,1,0:T(4,128)S(1)} %copy-done.3, f32[16,32]{1,0:T(8,128)S(1)} %far_up.1.up, f32[128,128]{1,0:T(8,128)S(1)} %get-tuple-element.15.masked.rest_0_, ...), custom_call_target="tpu_custom_call" | custom-call | tf_op jit(solution)/shard_map/near_remote/pallas_call | solution.py:529
  24.4 1.1 %collective-permute-start.4 = (f32[32,128]{1,0:T(8,128)S(1)}, f32[32,128]{1,0:T(8,128)S(1)}, u32[]{:S(2)}, u32[]{:S(2)}) collective-permute-start(f32[32,128]{1,0:T(8,128)S(1)} %get-tuple-element.20), channel_id=1, source_target_pairs={{0,12},{4,0},{8,4},{12,8},{1,13},{5,1},{9,5},{13,9},{2,14},{6,2},{... | collective-permute-start | bytes 49160 | tf_op jit(solution)/shard_map/ppermute | solution.py:479
  25.5 1.1 %collective-permute-start.5 = (f32[32,128]{1,0:T(8,128)S(1)}, f32[32,128]{1,0:T(8,128)S(1)}, u32[]{:S(2)}, u32[]{:S(2)}) collective-permute-start(f32[32,128]{1,0:T(8,128)S(1)} %get-tuple-element.21), channel_id=1, source_target_pairs={{0,8},{4,12},{8,0},{12,4},{1,9},{5,13},{9,1},{13,5},{2,10},{6,14},... | collective-permute-start | bytes 49160 | tf_op jit(solution)/shard_map/ppermute | solution.py:479
  26.6 0.2 collective-permute-start.6
  26.9 1.4 %collective-permute-done.4.rest_2_ = f32[32,128]{1,0:T(8,128)S(1)} collective-permute-done((f32[32,128]{1,0:T(8,128)S(1)}, f32[32,128]{1,0:T(8,128)S(1)}, u32[]{:S(2)}, u32[]{:S(2)}) %collective-permute-start.4) | collective-permute-done | bytes 16416 | tf_op jit(solution)/shard_map/ppermute | solution.py:479
  28.2 1.9 %collective-permute-done.5.rest_3_ = f32[32,128]{1,0:T(8,128)S(1)} collective-permute-done((f32[32,128]{1,0:T(8,128)S(1)}, f32[32,128]{1,0:T(8,128)S(1)}, u32[]{:S(2)}, u32[]{:S(2)}) %collective-permute-start.5) | collective-permute-done | bytes 16416 | tf_op jit(solution)/shard_map/ppermute | solution.py:479
  30.2 2.0 %collective-permute-done.6.rest_4_ = f32[32,128]{1,0:T(8,128)S(1)} collective-permute-done((f32[32,128]{1,0:T(8,128)S(1)}, f32[32,128]{1,0:T(8,128)S(1)}, u32[]{:S(2)}, u32[]{:S(2)}) %collective-permute-start.6) | collective-permute-done | bytes 16416 | tf_op jit(solution)/shard_map/ppermute | solution.py:479
  32.2 0.0 copy-done.10
  32.2 0.0 copy-done.15
  32.2 0.0 copy-done.11
  32.2 0.0 copy-done.4
  32.2 20.9 %near_local.1 = (f32[160,128]{1,0:T(8,128)S(1)}, f32[160,128]{1,0:T(8,128)S(1)}) custom-call(f32[128,4,256]{2,1,0:T(4,128)S(1)} %copy-done.3, s32[2,128]{1,0:T(2,128)S(1)} %bitcast.21, s32[4,16]{1,0:T(4,128)S(1)} %bitcast.15, s32[8,16]{1,0:T(8,128)S(1)} %bitcast.16, f32[16,8,32,32]{3,2,1,0:T(8,128)S(1)} %copy-done.4, f32[32,32,128]{2,1,0:T(8,128)S(1)} %bitcast.13, ...), custom_call_target="tpu_custom_call" | custom-call | tf_op jit(solution)/shard_map/near_local/pallas_call | solution.py:556
  53.1 0.1 collective-permute-start.7
  53.2 0.7 %collective-permute-start.9 = (f32[160,128]{1,0:T(8,128)S(1)}, f32[160,128]{1,0:T(8,128)S(1)}, u32[]{:S(2)}, u32[]{:S(2)}) collective-permute-start(f32[160,128]{1,0:T(8,128)S(1)} %get-tuple-element.24), channel_id=1, source_target_pairs={{0,3},{1,2},{2,1},{3,0},{4,7},{5,6},{6,5},{7,4},{8,11},{9,10},{10,... | collective-permute-start | bytes 245768 | tf_op jit(solution)/shard_map/ppermute | solution.py:479
  53.8 1.5 %collective-permute-start.8 = (f32[160,128]{1,0:T(8,128)S(1)}, f32[160,128]{1,0:T(8,128)S(1)}, u32[]{:S(2)}, u32[]{:S(2)}) collective-permute-start(f32[160,128]{1,0:T(8,128)S(1)} %get-tuple-element.24), channel_id=1, source_target_pairs={{0,2},{1,3},{2,0},{3,1},{4,6},{5,7},{6,4},{7,5},{8,10},{9,11},{10,... | collective-permute-start | bytes 245768 | tf_op jit(solution)/shard_map/ppermute | solution.py:479
  55.3 0.0 collective-permute-done.7.rest_1_
  55.3 2.1 %collective-permute-done.9.rest_3_ = f32[160,128]{1,0:T(8,128)S(1)} collective-permute-done((f32[160,128]{1,0:T(8,128)S(1)}, f32[160,128]{1,0:T(8,128)S(1)}, u32[]{:S(2)}, u32[]{:S(2)}) %collective-permute-start.9) | collective-permute-done | bytes 81952 | tf_op jit(solution)/shard_map/ppermute | solution.py:479
  57.4 2.3 %collective-permute-done.8.rest_2_ = f32[160,128]{1,0:T(8,128)S(1)} collective-permute-done((f32[160,128]{1,0:T(8,128)S(1)}, f32[160,128]{1,0:T(8,128)S(1)}, u32[]{:S(2)}, u32[]{:S(2)}) %collective-permute-start.8) | collective-permute-done | bytes 81952 | tf_op jit(solution)/shard_map/ppermute | solution.py:479
  59.7 0.0 copy-done.1
  59.7 0.0 copy-done.7
  59.7 1.5 %combine.1 = f32[128,128]{1,0:T(8,128)} custom-call(s32[128,128]{1,0:T(8,128)S(1)} %copy-done.7, f32[128,32,128]{2,1,0:T(8,128)S(1)} %bitcast.11, f32[160,128]{1,0:T(8,128)S(1)} %get-tuple-element.23.rest_0_, f32[160,128]{1,0:T(8,128)S(1)} %collective-permute-done.7.rest_1_, f32[160,128]{1,0:T(8,128)S(1)} %collective-permute-done.8.rest_2_, ...), custom_call_target="tpu_custom_call" | custom-call | tf_op jit(solution)/shard_map/combine/pallas_call | solution.py:587
  (9 shorter events, 0.0 us)
Async XLA Ops:
  0.0 32.2 %copy-start.10 = (s32[1,4,16]{2,1,0:T(4,128)S(1)}, s32[1,4,16]{2,1,0:T(4,128)}, u32[]{:S(2)}) copy-start(s32[1,4,16]{2,1,0:T(4,128)} %param.16) | copy-start | bytes 772
  0.0 32.2 %copy-start.15 = (s32[1,128,2]{1,2,0:T(2,128)S(1)}, s32[1,128,2]{1,2,0:T(2,128)}, u32[]{:S(2)}) copy-start(s32[1,128,2]{1,2,0:T(2,128)} %param.18) | copy-start | bytes 3076
  0.0 1.1 %copy-start.2 = (f32[128,4,256]{2,1,0:T(4,128)S(1)}, f32[128,4,256]{2,1,0:T(4,128)}, u32[]{:S(2)}) copy-start(f32[128,4,256]{2,1,0:T(4,128)} %geo.5) | copy-start | bytes 1572868
  1.1 0.8 %copy-start.6 = (s32[128,128]{1,0:T(8,128)S(1)}, s32[128,128]{1,0:T(8,128)}, u32[]{:S(2)}) copy-start(s32[128,128]{1,0:T(8,128)} %mask.3) | copy-start | bytes 196612
  1.9 0.8 %copy-start.8 = (f32[128,128]{1,0:T(8,128)S(1)}, f32[128,128]{1,0:T(8,128)}, u32[]{:S(2)}) copy-start(f32[128,128]{1,0:T(8,128)} %charges.1) | copy-start | bytes 196612
  2.8 0.7 %copy-start.9 = (s32[1,4,16]{2,1,0:T(4,128)S(1)}, s32[1,4,16]{2,1,0:T(4,128)}, u32[]{:S(2)}) copy-start(s32[1,4,16]{2,1,0:T(4,128)} %param.16) | copy-start | bytes 772
  3.4 0.7 %copy-start.12 = (s32[1,4,16]{2,1,0:T(4,128)S(1)}, s32[1,4,16]{2,1,0:T(4,128)}, u32[]{:S(2)}) copy-start(s32[1,4,16]{2,1,0:T(4,128)} %param.15) | copy-start | bytes 772
  4.1 0.7 %copy-start.13 = (s32[1,4,16]{2,1,0:T(4,128)S(1)}, s32[1,4,16]{2,1,0:T(4,128)}, u32[]{:S(2)}) copy-start(s32[1,4,16]{2,1,0:T(4,128)} %param.17) | copy-start | bytes 772
  4.8 13.5 %copy-start.3 = (f32[128,4,256]{2,1,0:T(4,128)S(1)}, f32[128,4,256]{2,1,0:T(4,128)}, u32[]{:S(2)}) copy-start(f32[128,4,256]{2,1,0:T(4,128)} %geo.5) | copy-start | bytes 1572868
  4.8 27.4 %copy-start.11 = (s32[16,8]{0,1:T(8,128)S(1)}, s32[16,8]{0,1:T(8,128)}, u32[]{:S(2)}) copy-start(s32[16,8]{0,1:T(8,128)} %param.22) | copy-start | bytes 1540
  5.6 12.6 %collective-permute-start = (f32[128,128]{1,0:T(8,128)S(1)}, f32[128,128]{1,0:T(8,128)S(1)}, u32[]{:S(2)}, u32[]{:S(2)}) collective-permute-start(f32[128,128]{1,0:T(8,128)S(1)} %get-tuple-element.15.masked.rest_0_), channel_id=1, source_target_pairs={{0,2},{2,0},{1,3},{3,1},{4,6},{6,4},{5,7},{7,5},{8,10},{10,8},{9,1... | collective-permute-start | bytes 196616 | tf_op jit(solution)/shard_map/ppermute | solution.py:479
  8.6 9.6 %collective-permute-start.1 = (f32[88,128]{1,0:T(8,128)S(1)}, f32[88,128]{1,0:T(8,128)S(1)}, u32[]{:S(2)}, u32[]{:S(2)}) collective-permute-start(f32[88,128]{1,0:T(8,128)S(1)} %get-tuple-element.16), channel_id=1, source_target_pairs={{0,4},{4,8},{8,12},{12,0},{1,5},{5,9},{9,13},{13,1},{2,6},{6,10},{... | collective-permute-start | bytes 135176 | tf_op jit(solution)/shard_map/ppermute | solution.py:479
  10.2 8.0 %collective-permute-start.2 = (f32[88,128]{1,0:T(8,128)S(1)}, f32[88,128]{1,0:T(8,128)S(1)}, u32[]{:S(2)}, u32[]{:S(2)}) collective-permute-start(f32[88,128]{1,0:T(8,128)S(1)} %get-tuple-element.17), channel_id=1, source_target_pairs={{0,8},{4,12},{8,0},{12,4},{1,9},{5,13},{9,1},{13,5},{2,10},{6,14},... | collective-permute-start | bytes 135176 | tf_op jit(solution)/shard_map/ppermute | solution.py:479
  12.8 5.4 %collective-permute-start.3 = (f32[88,128]{1,0:T(8,128)S(1)}, f32[88,128]{1,0:T(8,128)S(1)}, u32[]{:S(2)}, u32[]{:S(2)}) collective-permute-start(f32[88,128]{1,0:T(8,128)S(1)} %get-tuple-element.18), channel_id=1, source_target_pairs={{0,12},{4,0},{8,4},{12,8},{1,13},{5,1},{9,5},{13,9},{2,14},{6,2},{... | collective-permute-start | bytes 135176 | tf_op jit(solution)/shard_map/ppermute | solution.py:479
  14.2 1.6 %copy-start = (f32[128,128,32]{1,2,0:T(8,128)S(1)}, f32[128,128,32]{1,2,0:T(8,128)}, u32[]{:S(2)}) copy-start(f32[128,128,32]{1,2,0:T(8,128)} %param.19) | copy-start | bytes 6291460
  15.8 1.0 %copy-start.5 = (f32[128,32,32]{0,2,1:T(8,128)S(1)}, f32[128,32,32]{0,2,1:T(8,128)}, u32[]{:S(2)}) copy-start(f32[128,32,32]{0,2,1:T(8,128)} %param.20) | copy-start | bytes 1572868
  16.8 0.7 %copy-start.14 = (s32[128]{0:T(128)S(1)}, s32[128]{0:T(128)}, u32[]{:S(2)}) copy-start(s32[128]{0:T(128)} %param.21) | copy-start | bytes 1540
  17.5 14.7 %copy-start.4 = (f32[16,8,32,32]{3,2,1,0:T(8,128)S(1)}, f32[16,8,32,32]{3,2,1,0:T(8,128)}, u32[]{:S(2)}) copy-start(f32[16,8,32,32]{3,2,1,0:T(8,128)} %coupling.1) | copy-start | bytes 1572868
  18.2 41.5 %copy-start.1 = (f32[128,128,32]{1,2,0:T(8,128)S(1)}, f32[128,128,32]{1,2,0:T(8,128)}, u32[]{:S(2)}) copy-start(f32[128,128,32]{1,2,0:T(8,128)} %param.19) | copy-start | bytes 6291460
  18.2 41.5 %copy-start.7 = (s32[128,128]{1,0:T(8,128)S(1)}, s32[128,128]{1,0:T(8,128)}, u32[]{:S(2)}) copy-start(s32[128,128]{1,0:T(8,128)} %mask.3) | copy-start | bytes 196612
  24.4 3.8 %collective-permute-start.4 = (f32[32,128]{1,0:T(8,128)S(1)}, f32[32,128]{1,0:T(8,128)S(1)}, u32[]{:S(2)}, u32[]{:S(2)}) collective-permute-start(f32[32,128]{1,0:T(8,128)S(1)} %get-tuple-element.20), channel_id=1, source_target_pairs={{0,12},{4,0},{8,4},{12,8},{1,13},{5,1},{9,5},{13,9},{2,14},{6,2},{... | collective-permute-start | bytes 49160 | tf_op jit(solution)/shard_map/ppermute | solution.py:479
  25.5 4.6 %collective-permute-start.5 = (f32[32,128]{1,0:T(8,128)S(1)}, f32[32,128]{1,0:T(8,128)S(1)}, u32[]{:S(2)}, u32[]{:S(2)}) collective-permute-start(f32[32,128]{1,0:T(8,128)S(1)} %get-tuple-element.21), channel_id=1, source_target_pairs={{0,8},{4,12},{8,0},{12,4},{1,9},{5,13},{9,1},{13,5},{2,10},{6,14},... | collective-permute-start | bytes 49160 | tf_op jit(solution)/shard_map/ppermute | solution.py:479
  26.6 5.5 %collective-permute-start.6 = (f32[32,128]{1,0:T(8,128)S(1)}, f32[32,128]{1,0:T(8,128)S(1)}, u32[]{:S(2)}, u32[]{:S(2)}) collective-permute-start(f32[32,128]{1,0:T(8,128)S(1)} %get-tuple-element.22), channel_id=1, source_target_pairs={{0,4},{4,8},{8,12},{12,0},{1,5},{5,9},{9,13},{13,1},{2,6},{6,10},{... | collective-permute-start | bytes 49160 | tf_op jit(solution)/shard_map/ppermute | solution.py:479
  53.1 2.2 %collective-permute-start.7 = (f32[160,128]{1,0:T(8,128)S(1)}, f32[160,128]{1,0:T(8,128)S(1)}, u32[]{:S(2)}, u32[]{:S(2)}) collective-permute-start(f32[160,128]{1,0:T(8,128)S(1)} %get-tuple-element.23.rest_0_), channel_id=1, source_target_pairs={{0,1},{1,0},{2,3},{3,2},{4,5},{5,4},{6,7},{7,6},{8,9},{9,8},{10,11... | collective-permute-start | bytes 245768 | tf_op jit(solution)/shard_map/ppermute | solution.py:479
  53.2 4.2 %collective-permute-start.9 = (f32[160,128]{1,0:T(8,128)S(1)}, f32[160,128]{1,0:T(8,128)S(1)}, u32[]{:S(2)}, u32[]{:S(2)}) collective-permute-start(f32[160,128]{1,0:T(8,128)S(1)} %get-tuple-element.24), channel_id=1, source_target_pairs={{0,3},{1,2},{2,1},{3,0},{4,7},{5,6},{6,5},{7,4},{8,11},{9,10},{10,... | collective-permute-start | bytes 245768 | tf_op jit(solution)/shard_map/ppermute | solution.py:479
  53.8 5.9 %collective-permute-start.8 = (f32[160,128]{1,0:T(8,128)S(1)}, f32[160,128]{1,0:T(8,128)S(1)}, u32[]{:S(2)}, u32[]{:S(2)}) collective-permute-start(f32[160,128]{1,0:T(8,128)S(1)} %get-tuple-element.24), channel_id=1, source_target_pairs={{0,2},{1,3},{2,0},{3,1},{4,6},{5,7},{6,4},{7,5},{8,10},{9,11},{10,... | collective-permute-start | bytes 245768 | tf_op jit(solution)/shard_map/ppermute | solution.py:479

commit v13 on v12

--- a/solution.py
+++ b/solution.py
@@ -13,7 +13,14 @@
 ROWS = 40
 USED = 34
 LANES = 128
-PARAMS = pltpu.CompilerParams(vmem_limit_bytes=44 * 1024 * 1024)
+
+
+def limit(mib):
+    return pltpu.CompilerParams(vmem_limit_bytes=mib * 1024 * 1024)
+
+
+def about(us):
+    return pl.CostEstimate(flops=0, bytes_accessed=int(us * 3.5e6), transcendentals=0)
 
 
 def vmem():
@@ -103,6 +110,20 @@
 
 def contract(left, right):
     return jnp.dot(left, right, preferred_element_type=F32)
+
+
+def select_rows(index, value, count):
+    row = lax.broadcasted_iota(jnp.int32, (count, index.shape[1]), 0)
+    left = jnp.where(row == index, 1.0, 0.0).astype(BF16)
+    high = value.astype(BF16)
+    rest = value - high.astype(F32)
+    mid = rest.astype(BF16)
+    low = (rest - mid.astype(F32)).astype(BF16)
+    return jnp.dot(
+        jnp.concatenate([left] * 3, axis=1),
+        jnp.concatenate([high, mid, low], axis=0),
+        preferred_element_type=F32,
+    )
 
 
 def upright(row):
@@ -290,25 +311,26 @@
         sends[shift][slots:, :rank] = up[...]
 
 
-def local_kernel(
-    sizes, geo, pairs, targets, far_list, coupling, transfer, parent, up, acc_in, *rest
-):
-    C, S, L, R, slots, clusters, panels = sizes
-    pieces = rest[:S]
-    sums = rest[S : S + C - 1]
-    parts = rest[S + C - 1 : 2 * S + C - 1]
-    q, acc, acct, fa0, fa1, fb0, fb1, rads, got, parents, rows, *ring = rest[2 * S + C - 1 :]
-    fa, fb = (fa0, fa1), (fb0, fb1)
-    me, sub, rep = lax.axis_index("clu"), lax.axis_index("sub"), lax.axis_index("rep")
-    assemble(sub, S, L, q, pieces)
-    acc[...] = jnp.zeros_like(acc)
-    acct[...] = jnp.zeros_like(acct)
+def feature_kernel(geo, fa0, fa1, fb0, fb1, diag, scale):
     points = [geo[:, k, :] for k in range(4)]
     centre, inv = frame([points])
     left, right, rad = split_features(points, centre, inv)
-    store_features(fa, left)
-    store_features(fb, right)
-    rads[...] = rad
+    store_features((fa0, fa1), left)
+    store_features((fb0, fb1), right)
+    diag[...] = lax.rsqrt(2.0 * (rad * rad))
+    scale[...] = jnp.full(scale.shape, inv, F32)
+
+
+def local_kernel(sizes, geo_pairs, pairs, fa0, fa1, fb0, fb1, diags, scale, acc_in, *rest):
+    S, L, R, clusters, panels = sizes
+    pieces = rest[:S]
+    acc_out, q, acc, self_sums, pair_sums, *ring = rest[S:]
+    fa, fb = (fa0, fa1), (fb0, fb1)
+    sub, rep = lax.axis_index("sub"), lax.axis_index("rep")
+    assemble(sub, S, L, q, pieces)
+    acc[...] = jnp.zeros_like(acc)
+    self_sums[...] = jnp.zeros_like(self_sums)
+    pair_sums[...] = jnp.zeros_like(pair_sums)
 
     half = panels // 2
     share = clusters // (S * R)
@@ -325,8 +347,7 @@
         c = first + i
         qrow = q[pl.ds(c, 1), :]
         qcol = upright(qrow[:, :half])
-        radius = rads[pl.ds(c, 1), :]
-        diag = lax.rsqrt(2.0 * (radius * radius))
+        diag = diags[pl.ds(c, 1), :]
         back = [jnp.zeros((8, LANES), F32)]
 
         def eye(span):
@@ -352,7 +373,7 @@
             return jnp.sum(part, axis=1, keepdims=True)
 
         def store(span, held):
-            put_column(acct, span, i, held)
+            put_column(self_sums, span, c, held)
 
         staged(spans_of(panels), root, sums, store)
         back = jnp.sum(back[0], axis=0, keepdims=True)
@@ -370,22 +391,26 @@
     def finish(i, dist):
         ia, ib = pairs[0, start + i], pairs[1, start + i]
         acc[pl.ds(ib, 1), :] += tile_sums(
-            dist, q[pl.ds(ib, 1), :], q[pl.ds(ia, 1), :], acct, share + i
+            dist, q[pl.ds(ib, 1), :], q[pl.ds(ia, 1), :], pair_sums, start + i
         )
 
     pipeline(count, begin, finish, ring[: ring_size(count)])
-    rows[...] = acct[...].T
-    for i in range(share):
-        acc[pl.ds(first + i, 1), :] += rows[i : i + 1, :]
-    for i in range(count):
-        acc[pl.ds(pairs[0, start + i], 1), :] += rows[share + i : share + i + 1, :]
-    total = acc_in[...] + acc[...] * inv
-
-    got[...] = jnp.zeros_like(got)
-    for shift in range(1, C):
-        dest = lax.rem(me + shift, C)
-        for j in range(slots):
-            got[pl.ds(targets[dest, j], 1), :] += sums[shift - 1][j : j + 1, :]
+    total = acc[...] + self_sums[...].T
+    width = geo_pairs.shape[1]
+    total = total + select_rows(geo_pairs[0:1, :], pair_sums[...].T[:width, :], clusters)
+    acc_out[...] = acc_in[...] + total * scale[0:1, 0:1]
+
+
+def merge_kernel(sizes, far_list, targets, near, coupling, transfer, parent, up, *rest):
+    C, S, L, slots, clusters = sizes
+    sums = rest[: C - 1]
+    parts = rest[C - 1 : C - 1 + S]
+    parents = rest[-1]
+    me, sub = lax.axis_index("clu"), lax.axis_index("sub")
+    index = [targets[pl.ds(lax.rem(me + shift, C), 1), :] for shift in range(1, C)]
+    got = select_rows(
+        jnp.concatenate(index, axis=1), jnp.concatenate([v[:slots, :] for v in sums], axis=0), clusters
+    )
 
     par_dev, far_n, rank = coupling.shape[0], coupling.shape[1], coupling.shape[2]
     parents[pl.ds(pl.multiple_of(me * par_dev, 8), par_dev), :] = up[...]
@@ -409,8 +434,8 @@
     def give(s):
         for shift in range(S):
             other = (s + shift) % S
-            part = total[:, other * L : (other + 1) * L]
-            parts[shift][:clusters, :] = part + got[...] if shift == 0 else part
+            part = near[:, other * L : (other + 1) * L]
+            parts[shift][:clusters, :] = part + got if shift == 0 else part
             for t in range(clusters // L):
                 at = clusters + t * rank
                 parts[shift][at : at + rank, :] = fields[:, t * L : (t + 1) * L]
@@ -419,7 +444,8 @@
         pl.when(sub == s)(functools.partial(give, s))
 
 
-def up_kernel(basis, masked, transfer, parent, up):
+def up_kernel(basis, masked, transfer, parent, after, up):
+    del after
     clusters = basis.shape[0]
     rank = basis.shape[1]
     lane = lax.broadcasted_iota(jnp.int32, (rank, clusters), 1)
@@ -437,21 +463,14 @@
     )
 
 
-def final_kernel(sizes, mask, basis, *rest):
-    S, R, L = sizes
-    near, out = rest[: S * R], rest[-1]
+def far_kernel(basis, near, out):
     clusters, rank = basis.shape[0], basis.shape[1]
-    fields = []
-    for t in range(clusters // L):
-        rows = slice(clusters + t * rank, clusters + (t + 1) * rank)
-        fields.append(sum(near[d * R][rows, :] for d in range(1, S)) + near[0][rows, :])
+    L = out.shape[1]
+    fields = [near[clusters + t * rank : clusters + (t + 1) * rank, :] for t in range(clusters // L)]
     fields = jnp.concatenate(fields, axis=1) if len(fields) > 1 else fields[0]
     for c in range(clusters):
-        out[c : c + 1, :] = jnp.sum(basis[c] * fields[:, c : c + 1], axis=0, keepdims=True)
-    total = out[...]
-    for part in near:
-        total = total + part[:clusters, :]
-    out[...] = total * mask[...].astype(F32)
+        far = jnp.sum(basis[c] * fields[:, c : c + 1], axis=0, keepdims=True)
+        out[c : c + 1, :] = far + near[c : c + 1, :]
 
 
 def send(value, moves):
@@ -510,21 +529,34 @@
         out_shape=[pltpu.VMEM((clusters, L), F32)] + [pltpu.VMEM((5 * slots + 8, L), F32)] * (C - 1),
         in_specs=[vmem()] * 3 + [smem()] * 3,
         out_specs=[vmem()] * C,
-        compiler_params=PARAMS,
+        compiler_params=limit(60),
+        cost_estimate=about(2),
         name="packs",
-    )(*near_by(charges, panel_mask, geometry), targets, remote_source[0], remote_live[0])
+    )(charges, panel_mask, geometry, targets, remote_source[0], remote_live[0])
     masked, packs = made[0], made[1:]
     pieces = [masked] + [send(masked, (("sub", d),)) for d in range(1, S)]
     packs = [send(packs[d - 1], (("clu", d),)) for d in range(1, C)]
 
+    features = pl.pallas_call(
+        feature_kernel,
+        out_shape=[pltpu.VMEM((clusters * ROWS, LANES), F32)] * 4
+        + [pltpu.VMEM((clusters, panels), F32), pltpu.VMEM((8, LANES), F32)],
+        in_specs=[vmem()],
+        out_specs=[vmem()] * 6,
+        compiler_params=limit(32),
+        cost_estimate=about(4),
+        name="features",
+    )(*near_by(geometry))
+
     up = pl.pallas_call(
         up_kernel,
         out_shape=pltpu.VMEM((par_dev, rank), F32),
-        in_specs=[vmem()] * 4,
+        in_specs=[vmem()] * 5,
         out_specs=vmem(),
-        compiler_params=PARAMS,
+        compiler_params=limit(16),
+        cost_estimate=about(1),
         name="far_up",
-    )(*near_by(basis_t, masked, transfer_t, parent))
+    )(*near_by(basis_t, masked, transfer_t, parent, features[5]))
 
     made = pl.pallas_call(
         functools.partial(remote_kernel, (C, S, L, slots, clusters, panels)),
@@ -546,52 +578,57 @@
             pltpu.SemaphoreType.DMA((C - 1,)),
         ]
         + [pltpu.VMEM((L, panels), F32)] * 8,
-        compiler_params=PARAMS,
+        compiler_params=limit(24),
+        cost_estimate=about(6),
         name="near_remote",
     )(*near_by(geometry, up, *pieces, *packs))
     acc, sums = made[0], [send(made[d], (("clu", C - d),)) for d in range(1, C)]
 
-    columns = whole(clusters // (S * R) + local_pairs.shape[1] // S)
-    half = [pltpu.VMEM((clusters * ROWS, LANES), F32)] * 2
-    parts = pl.pallas_call(
-        functools.partial(local_kernel, (C, S, L, R, slots, clusters, panels)),
-        out_shape=[pltpu.VMEM((clusters + clusters // L * rank, L), F32)] * S,
-        in_specs=[vmem()] + [smem()] * 3 + [vmem()] * (5 + S + C - 1),
-        out_specs=[vmem()] * S,
+    wide = whole(local_pairs.shape[1])
+    acc = pl.pallas_call(
+        functools.partial(local_kernel, (S, L, R, clusters, panels)),
+        out_shape=pltpu.VMEM((clusters, panels), F32),
+        in_specs=[vmem(), smem()] + [vmem()] * (7 + S),
+        out_specs=vmem(),
         scratch_shapes=[
             pltpu.VMEM((clusters, panels), F32),
             pltpu.VMEM((clusters, panels), F32),
-            pltpu.VMEM((panels, columns), F32),
-            *half,
-            *half,
-            pltpu.VMEM((clusters, panels), F32),
-            pltpu.VMEM((clusters, L), F32),
-            pltpu.VMEM((C * par_dev, rank), F32),
-            pltpu.VMEM((columns, panels), F32),
+            pltpu.VMEM((panels, clusters), F32),
+            pltpu.VMEM((panels, wide), F32),
         ]
         + [pltpu.VMEM((panels, panels), F32)] * 16,
-        compiler_params=PARAMS,
+        compiler_params=limit(24),
+        cost_estimate=about(15),
         name="near_local",
-    )(
-        *near_by(geometry),
-        local_pairs[0].T,
-        targets,
-        far_list.T,
-        *near_by(coupling, transfer_t, parent, up, acc, *pieces, *sums),
-    )
-    near = []
-    for d in range(S):
-        for e in range(R):
-            near.append(send(parts[d], (("sub", d), ("rep", e))) if d or e else parts[0])
-
-    return pl.pallas_call(
-        functools.partial(final_kernel, (S, R, L)),
-        out_shape=shape((clusters, L), F32),
-        in_specs=[vmem()] * (2 + S * R),
+    )(*near_by(local_pairs[0].T), local_pairs[0].T, *near_by(*features, acc, *pieces))
+
+    parts = pl.pallas_call(
+        functools.partial(merge_kernel, (C, S, L, slots, clusters)),
+        out_shape=[pltpu.VMEM((clusters + clusters // L * rank, L), F32)] * S,
+        in_specs=[smem()] + [vmem()] * (6 + C - 1),
+        out_specs=[vmem()] * S,
+        scratch_shapes=[pltpu.VMEM((C * par_dev, rank), F32)],
+        compiler_params=limit(16),
+        cost_estimate=about(2),
+        name="merge",
+    )(far_list.T, *near_by(targets, acc, coupling, transfer_t, parent, up, *sums))
+    near = parts[0]
+    for d in range(1, S):
+        near = near + send(parts[d], (("sub", d),))
+    others = [send(near, (("rep", e),)) for e in range(1, R)]
+
+    total = pl.pallas_call(
+        far_kernel,
+        out_shape=pltpu.VMEM((clusters, L), F32),
+        in_specs=[vmem()] * 2,
         out_specs=vmem(),
-        compiler_params=PARAMS,
-        name="combine",
-    )(*near_by(panel_mask, basis_t, *near))
+        compiler_params=limit(16),
+        cost_estimate=about(1),
+        name="far_down",
+    )(*near_by(basis_t, near))
+    for other in others:
+        total = total + other[:clusters]
+    return total * panel_mask.astype(F32)
 
 
 def solution(mesh):

time: 61.6 us -> 52.2 us (0.85)
  waiting for transfers between devices: 9.76 us -> 4.56 us
  local copies, waits for them, and re-layouts: 8.1 us -> 4.36 us
  starting transfers between devices: 13.1 us -> 11.4 us
  Pallas kernels: 30.1 us -> 30.8 us
  other arithmetic: 0 us -> 0.65 us
    ppermute x10 -> x9, waiting for transfers between devices: 9.76 us -> 4.56 us  [send(): return lax.ppermute(value, names if len(names) > 1 else names[0], perm)]
    unnamed x32 -> x24, local copies, waits for them, and re-layouts: 8.1 us -> 4.36 us
    ppermute x10 -> x9, starting transfers between devices: 13.1 us -> 11.4 us  [send(): return lax.ppermute(value, names if len(names) > 1 else names[0], perm)]
    mul x0 -> x1, other arithmetic: none -> 0.64 us  [on_device(): return total * panel_mask.astype(F32)]
    pallas_call x2 -> x4, Pallas kernels: 22.4 us -> 22.5 us  [the longest x1 14.9 us: on_device(): pl.pallas_call(functools.partial(local_kernel, (S, L, R, clusters, panels...]
  transfers between devices with their start and end apart: 10 -> 9, of which waited for: 5 -> 2; matrix products, arithmetic and copies ran while one was open for 0% -> 0% of each run, Pallas kernels for 1% -> 42%
where the time goes in v13:
time: 52.2 us; the launch traced here: 51.9 us
  Pallas kernels  30.8 us (59%)
  starting transfers between devices  11.4 us (22%)
  waiting for transfers between devices  4.56 us (9%)
  local copies, waits for them, and re-layouts  4.36 us (8%)
  other arithmetic  0.65 us (1%)
    pallas_call x1, Pallas kernels, on_device(): pl.pallas_call(functools.partial(local_kernel, (S, L, R, clusters, panels...  14.9 us
    ppermute x9, starting transfers between devices, send(): return lax.ppermute(value, names if len(names) > 1 else names[0], perm)  11.4 us
    pallas_call x1, Pallas kernels, on_device(): pl.pallas_call(functools.partial(remote_kernel, (C, S, L, slots, clusters...  6.16 us
    pallas_call x1, Pallas kernels, on_device(): pl.pallas_call(feature_kernel, out_shape=[pltpu.VMEM((clusters * ROWS, LA...  5.51 us
    ppermute x9, waiting for transfers between devices, send(): return lax.ppermute(value, names if len(names) > 1 else names[0], perm)  4.56 us
    unnamed x24, local copies, waits for them, and re-layouts  4.36 us
    pallas_call x1, Pallas kernels, on_device(): pl.pallas_call(functools.partial(pack_kernel, (C, S, L, slots)), out_shap...  1.35 us
    pallas_call x1, Pallas kernels, on_device(): pl.pallas_call(functools.partial(merge_kernel, (C, S, L, slots, clusters)...  1.26 us
  transfers between devices with their start and end apart: 9, of which 2 were waited for; matrix products, arithmetic and copies ran while one was open for 0% of the time, Pallas kernels for 42%

profile of v13, /device:TPU:0, one launch (start us, length us, event | category | flops | bytes accessed | tf_op | source)
XLA Modules:
  0.0 51.9 jit_solution(360446255805987018)
XLA Ops:
  0.0 0.0 copy-start.8
  0.0 1.4 %packs.1 = (f32[128,128]{1,0:T(8,128)S(1)}, f32[88,128]{1,0:T(8,128)S(1)}, f32[88,128]{1,0:T(8,128)S(1)}, f32[88,128]{1,0:T(8,128)S(1)}) custom-call(f32[128,128]{1,0:T(8,128)} %charges.1, s32[128,128]{1,0:T(8,128)} %mask.1, f32[128,4,256]{2,1,0:T(4,128)} %geo.5, s32[4,16]{1,0:T(4,128)} %bitcast.14, s32[4,16]{1,0:T(4,128)} %bitcast.21, s32[4,16]{1,0:T(4,128)} %bitcast.22), custom_call_target="tpu_custom_call" | custom-call | bytes 7000000 | tf_op jit(solution)/shard_map/packs/pallas_call | solution.py:527
  1.4 3.0 %collective-permute-start = (f32[128,128]{1,0:T(8,128)S(1)}, f32[128,128]{1,0:T(8,128)S(1)}, u32[]{:S(2)}, u32[]{:S(2)}) collective-permute-start(f32[128,128]{1,0:T(8,128)S(1)} %get-tuple-element.27.masked.rest_0_), channel_id=1, source_target_pairs={{0,2},{2,0},{1,3},{3,1},{4,6},{6,4},{5,7},{7,5},{8,10},{10,8},{9,1... | collective-permute-start | bytes 196616 | tf_op jit(solution)/shard_map/ppermute | solution.py:498
  4.4 1.6 %collective-permute-start.1 = (f32[88,128]{1,0:T(8,128)S(1)}, f32[88,128]{1,0:T(8,128)S(1)}, u32[]{:S(2)}, u32[]{:S(2)}) collective-permute-start(f32[88,128]{1,0:T(8,128)S(1)} %get-tuple-element.28), channel_id=1, source_target_pairs={{0,4},{4,8},{8,12},{12,0},{1,5},{5,9},{9,13},{13,1},{2,6},{6,10},{... | collective-permute-start | bytes 135176 | tf_op jit(solution)/shard_map/ppermute | solution.py:498
  5.9 2.6 %collective-permute-start.2 = (f32[88,128]{1,0:T(8,128)S(1)}, f32[88,128]{1,0:T(8,128)S(1)}, u32[]{:S(2)}, u32[]{:S(2)}) collective-permute-start(f32[88,128]{1,0:T(8,128)S(1)} %get-tuple-element.29), channel_id=1, source_target_pairs={{0,8},{4,12},{8,0},{12,4},{1,9},{5,13},{9,1},{13,5},{2,10},{6,14},... | collective-permute-start | bytes 135176 | tf_op jit(solution)/shard_map/ppermute | solution.py:498
  8.5 1.3 %collective-permute-start.3 = (f32[88,128]{1,0:T(8,128)S(1)}, f32[88,128]{1,0:T(8,128)S(1)}, u32[]{:S(2)}, u32[]{:S(2)}) collective-permute-start(f32[88,128]{1,0:T(8,128)S(1)} %get-tuple-element.30), channel_id=1, source_target_pairs={{0,12},{4,0},{8,4},{12,8},{1,13},{5,1},{9,5},{13,9},{2,14},{6,2},{... | collective-permute-start | bytes 135176 | tf_op jit(solution)/shard_map/ppermute | solution.py:498
  9.9 0.0 copy-start.2
  9.9 1.0 %copy-done.2 = f32[128,4,256]{2,1,0:T(4,128)S(1)} copy-done((f32[128,4,256]{2,1,0:T(4,128)S(1)}, f32[128,4,256]{2,1,0:T(4,128)}, u32[]{:S(2)}) %copy-start.2) | copy-done | bytes 524312
  10.9 5.5 %features.1 = (f32[5120,128]{1,0:T(8,128)S(1)}, f32[5120,128]{1,0:T(8,128)S(1)}, f32[5120,128]{1,0:T(8,128)S(1)}, f32[5120,128]{1,0:T(8,128)S(1)}, f32[128,256]{1,0:T(8,128)S(1)}, /*index=5*/f32[8,128]{1,0:T(8,128)S(1)}) custom-call(f32[128,4,256]{2,1,0:T(4,128)S(1)} %copy-done.2), custom_call_target="tpu_custom_call" | custom-call | bytes 14000000 | tf_op jit(solution)/shard_map/features/pallas_call | solution.py:540
  16.4 0.0 copy-start
  16.5 1.6 %copy-done = f32[128,128,32]{1,2,0:T(8,128)S(1)} copy-done((f32[128,128,32]{1,2,0:T(8,128)S(1)}, f32[128,128,32]{1,2,0:T(8,128)}, u32[]{:S(2)}) %copy-start) | copy-done | bytes 2097176
  18.0 0.0 copy-start.4
  18.0 1.0 %copy-done.4 = f32[128,32,32]{0,2,1:T(8,128)S(1)} copy-done((f32[128,32,32]{0,2,1:T(8,128)S(1)}, f32[128,32,32]{0,2,1:T(8,128)}, u32[]{:S(2)}) %copy-start.4) | copy-done | bytes 524312
  19.1 0.0 copy-start.9
  19.1 0.7 %copy-done.9 = s32[128]{0:T(128)S(1)} copy-done((s32[128]{0:T(128)S(1)}, s32[128]{0:T(128)}, u32[]{:S(2)}) %copy-start.9) | copy-done | bytes 536
  19.7 0.8 %far_up.1.up = f32[16,32]{1,0:T(8,128)S(1)} custom-call(f32[128,32,128]{2,1,0:T(8,128)S(1)} %bitcast.10, f32[128,128]{1,0:T(8,128)S(1)} %get-tuple-element.27.masked.rest_0_, f32[32,32,128]{2,1,0:T(8,128)S(1)} %bitcast.12, s32[1,128]{1,0:T(1,128)S(1)} %bitcast.19, f32[8,128]{1,0:T(8,128)S(1)} %get-tuple-element.26.after.scale), custom_call_target="tpu_custom_call" | custom-call | bytes 3500000 | tf_op jit(solution)/shard_map/far_up/pallas_call | solution.py:551
  20.5 0.0 collective-permute-done.1.rest_2_
  20.5 0.0 collective-permute-done.2.rest_3_
  20.5 0.0 collective-permute-done.3.rest_4_
  20.5 0.0 collective-permute-done.rest_1_
  20.5 6.2 %near_remote.1 = (f32[128,256]{1,0:T(8,128)S(1)}, f32[32,128]{1,0:T(8,128)S(1)}, f32[32,128]{1,0:T(8,128)S(1)}, f32[32,128]{1,0:T(8,128)S(1)}) custom-call(f32[128,4,256]{2,1,0:T(4,128)S(1)} %copy-done.2, f32[16,32]{1,0:T(8,128)S(1)} %far_up.1.up, f32[128,128]{1,0:T(8,128)S(1)} %get-tuple-element.27.masked.rest_0_, ...), custom_call_target="tpu_custom_call" | custom-call | bytes 21000000 | tf_op jit(solution)/shard_map/near_remote/pallas_call | solution.py:561
  26.7 0.5 collective-permute-start.4
  27.2 1.7 %collective-permute-start.5 = (f32[32,128]{1,0:T(8,128)S(1)}, f32[32,128]{1,0:T(8,128)S(1)}, u32[]{:S(2)}, u32[]{:S(2)}) collective-permute-start(f32[32,128]{1,0:T(8,128)S(1)} %get-tuple-element.33), channel_id=1, source_target_pairs={{0,8},{4,12},{8,0},{12,4},{1,9},{5,13},{9,1},{13,5},{2,10},{6,14},... | collective-permute-start | bytes 49160 | tf_op jit(solution)/shard_map/ppermute | solution.py:498
  28.9 0.2 collective-permute-start.6
  29.1 0.0 copy-done.8
  29.1 0.0 copy-start.3
  29.1 0.0 copy-start.7
  29.1 0.0 copy-start.10
  29.1 14.9 %near_local.1.near = f32[128,256]{1,0:T(8,128)S(1)} custom-call(s32[2,128]{1,0:T(2,128)S(1)} %bitcast.17, s32[2,128]{1,0:T(2,128)S(1)} %bitcast.18, f32[5120,128]{1,0:T(8,128)S(1)} %get-tuple-element.21.fa0, f32[5120,128]{1,0:T(8,128)S(1)} %get-tuple-element.22.fa1, f32[5120,128]{1,0:T(8,128)S(1)} %get-tuple-element.23.fb0, ...), custom_call_target="tpu_custom_call" | custom-call | bytes 52500000 | tf_op jit(solution)/shard_map/near_local/pallas_call | solution.py:588
  44.0 0.0 copy-start.1
  44.1 0.0 collective-permute-done.4.rest_0_
  44.1 0.0 collective-permute-done.5.rest_1_
  44.1 0.0 collective-permute-done.6.rest_2_
  44.1 0.0 copy-done.3
  44.1 0.0 copy-done.5
  44.1 0.0 copy-done.6
  44.1 0.0 copy-done.7
  44.1 0.0 copy-done.10
  44.1 0.0 copy-start.11
  44.1 1.3 %merge.1 = (f32[160,128]{1,0:T(8,128)S(1)}, f32[160,128]{1,0:T(8,128)S(1)}) custom-call(s32[8,16]{1,0:T(8,128)S(1)} %bitcast.16, s32[4,16]{1,0:T(4,128)S(1)} %bitcast.15, f32[128,256]{1,0:T(8,128)S(1)} %near_local.1.near, f32[16,8,32,32]{3,2,1,0:T(8,128)S(1)} %copy-done.3, f32[32,32,128]{2,1,0:T(8,128)S(1)} %bitcast.13, s32[1,128]{1,0:T(1,128)S(1)} %bitcast.20, ...), custom_call_target="tpu_custom_call" | custom-call | bytes 7000000 | tf_op jit(solution)/shard_map/merge/pallas_call | solution.py:605
  45.4 0.4 collective-permute-start.7
  45.8 4.1 %collective-permute-done.7 = f32[160,128]{1,0:T(8,128)S(1)} collective-permute-done((f32[160,128]{1,0:T(8,128)S(1)}, f32[160,128]{1,0:T(8,128)S(1)}, u32[]{:S(2)}, u32[]{:S(2)}) %collective-permute-start.7) | collective-permute-done | bytes 81952 | tf_op jit(solution)/shard_map/ppermute | solution.py:498
  49.9 0.1 collective-permute-start.8
  50.0 0.0 copy-done.1
  50.0 0.8 %far_down.1 = f32[128,128]{1,0:T(8,128)S(1)} custom-call(f32[128,32,128]{2,1,0:T(8,128)S(1)} %bitcast.11, f32[160,128]{1,0:T(8,128)S(1)} %add.6.near), custom_call_target="tpu_custom_call" | custom-call | bytes 3500000 | tf_op jit(solution)/shard_map/far_down/pallas_call | solution.py:620
  50.9 0.4 collective-permute-done.8
  51.3 0.0 copy-done.11
  51.3 0.6 %fusion = f32[128,128]{1,0:T(8,128)} fusion(f32[128,128]{1,0:T(8,128)S(1)} %far_down.1, f32[160,128]{1,0:T(8,128)S(1)} %collective-permute-done.8, s32[128,128]{1,0:T(8,128)S(1)} %copy-done.11), kind=kLoop, calls=%fused_computation.1 | loop fusion | flops 49152 | bytes 262144 | tf_op jit(solution)/shard_map/mul | solution.py:631
  (3 shorter events, 0.0 us)
Async XLA Ops:
  0.0 29.1 %copy-start.8 = (s32[1,128,2]{1,2,0:T(2,128)S(1)}, s32[1,128,2]{1,2,0:T(2,128)}, u32[]{:S(2)}) copy-start(s32[1,128,2]{1,2,0:T(2,128)} %param.18) | copy-start | bytes 3076
  1.4 19.2 %collective-permute-start = (f32[128,128]{1,0:T(8,128)S(1)}, f32[128,128]{1,0:T(8,128)S(1)}, u32[]{:S(2)}, u32[]{:S(2)}) collective-permute-start(f32[128,128]{1,0:T(8,128)S(1)} %get-tuple-element.27.masked.rest_0_), channel_id=1, source_target_pairs={{0,2},{2,0},{1,3},{3,1},{4,6},{6,4},{5,7},{7,5},{8,10},{10,8},{9,1... | collective-permute-start | bytes 196616 | tf_op jit(solution)/shard_map/ppermute | solution.py:498
  4.4 16.1 %collective-permute-start.1 = (f32[88,128]{1,0:T(8,128)S(1)}, f32[88,128]{1,0:T(8,128)S(1)}, u32[]{:S(2)}, u32[]{:S(2)}) collective-permute-start(f32[88,128]{1,0:T(8,128)S(1)} %get-tuple-element.28), channel_id=1, source_target_pairs={{0,4},{4,8},{8,12},{12,0},{1,5},{5,9},{9,13},{13,1},{2,6},{6,10},{... | collective-permute-start | bytes 135176 | tf_op jit(solution)/shard_map/ppermute | solution.py:498
  5.9 14.5 %collective-permute-start.2 = (f32[88,128]{1,0:T(8,128)S(1)}, f32[88,128]{1,0:T(8,128)S(1)}, u32[]{:S(2)}, u32[]{:S(2)}) collective-permute-start(f32[88,128]{1,0:T(8,128)S(1)} %get-tuple-element.29), channel_id=1, source_target_pairs={{0,8},{4,12},{8,0},{12,4},{1,9},{5,13},{9,1},{13,5},{2,10},{6,14},... | collective-permute-start | bytes 135176 | tf_op jit(solution)/shard_map/ppermute | solution.py:498
  8.5 12.0 %collective-permute-start.3 = (f32[88,128]{1,0:T(8,128)S(1)}, f32[88,128]{1,0:T(8,128)S(1)}, u32[]{:S(2)}, u32[]{:S(2)}) collective-permute-start(f32[88,128]{1,0:T(8,128)S(1)} %get-tuple-element.30), channel_id=1, source_target_pairs={{0,12},{4,0},{8,4},{12,8},{1,13},{5,1},{9,5},{13,9},{2,14},{6,2},{... | collective-permute-start | bytes 135176 | tf_op jit(solution)/shard_map/ppermute | solution.py:498
  9.9 1.0 %copy-start.2 = (f32[128,4,256]{2,1,0:T(4,128)S(1)}, f32[128,4,256]{2,1,0:T(4,128)}, u32[]{:S(2)}) copy-start(f32[128,4,256]{2,1,0:T(4,128)} %geo.5) | copy-start | bytes 1572868
  16.4 1.6 %copy-start = (f32[128,128,32]{1,2,0:T(8,128)S(1)}, f32[128,128,32]{1,2,0:T(8,128)}, u32[]{:S(2)}) copy-start(f32[128,128,32]{1,2,0:T(8,128)} %param.19) | copy-start | bytes 6291460
  18.0 1.0 %copy-start.4 = (f32[128,32,32]{0,2,1:T(8,128)S(1)}, f32[128,32,32]{0,2,1:T(8,128)}, u32[]{:S(2)}) copy-start(f32[128,32,32]{0,2,1:T(8,128)} %param.20) | copy-start | bytes 1572868
  19.1 0.7 %copy-start.9 = (s32[128]{0:T(128)S(1)}, s32[128]{0:T(128)}, u32[]{:S(2)}) copy-start(s32[128]{0:T(128)} %param.21) | copy-start | bytes 1540
  26.7 17.4 %collective-permute-start.4 = (f32[32,128]{1,0:T(8,128)S(1)}, f32[32,128]{1,0:T(8,128)S(1)}, u32[]{:S(2)}, u32[]{:S(2)}) collective-permute-start(f32[32,128]{1,0:T(8,128)S(1)} %get-tuple-element.32), channel_id=1, source_target_pairs={{0,12},{4,0},{8,4},{12,8},{1,13},{5,1},{9,5},{13,9},{2,14},{6,2},{... | collective-permute-start | bytes 49160 | tf_op jit(solution)/shard_map/ppermute | solution.py:498
  27.2 16.9 %collective-permute-start.5 = (f32[32,128]{1,0:T(8,128)S(1)}, f32[32,128]{1,0:T(8,128)S(1)}, u32[]{:S(2)}, u32[]{:S(2)}) collective-permute-start(f32[32,128]{1,0:T(8,128)S(1)} %get-tuple-element.33), channel_id=1, source_target_pairs={{0,8},{4,12},{8,0},{12,4},{1,9},{5,13},{9,1},{13,5},{2,10},{6,14},... | collective-permute-start | bytes 49160 | tf_op jit(solution)/shard_map/ppermute | solution.py:498
  28.9 15.2 %collective-permute-start.6 = (f32[32,128]{1,0:T(8,128)S(1)}, f32[32,128]{1,0:T(8,128)S(1)}, u32[]{:S(2)}, u32[]{:S(2)}) collective-permute-start(f32[32,128]{1,0:T(8,128)S(1)} %get-tuple-element.34), channel_id=1, source_target_pairs={{0,4},{4,8},{8,12},{12,0},{1,5},{5,9},{9,13},{13,1},{2,6},{6,10},{... | collective-permute-start | bytes 49160 | tf_op jit(solution)/shard_map/ppermute | solution.py:498
  29.1 15.0 %copy-start.3 = (f32[16,8,32,32]{3,2,1,0:T(8,128)S(1)}, f32[16,8,32,32]{3,2,1,0:T(8,128)}, u32[]{:S(2)}) copy-start(f32[16,8,32,32]{3,2,1,0:T(8,128)} %coupling.1) | copy-start | bytes 1572868
  29.1 15.0 %copy-start.5 = (f32[128,32,32]{0,2,1:T(8,128)S(1)}, f32[128,32,32]{0,2,1:T(8,128)}, u32[]{:S(2)}) copy-start(f32[128,32,32]{0,2,1:T(8,128)} %param.20) | copy-start | bytes 1572868
  29.1 15.0 %copy-start.6 = (s32[1,4,16]{2,1,0:T(4,128)S(1)}, s32[1,4,16]{2,1,0:T(4,128)}, u32[]{:S(2)}) copy-start(s32[1,4,16]{2,1,0:T(4,128)} %param.16) | copy-start | bytes 772
  29.1 15.0 %copy-start.7 = (s32[16,8]{0,1:T(8,128)S(1)}, s32[16,8]{0,1:T(8,128)}, u32[]{:S(2)}) copy-start(s32[16,8]{0,1:T(8,128)} %param.22) | copy-start | bytes 1540
  29.1 15.0 %copy-start.10 = (s32[128]{0:T(128)S(1)}, s32[128]{0:T(128)}, u32[]{:S(2)}) copy-start(s32[128]{0:T(128)} %param.21) | copy-start | bytes 1540
  44.0 6.0 %copy-start.1 = (f32[128,128,32]{1,2,0:T(8,128)S(1)}, f32[128,128,32]{1,2,0:T(8,128)}, u32[]{:S(2)}) copy-start(f32[128,128,32]{1,2,0:T(8,128)} %param.19) | copy-start | bytes 6291460
  44.1 7.1 %copy-start.11 = (s32[128,128]{1,0:T(8,128)S(1)}, s32[128,128]{1,0:T(8,128)}, u32[]{:S(2)}) copy-start(s32[128,128]{1,0:T(8,128)} %mask.1) | copy-start | bytes 196612
  45.4 4.5 %collective-permute-start.7 = (f32[160,128]{1,0:T(8,128)S(1)}, f32[160,128]{1,0:T(8,128)S(1)}, u32[]{:S(2)}, u32[]{:S(2)}) collective-permute-start(f32[160,128]{1,0:T(8,128)S(1)} %get-tuple-element.36), channel_id=1, source_target_pairs={{0,2},{2,0},{1,3},{3,1},{4,6},{6,4},{5,7},{7,5},{8,10},{10,8},{9,1... | collective-permute-start | bytes 245768 | tf_op jit(solution)/shard_map/ppermute | solution.py:498
  49.9 1.3 %collective-permute-start.8 = (f32[160,128]{1,0:T(8,128)S(1)}, f32[160,128]{1,0:T(8,128)S(1)}, u32[]{:S(2)}, u32[]{:S(2)}) collective-permute-start(f32[160,128]{1,0:T(8,128)S(1)} %add.6.near), channel_id=1, source_target_pairs={{0,1},{1,0},{2,3},{3,2},{4,5},{5,4},{6,7},{7,6},{8,9},{9,8},{10,11... | collective-permute-start | bytes 245768 | tf_op jit(solution)/shard_map/ppermute | solution.py:498

commit v14 on v13

--- a/solution.py
+++ b/solution.py
@@ -10,8 +10,7 @@
 F32 = jnp.float32
 BF16 = jnp.bfloat16
 HIGHEST = lax.Precision.HIGHEST
-ROWS = 40
-USED = 34
+ROWS = 24
 LANES = 128
 
 
@@ -85,14 +84,21 @@
     rest1 = [cut(v) for v in rest]
     rest2 = [v - w for v, w in zip(rest, rest1)]
     neg = lambda vs: [-2.0 * v for v in vs]
-    one = jnp.ones_like(rad)
-    left = grid + [norm1, norm2, one, one]
-    right = neg(grid) + [one, one, norm1, norm2]
-    left += [extra1, extra2, extra3, one, one, one]
-    right += [one, one, one, extra1, extra2, extra3]
-    left += grid + grid + rest1 + rest2 + rest1 + rest1 + rest2
-    right += neg(rest1) + neg(rest2) + neg(grid) + neg(grid) + neg(rest1) + neg(rest2) + neg(rest1)
+    one, zero = jnp.ones_like(rad), jnp.zeros_like(rad)
+    left = grid + [norm1, norm2, one, one, zero]
+    left += rest1 + [extra1, extra2, zero, zero, zero]
+    left += rest2 + [extra3, zero, zero, zero, zero]
+    right = neg(grid) + [one, one, norm1, norm2, zero]
+    right += neg(rest1) + [zero, zero, extra1, extra2, zero]
+    right += neg(rest2) + [zero, zero, extra3, zero, zero]
     return left, right, rad
+
+
+def products(left, right):
+    a, b, c = [left[k : k + 8, :] for k in (0, 8, 16)]
+    x, y, z = [right[k : k + 8, :] for k in (0, 8, 16)]
+    pairs = [(a, x), (b, x), (a, y), (c, x), (a, z), (b, y), (b, z), (c, y)]
+    return [jnp.concatenate(v, axis=0).astype(BF16) for v in zip(*pairs)]
 
 
 def store_features(ref, rows):
@@ -105,7 +111,8 @@
 
 def load_features(ref, index):
     start = pl.multiple_of(index * ROWS, 8)
-    return [piece[pl.ds(start, USED), :].astype(BF16) for piece in ref]
+    blocks = [piece[pl.ds(start, ROWS), :] for piece in ref]
+    return jnp.concatenate(blocks, axis=1) if len(blocks) > 1 else blocks[0]
 
 
 def contract(left, right):
@@ -130,10 +137,21 @@
     return jnp.broadcast_to(row, (8, row.shape[1])).T[:, :1]
 
 
-def put_column(table, rows, index, value):
-    shape = (rows.stop - rows.start, table.shape[1])
+def keep(parts, rows, value):
+    high = value.astype(BF16)
+    parts[rows, :LANES] = high
+    parts[rows, LANES:] = (value - high.astype(F32)).astype(BF16)
+
+
+def add_columns(table, parts, indices):
+    shape = (2 * LANES, table.shape[1])
     lane = lax.broadcasted_iota(jnp.int32, shape, 1)
-    pltpu.store(table.at[rows, :], jnp.broadcast_to(value, shape), mask=lane == index)
+    picks = [jnp.where(lane == index, 1.0, 0.0).astype(BF16) for index in indices]
+    table[...] += jnp.dot(
+        jnp.concatenate([p[...] for p in parts], axis=1),
+        jnp.concatenate(picks, axis=0),
+        preferred_element_type=F32,
+    )
 
 
 def inverse_root(d):
@@ -145,8 +163,8 @@
 
 
 def distances(left, right, out):
-    whole_left = jnp.concatenate(left, axis=1) if len(left) > 1 else left[0]
-    out[...] = contract(whole_left.T, jnp.concatenate(right, axis=1))
+    left, right = products(left, right)
+    out[...] = contract(left.T, right)
 
 
 def staged(spans, *stages):
@@ -165,7 +183,7 @@
     return [slice(r, r + step) for r in range(0, height, step)]
 
 
-def tile_sums(dist, qrow, qleft, table, index):
+def tile_sums(dist, qrow, qleft, parts):
     q0, q1 = qrow[:, :LANES], qrow[:, LANES:]
     qcol = upright(qleft)
     back = [jnp.zeros((8, LANES), F32), jnp.zeros((8, LANES), F32)]
@@ -180,23 +198,26 @@
         g0, g1 = held
         back[0] = back[0] + fold(g0 * qcol[rows, :])
         back[1] = back[1] + fold(g1 * qcol[rows, :])
-        return jnp.sum(g0 * q0 + g1 * q1, axis=1, keepdims=True)
-
-    def store(rows, held):
-        put_column(table, rows, index, held)
-
-    staged(spans_of(dist.shape[0]), root, sums, store)
+        keep(parts, rows, g0 * q0 + g1 * q1)
+
+    staged(spans_of(dist.shape[0]), root, sums)
     return jnp.concatenate([jnp.sum(b, axis=0, keepdims=True) for b in back], axis=1)
 
 
-def pipeline(total, begin, finish, ring):
+def pipeline(total, begin, finish, table, ring, parts):
     size = len(ring)
     ahead = min(2, size - 1)
+    group = min(2, size)
 
     def body(i, carry):
+        indices = []
         for k in range(size):
             begin(i * size + k + ahead, ring[(k + ahead) % size])
-            finish(i * size + k, ring[k])
+            indices.append(finish(i * size + k, ring[k], parts[k % len(parts)]))
+            if len(indices) == group:
+                done = [parts[(k - n) % len(parts)] for n in reversed(range(group))]
+                add_columns(table, done, indices)
+                indices = []
         return carry
 
     for k in range(ahead):
@@ -218,10 +239,11 @@
         pl.when(sub == s)(functools.partial(place, s))
 
 
-def pack_kernel(sizes, charges, mask, geo, targets, sources, live, masked, *packs):
+def pack_kernel(sizes, charges, mask, geo, targets, sources, live, masked, geo_out, *packs):
     C, S, L, slots = sizes
     me, sub = lax.axis_index("clu"), lax.axis_index("sub")
     masked[...] = charges[...] * mask[...].astype(F32)
+    geo_out[...] = geo[...]
     lane = lax.broadcasted_iota(jnp.int32, (8, L), 1)
     for shift in range(1, C):
         dest = lax.rem(me + shift, C)
@@ -252,7 +274,7 @@
     packs = rest[S : S + C - 1]
     acc_out = rest[S + C - 1]
     sends = rest[S + C : S + C + C - 1]
-    q, tq, acc, fwdt, sgeo, fa0, fb0, fb1, order, codes, sems, *ring = rest[S + C + C - 1 :]
+    q, tq, acc, fwdt, sgeo, fa0, fb0, fb1, order, codes, sems, *work = rest[S + C + C - 1 :]
     fa, fb = (fa0,), (fb0, fb1)
     n = (C - 1) * slots
     copies = [
@@ -292,16 +314,17 @@
         slot = order[jnp.minimum(i, jnp.maximum(found - 1, 0))]
         distances(load_features(fa, slot), load_features(fb, slot), dist)
 
-    def finish(i, dist):
+    def finish(i, dist, part):
         ok = i < found
         slot = order[jnp.minimum(i, jnp.maximum(found - 1, 0))]
         source = order[n + 1 + slot]
         back = tile_sums(
-            dist, q[pl.ds(source, 1), :], tq[pl.ds(slot, 1), :], fwdt, jnp.where(ok, slot, -1)
+            dist, q[pl.ds(source, 1), :], tq[pl.ds(slot, 1), :], part
         )
         acc[pl.ds(source, 1), :] += jnp.where(ok, back, 0.0)
-
-    pipeline(found, begin, finish, ring)
+        return jnp.where(ok, slot, -1)
+
+    pipeline(found, begin, finish, fwdt, work[:8], work[8:])
     acc_out[...] = acc[...] * inv
     fwd = (fwdt[...] * inv).T
     rank = up.shape[1]
@@ -311,7 +334,18 @@
         sends[shift][slots:, :rank] = up[...]
 
 
-def feature_kernel(geo, fa0, fa1, fb0, fb1, diag, scale):
+def prepare_kernel(
+    geo, masked, basis_far, transfer_far, parent_far,
+    fa0, fa1, fb0, fb1, diag, scale, up, basis, transfer, parent, sems
+):
+    copies = [
+        pltpu.make_async_copy(src, dst, sems.at[k])
+        for k, (src, dst) in enumerate(
+            [(basis_far, basis), (transfer_far, transfer), (parent_far, parent)]
+        )
+    ]
+    for copy in copies:
+        copy.start()
     points = [geo[:, k, :] for k in range(4)]
     centre, inv = frame([points])
     left, right, rad = split_features(points, centre, inv)
@@ -319,12 +353,16 @@
     store_features((fb0, fb1), right)
     diag[...] = lax.rsqrt(2.0 * (rad * rad))
     scale[...] = jnp.full(scale.shape, inv, F32)
+    for copy in copies:
+        copy.wait()
+    up_sums(basis, masked, transfer, parent, up)
 
 
 def local_kernel(sizes, geo_pairs, pairs, fa0, fa1, fb0, fb1, diags, scale, acc_in, *rest):
     S, L, R, clusters, panels = sizes
     pieces = rest[:S]
-    acc_out, q, acc, self_sums, pair_sums, *ring = rest[S:]
+    acc_out, q, acc, self_sums, pair_sums, *work = rest[S:]
+    ring, sums = work[:16], work[16:]
     fa, fb = (fa0, fa1), (fb0, fb1)
     sub, rep = lax.axis_index("sub"), lax.axis_index("rep")
     assemble(sub, S, L, q, pieces)
@@ -338,12 +376,12 @@
 
     def begin_self(i, dist):
         c = first + jnp.minimum(i, share - 1)
-        a = load_features(fa, c)
-        b = load_features(fb, c)
-        dist[:half, :] = contract(a[0].T, jnp.concatenate(b, axis=1))
-        dist[half:, half:] = contract(a[1].T, b[1])
-
-    def finish_self(i, dist):
+        left, right = products(load_features(fa, c), load_features(fb, c))
+        left = left.T
+        dist[:half, :] = contract(left[:half, :], right)
+        dist[half:, half:] = contract(left[half:, :], right[:, half:])
+
+    def finish_self(i, dist, parts):
         c = first + i
         qrow = q[pl.ds(c, 1), :]
         qcol = upright(qrow[:, :half])
@@ -363,23 +401,20 @@
                 )
             return (jnp.where(eye(span), diag[:, half:], inverse_root(dist[span, half:])),)
 
-        def sums(span, held):
+        def partial(span, held):
             if span.start < half:
                 g0, g1 = held
                 back[0] = back[0] + fold(g1 * qcol[span, :])
-                part = g0 * qrow[:, :half] + g1 * qrow[:, half:]
+                keep(parts, span, g0 * qrow[:, :half] + g1 * qrow[:, half:])
             else:
-                part = held[0] * qrow[:, half:]
-            return jnp.sum(part, axis=1, keepdims=True)
-
-        def store(span, held):
-            put_column(self_sums, span, c, held)
-
-        staged(spans_of(panels), root, sums, store)
+                keep(parts, span, held[0] * qrow[:, half:])
+
+        staged(spans_of(panels), root, partial)
         back = jnp.sum(back[0], axis=0, keepdims=True)
         acc[pl.ds(c, 1), :] += jnp.concatenate([jnp.zeros_like(back), back], axis=1)
-
-    pipeline(share, begin_self, finish_self, ring[: ring_size(share)])
+        return c
+
+    pipeline(share, begin_self, finish_self, self_sums, ring[: ring_size(share)], sums)
 
     count = pairs.shape[1] // S
     start = sub * count
@@ -388,13 +423,14 @@
         p = start + jnp.minimum(i, count - 1)
         distances(load_features(fa, pairs[0, p]), load_features(fb, pairs[1, p]), dist)
 
-    def finish(i, dist):
+    def finish(i, dist, part):
         ia, ib = pairs[0, start + i], pairs[1, start + i]
         acc[pl.ds(ib, 1), :] += tile_sums(
-            dist, q[pl.ds(ib, 1), :], q[pl.ds(ia, 1), :], pair_sums, start + i
+            dist, q[pl.ds(ib, 1), :], q[pl.ds(ia, 1), :], part
         )
-
-    pipeline(count, begin, finish, ring[: ring_size(count)])
+        return start + i
+
+    pipeline(count, begin, finish, pair_sums, ring[: ring_size(count)], sums)
     total = acc[...] + self_sums[...].T
     width = geo_pairs.shape[1]
     total = total + select_rows(geo_pairs[0:1, :], pair_sums[...].T[:width, :], clusters)
@@ -444,8 +480,7 @@
         pl.when(sub == s)(functools.partial(give, s))
 
 
-def up_kernel(basis, masked, transfer, parent, after, up):
-    del after
+def up_sums(basis, masked, transfer, parent, up):
     clusters = basis.shape[0]
     rank = basis.shape[1]
     lane = lax.broadcasted_iota(jnp.int32, (rank, clusters), 1)
@@ -526,37 +561,38 @@
 
     made = pl.pallas_call(
         functools.partial(pack_kernel, (C, S, L, slots)),
-        out_shape=[pltpu.VMEM((clusters, L), F32)] + [pltpu.VMEM((5 * slots + 8, L), F32)] * (C - 1),
+        out_shape=[pltpu.VMEM((clusters, L), F32), pltpu.VMEM(geometry.shape, F32)]
+        + [pltpu.VMEM((5 * slots + 8, L), F32)] * (C - 1),
         in_specs=[vmem()] * 3 + [smem()] * 3,
-        out_specs=[vmem()] * C,
+        out_specs=[vmem()] * (C + 1),
         compiler_params=limit(60),
         cost_estimate=about(2),
         name="packs",
     )(charges, panel_mask, geometry, targets, remote_source[0], remote_live[0])
-    masked, packs = made[0], made[1:]
+    masked, geo, packs = made[0], made[1], made[2:]
     pieces = [masked] + [send(masked, (("sub", d),)) for d in range(1, S)]
     packs = [send(packs[d - 1], (("clu", d),)) for d in range(1, C)]
 
-    features = pl.pallas_call(
-        feature_kernel,
+    *features, up = pl.pallas_call(
+        prepare_kernel,
         out_shape=[pltpu.VMEM((clusters * ROWS, LANES), F32)] * 4
-        + [pltpu.VMEM((clusters, panels), F32), pltpu.VMEM((8, LANES), F32)],
-        in_specs=[vmem()],
-        out_specs=[vmem()] * 6,
+        + [
+            pltpu.VMEM((clusters, panels), F32),
+            pltpu.VMEM((8, LANES), F32),
+            pltpu.VMEM((par_dev, rank), F32),
+        ],
+        in_specs=[vmem()] * 2 + [pl.BlockSpec(memory_space=pl.ANY)] * 3,
+        out_specs=[vmem()] * 7,
+        scratch_shapes=[
+            pltpu.VMEM(basis_t.shape, F32),
+            pltpu.VMEM(transfer_t.shape, F32),
+            pltpu.VMEM(parent.shape, jnp.int32),
+            pltpu.SemaphoreType.DMA((3,)),
+        ],
         compiler_params=limit(32),
         cost_estimate=about(4),
-        name="features",
-    )(*near_by(geometry))
-
-    up = pl.pallas_call(
-        up_kernel,
-        out_shape=pltpu.VMEM((par_dev, rank), F32),
-        in_specs=[vmem()] * 5,
-        out_specs=vmem(),
-        compiler_params=limit(16),
-        cost_estimate=about(1),
-        name="far_up",
-    )(*near_by(basis_t, masked, transfer_t, parent, features[5]))
+        name="prepare",
+    )(*near_by(geo, masked), basis_t, transfer_t, parent)
 
     made = pl.pallas_call(
         functools.partial(remote_kernel, (C, S, L, slots, clusters, panels)),
@@ -577,11 +613,12 @@
             pltpu.SMEM((C - 1, 8, L), F32),
             pltpu.SemaphoreType.DMA((C - 1,)),
         ]
-        + [pltpu.VMEM((L, panels), F32)] * 8,
+        + [pltpu.VMEM((L, panels), F32)] * 8
+        + [pltpu.VMEM((L, 2 * LANES), BF16)] * 4,
         compiler_params=limit(24),
         cost_estimate=about(6),
         name="near_remote",
-    )(*near_by(geometry, up, *pieces, *packs))
+    )(*near_by(geo, up, *pieces, *packs))
     acc, sums = made[0], [send(made[d], (("clu", C - d),)) for d in range(1, C)]
 
     wide = whole(local_pairs.shape[1])
@@ -596,7 +633,8 @@
             pltpu.VMEM((panels, clusters), F32),
             pltpu.VMEM((panels, wide), F32),
         ]
-        + [pltpu.VMEM((panels, panels), F32)] * 16,
+        + [pltpu.VMEM((panels, panels), F32)] * 16
+        + [pltpu.VMEM((panels, 2 * LANES), BF16)] * 4,
         compiler_params=limit(24),
         cost_estimate=about(15),
         name="near_local",

time: 52.2 us -> 48.5 us (0.929)
  Pallas kernels: 30.8 us -> 28.2 us
  local copies, waits for them, and re-layouts: 4.36 us -> 3.32 us
    pallas_call x1, Pallas kernels: 14.9 us -> 12 us  [on_device(): pl.pallas_call(functools.partial(local_kernel, (S, L, R, clusters, panels...]
    unnamed x24 -> x20, local copies, waits for them, and re-layouts: 4.36 us -> 3.32 us
    pallas_call x2 -> x1, Pallas kernels: 6.26 us -> 6.48 us  [on_device(): pl.pallas_call(prepare_kernel, out_shape=[pltpu.VMEM((clusters * ROWS, LA...]
  transfers between devices with their start and end apart: 9 -> 9, of which waited for: 2 -> 2; matrix products, arithmetic and copies ran while one was open for 0% -> 0% of each run, Pallas kernels for 42% -> 40%
where the time goes in v14:
time: 48.5 us; the launch traced here: 48.3 us
  Pallas kernels  28.2 us (58%)
  starting transfers between devices  11.4 us (24%)
  waiting for transfers between devices  4.56 us (9%)
  local copies, waits for them, and re-layouts  3.32 us (7%)
  other arithmetic  0.65 us (1%)
    pallas_call x1, Pallas kernels, on_device(): pl.pallas_call(functools.partial(local_kernel, (S, L, R, clusters, panels...  12 us
    ppermute x9, starting transfers between devices, send(): return lax.ppermute(value, names if len(names) > 1 else names[0], perm)  11.4 us
    pallas_call x1, Pallas kernels, on_device(): pl.pallas_call(prepare_kernel, out_shape=[pltpu.VMEM((clusters * ROWS, LA...  6.48 us
    pallas_call x1, Pallas kernels, on_device(): pl.pallas_call(functools.partial(remote_kernel, (C, S, L, slots, clusters...  6.28 us
    ppermute x9, waiting for transfers between devices, send(): return lax.ppermute(value, names if len(names) > 1 else names[0], perm)  4.56 us
    unnamed x20, local copies, waits for them, and re-layouts  3.32 us
    pallas_call x1, Pallas kernels, on_device(): pl.pallas_call(functools.partial(pack_kernel, (C, S, L, slots)), out_shap...  1.34 us
    pallas_call x1, Pallas kernels, on_device(): pl.pallas_call(functools.partial(merge_kernel, (C, S, L, slots, clusters)...  1.26 us
  transfers between devices with their start and end apart: 9, of which 2 were waited for; matrix products, arithmetic and copies ran while one was open for 0% of the time, Pallas kernels for 40%

profile of v14, /device:TPU:0, one launch (start us, length us, event | category | flops | bytes accessed | tf_op | source)
XLA Modules:
  0.0 48.3 jit_solution(2706969943425773238)
XLA Ops:
  0.0 1.3 %packs.1 = (f32[128,128]{1,0:T(8,128)S(1)}, f32[128,4,256]{2,1,0:T(4,128)S(1)}, f32[88,128]{1,0:T(8,128)S(1)}, f32[88,128]{1,0:T(8,128)S(1)}, f32[88,128]{1,0:T(8,128)S(1)}) custom-call(f32[128,128]{1,0:T(8,128)} %charges.1, s32[128,128]{1,0:T(8,128)} %mask.1, f32[128,4,256]{2,1,0:T(4,128)} %geo.1, s32[4,16]{1,0:T(4,128)} %bitcast.14, s32[4,16]{1,0:T(4,128)} %bitcast.21, ...), custom_call_target="tpu_custom_call" | custom-call | bytes 7000000 | tf_op jit(solution)/shard_map/packs/pallas_call | solution.py:562
  1.4 3.0 %collective-permute-start = (f32[128,128]{1,0:T(8,128)S(1)}, f32[128,128]{1,0:T(8,128)S(1)}, u32[]{:S(2)}, u32[]{:S(2)}) collective-permute-start(f32[128,128]{1,0:T(8,128)S(1)} %get-tuple-element.24.masked.rest_0_), channel_id=1, source_target_pairs={{0,2},{2,0},{1,3},{3,1},{4,6},{6,4},{5,7},{7,5},{8,10},{10,8},{9,1... | collective-permute-start | bytes 196616 | tf_op jit(solution)/shard_map/ppermute | solution.py:533
  4.4 1.6 %collective-permute-start.1 = (f32[88,128]{1,0:T(8,128)S(1)}, f32[88,128]{1,0:T(8,128)S(1)}, u32[]{:S(2)}, u32[]{:S(2)}) collective-permute-start(f32[88,128]{1,0:T(8,128)S(1)} %get-tuple-element.32), channel_id=1, source_target_pairs={{0,4},{4,8},{8,12},{12,0},{1,5},{5,9},{9,13},{13,1},{2,6},{6,10},{... | collective-permute-start | bytes 135176 | tf_op jit(solution)/shard_map/ppermute | solution.py:533
  5.9 2.6 %collective-permute-start.2 = (f32[88,128]{1,0:T(8,128)S(1)}, f32[88,128]{1,0:T(8,128)S(1)}, u32[]{:S(2)}, u32[]{:S(2)}) collective-permute-start(f32[88,128]{1,0:T(8,128)S(1)} %get-tuple-element.33), channel_id=1, source_target_pairs={{0,8},{4,12},{8,0},{12,4},{1,9},{5,13},{9,1},{13,5},{2,10},{6,14},... | collective-permute-start | bytes 135176 | tf_op jit(solution)/shard_map/ppermute | solution.py:533
  8.5 1.3 %collective-permute-start.3 = (f32[88,128]{1,0:T(8,128)S(1)}, f32[88,128]{1,0:T(8,128)S(1)}, u32[]{:S(2)}, u32[]{:S(2)}) collective-permute-start(f32[88,128]{1,0:T(8,128)S(1)} %get-tuple-element.34), channel_id=1, source_target_pairs={{0,12},{4,0},{8,4},{12,8},{1,13},{5,1},{9,5},{13,9},{2,14},{6,2},{... | collective-permute-start | bytes 135176 | tf_op jit(solution)/shard_map/ppermute | solution.py:533
  9.9 0.0 copy-start
  9.9 1.6 %copy-done = f32[128,128,32]{1,2,0:T(8,128)S(1)} copy-done((f32[128,128,32]{1,2,0:T(8,128)S(1)}, f32[128,128,32]{1,2,0:T(8,128)}, u32[]{:S(2)}) %copy-start) | copy-done | bytes 2097176
  11.5 0.0 copy-start.2
  11.5 1.0 %copy-done.2 = f32[128,32,32]{0,2,1:T(8,128)S(1)} copy-done((f32[128,32,32]{0,2,1:T(8,128)S(1)}, f32[128,32,32]{0,2,1:T(8,128)}, u32[]{:S(2)}) %copy-start.2) | copy-done | bytes 524312
  12.5 0.0 copy-start.7
  12.5 0.7 %copy-done.7 = s32[128]{0:T(128)S(1)} copy-done((s32[128]{0:T(128)S(1)}, s32[128]{0:T(128)}, u32[]{:S(2)}) %copy-start.7) | copy-done | bytes 536
  13.2 0.0 copy-start.6
  13.2 6.5 %prepare.1 = (f32[3072,128]{1,0:T(8,128)S(1)}, f32[3072,128]{1,0:T(8,128)S(1)}, f32[3072,128]{1,0:T(8,128)S(1)}, f32[3072,128]{1,0:T(8,128)S(1)}, f32[128,256]{1...) custom-call(f32[128,4,256]{2,1,0:T(4,128)S(1)} %get-tuple-element.23.geo, ...), custom_call_target="tpu_custom_call" | custom-call | bytes 14000000 | tf_op jit(solution)/shard_map/prepare/pallas_call | solution.py:576
  19.7 0.0 collective-permute-done.1.rest_2_
  19.7 0.0 collective-permute-done.2.rest_3_
  19.7 0.0 collective-permute-done.3.rest_4_
  19.7 0.0 collective-permute-done.rest_1_
  19.7 6.3 %near_remote.1 = (f32[128,256]{1,0:T(8,128)S(1)}, f32[32,128]{1,0:T(8,128)S(1)}, f32[32,128]{1,0:T(8,128)S(1)}, f32[32,128]{1,0:T(8,128)S(1)}) custom-call(f32[128,4,256]{2,1,0:T(4,128)S(1)} %get-tuple-element.23.geo, f32[16,32]{1,0:T(8,128)S(1)} %get-tuple-element.31.up, f32[128,128]{1,0:T(8,128)S(1)} %get-tuple-element.24.masked.rest_0_, ...), custom_call_target="tpu_custom_call" | custom-call | bytes 21000000 | tf_op jit(solution)/shard_map/near_remote/pallas_call | solution.py:597
  26.0 0.5 %collective-permute-start.4 = (f32[32,128]{1,0:T(8,128)S(1)}, f32[32,128]{1,0:T(8,128)S(1)}, u32[]{:S(2)}, u32[]{:S(2)}) collective-permute-start(f32[32,128]{1,0:T(8,128)S(1)} %get-tuple-element.36), channel_id=1, source_target_pairs={{0,12},{4,0},{8,4},{12,8},{1,13},{5,1},{9,5},{13,9},{2,14},{6,2},{... | collective-permute-start | bytes 49160 | tf_op jit(solution)/shard_map/ppermute | solution.py:533
  26.5 1.7 %collective-permute-start.5 = (f32[32,128]{1,0:T(8,128)S(1)}, f32[32,128]{1,0:T(8,128)S(1)}, u32[]{:S(2)}, u32[]{:S(2)}) collective-permute-start(f32[32,128]{1,0:T(8,128)S(1)} %get-tuple-element.37), channel_id=1, source_target_pairs={{0,8},{4,12},{8,0},{12,4},{1,9},{5,13},{9,1},{13,5},{2,10},{6,14},... | collective-permute-start | bytes 49160 | tf_op jit(solution)/shard_map/ppermute | solution.py:533
  28.2 0.2 collective-permute-start.6
  28.4 0.0 copy-done.6
  28.4 0.0 copy-start.1
  28.4 0.0 copy-start.3
  28.4 0.0 copy-start.4
  28.4 0.0 copy-start.5
  28.4 0.0 copy-start.8
  28.4 12.0 %near_local.1.near = f32[128,256]{1,0:T(8,128)S(1)} custom-call(s32[2,128]{1,0:T(2,128)S(1)} %bitcast.17, s32[2,128]{1,0:T(2,128)S(1)} %bitcast.18, f32[3072,128]{1,0:T(8,128)S(1)} %get-tuple-element.25.fa0, f32[3072,128]{1,0:T(8,128)S(1)} %get-tuple-element.26.fa1, f32[3072,128]{1,0:T(8,128)S(1)} %get-tuple-element.27.fb0, ...), custom_call_target="tpu_custom_call" | custom-call | bytes 52500000 | tf_op jit(solution)/shard_map/near_local/pallas_call | solution.py:625
  40.5 0.0 collective-permute-done.4.rest_0_
  40.5 0.0 collective-permute-done.5.rest_1_
  40.5 0.0 collective-permute-done.6.rest_2_
  40.5 0.0 copy-done.1
  40.5 0.0 copy-done.3
  40.5 0.0 copy-done.4
  40.5 0.0 copy-done.5
  40.5 0.0 copy-done.8
  40.5 1.3 %merge.1 = (f32[160,128]{1,0:T(8,128)S(1)}, f32[160,128]{1,0:T(8,128)S(1)}) custom-call(s32[8,16]{1,0:T(8,128)S(1)} %bitcast.16, s32[4,16]{1,0:T(4,128)S(1)} %bitcast.15, f32[128,256]{1,0:T(8,128)S(1)} %near_local.1.near, f32[16,8,32,32]{3,2,1,0:T(8,128)S(1)} %copy-done.1, f32[32,32,128]{2,1,0:T(8,128)S(1)} %bitcast.13, s32[1,128]{1,0:T(1,128)S(1)} %bitcast.20, ...), custom_call_target="tpu_custom_call" | custom-call | bytes 7000000 | tf_op jit(solution)/shard_map/merge/pallas_call | solution.py:643
  41.8 0.0 copy-start.9
  41.8 0.4 collective-permute-start.7
  42.2 4.1 %collective-permute-done.7 = f32[160,128]{1,0:T(8,128)S(1)} collective-permute-done((f32[160,128]{1,0:T(8,128)S(1)}, f32[160,128]{1,0:T(8,128)S(1)}, u32[]{:S(2)}, u32[]{:S(2)}) %collective-permute-start.7) | collective-permute-done | bytes 81952 | tf_op jit(solution)/shard_map/ppermute | solution.py:533
  46.3 0.1 collective-permute-start.8
  46.4 0.8 %far_down.1 = f32[128,128]{1,0:T(8,128)S(1)} custom-call(f32[128,32,128]{2,1,0:T(8,128)S(1)} %bitcast.11, f32[160,128]{1,0:T(8,128)S(1)} %add.6.near), custom_call_target="tpu_custom_call" | custom-call | bytes 3500000 | tf_op jit(solution)/shard_map/far_down/pallas_call | solution.py:658
  47.2 0.4 collective-permute-done.8
  47.7 0.0 copy-done.9
  47.7 0.6 %fusion = f32[128,128]{1,0:T(8,128)} fusion(f32[128,128]{1,0:T(8,128)S(1)} %far_down.1, f32[160,128]{1,0:T(8,128)S(1)} %collective-permute-done.8, s32[128,128]{1,0:T(8,128)S(1)} %copy-done.9), kind=kLoop, calls=%fused_computation.1 | loop fusion | flops 49152 | bytes 262144 | tf_op jit(solution)/shard_map/mul | solution.py:669
  (1 shorter events, 0.0 us)
Async XLA Ops:
  1.4 18.3 %collective-permute-start = (f32[128,128]{1,0:T(8,128)S(1)}, f32[128,128]{1,0:T(8,128)S(1)}, u32[]{:S(2)}, u32[]{:S(2)}) collective-permute-start(f32[128,128]{1,0:T(8,128)S(1)} %get-tuple-element.24.masked.rest_0_), channel_id=1, source_target_pairs={{0,2},{2,0},{1,3},{3,1},{4,6},{6,4},{5,7},{7,5},{8,10},{10,8},{9,1... | collective-permute-start | bytes 196616 | tf_op jit(solution)/shard_map/ppermute | solution.py:533
  4.4 15.3 %collective-permute-start.1 = (f32[88,128]{1,0:T(8,128)S(1)}, f32[88,128]{1,0:T(8,128)S(1)}, u32[]{:S(2)}, u32[]{:S(2)}) collective-permute-start(f32[88,128]{1,0:T(8,128)S(1)} %get-tuple-element.32), channel_id=1, source_target_pairs={{0,4},{4,8},{8,12},{12,0},{1,5},{5,9},{9,13},{13,1},{2,6},{6,10},{... | collective-permute-start | bytes 135176 | tf_op jit(solution)/shard_map/ppermute | solution.py:533
  5.9 13.7 %collective-permute-start.2 = (f32[88,128]{1,0:T(8,128)S(1)}, f32[88,128]{1,0:T(8,128)S(1)}, u32[]{:S(2)}, u32[]{:S(2)}) collective-permute-start(f32[88,128]{1,0:T(8,128)S(1)} %get-tuple-element.33), channel_id=1, source_target_pairs={{0,8},{4,12},{8,0},{12,4},{1,9},{5,13},{9,1},{13,5},{2,10},{6,14},... | collective-permute-start | bytes 135176 | tf_op jit(solution)/shard_map/ppermute | solution.py:533
  8.5 11.2 %collective-permute-start.3 = (f32[88,128]{1,0:T(8,128)S(1)}, f32[88,128]{1,0:T(8,128)S(1)}, u32[]{:S(2)}, u32[]{:S(2)}) collective-permute-start(f32[88,128]{1,0:T(8,128)S(1)} %get-tuple-element.34), channel_id=1, source_target_pairs={{0,12},{4,0},{8,4},{12,8},{1,13},{5,1},{9,5},{13,9},{2,14},{6,2},{... | collective-permute-start | bytes 135176 | tf_op jit(solution)/shard_map/ppermute | solution.py:533
  9.9 1.6 %copy-start = (f32[128,128,32]{1,2,0:T(8,128)S(1)}, f32[128,128,32]{1,2,0:T(8,128)}, u32[]{:S(2)}) copy-start(f32[128,128,32]{1,2,0:T(8,128)} %param.19) | copy-start | bytes 6291460
  11.5 1.0 %copy-start.2 = (f32[128,32,32]{0,2,1:T(8,128)S(1)}, f32[128,32,32]{0,2,1:T(8,128)}, u32[]{:S(2)}) copy-start(f32[128,32,32]{0,2,1:T(8,128)} %param.20) | copy-start | bytes 1572868
  12.5 0.7 %copy-start.7 = (s32[128]{0:T(128)S(1)}, s32[128]{0:T(128)}, u32[]{:S(2)}) copy-start(s32[128]{0:T(128)} %param.21) | copy-start | bytes 1540
  13.2 15.2 %copy-start.6 = (s32[1,128,2]{1,2,0:T(2,128)S(1)}, s32[1,128,2]{1,2,0:T(2,128)}, u32[]{:S(2)}) copy-start(s32[1,128,2]{1,2,0:T(2,128)} %param.18) | copy-start | bytes 3076
  26.0 14.5 %collective-permute-start.4 = (f32[32,128]{1,0:T(8,128)S(1)}, f32[32,128]{1,0:T(8,128)S(1)}, u32[]{:S(2)}, u32[]{:S(2)}) collective-permute-start(f32[32,128]{1,0:T(8,128)S(1)} %get-tuple-element.36), channel_id=1, source_target_pairs={{0,12},{4,0},{8,4},{12,8},{1,13},{5,1},{9,5},{13,9},{2,14},{6,2},{... | collective-permute-start | bytes 49160 | tf_op jit(solution)/shard_map/ppermute | solution.py:533
  26.5 14.0 %collective-permute-start.5 = (f32[32,128]{1,0:T(8,128)S(1)}, f32[32,128]{1,0:T(8,128)S(1)}, u32[]{:S(2)}, u32[]{:S(2)}) collective-permute-start(f32[32,128]{1,0:T(8,128)S(1)} %get-tuple-element.37), channel_id=1, source_target_pairs={{0,8},{4,12},{8,0},{12,4},{1,9},{5,13},{9,1},{13,5},{2,10},{6,14},... | collective-permute-start | bytes 49160 | tf_op jit(solution)/shard_map/ppermute | solution.py:533
  28.2 12.3 %collective-permute-start.6 = (f32[32,128]{1,0:T(8,128)S(1)}, f32[32,128]{1,0:T(8,128)S(1)}, u32[]{:S(2)}, u32[]{:S(2)}) collective-permute-start(f32[32,128]{1,0:T(8,128)S(1)} %get-tuple-element.38), channel_id=1, source_target_pairs={{0,4},{4,8},{8,12},{12,0},{1,5},{5,9},{9,13},{13,1},{2,6},{6,10},{... | collective-permute-start | bytes 49160 | tf_op jit(solution)/shard_map/ppermute | solution.py:533
  28.4 12.1 %copy-start.1 = (f32[16,8,32,32]{3,2,1,0:T(8,128)S(1)}, f32[16,8,32,32]{3,2,1,0:T(8,128)}, u32[]{:S(2)}) copy-start(f32[16,8,32,32]{3,2,1,0:T(8,128)} %coupling.1) | copy-start | bytes 1572868
  28.4 12.1 %copy-start.3 = (f32[128,32,32]{0,2,1:T(8,128)S(1)}, f32[128,32,32]{0,2,1:T(8,128)}, u32[]{:S(2)}) copy-start(f32[128,32,32]{0,2,1:T(8,128)} %param.20) | copy-start | bytes 1572868
  28.4 12.1 %copy-start.4 = (s32[1,4,16]{2,1,0:T(4,128)S(1)}, s32[1,4,16]{2,1,0:T(4,128)}, u32[]{:S(2)}) copy-start(s32[1,4,16]{2,1,0:T(4,128)} %param.16) | copy-start | bytes 772
  28.4 12.1 %copy-start.5 = (s32[16,8]{0,1:T(8,128)S(1)}, s32[16,8]{0,1:T(8,128)}, u32[]{:S(2)}) copy-start(s32[16,8]{0,1:T(8,128)} %param.22) | copy-start | bytes 1540
  28.4 12.1 %copy-start.8 = (s32[128]{0:T(128)S(1)}, s32[128]{0:T(128)}, u32[]{:S(2)}) copy-start(s32[128]{0:T(128)} %param.21) | copy-start | bytes 1540
  41.8 5.9 %copy-start.9 = (s32[128,128]{1,0:T(8,128)S(1)}, s32[128,128]{1,0:T(8,128)}, u32[]{:S(2)}) copy-start(s32[128,128]{1,0:T(8,128)} %mask.1) | copy-start | bytes 196612
  41.8 4.5 %collective-permute-start.7 = (f32[160,128]{1,0:T(8,128)S(1)}, f32[160,128]{1,0:T(8,128)S(1)}, u32[]{:S(2)}, u32[]{:S(2)}) collective-permute-start(f32[160,128]{1,0:T(8,128)S(1)} %get-tuple-element.40), channel_id=1, source_target_pairs={{0,2},{2,0},{1,3},{3,1},{4,6},{6,4},{5,7},{7,5},{8,10},{10,8},{9,1... | collective-permute-start | bytes 245768 | tf_op jit(solution)/shard_map/ppermute | solution.py:533
  46.3 1.3 %collective-permute-start.8 = (f32[160,128]{1,0:T(8,128)S(1)}, f32[160,128]{1,0:T(8,128)S(1)}, u32[]{:S(2)}, u32[]{:S(2)}) collective-permute-start(f32[160,128]{1,0:T(8,128)S(1)} %add.6.near), channel_id=1, source_target_pairs={{0,1},{1,0},{2,3},{3,2},{4,5},{5,4},{6,7},{7,6},{8,9},{9,8},{10,11... | collective-permute-start | bytes 245768 | tf_op jit(solution)/shard_map/ppermute | solution.py:533

commit v15 on v14

--- a/solution.py
+++ b/solution.py
@@ -28,6 +28,10 @@
 
 def near_by(*arrays):
     return [pltpu.with_memory_space_constraint(x, pltpu.VMEM) for x in arrays]
+
+
+def far_off(*arrays):
+    return [pltpu.with_memory_space_constraint(x, pltpu.HBM) for x in arrays]
 
 
 def smem():
@@ -101,12 +105,12 @@
     return [jnp.concatenate(v, axis=0).astype(BF16) for v in zip(*pairs)]
 
 
-def store_features(ref, rows):
-    count = rows[0].shape[0]
+def store_features(ref, rows, first):
     width = rows[0].shape[1]
     for k, row in enumerate(rows):
         for t, piece in enumerate(ref):
-            piece[pl.ds(k, count, stride=ROWS), :] = row[:, t * LANES : min(width, (t + 1) * LANES)]
+            at = pl.ds(first * ROWS + k, 8, stride=ROWS)
+            piece[at, :] = row[:, t * LANES : min(width, (t + 1) * LANES)]
 
 
 def load_features(ref, index):
@@ -155,7 +159,7 @@
 
 
 def inverse_root(d):
-    return lax.rsqrt(d)
+    return lax.exp2(-0.5 * lax.log2(d))
 
 
 def fold(v):
@@ -304,10 +308,11 @@
     ]
     spoints = [sgeo[k * n : (k + 1) * n, :] for k in range(4)]
     centre, inv = frame([tpoints, spoints])
-    left, _, _ = split_features(tpoints, centre, inv)
-    _, right, _ = split_features(spoints, centre, inv)
-    store_features(fa, left)
-    store_features(fb, right)
+    for first in range(0, n, 8):
+        left, _, _ = split_features([v[first : first + 8, :] for v in tpoints], centre, inv)
+        store_features(fa, left, first)
+        _, right, _ = split_features([v[first : first + 8, :] for v in spoints], centre, inv)
+        store_features(fb, right, first)
     tq[...] = tpoints[4]
 
     def begin(i, dist):
@@ -346,12 +351,13 @@
     ]
     for copy in copies:
         copy.start()
-    points = [geo[:, k, :] for k in range(4)]
-    centre, inv = frame([points])
-    left, right, rad = split_features(points, centre, inv)
-    store_features((fa0, fa1), left)
-    store_features((fb0, fb1), right)
-    diag[...] = lax.rsqrt(2.0 * (rad * rad))
+    centre, inv = frame([[geo[:, k, :] for k in range(4)]])
+    for first in range(0, geo.shape[0], 8):
+        points = [geo[first : first + 8, k, :] for k in range(4)]
+        left, right, rad = split_features(points, centre, inv)
+        store_features((fa0, fa1), left, first)
+        store_features((fb0, fb1), right, first)
+        diag[first : first + 8, :] = lax.rsqrt(2.0 * (rad * rad))
     scale[...] = jnp.full(scale.shape, inv, F32)
     for copy in copies:
         copy.wait()
@@ -581,7 +587,7 @@
             pltpu.VMEM((8, LANES), F32),
             pltpu.VMEM((par_dev, rank), F32),
         ],
-        in_specs=[vmem()] * 2 + [pl.BlockSpec(memory_space=pl.ANY)] * 3,
+        in_specs=[vmem()] * 2 + [pl.BlockSpec(memory_space=pltpu.HBM)] * 3,
         out_specs=[vmem()] * 7,
         scratch_shapes=[
             pltpu.VMEM(basis_t.shape, F32),
@@ -592,7 +598,7 @@
         compiler_params=limit(32),
         cost_estimate=about(4),
         name="prepare",
-    )(*near_by(geo, masked), basis_t, transfer_t, parent)
+    )(*near_by(geo, masked), *far_off(basis_t, transfer_t, parent))
 
     made = pl.pallas_call(
         functools.partial(remote_kernel, (C, S, L, slots, clusters, panels)),

time: 48.5 us -> 44.4 us (0.915)
  local copies, waits for them, and re-layouts: 3.32 us -> 0.04 us
  Pallas kernels: 28.2 us -> 27.4 us
    unnamed x20 -> x16, local copies, waits for them, and re-layouts: 3.32 us -> 0.04 us
    pallas_call x1, Pallas kernels: 6.48 us -> 4.94 us  [on_device(): pl.pallas_call(prepare_kernel, out_shape=[pltpu.VMEM((clusters * ROWS, LA...]
    pallas_call x1, Pallas kernels: 12 us -> 12.9 us  [on_device(): pl.pallas_call(functools.partial(local_kernel, (S, L, R, clusters, panels...]
  transfers between devices with their start and end apart: 9 -> 9, of which waited for: 2 -> 2; matrix products, arithmetic and copies ran while one was open for 0% -> 0% of each run, Pallas kernels for 40% -> 42%
where the time goes in v15:
time: 44.4 us; the launch traced here: 44.3 us
  Pallas kernels  27.4 us (62%)
  starting transfers between devices  11.4 us (26%)
  waiting for transfers between devices  4.55 us (10%)
  other arithmetic  0.65 us (1%)
    pallas_call x1, Pallas kernels, on_device(): pl.pallas_call(functools.partial(local_kernel, (S, L, R, clusters, panels...  12.9 us
    ppermute x9, starting transfers between devices, send(): return lax.ppermute(value, names if len(names) > 1 else names[0], perm)  11.4 us
    pallas_call x1, Pallas kernels, on_device(): pl.pallas_call(functools.partial(remote_kernel, (C, S, L, slots, clusters...  6.13 us
    pallas_call x1, Pallas kernels, on_device(): pl.pallas_call(prepare_kernel, out_shape=[pltpu.VMEM((clusters * ROWS, LA...  4.94 us
    ppermute x9, waiting for transfers between devices, send(): return lax.ppermute(value, names if len(names) > 1 else names[0], perm)  4.55 us
    pallas_call x1, Pallas kernels, on_device(): pl.pallas_call(functools.partial(pack_kernel, (C, S, L, slots)), out_shap...  1.34 us
    pallas_call x1, Pallas kernels, on_device(): pl.pallas_call(functools.partial(merge_kernel, (C, S, L, slots, clusters)...  1.26 us
  transfers between devices with their start and end apart: 9, of which 2 were waited for; matrix products, arithmetic and copies ran while one was open for 0% of the time, Pallas kernels for 42%

profile of v15, /device:TPU:0, one launch (start us, length us, event | category | flops | bytes accessed | tf_op | source)
XLA Modules:
  0.0 44.3 jit_solution(2902632322404902162)
XLA Ops:
  0.0 1.3 %packs.1 = (f32[128,128]{1,0:T(8,128)S(1)}, f32[128,4,256]{2,1,0:T(4,128)S(1)}, f32[88,128]{1,0:T(8,128)S(1)}, f32[88,128]{1,0:T(8,128)S(1)}, f32[88,128]{1,0:T(8,128)S(1)}) custom-call(f32[128,128]{1,0:T(8,128)} %charges.1, s32[128,128]{1,0:T(8,128)} %mask.1, f32[128,4,256]{2,1,0:T(4,128)} %geo.1, s32[4,16]{1,0:T(4,128)} %bitcast.14, s32[4,16]{1,0:T(4,128)} %bitcast.21, ...), custom_call_target="tpu_custom_call" | custom-call | bytes 7000000 | tf_op jit(solution)/shard_map/packs/pallas_call | solution.py:568
  1.4 3.0 %collective-permute-start = (f32[128,128]{1,0:T(8,128)S(1)}, f32[128,128]{1,0:T(8,128)S(1)}, u32[]{:S(2)}, u32[]{:S(2)}) collective-permute-start(f32[128,128]{1,0:T(8,128)S(1)} %get-tuple-element.24.masked.rest_0_), channel_id=1, source_target_pairs={{0,2},{2,0},{1,3},{3,1},{4,6},{6,4},{5,7},{7,5},{8,10},{10,8},{9,1... | collective-permute-start | bytes 196616 | tf_op jit(solution)/shard_map/ppermute | solution.py:539
  4.4 1.6 %collective-permute-start.1 = (f32[88,128]{1,0:T(8,128)S(1)}, f32[88,128]{1,0:T(8,128)S(1)}, u32[]{:S(2)}, u32[]{:S(2)}) collective-permute-start(f32[88,128]{1,0:T(8,128)S(1)} %get-tuple-element.32), channel_id=1, source_target_pairs={{0,4},{4,8},{8,12},{12,0},{1,5},{5,9},{9,13},{13,1},{2,6},{6,10},{... | collective-permute-start | bytes 135176 | tf_op jit(solution)/shard_map/ppermute | solution.py:539
  5.9 2.6 %collective-permute-start.2 = (f32[88,128]{1,0:T(8,128)S(1)}, f32[88,128]{1,0:T(8,128)S(1)}, u32[]{:S(2)}, u32[]{:S(2)}) collective-permute-start(f32[88,128]{1,0:T(8,128)S(1)} %get-tuple-element.33), channel_id=1, source_target_pairs={{0,8},{4,12},{8,0},{12,4},{1,9},{5,13},{9,1},{13,5},{2,10},{6,14},... | collective-permute-start | bytes 135176 | tf_op jit(solution)/shard_map/ppermute | solution.py:539
  8.5 1.3 %collective-permute-start.3 = (f32[88,128]{1,0:T(8,128)S(1)}, f32[88,128]{1,0:T(8,128)S(1)}, u32[]{:S(2)}, u32[]{:S(2)}) collective-permute-start(f32[88,128]{1,0:T(8,128)S(1)} %get-tuple-element.34), channel_id=1, source_target_pairs={{0,12},{4,0},{8,4},{12,8},{1,13},{5,1},{9,5},{13,9},{2,14},{6,2},{... | collective-permute-start | bytes 135176 | tf_op jit(solution)/shard_map/ppermute | solution.py:539
  9.9 0.0 copy-start.5
  9.9 4.9 %prepare.1 = (f32[3072,128]{1,0:T(8,128)S(1)}, f32[3072,128]{1,0:T(8,128)S(1)}, f32[3072,128]{1,0:T(8,128)S(1)}, f32[3072,128]{1,0:T(8,128)S(1)}, f32[128,256]{1...) custom-call(f32[128,4,256]{2,1,0:T(4,128)S(1)} %get-tuple-element.23.geo, ...), custom_call_target="tpu_custom_call" | custom-call | bytes 14000000 | tf_op jit(solution)/shard_map/prepare/pallas_call | solution.py:582
  14.8 0.0 collective-permute-done.1.rest_2_
  14.8 0.0 collective-permute-done.2.rest_3_
  14.8 0.0 collective-permute-done.3.rest_4_
  14.9 0.0 collective-permute-done.rest_1_
  14.9 6.1 %near_remote.1 = (f32[128,256]{1,0:T(8,128)S(1)}, f32[32,128]{1,0:T(8,128)S(1)}, f32[32,128]{1,0:T(8,128)S(1)}, f32[32,128]{1,0:T(8,128)S(1)}) custom-call(f32[128,4,256]{2,1,0:T(4,128)S(1)} %get-tuple-element.23.geo, f32[16,32]{1,0:T(8,128)S(1)} %get-tuple-element.31.up, f32[128,128]{1,0:T(8,128)S(1)} %get-tuple-element.24.masked.rest_0_, ...), custom_call_target="tpu_custom_call" | custom-call | bytes 21000000 | tf_op jit(solution)/shard_map/near_remote/pallas_call | solution.py:603
  21.0 0.9 %collective-permute-start.4 = (f32[32,128]{1,0:T(8,128)S(1)}, f32[32,128]{1,0:T(8,128)S(1)}, u32[]{:S(2)}, u32[]{:S(2)}) collective-permute-start(f32[32,128]{1,0:T(8,128)S(1)} %get-tuple-element.36), channel_id=1, source_target_pairs={{0,12},{4,0},{8,4},{12,8},{1,13},{5,1},{9,5},{13,9},{2,14},{6,2},{... | collective-permute-start | bytes 49160 | tf_op jit(solution)/shard_map/ppermute | solution.py:539
  21.9 1.3 %collective-permute-start.5 = (f32[32,128]{1,0:T(8,128)S(1)}, f32[32,128]{1,0:T(8,128)S(1)}, u32[]{:S(2)}, u32[]{:S(2)}) collective-permute-start(f32[32,128]{1,0:T(8,128)S(1)} %get-tuple-element.37), channel_id=1, source_target_pairs={{0,8},{4,12},{8,0},{12,4},{1,9},{5,13},{9,1},{13,5},{2,10},{6,14},... | collective-permute-start | bytes 49160 | tf_op jit(solution)/shard_map/ppermute | solution.py:539
  23.2 0.2 collective-permute-start.6
  23.4 0.0 copy-done.5
  23.4 0.0 copy-start.1
  23.4 0.0 copy-start.2
  23.4 0.0 copy-start.3
  23.4 0.0 copy-start.4
  23.4 0.0 copy-start.6
  23.5 12.9 %near_local.1.near = f32[128,256]{1,0:T(8,128)S(1)} custom-call(s32[2,128]{1,0:T(2,128)S(1)} %bitcast.17, s32[2,128]{1,0:T(2,128)S(1)} %bitcast.18, f32[3072,128]{1,0:T(8,128)S(1)} %get-tuple-element.25.fa0, f32[3072,128]{1,0:T(8,128)S(1)} %get-tuple-element.26.fa1, f32[3072,128]{1,0:T(8,128)S(1)} %get-tuple-element.27.fb0, ...), custom_call_target="tpu_custom_call" | custom-call | bytes 52500000 | tf_op jit(solution)/shard_map/near_local/pallas_call | solution.py:631
  36.4 0.0 copy-start
  36.4 0.0 collective-permute-done.4.rest_0_
  36.4 0.0 collective-permute-done.5.rest_1_
  36.4 0.0 collective-permute-done.6.rest_2_
  36.4 0.0 copy-done.1
  36.4 0.0 copy-done.2
  36.4 0.0 copy-done.3
  36.5 0.0 copy-done.4
  36.5 0.0 copy-done.6
  36.5 1.3 %merge.1 = (f32[160,128]{1,0:T(8,128)S(1)}, f32[160,128]{1,0:T(8,128)S(1)}) custom-call(s32[8,16]{1,0:T(8,128)S(1)} %bitcast.16, s32[4,16]{1,0:T(4,128)S(1)} %bitcast.15, f32[128,256]{1,0:T(8,128)S(1)} %near_local.1.near, f32[16,8,32,32]{3,2,1,0:T(8,128)S(1)} %copy-done.1, f32[32,32,128]{2,1,0:T(8,128)S(1)} %bitcast.13, s32[1,128]{1,0:T(1,128)S(1)} %bitcast.20, ...), custom_call_target="tpu_custom_call" | custom-call | bytes 7000000 | tf_op jit(solution)/shard_map/merge/pallas_call | solution.py:649
  37.7 0.0 copy-start.7
  37.8 0.4 collective-permute-start.7
  38.1 4.1 %collective-permute-done.7 = f32[160,128]{1,0:T(8,128)S(1)} collective-permute-done((f32[160,128]{1,0:T(8,128)S(1)}, f32[160,128]{1,0:T(8,128)S(1)}, u32[]{:S(2)}, u32[]{:S(2)}) %collective-permute-start.7) | collective-permute-done | bytes 81952 | tf_op jit(solution)/shard_map/ppermute | solution.py:539
  42.3 0.1 collective-permute-start.8
  42.4 0.0 copy-done
  42.4 0.8 %far_down.1 = f32[128,128]{1,0:T(8,128)S(1)} custom-call(f32[128,32,128]{2,1,0:T(8,128)S(1)} %bitcast.11, f32[160,128]{1,0:T(8,128)S(1)} %add.6.near), custom_call_target="tpu_custom_call" | custom-call | bytes 3500000 | tf_op jit(solution)/shard_map/far_down/pallas_call | solution.py:664
  43.2 0.4 collective-permute-done.8
  43.6 0.0 copy-done.7
  43.6 0.6 %fusion = f32[128,128]{1,0:T(8,128)} fusion(f32[128,128]{1,0:T(8,128)S(1)} %far_down.1, f32[160,128]{1,0:T(8,128)S(1)} %collective-permute-done.8, s32[128,128]{1,0:T(8,128)S(1)} %copy-done.7), kind=kLoop, calls=%fused_computation.1 | loop fusion | flops 49152 | bytes 262144 | tf_op jit(solution)/shard_map/mul | solution.py:675
  (1 shorter events, 0.0 us)
Async XLA Ops:
  1.4 13.5 %collective-permute-start = (f32[128,128]{1,0:T(8,128)S(1)}, f32[128,128]{1,0:T(8,128)S(1)}, u32[]{:S(2)}, u32[]{:S(2)}) collective-permute-start(f32[128,128]{1,0:T(8,128)S(1)} %get-tuple-element.24.masked.rest_0_), channel_id=1, source_target_pairs={{0,2},{2,0},{1,3},{3,1},{4,6},{6,4},{5,7},{7,5},{8,10},{10,8},{9,1... | collective-permute-start | bytes 196616 | tf_op jit(solution)/shard_map/ppermute | solution.py:539
  4.4 10.5 %collective-permute-start.1 = (f32[88,128]{1,0:T(8,128)S(1)}, f32[88,128]{1,0:T(8,128)S(1)}, u32[]{:S(2)}, u32[]{:S(2)}) collective-permute-start(f32[88,128]{1,0:T(8,128)S(1)} %get-tuple-element.32), channel_id=1, source_target_pairs={{0,4},{4,8},{8,12},{12,0},{1,5},{5,9},{9,13},{13,1},{2,6},{6,10},{... | collective-permute-start | bytes 135176 | tf_op jit(solution)/shard_map/ppermute | solution.py:539
  5.9 8.9 %collective-permute-start.2 = (f32[88,128]{1,0:T(8,128)S(1)}, f32[88,128]{1,0:T(8,128)S(1)}, u32[]{:S(2)}, u32[]{:S(2)}) collective-permute-start(f32[88,128]{1,0:T(8,128)S(1)} %get-tuple-element.33), channel_id=1, source_target_pairs={{0,8},{4,12},{8,0},{12,4},{1,9},{5,13},{9,1},{13,5},{2,10},{6,14},... | collective-permute-start | bytes 135176 | tf_op jit(solution)/shard_map/ppermute | solution.py:539
  8.5 6.3 %collective-permute-start.3 = (f32[88,128]{1,0:T(8,128)S(1)}, f32[88,128]{1,0:T(8,128)S(1)}, u32[]{:S(2)}, u32[]{:S(2)}) collective-permute-start(f32[88,128]{1,0:T(8,128)S(1)} %get-tuple-element.34), channel_id=1, source_target_pairs={{0,12},{4,0},{8,4},{12,8},{1,13},{5,1},{9,5},{13,9},{2,14},{6,2},{... | collective-permute-start | bytes 135176 | tf_op jit(solution)/shard_map/ppermute | solution.py:539
  9.9 13.5 %copy-start.5 = (s32[1,128,2]{1,2,0:T(2,128)S(1)}, s32[1,128,2]{1,2,0:T(2,128)}, u32[]{:S(2)}) copy-start(s32[1,128,2]{1,2,0:T(2,128)} %param.18) | copy-start | bytes 3076
  21.0 15.4 %collective-permute-start.4 = (f32[32,128]{1,0:T(8,128)S(1)}, f32[32,128]{1,0:T(8,128)S(1)}, u32[]{:S(2)}, u32[]{:S(2)}) collective-permute-start(f32[32,128]{1,0:T(8,128)S(1)} %get-tuple-element.36), channel_id=1, source_target_pairs={{0,12},{4,0},{8,4},{12,8},{1,13},{5,1},{9,5},{13,9},{2,14},{6,2},{... | collective-permute-start | bytes 49160 | tf_op jit(solution)/shard_map/ppermute | solution.py:539
  21.9 14.5 %collective-permute-start.5 = (f32[32,128]{1,0:T(8,128)S(1)}, f32[32,128]{1,0:T(8,128)S(1)}, u32[]{:S(2)}, u32[]{:S(2)}) collective-permute-start(f32[32,128]{1,0:T(8,128)S(1)} %get-tuple-element.37), channel_id=1, source_target_pairs={{0,8},{4,12},{8,0},{12,4},{1,9},{5,13},{9,1},{13,5},{2,10},{6,14},... | collective-permute-start | bytes 49160 | tf_op jit(solution)/shard_map/ppermute | solution.py:539
  23.2 13.2 %collective-permute-start.6 = (f32[32,128]{1,0:T(8,128)S(1)}, f32[32,128]{1,0:T(8,128)S(1)}, u32[]{:S(2)}, u32[]{:S(2)}) collective-permute-start(f32[32,128]{1,0:T(8,128)S(1)} %get-tuple-element.38), channel_id=1, source_target_pairs={{0,4},{4,8},{8,12},{12,0},{1,5},{5,9},{9,13},{13,1},{2,6},{6,10},{... | collective-permute-start | bytes 49160 | tf_op jit(solution)/shard_map/ppermute | solution.py:539
  23.4 13.0 %copy-start.1 = (f32[16,8,32,32]{3,2,1,0:T(8,128)S(1)}, f32[16,8,32,32]{3,2,1,0:T(8,128)}, u32[]{:S(2)}) copy-start(f32[16,8,32,32]{3,2,1,0:T(8,128)} %coupling.1) | copy-start | bytes 1572868
  23.4 13.0 %copy-start.2 = (f32[128,32,32]{0,2,1:T(8,128)S(1)}, f32[128,32,32]{0,2,1:T(8,128)}, u32[]{:S(2)}) copy-start(f32[128,32,32]{0,2,1:T(8,128)} %param.20) | copy-start | bytes 1572868
  23.4 13.0 %copy-start.3 = (s32[1,4,16]{2,1,0:T(4,128)S(1)}, s32[1,4,16]{2,1,0:T(4,128)}, u32[]{:S(2)}) copy-start(s32[1,4,16]{2,1,0:T(4,128)} %param.16) | copy-start | bytes 772
  23.4 13.0 %copy-start.4 = (s32[16,8]{0,1:T(8,128)S(1)}, s32[16,8]{0,1:T(8,128)}, u32[]{:S(2)}) copy-start(s32[16,8]{0,1:T(8,128)} %param.22) | copy-start | bytes 1540
  23.4 13.0 %copy-start.6 = (s32[128]{0:T(128)S(1)}, s32[128]{0:T(128)}, u32[]{:S(2)}) copy-start(s32[128]{0:T(128)} %param.21) | copy-start | bytes 1540
  36.4 6.0 %copy-start = (f32[128,128,32]{1,2,0:T(8,128)S(1)}, f32[128,128,32]{1,2,0:T(8,128)}, u32[]{:S(2)}) copy-start(f32[128,128,32]{1,2,0:T(8,128)} %param.19) | copy-start | bytes 6291460
  37.7 5.9 %copy-start.7 = (s32[128,128]{1,0:T(8,128)S(1)}, s32[128,128]{1,0:T(8,128)}, u32[]{:S(2)}) copy-start(s32[128,128]{1,0:T(8,128)} %mask.1) | copy-start | bytes 196612
  37.8 4.5 %collective-permute-start.7 = (f32[160,128]{1,0:T(8,128)S(1)}, f32[160,128]{1,0:T(8,128)S(1)}, u32[]{:S(2)}, u32[]{:S(2)}) collective-permute-start(f32[160,128]{1,0:T(8,128)S(1)} %get-tuple-element.40), channel_id=1, source_target_pairs={{0,2},{2,0},{1,3},{3,1},{4,6},{6,4},{5,7},{7,5},{8,10},{10,8},{9,1... | collective-permute-start | bytes 245768 | tf_op jit(solution)/shard_map/ppermute | solution.py:539
  42.3 1.3 %collective-permute-start.8 = (f32[160,128]{1,0:T(8,128)S(1)}, f32[160,128]{1,0:T(8,128)S(1)}, u32[]{:S(2)}, u32[]{:S(2)}) collective-permute-start(f32[160,128]{1,0:T(8,128)S(1)} %add.6.near), channel_id=1, source_target_pairs={{0,1},{1,0},{2,3},{3,2},{4,5},{5,4},{6,7},{7,6},{8,9},{9,8},{10,11... | collective-permute-start | bytes 245768 | tf_op jit(solution)/shard_map/ppermute | solution.py:539

commit v16 on v15

--- a/solution.py
+++ b/solution.py
@@ -54,18 +54,30 @@
     return out
 
 
-def frame(parts):
-    low = [functools.reduce(jnp.minimum, [jnp.min(p[k]) for p in parts]) for k in range(3)]
-    high = [functools.reduce(jnp.maximum, [jnp.max(p[k]) for p in parts]) for k in range(3)]
-    width = functools.reduce(jnp.maximum, [jnp.max(jnp.abs(p[3])) for p in parts])
-    for lo, hi in zip(low, high):
-        width = jnp.maximum(width, 0.5 * (hi - lo))
+def frame(geo):
+    low, high = [None] * 8, [None] * 8
+    for c in range(geo.shape[0]):
+        g, k = geo[c], c % 8
+        low[k] = g if low[k] is None else jnp.minimum(low[k], g)
+        high[k] = g if high[k] is None else jnp.maximum(high[k], g)
+    low = jnp.min(functools.reduce(jnp.minimum, low), axis=1, keepdims=True)
+    high = jnp.max(functools.reduce(jnp.maximum, high), axis=1, keepdims=True)
+    row = lax.broadcasted_iota(jnp.int32, low.shape, 0)
+    radius = jnp.maximum(jnp.abs(low), jnp.abs(high))
+    width = jnp.max(jnp.where(row == 3, radius, 0.5 * (high - low)), axis=0, keepdims=True)
+
+    def over(table, least):
+        return least(least(table, axis=1, keepdims=True), axis=0, keepdims=True)
+
     up, down = powers(1), powers(-1)
-    size = jnp.min(jnp.where(up >= width, up, F32(2.0**63)))
-    inv = jnp.max(jnp.where(up >= width, down, F32(2.0**-63)))
+    size = over(jnp.where(up >= width, up, F32(2.0**63)), jnp.min)
+    inv = over(jnp.where(up >= width, down, F32(2.0**-63)), jnp.max)
     magic = size * F32(1.5 * 2.0**20)
-    centre = [(0.5 * (lo + hi) + magic) - magic for lo, hi in zip(low, high)]
-    return centre, inv
+    return inv, (0.5 * (low + high) + magic) - magic
+
+
+def split_frame(scale):
+    return scale[0:1, 0:1], [scale[k : k + 1, 0:1] for k in range(1, 4)]
 
 
 def split_features(points, centre, inv):
@@ -73,15 +85,16 @@
     grid, rest = [], []
     for k in range(3):
         u = (points[k] - centre[k]) * inv
-        h = (u + magic) - magic
+        h = cut((u + magic) - magic)
         grid.append(h)
         rest.append(u - h)
     rad = points[3] * inv
     norm = grid[0] * grid[0] + grid[1] * grid[1] + grid[2] * grid[2]
     norm1 = cut(norm)
-    norm2 = norm - norm1
+    norm2 = cut(norm - norm1)
     cross = grid[0] * rest[0] + grid[1] * rest[1] + grid[2] * rest[2]
     extra = 2.0 * cross + (rest[0] * rest[0] + rest[1] * rest[1] + rest[2] * rest[2]) + rad * rad
+    extra = extra + ((norm - norm1) - norm2)
     extra1 = cut(extra)
     extra2 = cut(extra - extra1)
     extra3 = (extra - extra1) - extra2
@@ -159,7 +172,7 @@
 
 
 def inverse_root(d):
-    return lax.exp2(-0.5 * lax.log2(d))
+    return lax.rsqrt(d)
 
 
 def fold(v):
@@ -237,16 +250,28 @@
     def place(s):
         for shift in range(S):
             owner = (s - shift) % S
-            q[:, owner * L : (owner + 1) * L] = pieces[shift][...]
+            q[:, owner * L : (owner + 1) * L] = pieces[shift][: q.shape[0], :]
 
     for s in range(S):
         pl.when(sub == s)(functools.partial(place, s))
 
 
-def pack_kernel(sizes, charges, mask, geo, targets, sources, live, masked, geo_out, *packs):
+def pack_kernel(
+    sizes, charges, mask, geo, basis_far, transfer_far, parent_far, targets, sources, live, masked, geo_out, *rest
+):
     C, S, L, slots = sizes
+    clusters = charges.shape[0]
+    *packs, basis, transfer, parent, sems = rest
+    copies = [
+        pltpu.make_async_copy(src, dst, sems.at[k])
+        for k, (src, dst) in enumerate(
+            [(basis_far, basis), (transfer_far, transfer), (parent_far, parent)]
+        )
+    ]
+    for copy in copies:
+        copy.start()
     me, sub = lax.axis_index("clu"), lax.axis_index("sub")
-    masked[...] = charges[...] * mask[...].astype(F32)
+    masked[:clusters, :] = charges[...] * mask[...].astype(F32)
     geo_out[...] = geo[...]
     lane = lax.broadcasted_iota(jnp.int32, (8, L), 1)
     for shift in range(1, C):
@@ -270,15 +295,20 @@
 
     for s in range(S):
         pl.when(sub == s)(functools.partial(fill, s))
-
-
-def remote_kernel(sizes, geo, up, *rest):
+    for copy in copies:
+        copy.wait()
+    up = up_sums(basis, masked, transfer, parent, masked.shape[0] - clusters)
+    masked[clusters:, :] = jnp.zeros((up.shape[0], L), F32)
+    masked[clusters:, : up.shape[1]] = up
+
+
+def remote_kernel(sizes, fb0, fb1, scale, *rest):
     C, S, L, slots, clusters, panels = sizes
     pieces = rest[:S]
     packs = rest[S : S + C - 1]
     acc_out = rest[S + C - 1]
     sends = rest[S + C : S + C + C - 1]
-    q, tq, acc, fwdt, sgeo, fa0, fb0, fb1, order, codes, sems, *work = rest[S + C + C - 1 :]
+    q, tq, acc, fwdt, fa0, order, codes, sems, *work = rest[S + C + C - 1 :]
     fa, fb = (fa0,), (fb0, fb1)
     n = (C - 1) * slots
     copies = [
@@ -299,25 +329,18 @@
             order[n + 1 + shift * slots + j] = jnp.maximum(code, 0)
             order[found] = shift * slots + j
             found = found + (code >= 0).astype(jnp.int32)
-            g = geo[jnp.maximum(code, 0)]
-            for k in range(4):
-                row = k * n + shift * slots + j
-                sgeo[row : row + 1, :] = g[k : k + 1]
-    tpoints = [
-        jnp.concatenate([p[k * slots : (k + 1) * slots, :] for p in packs], axis=0) for k in range(5)
-    ]
-    spoints = [sgeo[k * n : (k + 1) * n, :] for k in range(4)]
-    centre, inv = frame([tpoints, spoints])
-    for first in range(0, n, 8):
-        left, _, _ = split_features([v[first : first + 8, :] for v in tpoints], centre, inv)
-        store_features(fa, left, first)
-        _, right, _ = split_features([v[first : first + 8, :] for v in spoints], centre, inv)
-        store_features(fb, right, first)
-    tq[...] = tpoints[4]
+    inv, centre = split_frame(scale)
+    for shift in range(C - 1):
+        for first in range(0, slots, 8):
+            points = [packs[shift][k * slots + first : k * slots + first + 8, :] for k in range(5)]
+            left, _, _ = split_features(points, centre, inv)
+            store_features(fa, left, shift * slots + first)
+            at = shift * slots + first
+            tq[at : at + 8, :] = points[4]
 
     def begin(i, dist):
         slot = order[jnp.minimum(i, jnp.maximum(found - 1, 0))]
-        distances(load_features(fa, slot), load_features(fb, slot), dist)
+        distances(load_features(fa, slot), load_features(fb, order[n + 1 + slot]), dist)
 
     def finish(i, dist, part):
         ok = i < found
@@ -332,42 +355,32 @@
     pipeline(found, begin, finish, fwdt, work[:8], work[8:])
     acc_out[...] = acc[...] * inv
     fwd = (fwdt[...] * inv).T
-    rank = up.shape[1]
+    up = sum(p[clusters:, :] for p in pieces)
     for shift in range(C - 1):
         sends[shift][:slots, :] = fwd[shift * slots : (shift + 1) * slots, :]
-        sends[shift][slots:, :] = jnp.zeros((up.shape[0], L), F32)
-        sends[shift][slots:, :rank] = up[...]
-
-
-def prepare_kernel(
-    geo, masked, basis_far, transfer_far, parent_far,
-    fa0, fa1, fb0, fb1, diag, scale, up, basis, transfer, parent, sems
-):
-    copies = [
-        pltpu.make_async_copy(src, dst, sems.at[k])
-        for k, (src, dst) in enumerate(
-            [(basis_far, basis), (transfer_far, transfer), (parent_far, parent)]
-        )
-    ]
-    for copy in copies:
-        copy.start()
-    centre, inv = frame([[geo[:, k, :] for k in range(4)]])
+        sends[shift][slots:, :] = up
+
+
+def prepare_kernel(geo, fa0, fa1, fb0, fb1, diag, scale):
+    inv, centre = frame(geo)
+    scale[...] = jnp.zeros_like(scale)
+    scale[0:1, :] = jnp.broadcast_to(inv, (1, LANES))
+    for k in range(3):
+        scale[k + 1 : k + 2, :] = jnp.broadcast_to(centre[k : k + 1, :], (1, LANES))
+    inv, centre = split_frame(scale)
     for first in range(0, geo.shape[0], 8):
         points = [geo[first : first + 8, k, :] for k in range(4)]
         left, right, rad = split_features(points, centre, inv)
         store_features((fa0, fa1), left, first)
         store_features((fb0, fb1), right, first)
         diag[first : first + 8, :] = lax.rsqrt(2.0 * (rad * rad))
-    scale[...] = jnp.full(scale.shape, inv, F32)
-    for copy in copies:
-        copy.wait()
-    up_sums(basis, masked, transfer, parent, up)
 
 
 def local_kernel(sizes, geo_pairs, pairs, fa0, fa1, fb0, fb1, diags, scale, acc_in, *rest):
     S, L, R, clusters, panels = sizes
     pieces = rest[:S]
-    acc_out, q, acc, self_sums, pair_sums, *work = rest[S:]
+    parts = rest[S : 2 * S]
+    q, acc, self_sums, pair_sums, *work = rest[2 * S :]
     ring, sums = work[:16], work[16:]
     fa, fb = (fa0, fa1), (fb0, fb1)
     sub, rep = lax.axis_index("sub"), lax.axis_index("rep")
@@ -440,22 +453,34 @@
     total = acc[...] + self_sums[...].T
     width = geo_pairs.shape[1]
     total = total + select_rows(geo_pairs[0:1, :], pair_sums[...].T[:width, :], clusters)
-    acc_out[...] = acc_in[...] + total * scale[0:1, 0:1]
-
-
-def merge_kernel(sizes, far_list, targets, near, coupling, transfer, parent, up, *rest):
+    total = acc_in[...] + total * scale[0:1, 0:1]
+
+    def give(s):
+        for shift in range(S):
+            other = (s + shift) % S
+            parts[shift][...] = total[:, other * L : (other + 1) * L]
+
+    for s in range(S):
+        pl.when(sub == s)(functools.partial(give, s))
+
+
+def merge_kernel(sizes, far_list, targets, coupling, transfer, parent, *rest):
     C, S, L, slots, clusters = sizes
-    sums = rest[: C - 1]
-    parts = rest[C - 1 : C - 1 + S]
-    parents = rest[-1]
-    me, sub = lax.axis_index("clu"), lax.axis_index("sub")
+    near = rest[:S]
+    pieces = rest[S : 2 * S]
+    sums = rest[2 * S : 2 * S + C - 1]
+    near_out, field_out, parents = rest[2 * S + C - 1 :]
+    me = lax.axis_index("clu")
     index = [targets[pl.ds(lax.rem(me + shift, C), 1), :] for shift in range(1, C)]
     got = select_rows(
         jnp.concatenate(index, axis=1), jnp.concatenate([v[:slots, :] for v in sums], axis=0), clusters
     )
 
+    near_out[...] = got + sum(v[...] for v in near)
+
     par_dev, far_n, rank = coupling.shape[0], coupling.shape[1], coupling.shape[2]
-    parents[pl.ds(pl.multiple_of(me * par_dev, 8), par_dev), :] = up[...]
+    own = sum(p[clusters:, :rank] for p in pieces)
+    parents[pl.ds(pl.multiple_of(me * par_dev, 8), par_dev), :] = own
     for shift in range(1, C):
         owner = lax.rem(me + shift, C)
         parents[pl.ds(pl.multiple_of(owner * par_dev, 8), par_dev), :] = sums[shift - 1][slots:, :rank]
@@ -469,24 +494,11 @@
     which = lax.broadcasted_iota(jnp.int32, (LANES, clusters), 0)
     onehot = (parent[...] == which).astype(F32)
     down = jnp.dot(field, onehot, precision=HIGHEST, preferred_element_type=F32)
-    fields = jnp.concatenate(
-        [jnp.sum(transfer[r] * down, axis=0, keepdims=True) for r in range(rank)], axis=0
-    )
-
-    def give(s):
-        for shift in range(S):
-            other = (s + shift) % S
-            part = near[:, other * L : (other + 1) * L]
-            parts[shift][:clusters, :] = part + got if shift == 0 else part
-            for t in range(clusters // L):
-                at = clusters + t * rank
-                parts[shift][at : at + rank, :] = fields[:, t * L : (t + 1) * L]
-
-    for s in range(S):
-        pl.when(sub == s)(functools.partial(give, s))
-
-
-def up_sums(basis, masked, transfer, parent, up):
+    for r in range(rank):
+        field_out[r : r + 1, :] = jnp.sum(transfer[r] * down, axis=0, keepdims=True)
+
+
+def up_sums(basis, masked, transfer, parent, count):
     clusters = basis.shape[0]
     rank = basis.shape[1]
     lane = lax.broadcasted_iota(jnp.int32, (rank, clusters), 1)
@@ -497,20 +509,16 @@
     lifted = jnp.zeros((rank, clusters), F32)
     for r in range(rank):
         lifted = lifted + transfer[r] * leaf[r : r + 1, :]
-    which = lax.broadcasted_iota(jnp.int32, (up.shape[0], clusters), 0)
+    which = lax.broadcasted_iota(jnp.int32, (count, clusters), 0)
     onehot = (parent[...] == which).astype(F32)
-    up[...] = lax.dot_general(
+    return lax.dot_general(
         onehot, lifted, (((1,), (1,)), ((), ())), precision=HIGHEST, preferred_element_type=F32
     )
 
 
-def far_kernel(basis, near, out):
-    clusters, rank = basis.shape[0], basis.shape[1]
-    L = out.shape[1]
-    fields = [near[clusters + t * rank : clusters + (t + 1) * rank, :] for t in range(clusters // L)]
-    fields = jnp.concatenate(fields, axis=1) if len(fields) > 1 else fields[0]
-    for c in range(clusters):
-        far = jnp.sum(basis[c] * fields[:, c : c + 1], axis=0, keepdims=True)
+def far_kernel(basis, field, near, out):
+    for c in range(basis.shape[0]):
+        far = jnp.sum(basis[c] * field[:, c : c + 1], axis=0, keepdims=True)
         out[c : c + 1, :] = far + near[c : c + 1, :]
 
 
@@ -567,54 +575,56 @@
 
     made = pl.pallas_call(
         functools.partial(pack_kernel, (C, S, L, slots)),
-        out_shape=[pltpu.VMEM((clusters, L), F32), pltpu.VMEM(geometry.shape, F32)]
+        out_shape=[pltpu.VMEM((clusters + par_dev, L), F32), pltpu.VMEM(geometry.shape, F32)]
         + [pltpu.VMEM((5 * slots + 8, L), F32)] * (C - 1),
-        in_specs=[vmem()] * 3 + [smem()] * 3,
+        in_specs=[vmem()] * 3 + [pl.BlockSpec(memory_space=pltpu.HBM)] * 3 + [smem()] * 3,
         out_specs=[vmem()] * (C + 1),
-        compiler_params=limit(60),
-        cost_estimate=about(2),
-        name="packs",
-    )(charges, panel_mask, geometry, targets, remote_source[0], remote_live[0])
-    masked, geo, packs = made[0], made[1], made[2:]
-    pieces = [masked] + [send(masked, (("sub", d),)) for d in range(1, S)]
-    packs = [send(packs[d - 1], (("clu", d),)) for d in range(1, C)]
-
-    *features, up = pl.pallas_call(
-        prepare_kernel,
-        out_shape=[pltpu.VMEM((clusters * ROWS, LANES), F32)] * 4
-        + [
-            pltpu.VMEM((clusters, panels), F32),
-            pltpu.VMEM((8, LANES), F32),
-            pltpu.VMEM((par_dev, rank), F32),
-        ],
-        in_specs=[vmem()] * 2 + [pl.BlockSpec(memory_space=pltpu.HBM)] * 3,
-        out_specs=[vmem()] * 7,
         scratch_shapes=[
             pltpu.VMEM(basis_t.shape, F32),
             pltpu.VMEM(transfer_t.shape, F32),
             pltpu.VMEM(parent.shape, jnp.int32),
             pltpu.SemaphoreType.DMA((3,)),
         ],
-        compiler_params=limit(32),
+        compiler_params=limit(60),
+        cost_estimate=about(3),
+        name="packs",
+    )(
+        charges,
+        panel_mask,
+        geometry,
+        *far_off(basis_t, transfer_t, parent),
+        targets,
+        remote_source[0],
+        remote_live[0],
+    )
+    masked, geo, packs = made[0], made[1], made[2:]
+    pieces = [masked] + [send(masked, (("sub", d),)) for d in range(1, S)]
+    packs = [send(packs[d - 1], (("clu", d),)) for d in range(1, C)]
+
+    features = pl.pallas_call(
+        prepare_kernel,
+        out_shape=[pltpu.VMEM((clusters * ROWS, LANES), F32)] * 4
+        + [pltpu.VMEM((clusters, panels), F32), pltpu.VMEM((8, LANES), F32)],
+        in_specs=[vmem()],
+        out_specs=[vmem()] * 6,
+        compiler_params=limit(24),
         cost_estimate=about(4),
         name="prepare",
-    )(*near_by(geo, masked), *far_off(basis_t, transfer_t, parent))
+    )(*near_by(geo))
+    fb0, fb1, scale = features[2], features[3], features[5]
 
     made = pl.pallas_call(
         functools.partial(remote_kernel, (C, S, L, slots, clusters, panels)),
         out_shape=[pltpu.VMEM((clusters, panels), F32)]
         + [pltpu.VMEM((slots + par_dev, L), F32)] * (C - 1),
-        in_specs=[vmem()] * (2 + S + C - 1),
+        in_specs=[vmem()] * (3 + S + C - 1),
         out_specs=[vmem()] * C,
         scratch_shapes=[
             pltpu.VMEM((clusters, panels), F32),
             pltpu.VMEM((n, L), F32),
             pltpu.VMEM((clusters, panels), F32),
             pltpu.VMEM((L, whole(n)), F32),
-            pltpu.VMEM((4 * n, panels), F32),
             pltpu.VMEM((n * ROWS, L), F32),
-            pltpu.VMEM((n * ROWS, LANES), F32),
-            pltpu.VMEM((n * ROWS, LANES), F32),
             pltpu.SMEM((2 * n + 1,), jnp.int32),
             pltpu.SMEM((C - 1, 8, L), F32),
             pltpu.SemaphoreType.DMA((C - 1,)),
@@ -624,15 +634,15 @@
         compiler_params=limit(24),
         cost_estimate=about(6),
         name="near_remote",
-    )(*near_by(geo, up, *pieces, *packs))
-    acc, sums = made[0], [send(made[d], (("clu", C - d),)) for d in range(1, C)]
+    )(*near_by(fb0, fb1, scale, *pieces, *packs))
+    acc, sums = made[0], made[1:]
 
     wide = whole(local_pairs.shape[1])
-    acc = pl.pallas_call(
+    parts = pl.pallas_call(
         functools.partial(local_kernel, (S, L, R, clusters, panels)),
-        out_shape=pltpu.VMEM((clusters, panels), F32),
+        out_shape=[pltpu.VMEM((clusters, L), F32)] * S,
         in_specs=[vmem(), smem()] + [vmem()] * (7 + S),
-        out_specs=vmem(),
+        out_specs=[vmem()] * S,
         scratch_shapes=[
             pltpu.VMEM((clusters, panels), F32),
             pltpu.VMEM((clusters, panels), F32),
@@ -642,36 +652,35 @@
         + [pltpu.VMEM((panels, panels), F32)] * 16
         + [pltpu.VMEM((panels, 2 * LANES), BF16)] * 4,
         compiler_params=limit(24),
-        cost_estimate=about(15),
+        cost_estimate=about(12),
         name="near_local",
     )(*near_by(local_pairs[0].T), local_pairs[0].T, *near_by(*features, acc, *pieces))
-
-    parts = pl.pallas_call(
+    near = [parts[0]] + [send(parts[d], (("sub", d),)) for d in range(1, S)]
+    sums = [send(sums[d - 1], (("clu", C - d),)) for d in range(1, C)]
+
+    near, field = pl.pallas_call(
         functools.partial(merge_kernel, (C, S, L, slots, clusters)),
-        out_shape=[pltpu.VMEM((clusters + clusters // L * rank, L), F32)] * S,
-        in_specs=[smem()] + [vmem()] * (6 + C - 1),
-        out_specs=[vmem()] * S,
+        out_shape=[pltpu.VMEM((clusters, L), F32), pltpu.VMEM((rank, clusters), F32)],
+        in_specs=[smem()] + [vmem()] * (4 + 2 * S + C - 1),
+        out_specs=[vmem()] * 2,
         scratch_shapes=[pltpu.VMEM((C * par_dev, rank), F32)],
         compiler_params=limit(16),
         cost_estimate=about(2),
         name="merge",
-    )(far_list.T, *near_by(targets, acc, coupling, transfer_t, parent, up, *sums))
-    near = parts[0]
-    for d in range(1, S):
-        near = near + send(parts[d], (("sub", d),))
+    )(far_list.T, *near_by(targets, coupling, transfer_t, parent, *near, *pieces, *sums))
     others = [send(near, (("rep", e),)) for e in range(1, R)]
 
     total = pl.pallas_call(
         far_kernel,
         out_shape=pltpu.VMEM((clusters, L), F32),
-        in_specs=[vmem()] * 2,
+        in_specs=[vmem()] * 3,
         out_specs=vmem(),
         compiler_params=limit(16),
         cost_estimate=about(1),
         name="far_down",
-    )(*near_by(basis_t, near))
+    )(*near_by(basis_t, field, near))
     for other in others:
-        total = total + other[:clusters]
+        total = total + other
     return total * panel_mask.astype(F32)
 
 

time: 44.4 us -> 46.3 us (1.043)
  waiting for transfers between devices: 4.55 us -> 5.95 us
  Pallas kernels: 27.4 us -> 28 us
    pallas_call x1, Pallas kernels: 1.34 us -> 3.6 us  [on_device(): pl.pallas_call(functools.partial(pack_kernel, (C, S, L, slots)), out_shap...]
    ppermute x9, waiting for transfers between devices: 4.55 us -> 5.95 us  [send(): return lax.ppermute(value, names if len(names) > 1 else names[0], perm)]
    pallas_call x1, Pallas kernels: 12.9 us -> 11.8 us  [on_device(): pl.pallas_call(functools.partial(local_kernel, (S, L, R, clusters, panels...]
  transfers between devices with their start and end apart: 9 -> 9, of which waited for: 2 -> 4; matrix products, arithmetic and copies ran while one was open for 0% -> 0% of each run, Pallas kernels for 42% -> 12%
where the time goes in v16:
time: 46.3 us; the launch traced here: 46.1 us
  Pallas kernels  28 us (60%)
  starting transfers between devices  11.3 us (24%)
  waiting for transfers between devices  5.95 us (13%)
  other arithmetic  0.64 us (1%)
    pallas_call x1, Pallas kernels, on_device(): pl.pallas_call(functools.partial(local_kernel, (S, L, R, clusters, panels...  11.8 us
    ppermute x9, starting transfers between devices, send(): return lax.ppermute(value, names if len(names) > 1 else names[0], perm)  11.3 us
    ppermute x9, waiting for transfers between devices, send(): return lax.ppermute(value, names if len(names) > 1 else names[0], perm)  5.95 us
    pallas_call x1, Pallas kernels, on_device(): pl.pallas_call(functools.partial(remote_kernel, (C, S, L, slots, clusters...  5.71 us
    pallas_call x1, Pallas kernels, on_device(): pl.pallas_call(prepare_kernel, out_shape=[pltpu.VMEM((clusters * ROWS, LA...  4.74 us
    pallas_call x1, Pallas kernels, on_device(): pl.pallas_call(functools.partial(pack_kernel, (C, S, L, slots)), out_shap...  3.6 us
    pallas_call x1, Pallas kernels, on_device(): pl.pallas_call(functools.partial(merge_kernel, (C, S, L, slots, clusters)...  1.25 us
  transfers between devices with their start and end apart: 9, of which 4 were waited for; matrix products, arithmetic and copies ran while one was open for 0% of the time, Pallas kernels for 12%

profile of v16, /device:TPU:0, one launch (start us, length us, event | category | flops | bytes accessed | tf_op | source)
XLA Modules:
  0.0 46.1 jit_solution(16506988721894701200)
XLA Ops:
  0.0 3.6 %packs.1 = (f32[144,128]{1,0:T(8,128)S(1)}, f32[128,4,256]{2,1,0:T(4,128)S(1)}, f32[88,128]{1,0:T(8,128)S(1)}, f32[88,128]{1,0:T(8,128)S(1)}, f32[88,128]{1,0:T(8,128)S(1)}) custom-call(f32[128,128]{1,0:T(8,128)} %charges.1, s32[128,128]{1,0:T(8,128)} %mask.1, f32[128,4,256]{2,1,0:T(4,128)} %geo.1, f32[128,32,128]{2,1,0:T(8,128)} %bitcast.10, ...), custom_call_target="tpu_custom_call" | custom-call | bytes 10500000 | tf_op jit(solution)/shard_map/packs/pallas_call | solution.py:576
  3.6 3.0 %collective-permute-start = (f32[144,128]{1,0:T(8,128)S(1)}, f32[144,128]{1,0:T(8,128)S(1)}, u32[]{:S(2)}, u32[]{:S(2)}) collective-permute-start(f32[144,128]{1,0:T(8,128)S(1)} %get-tuple-element.31.rest_0_.rest_2_), channel_id=1, source_target_pairs={{0,2},{2,0},{1,3},{3,1},{4,6},{6,4},{5,7},{7,5},{8,10},{10,8},{9,1... | collective-permute-start | bytes 221192 | tf_op jit(solution)/shard_map/ppermute | solution.py:547
  6.6 1.6 %collective-permute-start.1 = (f32[88,128]{1,0:T(8,128)S(1)}, f32[88,128]{1,0:T(8,128)S(1)}, u32[]{:S(2)}, u32[]{:S(2)}) collective-permute-start(f32[88,128]{1,0:T(8,128)S(1)} %get-tuple-element.32), channel_id=1, source_target_pairs={{0,4},{4,8},{8,12},{12,0},{1,5},{5,9},{9,13},{13,1},{2,6},{6,10},{... | collective-permute-start | bytes 135176 | tf_op jit(solution)/shard_map/ppermute | solution.py:547
  8.2 2.6 %collective-permute-start.2 = (f32[88,128]{1,0:T(8,128)S(1)}, f32[88,128]{1,0:T(8,128)S(1)}, u32[]{:S(2)}, u32[]{:S(2)}) collective-permute-start(f32[88,128]{1,0:T(8,128)S(1)} %get-tuple-element.33), channel_id=1, source_target_pairs={{0,8},{4,12},{8,0},{12,4},{1,9},{5,13},{9,1},{13,5},{2,10},{6,14},... | collective-permute-start | bytes 135176 | tf_op jit(solution)/shard_map/ppermute | solution.py:547
  10.8 1.3 %collective-permute-start.3 = (f32[88,128]{1,0:T(8,128)S(1)}, f32[88,128]{1,0:T(8,128)S(1)}, u32[]{:S(2)}, u32[]{:S(2)}) collective-permute-start(f32[88,128]{1,0:T(8,128)S(1)} %get-tuple-element.34), channel_id=1, source_target_pairs={{0,12},{4,0},{8,4},{12,8},{1,13},{5,1},{9,5},{13,9},{2,14},{6,2},{... | collective-permute-start | bytes 135176 | tf_op jit(solution)/shard_map/ppermute | solution.py:547
  12.1 4.7 %prepare.1 = (f32[3072,128]{1,0:T(8,128)S(1)}, f32[3072,128]{1,0:T(8,128)S(1)}, f32[3072,128]{1,0:T(8,128)S(1)}, f32[3072,128]{1,0:T(8,128)S(1)}, f32[128,256]{1,0:T(8,128)S(1)}, /*index=5*/f32[8,128]{1,0:T(8,128)S(1)}) custom-call(f32[128,4,256]{2,1,0:T(4,128)S(1)} %get-tuple-element.24.geo), custom_call_target="tpu_custom_call" | custom-call | bytes 14000000 | tf_op jit(solution)/shard_map/prepare/pallas_call | solution.py:604
  16.9 0.0 collective-permute-done.1.rest_2_
  16.9 0.0 collective-permute-done.2.rest_3_
  16.9 0.0 collective-permute-done.3.rest_4_
  16.9 0.0 collective-permute-done.rest_1_.rest_3_
  16.9 0.0 copy-start.5
  16.9 5.7 %near_remote.1 = (f32[128,256]{1,0:T(8,128)S(1)}, f32[32,128]{1,0:T(8,128)S(1)}, f32[32,128]{1,0:T(8,128)S(1)}, f32[32,128]{1,0:T(8,128)S(1)}) custom-call(f32[3072,128]{1,0:T(8,128)S(1)} %get-tuple-element.27.fb0, f32[3072,128]{1,0:T(8,128)S(1)} %get-tuple-element.28.fb1, f32[8,128]{1,0:T(8,128)S(1)} %get-tuple-element.30.scale, ...), custom_call_target="tpu_custom_call" | custom-call | bytes 21000000 | tf_op jit(solution)/shard_map/near_remote/pallas_call | solution.py:616
  22.7 0.0 copy-done.5
  22.7 0.0 copy-start.1
  22.7 0.0 copy-start.2
  22.7 0.0 copy-start.3
  22.7 0.0 copy-start.4
  22.7 0.0 copy-start.6
  22.7 11.8 %near_local.1 = (f32[128,128]{1,0:T(8,128)S(1)}, f32[128,128]{1,0:T(8,128)S(1)}) custom-call(s32[2,128]{1,0:T(2,128)S(1)} %bitcast.17, s32[2,128]{1,0:T(2,128)S(1)} %bitcast.18, f32[3072,128]{1,0:T(8,128)S(1)} %get-tuple-element.25.fa0, f32[3072,128]{1,0:T(8,128)S(1)} %get-tuple-element.26.fa1, f32[3072,128]{1,0:T(8,128)S(1)} %get-tuple-element.27.fb0, ...), custom_call_target="tpu_custom_call" | custom-call | bytes 42000000 | tf_op jit(solution)/shard_map/near_local/pallas_call | solution.py:641
  34.6 0.0 copy-start
  34.6 0.6 %collective-permute-start.4 = (f32[128,128]{1,0:T(8,128)S(1)}, f32[128,128]{1,0:T(8,128)S(1)}, u32[]{:S(2)}, u32[]{:S(2)}) collective-permute-start(f32[128,128]{1,0:T(8,128)S(1)} %get-tuple-element.37), channel_id=1, source_target_pairs={{0,2},{2,0},{1,3},{3,1},{4,6},{6,4},{5,7},{7,5},{8,10},{10,8},{9,1... | collective-permute-start | bytes 196616 | tf_op jit(solution)/shard_map/ppermute | solution.py:547
  35.2 1.0 %collective-permute-start.5 = (f32[32,128]{1,0:T(8,128)S(1)}, f32[32,128]{1,0:T(8,128)S(1)}, u32[]{:S(2)}, u32[]{:S(2)}) collective-permute-start(f32[32,128]{1,0:T(8,128)S(1)} %get-tuple-element.38), channel_id=1, source_target_pairs={{0,12},{4,0},{8,4},{12,8},{1,13},{5,1},{9,5},{13,9},{2,14},{6,2},{... | collective-permute-start | bytes 49160 | tf_op jit(solution)/shard_map/ppermute | solution.py:547
  36.2 1.1 %collective-permute-start.6 = (f32[32,128]{1,0:T(8,128)S(1)}, f32[32,128]{1,0:T(8,128)S(1)}, u32[]{:S(2)}, u32[]{:S(2)}) collective-permute-start(f32[32,128]{1,0:T(8,128)S(1)} %get-tuple-element.39), channel_id=1, source_target_pairs={{0,8},{4,12},{8,0},{12,4},{1,9},{5,13},{9,1},{13,5},{2,10},{6,14},... | collective-permute-start | bytes 49160 | tf_op jit(solution)/shard_map/ppermute | solution.py:547
  37.3 0.0 collective-permute-start.7
  37.3 1.6 %collective-permute-done.5.rest_4_ = f32[32,128]{1,0:T(8,128)S(1)} collective-permute-done((f32[32,128]{1,0:T(8,128)S(1)}, f32[32,128]{1,0:T(8,128)S(1)}, u32[]{:S(2)}, u32[]{:S(2)}) %collective-permute-start.5) | collective-permute-done | bytes 16416 | tf_op jit(solution)/shard_map/ppermute | solution.py:547
  38.9 1.9 %collective-permute-done.6.rest_5_ = f32[32,128]{1,0:T(8,128)S(1)} collective-permute-done((f32[32,128]{1,0:T(8,128)S(1)}, f32[32,128]{1,0:T(8,128)S(1)}, u32[]{:S(2)}, u32[]{:S(2)}) %collective-permute-start.6) | collective-permute-done | bytes 16416 | tf_op jit(solution)/shard_map/ppermute | solution.py:547
  40.9 2.0 %collective-permute-done.7.rest_6_ = f32[32,128]{1,0:T(8,128)S(1)} collective-permute-done((f32[32,128]{1,0:T(8,128)S(1)}, f32[32,128]{1,0:T(8,128)S(1)}, u32[]{:S(2)}, u32[]{:S(2)}) %collective-permute-start.7) | collective-permute-done | bytes 16416 | tf_op jit(solution)/shard_map/ppermute | solution.py:547
  42.9 0.0 collective-permute-done.4.rest_1_
  42.9 0.0 copy-done.1
  42.9 0.0 copy-done.2
  42.9 0.0 copy-done.3
  42.9 0.0 copy-done.4
  42.9 0.0 copy-done.6
  42.9 1.2 %merge.1 = (f32[128,128]{1,0:T(8,128)S(1)}, f32[32,128]{1,0:T(8,128)S(1)}) custom-call(s32[8,16]{1,0:T(8,128)S(1)} %bitcast.16, s32[4,16]{1,0:T(4,128)S(1)} %bitcast.15, f32[16,8,32,32]{3,2,1,0:T(8,128)S(1)} %copy-done.1, f32[32,32,128]{2,1,0:T(8,128)S(1)} %bitcast.13, s32[1,128]{1,0:T(1,128)S(1)} %bitcast.20, f32[128,128]{1,0:T(8,128)S(1)} %get-tuple-element.36.rest_0_, ...), custom_call_target="tpu_custom_call" | custom-call | bytes 7000000 | tf_op jit(solution)/shard_map/merge/pallas_call | solution.py:661
  44.2 0.0 copy-start.7
  44.2 0.1 collective-permute-start.8
  44.3 0.0 copy-done
  44.3 0.8 %far_down.1 = f32[128,128]{1,0:T(8,128)S(1)} custom-call(f32[128,32,128]{2,1,0:T(8,128)S(1)} %bitcast.11, f32[32,128]{1,0:T(8,128)S(1)} %get-tuple-element.41.field, f32[128,128]{1,0:T(8,128)S(1)} %get-tuple-element.42.near), custom_call_target="tpu_custom_call" | custom-call | bytes 3500000 | tf_op jit(solution)/shard_map/far_down/pallas_call | solution.py:673
  45.1 0.4 collective-permute-done.8
  45.5 0.0 copy-done.7
  45.5 0.6 %convert_multiply_fusion = f32[128,128]{1,0:T(8,128)} fusion(s32[128,128]{1,0:T(8,128)S(1)} %copy-done.7, f32[128,128]{1,0:T(8,128)S(1)} %far_down.1, f32[128,128]{1,0:T(8,128)S(1)} %collective-permute-done.8), kind=kLoop, calls=%fused_computation | loop fusion | flops 49152 | bytes 262144 | tf_op jit(solution)/shard_map/mul | solution.py:684
Async XLA Ops:
  3.6 13.3 %collective-permute-start = (f32[144,128]{1,0:T(8,128)S(1)}, f32[144,128]{1,0:T(8,128)S(1)}, u32[]{:S(2)}, u32[]{:S(2)}) collective-permute-start(f32[144,128]{1,0:T(8,128)S(1)} %get-tuple-element.31.rest_0_.rest_2_), channel_id=1, source_target_pairs={{0,2},{2,0},{1,3},{3,1},{4,6},{6,4},{5,7},{7,5},{8,10},{10,8},{9,1... | collective-permute-start | bytes 221192 | tf_op jit(solution)/shard_map/ppermute | solution.py:547
  6.6 10.3 %collective-permute-start.1 = (f32[88,128]{1,0:T(8,128)S(1)}, f32[88,128]{1,0:T(8,128)S(1)}, u32[]{:S(2)}, u32[]{:S(2)}) collective-permute-start(f32[88,128]{1,0:T(8,128)S(1)} %get-tuple-element.32), channel_id=1, source_target_pairs={{0,4},{4,8},{8,12},{12,0},{1,5},{5,9},{9,13},{13,1},{2,6},{6,10},{... | collective-permute-start | bytes 135176 | tf_op jit(solution)/shard_map/ppermute | solution.py:547
  8.2 8.7 %collective-permute-start.2 = (f32[88,128]{1,0:T(8,128)S(1)}, f32[88,128]{1,0:T(8,128)S(1)}, u32[]{:S(2)}, u32[]{:S(2)}) collective-permute-start(f32[88,128]{1,0:T(8,128)S(1)} %get-tuple-element.33), channel_id=1, source_target_pairs={{0,8},{4,12},{8,0},{12,4},{1,9},{5,13},{9,1},{13,5},{2,10},{6,14},... | collective-permute-start | bytes 135176 | tf_op jit(solution)/shard_map/ppermute | solution.py:547
  10.8 6.1 %collective-permute-start.3 = (f32[88,128]{1,0:T(8,128)S(1)}, f32[88,128]{1,0:T(8,128)S(1)}, u32[]{:S(2)}, u32[]{:S(2)}) collective-permute-start(f32[88,128]{1,0:T(8,128)S(1)} %get-tuple-element.34), channel_id=1, source_target_pairs={{0,12},{4,0},{8,4},{12,8},{1,13},{5,1},{9,5},{13,9},{2,14},{6,2},{... | collective-permute-start | bytes 135176 | tf_op jit(solution)/shard_map/ppermute | solution.py:547
  16.9 5.7 %copy-start.5 = (s32[1,128,2]{1,2,0:T(2,128)S(1)}, s32[1,128,2]{1,2,0:T(2,128)}, u32[]{:S(2)}) copy-start(s32[1,128,2]{1,2,0:T(2,128)} %param.18) | copy-start | bytes 3076
  22.7 20.2 %copy-start.1 = (f32[16,8,32,32]{3,2,1,0:T(8,128)S(1)}, f32[16,8,32,32]{3,2,1,0:T(8,128)}, u32[]{:S(2)}) copy-start(f32[16,8,32,32]{3,2,1,0:T(8,128)} %coupling.1) | copy-start | bytes 1572868
  22.7 20.2 %copy-start.2 = (f32[128,32,32]{0,2,1:T(8,128)S(1)}, f32[128,32,32]{0,2,1:T(8,128)}, u32[]{:S(2)}) copy-start(f32[128,32,32]{0,2,1:T(8,128)} %param.20) | copy-start | bytes 1572868
  22.7 20.2 %copy-start.3 = (s32[1,4,16]{2,1,0:T(4,128)S(1)}, s32[1,4,16]{2,1,0:T(4,128)}, u32[]{:S(2)}) copy-start(s32[1,4,16]{2,1,0:T(4,128)} %param.16) | copy-start | bytes 772
  22.7 20.2 %copy-start.4 = (s32[16,8]{0,1:T(8,128)S(1)}, s32[16,8]{0,1:T(8,128)}, u32[]{:S(2)}) copy-start(s32[16,8]{0,1:T(8,128)} %param.22) | copy-start | bytes 1540
  22.7 20.2 %copy-start.6 = (s32[128]{0:T(128)S(1)}, s32[128]{0:T(128)}, u32[]{:S(2)}) copy-start(s32[128]{0:T(128)} %param.21) | copy-start | bytes 1540
  34.6 9.7 %copy-start = (f32[128,128,32]{1,2,0:T(8,128)S(1)}, f32[128,128,32]{1,2,0:T(8,128)}, u32[]{:S(2)}) copy-start(f32[128,128,32]{1,2,0:T(8,128)} %param.19) | copy-start | bytes 6291460
  34.6 8.3 %collective-permute-start.4 = (f32[128,128]{1,0:T(8,128)S(1)}, f32[128,128]{1,0:T(8,128)S(1)}, u32[]{:S(2)}, u32[]{:S(2)}) collective-permute-start(f32[128,128]{1,0:T(8,128)S(1)} %get-tuple-element.37), channel_id=1, source_target_pairs={{0,2},{2,0},{1,3},{3,1},{4,6},{6,4},{5,7},{7,5},{8,10},{10,8},{9,1... | collective-permute-start | bytes 196616 | tf_op jit(solution)/shard_map/ppermute | solution.py:547
  35.2 3.7 %collective-permute-start.5 = (f32[32,128]{1,0:T(8,128)S(1)}, f32[32,128]{1,0:T(8,128)S(1)}, u32[]{:S(2)}, u32[]{:S(2)}) collective-permute-start(f32[32,128]{1,0:T(8,128)S(1)} %get-tuple-element.38), channel_id=1, source_target_pairs={{0,12},{4,0},{8,4},{12,8},{1,13},{5,1},{9,5},{13,9},{2,14},{6,2},{... | collective-permute-start | bytes 49160 | tf_op jit(solution)/shard_map/ppermute | solution.py:547
  36.2 4.6 %collective-permute-start.6 = (f32[32,128]{1,0:T(8,128)S(1)}, f32[32,128]{1,0:T(8,128)S(1)}, u32[]{:S(2)}, u32[]{:S(2)}) collective-permute-start(f32[32,128]{1,0:T(8,128)S(1)} %get-tuple-element.39), channel_id=1, source_target_pairs={{0,8},{4,12},{8,0},{12,4},{1,9},{5,13},{9,1},{13,5},{2,10},{6,14},... | collective-permute-start | bytes 49160 | tf_op jit(solution)/shard_map/ppermute | solution.py:547
  37.3 5.5 %collective-permute-start.7 = (f32[32,128]{1,0:T(8,128)S(1)}, f32[32,128]{1,0:T(8,128)S(1)}, u32[]{:S(2)}, u32[]{:S(2)}) collective-permute-start(f32[32,128]{1,0:T(8,128)S(1)} %get-tuple-element.40), channel_id=1, source_target_pairs={{0,4},{4,8},{8,12},{12,0},{1,5},{5,9},{9,13},{13,1},{2,6},{6,10},{... | collective-permute-start | bytes 49160 | tf_op jit(solution)/shard_map/ppermute | solution.py:547
  44.2 1.3 %copy-start.7 = (s32[128,128]{1,0:T(8,128)S(1)}, s32[128,128]{1,0:T(8,128)}, u32[]{:S(2)}) copy-start(s32[128,128]{1,0:T(8,128)} %mask.1) | copy-start | bytes 196612
  44.2 1.3 %collective-permute-start.8 = (f32[128,128]{1,0:T(8,128)S(1)}, f32[128,128]{1,0:T(8,128)S(1)}, u32[]{:S(2)}, u32[]{:S(2)}) collective-permute-start(f32[128,128]{1,0:T(8,128)S(1)} %get-tuple-element.42.near), channel_id=1, source_target_pairs={{0,1},{1,0},{2,3},{3,2},{4,5},{5,4},{6,7},{7,6},{8,9},{9,8},{10,11... | collective-permute-start | bytes 196616 | tf_op jit(solution)/shard_map/ppermute | solution.py:547

commit v17 on v15

--- a/solution.py
+++ b/solution.py
@@ -54,18 +54,30 @@
     return out
 
 
-def frame(parts):
-    low = [functools.reduce(jnp.minimum, [jnp.min(p[k]) for p in parts]) for k in range(3)]
-    high = [functools.reduce(jnp.maximum, [jnp.max(p[k]) for p in parts]) for k in range(3)]
-    width = functools.reduce(jnp.maximum, [jnp.max(jnp.abs(p[3])) for p in parts])
-    for lo, hi in zip(low, high):
-        width = jnp.maximum(width, 0.5 * (hi - lo))
+def frame(geo):
+    low, high = [None] * 8, [None] * 8
+    for c in range(geo.shape[0]):
+        g, k = geo[c], c % 8
+        low[k] = g if low[k] is None else jnp.minimum(low[k], g)
+        high[k] = g if high[k] is None else jnp.maximum(high[k], g)
+    low = jnp.min(functools.reduce(jnp.minimum, low), axis=1, keepdims=True)
+    high = jnp.max(functools.reduce(jnp.maximum, high), axis=1, keepdims=True)
+    row = lax.broadcasted_iota(jnp.int32, low.shape, 0)
+    radius = jnp.maximum(jnp.abs(low), jnp.abs(high))
+    width = jnp.max(jnp.where(row == 3, radius, 0.5 * (high - low)), axis=0, keepdims=True)
+
+    def over(table, least):
+        return least(least(table, axis=1, keepdims=True), axis=0, keepdims=True)
+
     up, down = powers(1), powers(-1)
-    size = jnp.min(jnp.where(up >= width, up, F32(2.0**63)))
-    inv = jnp.max(jnp.where(up >= width, down, F32(2.0**-63)))
+    size = over(jnp.where(up >= width, up, F32(2.0**63)), jnp.min)
+    inv = over(jnp.where(up >= width, down, F32(2.0**-63)), jnp.max)
     magic = size * F32(1.5 * 2.0**20)
-    centre = [(0.5 * (lo + hi) + magic) - magic for lo, hi in zip(low, high)]
-    return centre, inv
+    return inv, (0.5 * (low + high) + magic) - magic
+
+
+def split_frame(scale):
+    return scale[0:1, 0:1], [scale[k : k + 1, 0:1] for k in range(1, 4)]
 
 
 def split_features(points, centre, inv):
@@ -73,15 +85,16 @@
     grid, rest = [], []
     for k in range(3):
         u = (points[k] - centre[k]) * inv
-        h = (u + magic) - magic
+        h = cut((u + magic) - magic)
         grid.append(h)
         rest.append(u - h)
     rad = points[3] * inv
     norm = grid[0] * grid[0] + grid[1] * grid[1] + grid[2] * grid[2]
     norm1 = cut(norm)
-    norm2 = norm - norm1
+    norm2 = cut(norm - norm1)
     cross = grid[0] * rest[0] + grid[1] * rest[1] + grid[2] * rest[2]
     extra = 2.0 * cross + (rest[0] * rest[0] + rest[1] * rest[1] + rest[2] * rest[2]) + rad * rad
+    extra = extra + ((norm - norm1) - norm2)
     extra1 = cut(extra)
     extra2 = cut(extra - extra1)
     extra3 = (extra - extra1) - extra2
@@ -107,15 +120,19 @@
 
 def store_features(ref, rows, first):
     width = rows[0].shape[1]
-    for k, row in enumerate(rows):
-        for t, piece in enumerate(ref):
-            at = pl.ds(first * ROWS + k, 8, stride=ROWS)
-            piece[at, :] = row[:, t * LANES : min(width, (t + 1) * LANES)]
+    for t, piece in enumerate(ref):
+        count = piece.shape[0] // ROWS
+        for k, row in enumerate(rows):
+            at = k * count + first
+            piece[at : at + 8, :] = row[:, t * LANES : min(width, (t + 1) * LANES)]
 
 
 def load_features(ref, index):
-    start = pl.multiple_of(index * ROWS, 8)
-    blocks = [piece[pl.ds(start, ROWS), :] for piece in ref]
+    blocks = []
+    for piece in ref:
+        count = piece.shape[0] // ROWS
+        groups = [piece[pl.ds(k * count + index, 8, stride=count), :] for k in range(0, ROWS, 8)]
+        blocks.append(jnp.concatenate(groups, axis=0))
     return jnp.concatenate(blocks, axis=1) if len(blocks) > 1 else blocks[0]
 
 
@@ -159,7 +176,7 @@
 
 
 def inverse_root(d):
-    return lax.exp2(-0.5 * lax.log2(d))
+    return lax.rsqrt(d)
 
 
 def fold(v):
@@ -237,7 +254,7 @@
     def place(s):
         for shift in range(S):
             owner = (s - shift) % S
-            q[:, owner * L : (owner + 1) * L] = pieces[shift][...]
+            q[:, owner * L : (owner + 1) * L] = pieces[shift][: q.shape[0], :]
 
     for s in range(S):
         pl.when(sub == s)(functools.partial(place, s))
@@ -272,13 +289,13 @@
         pl.when(sub == s)(functools.partial(fill, s))
 
 
-def remote_kernel(sizes, geo, up, *rest):
+def remote_kernel(sizes, fb0, fb1, scale, up, *rest):
     C, S, L, slots, clusters, panels = sizes
     pieces = rest[:S]
     packs = rest[S : S + C - 1]
     acc_out = rest[S + C - 1]
     sends = rest[S + C : S + C + C - 1]
-    q, tq, acc, fwdt, sgeo, fa0, fb0, fb1, order, codes, sems, *work = rest[S + C + C - 1 :]
+    q, tq, acc, fwdt, fa0, order, codes, sems, *work = rest[S + C + C - 1 :]
     fa, fb = (fa0,), (fb0, fb1)
     n = (C - 1) * slots
     copies = [
@@ -299,25 +316,18 @@
             order[n + 1 + shift * slots + j] = jnp.maximum(code, 0)
             order[found] = shift * slots + j
             found = found + (code >= 0).astype(jnp.int32)
-            g = geo[jnp.maximum(code, 0)]
-            for k in range(4):
-                row = k * n + shift * slots + j
-                sgeo[row : row + 1, :] = g[k : k + 1]
-    tpoints = [
-        jnp.concatenate([p[k * slots : (k + 1) * slots, :] for p in packs], axis=0) for k in range(5)
-    ]
-    spoints = [sgeo[k * n : (k + 1) * n, :] for k in range(4)]
-    centre, inv = frame([tpoints, spoints])
-    for first in range(0, n, 8):
-        left, _, _ = split_features([v[first : first + 8, :] for v in tpoints], centre, inv)
-        store_features(fa, left, first)
-        _, right, _ = split_features([v[first : first + 8, :] for v in spoints], centre, inv)
-        store_features(fb, right, first)
-    tq[...] = tpoints[4]
+    inv, centre = split_frame(scale)
+    for shift in range(C - 1):
+        for first in range(0, slots, 8):
+            points = [packs[shift][k * slots + first : k * slots + first + 8, :] for k in range(5)]
+            left, _, _ = split_features(points, centre, inv)
+            store_features(fa, left, shift * slots + first)
+            at = shift * slots + first
+            tq[at : at + 8, :] = points[4]
 
     def begin(i, dist):
         slot = order[jnp.minimum(i, jnp.maximum(found - 1, 0))]
-        distances(load_features(fa, slot), load_features(fb, slot), dist)
+        distances(load_features(fa, slot), load_features(fb, order[n + 1 + slot]), dist)
 
     def finish(i, dist, part):
         ok = i < found
@@ -351,76 +361,34 @@
     ]
     for copy in copies:
         copy.start()
-    centre, inv = frame([[geo[:, k, :] for k in range(4)]])
+    inv, centre = frame(geo)
+    scale[...] = jnp.zeros_like(scale)
+    scale[0:1, :] = jnp.broadcast_to(inv, (1, LANES))
+    for k in range(3):
+        scale[k + 1 : k + 2, :] = jnp.broadcast_to(centre[k : k + 1, :], (1, LANES))
+    inv, centre = split_frame(scale)
     for first in range(0, geo.shape[0], 8):
         points = [geo[first : first + 8, k, :] for k in range(4)]
         left, right, rad = split_features(points, centre, inv)
         store_features((fa0, fa1), left, first)
         store_features((fb0, fb1), right, first)
         diag[first : first + 8, :] = lax.rsqrt(2.0 * (rad * rad))
-    scale[...] = jnp.full(scale.shape, inv, F32)
     for copy in copies:
         copy.wait()
-    up_sums(basis, masked, transfer, parent, up)
-
-
-def local_kernel(sizes, geo_pairs, pairs, fa0, fa1, fb0, fb1, diags, scale, acc_in, *rest):
+    up[...] = up_sums(basis, masked, transfer, parent, up.shape[0])
+
+
+def local_kernel(sizes, pair_rows, pairs, fa0, fa1, fb0, fb1, scale, acc_in, *rest):
     S, L, R, clusters, panels = sizes
     pieces = rest[:S]
-    acc_out, q, acc, self_sums, pair_sums, *work = rest[S:]
+    acc_out = rest[S]
+    q, acc, pair_sums, *work = rest[S + 1 :]
     ring, sums = work[:16], work[16:]
     fa, fb = (fa0, fa1), (fb0, fb1)
-    sub, rep = lax.axis_index("sub"), lax.axis_index("rep")
+    sub = lax.axis_index("sub")
     assemble(sub, S, L, q, pieces)
     acc[...] = jnp.zeros_like(acc)
-    self_sums[...] = jnp.zeros_like(self_sums)
     pair_sums[...] = jnp.zeros_like(pair_sums)
-
-    half = panels // 2
-    share = clusters // (S * R)
-    first = (rep * S + sub) * share
-
-    def begin_self(i, dist):
-        c = first + jnp.minimum(i, share - 1)
-        left, right = products(load_features(fa, c), load_features(fb, c))
-        left = left.T
-        dist[:half, :] = contract(left[:half, :], right)
-        dist[half:, half:] = contract(left[half:, :], right[:, half:])
-
-    def finish_self(i, dist, parts):
-        c = first + i
-        qrow = q[pl.ds(c, 1), :]
-        qcol = upright(qrow[:, :half])
-        diag = diags[pl.ds(c, 1), :]
-        back = [jnp.zeros((8, LANES), F32)]
-
-        def eye(span):
-            shape = (span.stop - span.start, half)
-            row = lax.broadcasted_iota(jnp.int32, shape, 0) + span.start % half
-            return row == lax.broadcasted_iota(jnp.int32, shape, 1)
-
-        def root(span, _):
-            if span.start < half:
-                return (
-                    jnp.where(eye(span), diag[:, :half], inverse_root(dist[span, :half])),
-                    inverse_root(dist[span, half:]),
-                )
-            return (jnp.where(eye(span), diag[:, half:], inverse_root(dist[span, half:])),)
-
-        def partial(span, held):
-            if span.start < half:
-                g0, g1 = held
-                back[0] = back[0] + fold(g1 * qcol[span, :])
-                keep(parts, span, g0 * qrow[:, :half] + g1 * qrow[:, half:])
-            else:
-                keep(parts, span, held[0] * qrow[:, half:])
-
-        staged(spans_of(panels), root, partial)
-        back = jnp.sum(back[0], axis=0, keepdims=True)
-        acc[pl.ds(c, 1), :] += jnp.concatenate([jnp.zeros_like(back), back], axis=1)
-        return c
-
-    pipeline(share, begin_self, finish_self, self_sums, ring[: ring_size(share)], sums)
 
     count = pairs.shape[1] // S
     start = sub * count
@@ -437,10 +405,64 @@
         return start + i
 
     pipeline(count, begin, finish, pair_sums, ring[: ring_size(count)], sums)
-    total = acc[...] + self_sums[...].T
-    width = geo_pairs.shape[1]
-    total = total + select_rows(geo_pairs[0:1, :], pair_sums[...].T[:width, :], clusters)
+    width = pair_rows.shape[1]
+    total = acc[...] + select_rows(pair_rows[0:1, :], pair_sums[...].T[:width, :], clusters)
     acc_out[...] = acc_in[...] + total * scale[0:1, 0:1]
+
+
+def self_shares(clusters, S, R):
+    base = clusters // R
+    unit = base // 4 if R > 1 else 0
+    return base, unit
+
+
+def self_kernel(sizes, fa0, fa1, fb0, fb1, diags, scale, part, *rest):
+    S, L, R, clusters, panels = sizes
+    pieces = rest[:S]
+    out, q, fs, spots, self_sums, *work = rest[S:]
+    ring, sums = work[:16], work[16:]
+    sub, rep = lax.axis_index("sub"), lax.axis_index("rep")
+    assemble(sub, S, L, q, pieces)
+    self_sums[...] = jnp.zeros_like(self_sums)
+
+    def place(s):
+        t, at = (s * L) // LANES, (s * L) % LANES
+        fs[...] = (fa0, fa1)[t][:, at : at + L]
+        spots[...] = diags[:, s * L : (s + 1) * L]
+
+    for s in range(S):
+        pl.when(sub == s)(functools.partial(place, s))
+    base, unit = self_shares(clusters, S, R)
+    first = rep * base - jnp.where(rep > 0, unit, 0)
+    share = base + jnp.where(rep == R - 1, unit, 0) - jnp.where(rep == 0, unit, 0)
+
+    def begin(i, dist):
+        c = first + jnp.minimum(i, share - 1)
+        distances(load_features((fs,), c), load_features((fb0, fb1), c), dist)
+
+    def finish(i, dist, parts):
+        c = first + i
+        qrow = q[pl.ds(c, 1), :]
+        diag = upright(spots[pl.ds(c, 1), :])
+
+        def root(span, _):
+            shape = (span.stop - span.start, LANES)
+            row = lax.broadcasted_iota(jnp.int32, shape, 0) + (sub * L + span.start)
+            col = lax.broadcasted_iota(jnp.int32, shape, 1)
+            return [
+                jnp.where(row == col + t, diag[span, :], inverse_root(dist[span, t : t + LANES]))
+                for t in range(0, panels, LANES)
+            ]
+
+        def partial(span, held):
+            keep(parts, span, sum(g * qrow[:, t * LANES : (t + 1) * LANES] for t, g in enumerate(held)))
+
+        staged(spans_of(L), root, partial)
+        return c
+
+    pipeline(share, begin, finish, self_sums, ring[: ring_size(unit or base)], sums)
+    out[...] = part[...]
+    out[:clusters, :] = part[:clusters, :] + self_sums[...].T * scale[0:1, 0:1]
 
 
 def merge_kernel(sizes, far_list, targets, near, coupling, transfer, parent, up, *rest):
@@ -486,7 +508,7 @@
         pl.when(sub == s)(functools.partial(give, s))
 
 
-def up_sums(basis, masked, transfer, parent, up):
+def up_sums(basis, masked, transfer, parent, count):
     clusters = basis.shape[0]
     rank = basis.shape[1]
     lane = lax.broadcasted_iota(jnp.int32, (rank, clusters), 1)
@@ -497,9 +519,9 @@
     lifted = jnp.zeros((rank, clusters), F32)
     for r in range(rank):
         lifted = lifted + transfer[r] * leaf[r : r + 1, :]
-    which = lax.broadcasted_iota(jnp.int32, (up.shape[0], clusters), 0)
+    which = lax.broadcasted_iota(jnp.int32, (count, clusters), 0)
     onehot = (parent[...] == which).astype(F32)
-    up[...] = lax.dot_general(
+    return lax.dot_general(
         onehot, lifted, (((1,), (1,)), ((), ())), precision=HIGHEST, preferred_element_type=F32
     )
 
@@ -595,26 +617,24 @@
             pltpu.VMEM(parent.shape, jnp.int32),
             pltpu.SemaphoreType.DMA((3,)),
         ],
-        compiler_params=limit(32),
+        compiler_params=limit(24),
         cost_estimate=about(4),
         name="prepare",
     )(*near_by(geo, masked), *far_off(basis_t, transfer_t, parent))
+    *tables, diags, scale = features
 
     made = pl.pallas_call(
         functools.partial(remote_kernel, (C, S, L, slots, clusters, panels)),
         out_shape=[pltpu.VMEM((clusters, panels), F32)]
         + [pltpu.VMEM((slots + par_dev, L), F32)] * (C - 1),
-        in_specs=[vmem()] * (2 + S + C - 1),
+        in_specs=[vmem()] * (4 + S + C - 1),
         out_specs=[vmem()] * C,
         scratch_shapes=[
             pltpu.VMEM((clusters, panels), F32),
             pltpu.VMEM((n, L), F32),
             pltpu.VMEM((clusters, panels), F32),
             pltpu.VMEM((L, whole(n)), F32),
-            pltpu.VMEM((4 * n, panels), F32),
             pltpu.VMEM((n * ROWS, L), F32),
-            pltpu.VMEM((n * ROWS, LANES), F32),
-            pltpu.VMEM((n * ROWS, LANES), F32),
             pltpu.SMEM((2 * n + 1,), jnp.int32),
             pltpu.SMEM((C - 1, 8, L), F32),
             pltpu.SemaphoreType.DMA((C - 1,)),
@@ -624,41 +644,59 @@
         compiler_params=limit(24),
         cost_estimate=about(6),
         name="near_remote",
-    )(*near_by(geo, up, *pieces, *packs))
+    )(*near_by(*tables[2:], scale, up, *pieces, *packs))
     acc, sums = made[0], [send(made[d], (("clu", C - d),)) for d in range(1, C)]
 
     wide = whole(local_pairs.shape[1])
-    acc = pl.pallas_call(
+    near = pl.pallas_call(
         functools.partial(local_kernel, (S, L, R, clusters, panels)),
         out_shape=pltpu.VMEM((clusters, panels), F32),
-        in_specs=[vmem(), smem()] + [vmem()] * (7 + S),
+        in_specs=[vmem(), smem()] + [vmem()] * (6 + S),
         out_specs=vmem(),
         scratch_shapes=[
             pltpu.VMEM((clusters, panels), F32),
             pltpu.VMEM((clusters, panels), F32),
-            pltpu.VMEM((panels, clusters), F32),
             pltpu.VMEM((panels, wide), F32),
         ]
         + [pltpu.VMEM((panels, panels), F32)] * 16
         + [pltpu.VMEM((panels, 2 * LANES), BF16)] * 4,
         compiler_params=limit(24),
-        cost_estimate=about(15),
+        cost_estimate=about(9),
         name="near_local",
-    )(*near_by(local_pairs[0].T), local_pairs[0].T, *near_by(*features, acc, *pieces))
-
+    )(*near_by(local_pairs[0].T), local_pairs[0].T, *near_by(*tables, scale, acc, *pieces))
+
+    height = clusters + clusters // L * rank
     parts = pl.pallas_call(
         functools.partial(merge_kernel, (C, S, L, slots, clusters)),
-        out_shape=[pltpu.VMEM((clusters + clusters // L * rank, L), F32)] * S,
+        out_shape=[pltpu.VMEM((height, L), F32)] * S,
         in_specs=[smem()] + [vmem()] * (6 + C - 1),
         out_specs=[vmem()] * S,
         scratch_shapes=[pltpu.VMEM((C * par_dev, rank), F32)],
         compiler_params=limit(16),
-        cost_estimate=about(2),
+        cost_estimate=about(1),
         name="merge",
-    )(far_list.T, *near_by(targets, acc, coupling, transfer_t, parent, up, *sums))
-    near = parts[0]
-    for d in range(1, S):
-        near = near + send(parts[d], (("sub", d),))
+    )(far_list.T, *near_by(targets, near, coupling, transfer_t, parent, up, *sums))
+    others = [send(parts[d], (("sub", d),)) for d in range(1, S)]
+
+    near = pl.pallas_call(
+        functools.partial(self_kernel, (S, L, R, clusters, panels)),
+        out_shape=pltpu.VMEM((height, L), F32),
+        in_specs=[vmem()] * (7 + S),
+        out_specs=vmem(),
+        scratch_shapes=[
+            pltpu.VMEM((clusters, panels), F32),
+            pltpu.VMEM((clusters * ROWS, L), F32),
+            pltpu.VMEM((clusters, L), F32),
+            pltpu.VMEM((L, clusters), F32),
+        ]
+        + [pltpu.VMEM((L, panels), F32)] * 16
+        + [pltpu.VMEM((L, 2 * LANES), BF16)] * 4,
+        compiler_params=limit(24),
+        cost_estimate=about(4),
+        name="near_self",
+    )(*near_by(*tables, diags, scale, parts[0], *pieces))
+    for other in others:
+        near = near + other
     others = [send(near, (("rep", e),)) for e in range(1, R)]
 
     total = pl.pallas_call(

time: 44.4 us -> 42.6 us (0.959)
  waiting for transfers between devices: 4.55 us -> 0.12 us
  Pallas kernels: 27.4 us -> 29.4 us
  starting transfers between devices: 11.4 us -> 12.1 us
    pallas_call x0 -> x1, Pallas kernels: none -> 4.86 us  [on_device(): pl.pallas_call(functools.partial(self_kernel, (S, L, R, clusters, panels)...]
    ppermute x9, waiting for transfers between devices: 4.55 us -> 0.12 us  [send(): return lax.ppermute(value, names if len(names) > 1 else names[0], perm)]
    pallas_call x1, Pallas kernels: 12.9 us -> 9.89 us  [on_device(): pl.pallas_call(functools.partial(local_kernel, (S, L, R, clusters, panels...]
    ppermute x9, starting transfers between devices: 11.4 us -> 12.1 us  [send(): return lax.ppermute(value, names if len(names) > 1 else names[0], perm)]
    pallas_call x1, Pallas kernels: 4.94 us -> 5.41 us  [on_device(): pl.pallas_call(prepare_kernel, out_shape=[pltpu.VMEM((clusters * ROWS, LA...]
  transfers between devices with their start and end apart: 9 -> 9, of which waited for: 2 -> 1; matrix products, arithmetic and copies ran while one was open for 0% -> 0% of each run, Pallas kernels for 42% -> 49%
where the time goes in v17:
time: 42.6 us
  Pallas kernels  29.4 us (69%)
  starting transfers between devices  12.1 us (28%)
  other arithmetic  0.66 us (2%)
    ppermute x9, starting transfers between devices, send(): return lax.ppermute(value, names if len(names) > 1 else names[0], perm)  12.1 us
    pallas_call x1, Pallas kernels, on_device(): pl.pallas_call(functools.partial(local_kernel, (S, L, R, clusters, panels...  9.89 us
    pallas_call x1, Pallas kernels, on_device(): pl.pallas_call(functools.partial(remote_kernel, (C, S, L, slots, clusters...  5.87 us
    pallas_call x1, Pallas kernels, on_device(): pl.pallas_call(prepare_kernel, out_shape=[pltpu.VMEM((clusters * ROWS, LA...  5.41 us
    pallas_call x1, Pallas kernels, on_device(): pl.pallas_call(functools.partial(self_kernel, (S, L, R, clusters, panels)...  4.86 us
    pallas_call x1, Pallas kernels, on_device(): pl.pallas_call(functools.partial(pack_kernel, (C, S, L, slots)), out_shap...  1.34 us
    pallas_call x1, Pallas kernels, on_device(): pl.pallas_call(functools.partial(merge_kernel, (C, S, L, slots, clusters)...  1.26 us
  transfers between devices with their start and end apart: 9, of which 1 were waited for; matrix products, arithmetic and copies ran while one was open for 0% of the time, Pallas kernels for 49%

profile of v17, /device:TPU:0, one launch (start us, length us, event | category | flops | bytes accessed | tf_op | source)
XLA Modules:
  0.0 42.6 jit_solution(11298030311333735533)
XLA Ops:
  0.0 1.3 %packs.1 = (f32[128,128]{1,0:T(8,128)S(1)}, f32[128,4,256]{2,1,0:T(4,128)S(1)}, f32[88,128]{1,0:T(8,128)S(1)}, f32[88,128]{1,0:T(8,128)S(1)}, f32[88,128]{1,0:T(8,128)S(1)}) custom-call(f32[128,128]{1,0:T(8,128)} %charges.1, s32[128,128]{1,0:T(8,128)} %mask.1, f32[128,4,256]{2,1,0:T(4,128)} %geo.1, s32[4,16]{1,0:T(4,128)} %bitcast.14, s32[4,16]{1,0:T(4,128)} %bitcast.21, ...), custom_call_target="tpu_custom_call" | custom-call | bytes 7000000 | tf_op jit(solution)/shard_map/packs/pallas_call | solution.py:590
  1.4 3.0 %collective-permute-start = (f32[128,128]{1,0:T(8,128)S(1)}, f32[128,128]{1,0:T(8,128)S(1)}, u32[]{:S(2)}, u32[]{:S(2)}) collective-permute-start(f32[128,128]{1,0:T(8,128)S(1)} %get-tuple-element.24.masked.rest_0_), channel_id=1, source_target_pairs={{0,2},{2,0},{1,3},{3,1},{4,6},{6,4},{5,7},{7,5},{8,10},{10,8},{9,1... | collective-permute-start | bytes 196616 | tf_op jit(solution)/shard_map/ppermute | solution.py:561
  4.4 1.6 %collective-permute-start.1 = (f32[88,128]{1,0:T(8,128)S(1)}, f32[88,128]{1,0:T(8,128)S(1)}, u32[]{:S(2)}, u32[]{:S(2)}) collective-permute-start(f32[88,128]{1,0:T(8,128)S(1)} %get-tuple-element.32), channel_id=1, source_target_pairs={{0,4},{4,8},{8,12},{12,0},{1,5},{5,9},{9,13},{13,1},{2,6},{6,10},{... | collective-permute-start | bytes 135176 | tf_op jit(solution)/shard_map/ppermute | solution.py:561
  5.9 2.6 %collective-permute-start.2 = (f32[88,128]{1,0:T(8,128)S(1)}, f32[88,128]{1,0:T(8,128)S(1)}, u32[]{:S(2)}, u32[]{:S(2)}) collective-permute-start(f32[88,128]{1,0:T(8,128)S(1)} %get-tuple-element.33), channel_id=1, source_target_pairs={{0,8},{4,12},{8,0},{12,4},{1,9},{5,13},{9,1},{13,5},{2,10},{6,14},... | collective-permute-start | bytes 135176 | tf_op jit(solution)/shard_map/ppermute | solution.py:561
  8.5 1.3 %collective-permute-start.3 = (f32[88,128]{1,0:T(8,128)S(1)}, f32[88,128]{1,0:T(8,128)S(1)}, u32[]{:S(2)}, u32[]{:S(2)}) collective-permute-start(f32[88,128]{1,0:T(8,128)S(1)} %get-tuple-element.34), channel_id=1, source_target_pairs={{0,12},{4,0},{8,4},{12,8},{1,13},{5,1},{9,5},{13,9},{2,14},{6,2},{... | collective-permute-start | bytes 135176 | tf_op jit(solution)/shard_map/ppermute | solution.py:561
  9.9 5.4 %prepare.1 = (f32[3072,128]{1,0:T(8,128)S(1)}, f32[3072,128]{1,0:T(8,128)S(1)}, f32[3072,128]{1,0:T(8,128)S(1)}, f32[3072,128]{1,0:T(8,128)S(1)}, f32[128,256]{1...) custom-call(f32[128,4,256]{2,1,0:T(4,128)S(1)} %get-tuple-element.23.geo, ...), custom_call_target="tpu_custom_call" | custom-call | bytes 14000000 | tf_op jit(solution)/shard_map/prepare/pallas_call | solution.py:604
  15.3 0.0 collective-permute-done.1.rest_2_
  15.3 0.0 collective-permute-done.2.rest_3_
  15.3 0.0 collective-permute-done.3.rest_4_
  15.3 0.0 collective-permute-done.rest_1_
  15.3 0.0 copy-start.5
  15.3 5.9 %near_remote.1 = (f32[128,256]{1,0:T(8,128)S(1)}, f32[32,128]{1,0:T(8,128)S(1)}, f32[32,128]{1,0:T(8,128)S(1)}, f32[32,128]{1,0:T(8,128)S(1)}) custom-call(f32[3072,128]{1,0:T(8,128)S(1)} %get-tuple-element.27.fb0, f32[3072,128]{1,0:T(8,128)S(1)} %get-tuple-element.28.fb1, f32[8,128]{1,0:T(8,128)S(1)} %get-tuple-element.30.scale, ...), custom_call_target="tpu_custom_call" | custom-call | bytes 21000000 | tf_op jit(solution)/shard_map/near_remote/pallas_call | solution.py:626
  21.2 0.5 %collective-permute-start.4 = (f32[32,128]{1,0:T(8,128)S(1)}, f32[32,128]{1,0:T(8,128)S(1)}, u32[]{:S(2)}, u32[]{:S(2)}) collective-permute-start(f32[32,128]{1,0:T(8,128)S(1)} %get-tuple-element.36), channel_id=1, source_target_pairs={{0,12},{4,0},{8,4},{12,8},{1,13},{5,1},{9,5},{13,9},{2,14},{6,2},{... | collective-permute-start | bytes 49160 | tf_op jit(solution)/shard_map/ppermute | solution.py:561
  21.7 1.7 %collective-permute-start.5 = (f32[32,128]{1,0:T(8,128)S(1)}, f32[32,128]{1,0:T(8,128)S(1)}, u32[]{:S(2)}, u32[]{:S(2)}) collective-permute-start(f32[32,128]{1,0:T(8,128)S(1)} %get-tuple-element.37), channel_id=1, source_target_pairs={{0,8},{4,12},{8,0},{12,4},{1,9},{5,13},{9,1},{13,5},{2,10},{6,14},... | collective-permute-start | bytes 49160 | tf_op jit(solution)/shard_map/ppermute | solution.py:561
  23.4 0.2 collective-permute-start.6
  23.6 0.0 copy-done.5
  23.6 0.0 copy-start.1
  23.6 0.0 copy-start.2
  23.6 0.0 copy-start.3
  23.7 0.0 copy-start.4
  23.7 0.0 copy-start.6
  23.7 9.9 %near_local.1.near = f32[128,256]{1,0:T(8,128)S(1)} custom-call(s32[2,128]{1,0:T(2,128)S(1)} %bitcast.17, s32[2,128]{1,0:T(2,128)S(1)} %bitcast.18, f32[3072,128]{1,0:T(8,128)S(1)} %get-tuple-element.25.fa0, f32[3072,128]{1,0:T(8,128)S(1)} %get-tuple-element.26.fa1, f32[3072,128]{1,0:T(8,128)S(1)} %get-tuple-element.27.fb0, ...), custom_call_target="tpu_custom_call" | custom-call | bytes 31500000 | tf_op jit(solution)/shard_map/near_local/pallas_call | solution.py:651
  33.6 0.0 collective-permute-done.4.rest_0_
  33.6 0.0 collective-permute-done.5.rest_1_
  33.6 0.0 collective-permute-done.6.rest_2_
  33.6 0.0 copy-done.1
  33.6 0.0 copy-done.2
  33.6 0.0 copy-done.3
  33.6 0.0 copy-done.4
  33.6 0.0 copy-done.6
  33.7 1.3 %merge.1 = (f32[160,128]{1,0:T(8,128)S(1)}, f32[160,128]{1,0:T(8,128)S(1)}) custom-call(s32[8,16]{1,0:T(8,128)S(1)} %bitcast.16, s32[4,16]{1,0:T(4,128)S(1)} %bitcast.15, f32[128,256]{1,0:T(8,128)S(1)} %near_local.1.near, f32[16,8,32,32]{3,2,1,0:T(8,128)S(1)} %copy-done.1, f32[32,32,128]{2,1,0:T(8,128)S(1)} %bitcast.13, s32[1,128]{1,0:T(1,128)S(1)} %bitcast.20, ...), custom_call_target="tpu_custom_call" | custom-call | bytes 3500000 | tf_op jit(solution)/shard_map/merge/pallas_call | solution.py:669
  34.9 0.4 collective-permute-start.7
  35.3 0.0 copy-start
  35.3 4.9 %near_self.1 = f32[160,128]{1,0:T(8,128)S(1)} custom-call(f32[3072,128]{1,0:T(8,128)S(1)} %get-tuple-element.25.fa0, f32[3072,128]{1,0:T(8,128)S(1)} %get-tuple-element.26.fa1, f32[3072,128]{1,0:T(8,128)S(1)} %get-tuple-element.27.fb0, f32[3072,128]{1,0:T(8,128)S(1)} %get-tuple-element.28.fb1, f32[128,256]{1,0:T(8,128)S(1)} %get-tuple-element.29.diags, ...), custom_call_target="tpu_custom_call" | custom-call | bytes 14000000 | tf_op jit(solution)/shard_map/near_self/pallas_call | solution.py:681
  40.2 0.0 copy-start.7
  40.2 0.0 collective-permute-done.7
  40.2 0.8 %collective-permute-start.8 = (f32[160,128]{1,0:T(8,128)S(1)}, f32[160,128]{1,0:T(8,128)S(1)}, u32[]{:S(2)}, u32[]{:S(2)}) collective-permute-start(f32[160,128]{1,0:T(8,128)S(1)} %add.6.near), channel_id=1, source_target_pairs={{0,1},{1,0},{2,3},{3,2},{4,5},{5,4},{6,7},{7,6},{8,9},{9,8},{10,11... | collective-permute-start | bytes 245768 | tf_op jit(solution)/shard_map/ppermute | solution.py:561
  41.0 0.0 copy-done
  41.0 0.8 %far_down.1 = f32[128,128]{1,0:T(8,128)S(1)} custom-call(f32[128,32,128]{2,1,0:T(8,128)S(1)} %bitcast.11, f32[160,128]{1,0:T(8,128)S(1)} %add.6.near), custom_call_target="tpu_custom_call" | custom-call | bytes 3500000 | tf_op jit(solution)/shard_map/far_down/pallas_call | solution.py:702
  41.8 0.1 collective-permute-done.8
  41.9 0.0 copy-done.7
  41.9 0.6 %fusion = f32[128,128]{1,0:T(8,128)} fusion(f32[128,128]{1,0:T(8,128)S(1)} %far_down.1, f32[160,128]{1,0:T(8,128)S(1)} %collective-permute-done.8, s32[128,128]{1,0:T(8,128)S(1)} %copy-done.7), kind=kLoop, calls=%fused_computation.1 | loop fusion | flops 49152 | bytes 262144 | tf_op jit(solution)/shard_map/mul | solution.py:713
  (1 shorter events, 0.0 us)
Async XLA Ops:
  1.4 14.0 %collective-permute-start = (f32[128,128]{1,0:T(8,128)S(1)}, f32[128,128]{1,0:T(8,128)S(1)}, u32[]{:S(2)}, u32[]{:S(2)}) collective-permute-start(f32[128,128]{1,0:T(8,128)S(1)} %get-tuple-element.24.masked.rest_0_), channel_id=1, source_target_pairs={{0,2},{2,0},{1,3},{3,1},{4,6},{6,4},{5,7},{7,5},{8,10},{10,8},{9,1... | collective-permute-start | bytes 196616 | tf_op jit(solution)/shard_map/ppermute | solution.py:561
  4.4 10.9 %collective-permute-start.1 = (f32[88,128]{1,0:T(8,128)S(1)}, f32[88,128]{1,0:T(8,128)S(1)}, u32[]{:S(2)}, u32[]{:S(2)}) collective-permute-start(f32[88,128]{1,0:T(8,128)S(1)} %get-tuple-element.32), channel_id=1, source_target_pairs={{0,4},{4,8},{8,12},{12,0},{1,5},{5,9},{9,13},{13,1},{2,6},{6,10},{... | collective-permute-start | bytes 135176 | tf_op jit(solution)/shard_map/ppermute | solution.py:561
  5.9 9.4 %collective-permute-start.2 = (f32[88,128]{1,0:T(8,128)S(1)}, f32[88,128]{1,0:T(8,128)S(1)}, u32[]{:S(2)}, u32[]{:S(2)}) collective-permute-start(f32[88,128]{1,0:T(8,128)S(1)} %get-tuple-element.33), channel_id=1, source_target_pairs={{0,8},{4,12},{8,0},{12,4},{1,9},{5,13},{9,1},{13,5},{2,10},{6,14},... | collective-permute-start | bytes 135176 | tf_op jit(solution)/shard_map/ppermute | solution.py:561
  8.5 6.8 %collective-permute-start.3 = (f32[88,128]{1,0:T(8,128)S(1)}, f32[88,128]{1,0:T(8,128)S(1)}, u32[]{:S(2)}, u32[]{:S(2)}) collective-permute-start(f32[88,128]{1,0:T(8,128)S(1)} %get-tuple-element.34), channel_id=1, source_target_pairs={{0,12},{4,0},{8,4},{12,8},{1,13},{5,1},{9,5},{13,9},{2,14},{6,2},{... | collective-permute-start | bytes 135176 | tf_op jit(solution)/shard_map/ppermute | solution.py:561
  15.3 8.3 %copy-start.5 = (s32[1,128,2]{1,2,0:T(2,128)S(1)}, s32[1,128,2]{1,2,0:T(2,128)}, u32[]{:S(2)}) copy-start(s32[1,128,2]{1,2,0:T(2,128)} %param.18) | copy-start | bytes 3076
  21.2 12.4 %collective-permute-start.4 = (f32[32,128]{1,0:T(8,128)S(1)}, f32[32,128]{1,0:T(8,128)S(1)}, u32[]{:S(2)}, u32[]{:S(2)}) collective-permute-start(f32[32,128]{1,0:T(8,128)S(1)} %get-tuple-element.36), channel_id=1, source_target_pairs={{0,12},{4,0},{8,4},{12,8},{1,13},{5,1},{9,5},{13,9},{2,14},{6,2},{... | collective-permute-start | bytes 49160 | tf_op jit(solution)/shard_map/ppermute | solution.py:561
  21.7 11.9 %collective-permute-start.5 = (f32[32,128]{1,0:T(8,128)S(1)}, f32[32,128]{1,0:T(8,128)S(1)}, u32[]{:S(2)}, u32[]{:S(2)}) collective-permute-start(f32[32,128]{1,0:T(8,128)S(1)} %get-tuple-element.37), channel_id=1, source_target_pairs={{0,8},{4,12},{8,0},{12,4},{1,9},{5,13},{9,1},{13,5},{2,10},{6,14},... | collective-permute-start | bytes 49160 | tf_op jit(solution)/shard_map/ppermute | solution.py:561
  23.4 10.2 %collective-permute-start.6 = (f32[32,128]{1,0:T(8,128)S(1)}, f32[32,128]{1,0:T(8,128)S(1)}, u32[]{:S(2)}, u32[]{:S(2)}) collective-permute-start(f32[32,128]{1,0:T(8,128)S(1)} %get-tuple-element.38), channel_id=1, source_target_pairs={{0,4},{4,8},{8,12},{12,0},{1,5},{5,9},{9,13},{13,1},{2,6},{6,10},{... | collective-permute-start | bytes 49160 | tf_op jit(solution)/shard_map/ppermute | solution.py:561
  23.6 10.0 %copy-start.1 = (f32[16,8,32,32]{3,2,1,0:T(8,128)S(1)}, f32[16,8,32,32]{3,2,1,0:T(8,128)}, u32[]{:S(2)}) copy-start(f32[16,8,32,32]{3,2,1,0:T(8,128)} %coupling.1) | copy-start | bytes 1572868
  23.6 10.0 %copy-start.2 = (f32[128,32,32]{0,2,1:T(8,128)S(1)}, f32[128,32,32]{0,2,1:T(8,128)}, u32[]{:S(2)}) copy-start(f32[128,32,32]{0,2,1:T(8,128)} %param.20) | copy-start | bytes 1572868
  23.6 10.0 %copy-start.3 = (s32[1,4,16]{2,1,0:T(4,128)S(1)}, s32[1,4,16]{2,1,0:T(4,128)}, u32[]{:S(2)}) copy-start(s32[1,4,16]{2,1,0:T(4,128)} %param.16) | copy-start | bytes 772
  23.7 10.0 %copy-start.4 = (s32[16,8]{0,1:T(8,128)S(1)}, s32[16,8]{0,1:T(8,128)}, u32[]{:S(2)}) copy-start(s32[16,8]{0,1:T(8,128)} %param.22) | copy-start | bytes 1540
  23.7 10.0 %copy-start.6 = (s32[128]{0:T(128)S(1)}, s32[128]{0:T(128)}, u32[]{:S(2)}) copy-start(s32[128]{0:T(128)} %param.21) | copy-start | bytes 1540
  34.9 5.3 %collective-permute-start.7 = (f32[160,128]{1,0:T(8,128)S(1)}, f32[160,128]{1,0:T(8,128)S(1)}, u32[]{:S(2)}, u32[]{:S(2)}) collective-permute-start(f32[160,128]{1,0:T(8,128)S(1)} %get-tuple-element.40), channel_id=1, source_target_pairs={{0,2},{2,0},{1,3},{3,1},{4,6},{6,4},{5,7},{7,5},{8,10},{10,8},{9,1... | collective-permute-start | bytes 245768 | tf_op jit(solution)/shard_map/ppermute | solution.py:561
  35.3 5.7 %copy-start = (f32[128,128,32]{1,2,0:T(8,128)S(1)}, f32[128,128,32]{1,2,0:T(8,128)}, u32[]{:S(2)}) copy-start(f32[128,128,32]{1,2,0:T(8,128)} %param.19) | copy-start | bytes 6291460
  40.2 1.8 %copy-start.7 = (s32[128,128]{1,0:T(8,128)S(1)}, s32[128,128]{1,0:T(8,128)}, u32[]{:S(2)}) copy-start(s32[128,128]{1,0:T(8,128)} %mask.1) | copy-start | bytes 196612
  40.2 1.7 %collective-permute-start.8 = (f32[160,128]{1,0:T(8,128)S(1)}, f32[160,128]{1,0:T(8,128)S(1)}, u32[]{:S(2)}, u32[]{:S(2)}) collective-permute-start(f32[160,128]{1,0:T(8,128)S(1)} %add.6.near), channel_id=1, source_target_pairs={{0,1},{1,0},{2,3},{3,2},{4,5},{5,4},{6,7},{7,6},{8,9},{9,8},{10,11... | collective-permute-start | bytes 245768 | tf_op jit(solution)/shard_map/ppermute | solution.py:561

commit v18 on v17

--- a/solution.py
+++ b/solution.py
@@ -56,12 +56,14 @@
 
 def frame(geo):
     low, high = [None] * 8, [None] * 8
-    for c in range(geo.shape[0]):
-        g, k = geo[c], c % 8
+    blocks = [(t, c) for c in range(0, geo.shape[1], 8) for t in range(geo.shape[0])]
+    for i, (t, c) in enumerate(blocks):
+        g, k = geo[t, c : c + 8, :], i % 8
         low[k] = g if low[k] is None else jnp.minimum(low[k], g)
         high[k] = g if high[k] is None else jnp.maximum(high[k], g)
     low = jnp.min(functools.reduce(jnp.minimum, low), axis=1, keepdims=True)
     high = jnp.max(functools.reduce(jnp.maximum, high), axis=1, keepdims=True)
+    low, high = jnp.minimum(low[:4], low[4:]), jnp.maximum(high[:4], high[4:])
     row = lax.broadcasted_iota(jnp.int32, low.shape, 0)
     radius = jnp.maximum(jnp.abs(low), jnp.abs(high))
     width = jnp.max(jnp.where(row == 3, radius, 0.5 * (high - low)), axis=0, keepdims=True)
@@ -120,19 +122,16 @@
 
 def store_features(ref, rows, first):
     width = rows[0].shape[1]
-    for t, piece in enumerate(ref):
-        count = piece.shape[0] // ROWS
-        for k, row in enumerate(rows):
-            at = k * count + first
-            piece[at : at + 8, :] = row[:, t * LANES : min(width, (t + 1) * LANES)]
-
-
-def load_features(ref, index):
-    blocks = []
-    for piece in ref:
-        count = piece.shape[0] // ROWS
-        groups = [piece[pl.ds(k * count + index, 8, stride=count), :] for k in range(0, ROWS, 8)]
-        blocks.append(jnp.concatenate(groups, axis=0))
+    for k, row in enumerate(rows):
+        for t in range(ref.shape[0]):
+            at = pl.ds(first * ROWS + k, 8, stride=ROWS)
+            ref[t, at, :] = row[:, t * LANES : min(width, (t + 1) * LANES)]
+
+
+def load_features(ref, index, order=None):
+    start = pl.multiple_of(index * ROWS, 8)
+    order = range(ref.shape[0]) if order is None else order
+    blocks = [ref[t, pl.ds(start, ROWS), :] for t in order]
     return jnp.concatenate(blocks, axis=1) if len(blocks) > 1 else blocks[0]
 
 
@@ -264,7 +263,8 @@
     C, S, L, slots = sizes
     me, sub = lax.axis_index("clu"), lax.axis_index("sub")
     masked[...] = charges[...] * mask[...].astype(F32)
-    geo_out[...] = geo[...]
+    for t in range(geo_out.shape[0]):
+        geo_out[t, :, :] = geo[:, :, t * LANES : (t + 1) * LANES].reshape(geo_out.shape[1:])
     lane = lax.broadcasted_iota(jnp.int32, (8, L), 1)
     for shift in range(1, C):
         dest = lax.rem(me + shift, C)
@@ -289,14 +289,13 @@
         pl.when(sub == s)(functools.partial(fill, s))
 
 
-def remote_kernel(sizes, fb0, fb1, scale, up, *rest):
+def remote_kernel(sizes, fb, scale, up, *rest):
     C, S, L, slots, clusters, panels = sizes
     pieces = rest[:S]
     packs = rest[S : S + C - 1]
     acc_out = rest[S + C - 1]
     sends = rest[S + C : S + C + C - 1]
-    q, tq, acc, fwdt, fa0, order, codes, sems, *work = rest[S + C + C - 1 :]
-    fa, fb = (fa0,), (fb0, fb1)
+    q, tq, acc, fwdt, fa, order, codes, sems, *work = rest[S + C + C - 1 :]
     n = (C - 1) * slots
     copies = [
         pltpu.make_async_copy(packs[k].at[pl.ds(5 * slots, 8), :], codes.at[k], sems.at[k])
@@ -351,7 +350,7 @@
 
 def prepare_kernel(
     geo, masked, basis_far, transfer_far, parent_far,
-    fa0, fa1, fb0, fb1, diag, scale, up, basis, transfer, parent, sems
+    fa, fb, diag, scale, up, basis, transfer, parent, sems
 ):
     copies = [
         pltpu.make_async_copy(src, dst, sems.at[k])
@@ -367,24 +366,28 @@
     for k in range(3):
         scale[k + 1 : k + 2, :] = jnp.broadcast_to(centre[k : k + 1, :], (1, LANES))
     inv, centre = split_frame(scale)
-    for first in range(0, geo.shape[0], 8):
-        points = [geo[first : first + 8, k, :] for k in range(4)]
+    for first in range(0, diag.shape[0], 8):
+        points = [
+            jnp.concatenate(
+                [geo[t, pl.ds(first * 4 + k, 8, stride=4), :] for t in range(geo.shape[0])], axis=1
+            )
+            for k in range(4)
+        ]
         left, right, rad = split_features(points, centre, inv)
-        store_features((fa0, fa1), left, first)
-        store_features((fb0, fb1), right, first)
+        store_features(fa, left, first)
+        store_features(fb, right, first)
         diag[first : first + 8, :] = lax.rsqrt(2.0 * (rad * rad))
     for copy in copies:
         copy.wait()
     up[...] = up_sums(basis, masked, transfer, parent, up.shape[0])
 
 
-def local_kernel(sizes, pair_rows, pairs, fa0, fa1, fb0, fb1, scale, acc_in, *rest):
+def local_kernel(sizes, pair_rows, pairs, fa, fb, scale, acc_in, *rest):
     S, L, R, clusters, panels = sizes
     pieces = rest[:S]
     acc_out = rest[S]
     q, acc, pair_sums, *work = rest[S + 1 :]
     ring, sums = work[:16], work[16:]
-    fa, fb = (fa0, fa1), (fb0, fb1)
     sub = lax.axis_index("sub")
     assemble(sub, S, L, q, pieces)
     acc[...] = jnp.zeros_like(acc)
@@ -416,18 +419,26 @@
     return base, unit
 
 
-def self_kernel(sizes, fa0, fa1, fb0, fb1, diags, scale, part, *rest):
+def self_kernel(sizes, fa, fb, diags, scale, part, *rest):
     S, L, R, clusters, panels = sizes
     pieces = rest[:S]
     out, q, fs, spots, self_sums, *work = rest[S:]
     ring, sums = work[:16], work[16:]
     sub, rep = lax.axis_index("sub"), lax.axis_index("rep")
-    assemble(sub, S, L, q, pieces)
     self_sums[...] = jnp.zeros_like(self_sums)
+    blocks = L == LANES
+    if blocks:
+        order = [lax.rem(sub + S - shift, S) for shift in range(S)]
+        for shift in range(S):
+            q[:, shift * L : (shift + 1) * L] = pieces[shift][...]
+    else:
+        order = None
+        assemble(sub, S, L, q, pieces)
 
     def place(s):
-        t, at = (s * L) // LANES, (s * L) % LANES
-        fs[...] = (fa0, fa1)[t][:, at : at + L]
+        if not blocks:
+            t, at = (s * L) // LANES, (s * L) % LANES
+            fs[0, :, :] = fa[t, :, at : at + L]
         spots[...] = diags[:, s * L : (s + 1) * L]
 
     for s in range(S):
@@ -438,7 +449,8 @@
 
     def begin(i, dist):
         c = first + jnp.minimum(i, share - 1)
-        distances(load_features((fs,), c), load_features((fb0, fb1), c), dist)
+        own = load_features(fa, c, order[:1]) if blocks else load_features(fs, c)
+        distances(own, load_features(fb, c, order), dist)
 
     def finish(i, dist, parts):
         c = first + i
@@ -447,12 +459,13 @@
 
         def root(span, _):
             shape = (span.stop - span.start, LANES)
-            row = lax.broadcasted_iota(jnp.int32, shape, 0) + (sub * L + span.start)
+            row = lax.broadcasted_iota(jnp.int32, shape, 0) + span.start
+            row = row if blocks else row + sub * L
             col = lax.broadcasted_iota(jnp.int32, shape, 1)
-            return [
-                jnp.where(row == col + t, diag[span, :], inverse_root(dist[span, t : t + LANES]))
-                for t in range(0, panels, LANES)
-            ]
+            values = [inverse_root(dist[span, t : t + LANES]) for t in range(0, panels, LANES)]
+            for t in range(1 if blocks else len(values)):
+                values[t] = jnp.where(row == col + t * LANES, diag[span, :], values[t])
+            return values
 
         def partial(span, held):
             keep(parts, span, sum(g * qrow[:, t * LANES : (t + 1) * LANES] for t, g in enumerate(held)))
@@ -589,7 +602,7 @@
 
     made = pl.pallas_call(
         functools.partial(pack_kernel, (C, S, L, slots)),
-        out_shape=[pltpu.VMEM((clusters, L), F32), pltpu.VMEM(geometry.shape, F32)]
+        out_shape=[pltpu.VMEM((clusters, L), F32), pltpu.VMEM((panels // LANES, clusters * 4, LANES), F32)]
         + [pltpu.VMEM((5 * slots + 8, L), F32)] * (C - 1),
         in_specs=[vmem()] * 3 + [smem()] * 3,
         out_specs=[vmem()] * (C + 1),
@@ -603,14 +616,14 @@
 
     *features, up = pl.pallas_call(
         prepare_kernel,
-        out_shape=[pltpu.VMEM((clusters * ROWS, LANES), F32)] * 4
+        out_shape=[pltpu.VMEM((panels // LANES, clusters * ROWS, LANES), F32)] * 2
         + [
             pltpu.VMEM((clusters, panels), F32),
             pltpu.VMEM((8, LANES), F32),
             pltpu.VMEM((par_dev, rank), F32),
         ],
         in_specs=[vmem()] * 2 + [pl.BlockSpec(memory_space=pltpu.HBM)] * 3,
-        out_specs=[vmem()] * 7,
+        out_specs=[vmem()] * 5,
         scratch_shapes=[
             pltpu.VMEM(basis_t.shape, F32),
             pltpu.VMEM(transfer_t.shape, F32),
@@ -627,14 +640,14 @@
         functools.partial(remote_kernel, (C, S, L, slots, clusters, panels)),
         out_shape=[pltpu.VMEM((clusters, panels), F32)]
         + [pltpu.VMEM((slots + par_dev, L), F32)] * (C - 1),
-        in_specs=[vmem()] * (4 + S + C - 1),
+        in_specs=[vmem()] * (3 + S + C - 1),
         out_specs=[vmem()] * C,
         scratch_shapes=[
             pltpu.VMEM((clusters, panels), F32),
             pltpu.VMEM((n, L), F32),
             pltpu.VMEM((clusters, panels), F32),
             pltpu.VMEM((L, whole(n)), F32),
-            pltpu.VMEM((n * ROWS, L), F32),
+            pltpu.VMEM((1, n * ROWS, L), F32),
             pltpu.SMEM((2 * n + 1,), jnp.int32),
             pltpu.SMEM((C - 1, 8, L), F32),
             pltpu.SemaphoreType.DMA((C - 1,)),
@@ -644,14 +657,14 @@
         compiler_params=limit(24),
         cost_estimate=about(6),
         name="near_remote",
-    )(*near_by(*tables[2:], scale, up, *pieces, *packs))
+    )(*near_by(tables[1], scale, up, *pieces, *packs))
     acc, sums = made[0], [send(made[d], (("clu", C - d),)) for d in range(1, C)]
 
     wide = whole(local_pairs.shape[1])
     near = pl.pallas_call(
         functools.partial(local_kernel, (S, L, R, clusters, panels)),
         out_shape=pltpu.VMEM((clusters, panels), F32),
-        in_specs=[vmem(), smem()] + [vmem()] * (6 + S),
+        in_specs=[vmem(), smem()] + [vmem()] * (4 + S),
         out_specs=vmem(),
         scratch_shapes=[
             pltpu.VMEM((clusters, panels), F32),
@@ -681,11 +694,11 @@
     near = pl.pallas_call(
         functools.partial(self_kernel, (S, L, R, clusters, panels)),
         out_shape=pltpu.VMEM((height, L), F32),
-        in_specs=[vmem()] * (7 + S),
+        in_specs=[vmem()] * (5 + S),
         out_specs=vmem(),
         scratch_shapes=[
             pltpu.VMEM((clusters, panels), F32),
-            pltpu.VMEM((clusters * ROWS, L), F32),
+            pltpu.VMEM((1, 8 if L == LANES else clusters * ROWS, L), F32),
             pltpu.VMEM((clusters, L), F32),
             pltpu.VMEM((L, clusters), F32),
         ]

time: 42.6 us -> 39.2 us (0.920)
  Pallas kernels: 29.4 us -> 24.4 us
  starting transfers between devices: 12.1 us -> 13 us
  waiting for transfers between devices: 0.12 us -> 0.68 us
    pallas_call x1, Pallas kernels: 5.41 us -> 2.48 us  [on_device(): pl.pallas_call(prepare_kernel, out_shape=[pltpu.VMEM((panels // LANES, cl...]
    pallas_call x1, Pallas kernels: 9.89 us -> 8.44 us  [on_device(): pl.pallas_call(functools.partial(local_kernel, (S, L, R, clusters, panels...]
    ppermute x9, starting transfers between devices: 12.1 us -> 13 us  [send(): return lax.ppermute(value, names if len(names) > 1 else names[0], perm)]
    ppermute x9, waiting for transfers between devices: 0.12 us -> 0.68 us  [send(): return lax.ppermute(value, names if len(names) > 1 else names[0], perm)]
    pallas_call x1, Pallas kernels: 4.86 us -> 4.3 us  [on_device(): pl.pallas_call(functools.partial(self_kernel, (S, L, R, clusters, panels)...]
  transfers between devices with their start and end apart: 9 -> 9, of which waited for: 1 -> 2; matrix products, arithmetic and copies ran while one was open for 0% -> 0% of each run, Pallas kernels for 49% -> 41%
where the time goes in v18:
time: 39.2 us; the launch traced here: 38.9 us
  Pallas kernels  24.4 us (62%)
  starting transfers between devices  13 us (33%)
  waiting for transfers between devices  0.68 us (2%)
  other arithmetic  0.65 us (2%)
    ppermute x9, starting transfers between devices, send(): return lax.ppermute(value, names if len(names) > 1 else names[0], perm)  13 us
    pallas_call x1, Pallas kernels, on_device(): pl.pallas_call(functools.partial(local_kernel, (S, L, R, clusters, panels...  8.44 us
    pallas_call x1, Pallas kernels, on_device(): pl.pallas_call(functools.partial(remote_kernel, (C, S, L, slots, clusters...  5.7 us
    pallas_call x1, Pallas kernels, on_device(): pl.pallas_call(functools.partial(self_kernel, (S, L, R, clusters, panels)...  4.3 us
    pallas_call x1, Pallas kernels, on_device(): pl.pallas_call(prepare_kernel, out_shape=[pltpu.VMEM((panels // LANES, cl...  2.48 us
    pallas_call x1, Pallas kernels, on_device(): pl.pallas_call(functools.partial(pack_kernel, (C, S, L, slots)), out_shap...  1.37 us
    pallas_call x1, Pallas kernels, on_device(): pl.pallas_call(functools.partial(merge_kernel, (C, S, L, slots, clusters)...  1.25 us
    pallas_call x1, Pallas kernels, on_device(): pl.pallas_call(far_kernel, out_shape=pltpu.VMEM((clusters, L), F32), in_s...  0.82 us
  transfers between devices with their start and end apart: 9, of which 2 were waited for; matrix products, arithmetic and copies ran while one was open for 0% of the time, Pallas kernels for 41%

profile of v18, /device:TPU:0, one launch (start us, length us, event | category | flops | bytes accessed | tf_op | source)
XLA Modules:
  0.0 38.9 jit_solution(4272713084300413872)
XLA Ops:
  0.0 1.4 %packs.1 = (f32[128,128]{1,0:T(8,128)S(1)}, f32[2,512,128]{2,1,0:T(8,128)S(1)}, f32[88,128]{1,0:T(8,128)S(1)}, f32[88,128]{1,0:T(8,128)S(1)}, f32[88,128]{1,0:T(8,128)S(1)}) custom-call(f32[128,128]{1,0:T(8,128)} %charges.1, s32[128,128]{1,0:T(8,128)} %mask.1, f32[128,4,256]{2,1,0:T(4,128)} %geo.1, s32[4,16]{1,0:T(4,128)} %bitcast.14, s32[4,16]{1,0:T(4,128)} %bitcast.21, ...), custom_call_target="tpu_custom_call" | custom-call | bytes 7000000 | tf_op jit(solution)/shard_map/packs/pallas_call | solution.py:603
  1.4 3.0 %collective-permute-start = (f32[128,128]{1,0:T(8,128)S(1)}, f32[128,128]{1,0:T(8,128)S(1)}, u32[]{:S(2)}, u32[]{:S(2)}) collective-permute-start(f32[128,128]{1,0:T(8,128)S(1)} %get-tuple-element.22.masked.rest_0_), channel_id=1, source_target_pairs={{0,2},{2,0},{1,3},{3,1},{4,6},{6,4},{5,7},{7,5},{8,10},{10,8},{9,1... | collective-permute-start | bytes 196616 | tf_op jit(solution)/shard_map/ppermute | solution.py:574
  4.4 1.6 %collective-permute-start.1 = (f32[88,128]{1,0:T(8,128)S(1)}, f32[88,128]{1,0:T(8,128)S(1)}, u32[]{:S(2)}, u32[]{:S(2)}) collective-permute-start(f32[88,128]{1,0:T(8,128)S(1)} %get-tuple-element.28), channel_id=1, source_target_pairs={{0,4},{4,8},{8,12},{12,0},{1,5},{5,9},{9,13},{13,1},{2,6},{6,10},{... | collective-permute-start | bytes 135176 | tf_op jit(solution)/shard_map/ppermute | solution.py:574
  6.0 2.6 %collective-permute-start.2 = (f32[88,128]{1,0:T(8,128)S(1)}, f32[88,128]{1,0:T(8,128)S(1)}, u32[]{:S(2)}, u32[]{:S(2)}) collective-permute-start(f32[88,128]{1,0:T(8,128)S(1)} %get-tuple-element.29), channel_id=1, source_target_pairs={{0,8},{4,12},{8,0},{12,4},{1,9},{5,13},{9,1},{13,5},{2,10},{6,14},... | collective-permute-start | bytes 135176 | tf_op jit(solution)/shard_map/ppermute | solution.py:574
  8.6 1.3 %collective-permute-start.3 = (f32[88,128]{1,0:T(8,128)S(1)}, f32[88,128]{1,0:T(8,128)S(1)}, u32[]{:S(2)}, u32[]{:S(2)}) collective-permute-start(f32[88,128]{1,0:T(8,128)S(1)} %get-tuple-element.30), channel_id=1, source_target_pairs={{0,12},{4,0},{8,4},{12,8},{1,13},{5,1},{9,5},{13,9},{2,14},{6,2},{... | collective-permute-start | bytes 135176 | tf_op jit(solution)/shard_map/ppermute | solution.py:574
  9.9 0.0 copy-start.5
  9.9 2.5 %prepare.1 = (f32[2,3072,128]{2,1,0:T(8,128)S(1)}, f32[2,3072,128]{2,1,0:T(8,128)S(1)}, f32[128,256]{1,0:T(8,128)S(1)}, f32[8,128]{1,0:T(8,128)S(1)}, f32[16,32]{1,0:T(8,128)S(1)}) custom-call(f32[2,512,128]{2,1,0:T(8,128)S(1)} %get-tuple-element.21.geo, f32[128,128]{1,0:T(8,128)S(1)} %get-tuple-element.22.masked.rest_0_, f32[128,32,128]{2,1,0:T(8,128)} %bitcast.10, ...), custom_call_target="tpu_custom_call" | custom-call | bytes 14000000 | tf_op jit(solution)/shard_map/prepare/pallas_call | solution.py:617
  12.4 0.0 collective-permute-done.1.rest_2_
  12.4 0.0 collective-permute-done.2.rest_3_
  12.4 0.2 collective-permute-done.3.rest_4_
  12.6 0.0 collective-permute-done.rest_1_
  12.6 5.7 %near_remote.1 = (f32[128,256]{1,0:T(8,128)S(1)}, f32[32,128]{1,0:T(8,128)S(1)}, f32[32,128]{1,0:T(8,128)S(1)}, f32[32,128]{1,0:T(8,128)S(1)}) custom-call(f32[2,3072,128]{2,1,0:T(8,128)S(1)} %get-tuple-element.24.fb, f32[8,128]{1,0:T(8,128)S(1)} %get-tuple-element.26.scale, f32[16,32]{1,0:T(8,128)S(1)} %get-tuple-element.27.up, ...), custom_call_target="tpu_custom_call" | custom-call | bytes 21000000 | tf_op jit(solution)/shard_map/near_remote/pallas_call | solution.py:639
  18.4 3.2 %collective-permute-start.4 = (f32[32,128]{1,0:T(8,128)S(1)}, f32[32,128]{1,0:T(8,128)S(1)}, u32[]{:S(2)}, u32[]{:S(2)}) collective-permute-start(f32[32,128]{1,0:T(8,128)S(1)} %get-tuple-element.32), channel_id=1, source_target_pairs={{0,12},{4,0},{8,4},{12,8},{1,13},{5,1},{9,5},{13,9},{2,14},{6,2},{... | collective-permute-start | bytes 49160 | tf_op jit(solution)/shard_map/ppermute | solution.py:574
  21.5 0.0 collective-permute-start.5
  21.5 0.6 %collective-permute-start.6 = (f32[32,128]{1,0:T(8,128)S(1)}, f32[32,128]{1,0:T(8,128)S(1)}, u32[]{:S(2)}, u32[]{:S(2)}) collective-permute-start(f32[32,128]{1,0:T(8,128)S(1)} %get-tuple-element.34), channel_id=1, source_target_pairs={{0,4},{4,8},{8,12},{12,0},{1,5},{5,9},{9,13},{13,1},{2,6},{6,10},{... | collective-permute-start | bytes 49160 | tf_op jit(solution)/shard_map/ppermute | solution.py:574
  22.2 0.0 copy-done.5
  22.2 0.0 copy-start.1
  22.2 0.0 copy-start.2
  22.2 0.0 copy-start.3
  22.2 0.0 copy-start.4
  22.2 0.0 copy-start.6
  22.2 8.4 %near_local.1.near = f32[128,256]{1,0:T(8,128)S(1)} custom-call(s32[2,128]{1,0:T(2,128)S(1)} %bitcast.17, s32[2,128]{1,0:T(2,128)S(1)} %bitcast.18, f32[2,3072,128]{2,1,0:T(8,128)S(1)} %get-tuple-element.23.fa, f32[2,3072,128]{2,1,0:T(8,128)S(1)} %get-tuple-element.24.fb, f32[8,128]{1,0:T(8,128)S(1)} %get-tuple-element.26.scale, ...), custom_call_target="tpu_custom_call" | custom-call | bytes 31500000 | tf_op jit(solution)/shard_map/near_local/pallas_call | solution.py:664
  30.6 0.0 collective-permute-done.4.rest_0_
  30.7 0.0 collective-permute-done.5.rest_1_
  30.7 0.0 collective-permute-done.6.rest_2_
  30.7 0.0 copy-done.1
  30.7 0.0 copy-done.2
  30.7 0.0 copy-done.3
  30.7 0.0 copy-done.4
  30.7 0.0 copy-done.6
  30.7 1.3 %merge.1 = (f32[160,128]{1,0:T(8,128)S(1)}, f32[160,128]{1,0:T(8,128)S(1)}) custom-call(s32[8,16]{1,0:T(8,128)S(1)} %bitcast.16, s32[4,16]{1,0:T(4,128)S(1)} %bitcast.15, f32[128,256]{1,0:T(8,128)S(1)} %near_local.1.near, f32[16,8,32,32]{3,2,1,0:T(8,128)S(1)} %copy-done.1, f32[32,32,128]{2,1,0:T(8,128)S(1)} %bitcast.13, s32[1,128]{1,0:T(1,128)S(1)} %bitcast.20, ...), custom_call_target="tpu_custom_call" | custom-call | bytes 3500000 | tf_op jit(solution)/shard_map/merge/pallas_call | solution.py:682
  32.0 0.6 %collective-permute-start.7 = (f32[160,128]{1,0:T(8,128)S(1)}, f32[160,128]{1,0:T(8,128)S(1)}, u32[]{:S(2)}, u32[]{:S(2)}) collective-permute-start(f32[160,128]{1,0:T(8,128)S(1)} %get-tuple-element.36), channel_id=1, source_target_pairs={{0,2},{2,0},{1,3},{3,1},{4,6},{6,4},{5,7},{7,5},{8,10},{10,8},{9,1... | collective-permute-start | bytes 245768 | tf_op jit(solution)/shard_map/ppermute | solution.py:574
  32.6 0.0 copy-start
  32.6 0.0 copy-start.7
  32.6 4.3 %near_self.1 = f32[160,128]{1,0:T(8,128)S(1)} custom-call(f32[2,3072,128]{2,1,0:T(8,128)S(1)} %get-tuple-element.23.fa, f32[2,3072,128]{2,1,0:T(8,128)S(1)} %get-tuple-element.24.fb, f32[128,256]{1,0:T(8,128)S(1)} %get-tuple-element.25.diags, f32[8,128]{1,0:T(8,128)S(1)} %get-tuple-element.26.scale, f32[160,128]{1,0:T(8,128)S(1)} %get-tuple-element.35.part, ...), custom_call_target="tpu_custom_call" | custom-call | bytes 14000000 | tf_op jit(solution)/shard_map/near_self/pallas_call | solution.py:694
  36.9 0.0 collective-permute-done.7
  36.9 0.1 collective-permute-start.8
  37.0 0.0 copy-done
  37.0 0.8 %far_down.1 = f32[128,128]{1,0:T(8,128)S(1)} custom-call(f32[128,32,128]{2,1,0:T(8,128)S(1)} %bitcast.11, f32[160,128]{1,0:T(8,128)S(1)} %add.6.near), custom_call_target="tpu_custom_call" | custom-call | bytes 3500000 | tf_op jit(solution)/shard_map/far_down/pallas_call | solution.py:715
  37.8 0.4 %collective-permute-done.8 = f32[160,128]{1,0:T(8,128)S(1)} collective-permute-done((f32[160,128]{1,0:T(8,128)S(1)}, f32[160,128]{1,0:T(8,128)S(1)}, u32[]{:S(2)}, u32[]{:S(2)}) %collective-permute-start.8) | collective-permute-done | bytes 81952 | tf_op jit(solution)/shard_map/ppermute | solution.py:574
  38.3 0.0 copy-done.7
  38.3 0.6 %fusion = f32[128,128]{1,0:T(8,128)} fusion(f32[128,128]{1,0:T(8,128)S(1)} %far_down.1, f32[160,128]{1,0:T(8,128)S(1)} %collective-permute-done.8, s32[128,128]{1,0:T(8,128)S(1)} %copy-done.7), kind=kLoop, calls=%fused_computation.1 | loop fusion | flops 49152 | bytes 262144 | tf_op jit(solution)/shard_map/mul | solution.py:726
  (1 shorter events, 0.0 us)
Async XLA Ops:
  1.4 11.3 %collective-permute-start = (f32[128,128]{1,0:T(8,128)S(1)}, f32[128,128]{1,0:T(8,128)S(1)}, u32[]{:S(2)}, u32[]{:S(2)}) collective-permute-start(f32[128,128]{1,0:T(8,128)S(1)} %get-tuple-element.22.masked.rest_0_), channel_id=1, source_target_pairs={{0,2},{2,0},{1,3},{3,1},{4,6},{6,4},{5,7},{7,5},{8,10},{10,8},{9,1... | collective-permute-start | bytes 196616 | tf_op jit(solution)/shard_map/ppermute | solution.py:574
  4.4 8.0 %collective-permute-start.1 = (f32[88,128]{1,0:T(8,128)S(1)}, f32[88,128]{1,0:T(8,128)S(1)}, u32[]{:S(2)}, u32[]{:S(2)}) collective-permute-start(f32[88,128]{1,0:T(8,128)S(1)} %get-tuple-element.28), channel_id=1, source_target_pairs={{0,4},{4,8},{8,12},{12,0},{1,5},{5,9},{9,13},{13,1},{2,6},{6,10},{... | collective-permute-start | bytes 135176 | tf_op jit(solution)/shard_map/ppermute | solution.py:574
  6.0 6.4 %collective-permute-start.2 = (f32[88,128]{1,0:T(8,128)S(1)}, f32[88,128]{1,0:T(8,128)S(1)}, u32[]{:S(2)}, u32[]{:S(2)}) collective-permute-start(f32[88,128]{1,0:T(8,128)S(1)} %get-tuple-element.29), channel_id=1, source_target_pairs={{0,8},{4,12},{8,0},{12,4},{1,9},{5,13},{9,1},{13,5},{2,10},{6,14},... | collective-permute-start | bytes 135176 | tf_op jit(solution)/shard_map/ppermute | solution.py:574
  8.6 4.1 %collective-permute-start.3 = (f32[88,128]{1,0:T(8,128)S(1)}, f32[88,128]{1,0:T(8,128)S(1)}, u32[]{:S(2)}, u32[]{:S(2)}) collective-permute-start(f32[88,128]{1,0:T(8,128)S(1)} %get-tuple-element.30), channel_id=1, source_target_pairs={{0,12},{4,0},{8,4},{12,8},{1,13},{5,1},{9,5},{13,9},{2,14},{6,2},{... | collective-permute-start | bytes 135176 | tf_op jit(solution)/shard_map/ppermute | solution.py:574
  9.9 12.3 %copy-start.5 = (s32[1,128,2]{1,2,0:T(2,128)S(1)}, s32[1,128,2]{1,2,0:T(2,128)}, u32[]{:S(2)}) copy-start(s32[1,128,2]{1,2,0:T(2,128)} %param.18) | copy-start | bytes 3076
  18.4 12.3 %collective-permute-start.4 = (f32[32,128]{1,0:T(8,128)S(1)}, f32[32,128]{1,0:T(8,128)S(1)}, u32[]{:S(2)}, u32[]{:S(2)}) collective-permute-start(f32[32,128]{1,0:T(8,128)S(1)} %get-tuple-element.32), channel_id=1, source_target_pairs={{0,12},{4,0},{8,4},{12,8},{1,13},{5,1},{9,5},{13,9},{2,14},{6,2},{... | collective-permute-start | bytes 49160 | tf_op jit(solution)/shard_map/ppermute | solution.py:574
  21.5 9.1 %collective-permute-start.5 = (f32[32,128]{1,0:T(8,128)S(1)}, f32[32,128]{1,0:T(8,128)S(1)}, u32[]{:S(2)}, u32[]{:S(2)}) collective-permute-start(f32[32,128]{1,0:T(8,128)S(1)} %get-tuple-element.33), channel_id=1, source_target_pairs={{0,8},{4,12},{8,0},{12,4},{1,9},{5,13},{9,1},{13,5},{2,10},{6,14},... | collective-permute-start | bytes 49160 | tf_op jit(solution)/shard_map/ppermute | solution.py:574
  21.5 9.1 %collective-permute-start.6 = (f32[32,128]{1,0:T(8,128)S(1)}, f32[32,128]{1,0:T(8,128)S(1)}, u32[]{:S(2)}, u32[]{:S(2)}) collective-permute-start(f32[32,128]{1,0:T(8,128)S(1)} %get-tuple-element.34), channel_id=1, source_target_pairs={{0,4},{4,8},{8,12},{12,0},{1,5},{5,9},{9,13},{13,1},{2,6},{6,10},{... | collective-permute-start | bytes 49160 | tf_op jit(solution)/shard_map/ppermute | solution.py:574
  22.2 8.5 %copy-start.1 = (f32[16,8,32,32]{3,2,1,0:T(8,128)S(1)}, f32[16,8,32,32]{3,2,1,0:T(8,128)}, u32[]{:S(2)}) copy-start(f32[16,8,32,32]{3,2,1,0:T(8,128)} %coupling.1) | copy-start | bytes 1572868
  22.2 8.5 %copy-start.2 = (f32[128,32,32]{0,2,1:T(8,128)S(1)}, f32[128,32,32]{0,2,1:T(8,128)}, u32[]{:S(2)}) copy-start(f32[128,32,32]{0,2,1:T(8,128)} %param.20) | copy-start | bytes 1572868
  22.2 8.5 %copy-start.3 = (s32[1,4,16]{2,1,0:T(4,128)S(1)}, s32[1,4,16]{2,1,0:T(4,128)}, u32[]{:S(2)}) copy-start(s32[1,4,16]{2,1,0:T(4,128)} %param.16) | copy-start | bytes 772
  22.2 8.5 %copy-start.4 = (s32[16,8]{0,1:T(8,128)S(1)}, s32[16,8]{0,1:T(8,128)}, u32[]{:S(2)}) copy-start(s32[16,8]{0,1:T(8,128)} %param.22) | copy-start | bytes 1540
  22.2 8.5 %copy-start.6 = (s32[128]{0:T(128)S(1)}, s32[128]{0:T(128)}, u32[]{:S(2)}) copy-start(s32[128]{0:T(128)} %param.21) | copy-start | bytes 1540
  32.0 4.9 %collective-permute-start.7 = (f32[160,128]{1,0:T(8,128)S(1)}, f32[160,128]{1,0:T(8,128)S(1)}, u32[]{:S(2)}, u32[]{:S(2)}) collective-permute-start(f32[160,128]{1,0:T(8,128)S(1)} %get-tuple-element.36), channel_id=1, source_target_pairs={{0,2},{2,0},{1,3},{3,1},{4,6},{6,4},{5,7},{7,5},{8,10},{10,8},{9,1... | collective-permute-start | bytes 245768 | tf_op jit(solution)/shard_map/ppermute | solution.py:574
  32.6 4.4 %copy-start = (f32[128,128,32]{1,2,0:T(8,128)S(1)}, f32[128,128,32]{1,2,0:T(8,128)}, u32[]{:S(2)}) copy-start(f32[128,128,32]{1,2,0:T(8,128)} %param.19) | copy-start | bytes 6291460
  32.6 5.7 %copy-start.7 = (s32[128,128]{1,0:T(8,128)S(1)}, s32[128,128]{1,0:T(8,128)}, u32[]{:S(2)}) copy-start(s32[128,128]{1,0:T(8,128)} %mask.1) | copy-start | bytes 196612
  36.9 1.3 %collective-permute-start.8 = (f32[160,128]{1,0:T(8,128)S(1)}, f32[160,128]{1,0:T(8,128)S(1)}, u32[]{:S(2)}, u32[]{:S(2)}) collective-permute-start(f32[160,128]{1,0:T(8,128)S(1)} %add.6.near), channel_id=1, source_target_pairs={{0,1},{1,0},{2,3},{3,2},{4,5},{5,4},{6,7},{7,6},{8,9},{9,8},{10,11... | collective-permute-start | bytes 245768 | tf_op jit(solution)/shard_map/ppermute | solution.py:574

commit v19 on v18

--- a/solution.py
+++ b/solution.py
@@ -246,7 +246,7 @@
 
 
 def ring_size(total):
-    return next(size for size in (16, 8, 4, 2, 1) if total % size == 0)
+    return next(size for size in (32, 16, 8, 4, 2, 1) if total % size == 0)
 
 
 def assemble(sub, S, L, q, pieces):
@@ -259,31 +259,28 @@
         pl.when(sub == s)(functools.partial(place, s))
 
 
-def pack_kernel(sizes, charges, mask, geo, targets, sources, live, masked, geo_out, *packs):
+def pack_kernel(sizes, charges, mask, geo, targets, sources, live, masked, geo_out, packs):
     C, S, L, slots = sizes
-    me, sub = lax.axis_index("clu"), lax.axis_index("sub")
+    sub = lax.axis_index("sub")
     masked[...] = charges[...] * mask[...].astype(F32)
     for t in range(geo_out.shape[0]):
         geo_out[t, :, :] = geo[:, :, t * LANES : (t + 1) * LANES].reshape(geo_out.shape[1:])
     lane = lax.broadcasted_iota(jnp.int32, (8, L), 1)
-    for shift in range(1, C):
-        dest = lax.rem(me + shift, C)
+    for dest in range(C):
         codes = jnp.full((8, L), -1.0, F32)
         for j in range(slots):
             code = jnp.where(live[dest, j] > 0, sources[dest, j], -1)
             codes = jnp.where(lane == j, code.astype(F32), codes)
-        packs[shift - 1][5 * slots :, :] = codes
+        packs[dest, 5 * slots :, :] = codes
 
     def fill(s):
-        for shift in range(1, C):
-            dest = lax.rem(me + shift, C)
-            pack = packs[shift - 1]
+        for dest in range(C):
             for j in range(slots):
                 t = targets[dest, j]
                 g = geo[t, :, s * L : (s + 1) * L]
                 for k in range(4):
-                    pack[k * slots + j : k * slots + j + 1, :] = g[k : k + 1]
-                pack[4 * slots + j : 4 * slots + j + 1, :] = masked[pl.ds(t, 1), :]
+                    packs[dest, k * slots + j : k * slots + j + 1, :] = g[k : k + 1]
+                packs[dest, 4 * slots + j : 4 * slots + j + 1, :] = masked[pl.ds(t, 1), :]
 
     for s in range(S):
         pl.when(sub == s)(functools.partial(fill, s))
@@ -292,14 +289,13 @@
 def remote_kernel(sizes, fb, scale, up, *rest):
     C, S, L, slots, clusters, panels = sizes
     pieces = rest[:S]
-    packs = rest[S : S + C - 1]
-    acc_out = rest[S + C - 1]
-    sends = rest[S + C : S + C + C - 1]
-    q, tq, acc, fwdt, fa, order, codes, sems, *work = rest[S + C + C - 1 :]
-    n = (C - 1) * slots
+    packs, acc_out, sends = rest[S : S + 3]
+    q, tq, acc, fwdt, fa, order, codes, sems, *work = rest[S + 3 :]
+    ring, sums = work[:16], work[16:]
+    n = C * slots
     copies = [
-        pltpu.make_async_copy(packs[k].at[pl.ds(5 * slots, 8), :], codes.at[k], sems.at[k])
-        for k in range(C - 1)
+        pltpu.make_async_copy(packs.at[k, pl.ds(5 * slots, 8), :], codes.at[k], sems.at[k])
+        for k in range(C)
     ]
     for copy in copies:
         copy.start()
@@ -309,16 +305,16 @@
     for copy in copies:
         copy.wait()
     found = jnp.int32(0)
-    for shift in range(C - 1):
+    for shift in range(C):
         for j in range(slots):
             code = codes[shift, 0, j].astype(jnp.int32)
             order[n + 1 + shift * slots + j] = jnp.maximum(code, 0)
             order[found] = shift * slots + j
             found = found + (code >= 0).astype(jnp.int32)
     inv, centre = split_frame(scale)
-    for shift in range(C - 1):
+    for shift in range(C):
         for first in range(0, slots, 8):
-            points = [packs[shift][k * slots + first : k * slots + first + 8, :] for k in range(5)]
+            points = [packs[shift, k * slots + first : k * slots + first + 8, :] for k in range(5)]
             left, _, _ = split_features(points, centre, inv)
             store_features(fa, left, shift * slots + first)
             at = shift * slots + first
@@ -338,14 +334,14 @@
         acc[pl.ds(source, 1), :] += jnp.where(ok, back, 0.0)
         return jnp.where(ok, slot, -1)
 
-    pipeline(found, begin, finish, fwdt, work[:8], work[8:])
+    pipeline(found, begin, finish, fwdt, ring, sums)
     acc_out[...] = acc[...] * inv
     fwd = (fwdt[...] * inv).T
     rank = up.shape[1]
-    for shift in range(C - 1):
-        sends[shift][:slots, :] = fwd[shift * slots : (shift + 1) * slots, :]
-        sends[shift][slots:, :] = jnp.zeros((up.shape[0], L), F32)
-        sends[shift][slots:, :rank] = up[...]
+    for shift in range(C):
+        sends[shift, :slots, :] = fwd[shift * slots : (shift + 1) * slots, :]
+        sends[shift, slots:, :] = jnp.zeros((up.shape[0], L), F32)
+        sends[shift, slots:, :rank] = up[...]
 
 
 def prepare_kernel(
@@ -387,7 +383,7 @@
     pieces = rest[:S]
     acc_out = rest[S]
     q, acc, pair_sums, *work = rest[S + 1 :]
-    ring, sums = work[:16], work[16:]
+    ring, sums = work[:32], work[32:]
     sub = lax.axis_index("sub")
     assemble(sub, S, L, q, pieces)
     acc[...] = jnp.zeros_like(acc)
@@ -478,22 +474,19 @@
     out[:clusters, :] = part[:clusters, :] + self_sums[...].T * scale[0:1, 0:1]
 
 
-def merge_kernel(sizes, far_list, targets, near, coupling, transfer, parent, up, *rest):
+def merge_kernel(sizes, far_list, targets, near, coupling, transfer, parent, sums, *rest):
     C, S, L, slots, clusters = sizes
-    sums = rest[: C - 1]
-    parts = rest[C - 1 : C - 1 + S]
-    parents = rest[-1]
-    me, sub = lax.axis_index("clu"), lax.axis_index("sub")
-    index = [targets[pl.ds(lax.rem(me + shift, C), 1), :] for shift in range(1, C)]
+    parts, parents = rest[:S], rest[S]
+    sub = lax.axis_index("sub")
     got = select_rows(
-        jnp.concatenate(index, axis=1), jnp.concatenate([v[:slots, :] for v in sums], axis=0), clusters
+        jnp.concatenate([targets[d : d + 1, :] for d in range(C)], axis=1),
+        jnp.concatenate([sums[d, :slots, :] for d in range(C)], axis=0),
+        clusters,
     )
 
     par_dev, far_n, rank = coupling.shape[0], coupling.shape[1], coupling.shape[2]
-    parents[pl.ds(pl.multiple_of(me * par_dev, 8), par_dev), :] = up[...]
-    for shift in range(1, C):
-        owner = lax.rem(me + shift, C)
-        parents[pl.ds(pl.multiple_of(owner * par_dev, 8), par_dev), :] = sums[shift - 1][slots:, :rank]
+    for d in range(C):
+        parents[d * par_dev : (d + 1) * par_dev, :] = sums[d, slots:, :rank]
     lane = lax.broadcasted_iota(jnp.int32, (rank, LANES), 1)
     field = jnp.zeros((rank, LANES), F32)
     for p in range(par_dev):
@@ -593,7 +586,7 @@
     C, S, R = lax.axis_size("clu"), lax.axis_size("sub"), lax.axis_size("rep")
     slots = remote_source.shape[2]
     par_dev, rank = far_list.shape[0], transfer.shape[1]
-    n = (C - 1) * slots
+    n = C * slots
     shape = jax.ShapeDtypeStruct
     targets = remote_target[0]
     basis_t = jnp.transpose(basis, (0, 2, 1))
@@ -603,16 +596,16 @@
     made = pl.pallas_call(
         functools.partial(pack_kernel, (C, S, L, slots)),
         out_shape=[pltpu.VMEM((clusters, L), F32), pltpu.VMEM((panels // LANES, clusters * 4, LANES), F32)]
-        + [pltpu.VMEM((5 * slots + 8, L), F32)] * (C - 1),
+        + [pltpu.VMEM((C, 5 * slots + 8, L), F32)],
         in_specs=[vmem()] * 3 + [smem()] * 3,
-        out_specs=[vmem()] * (C + 1),
+        out_specs=[vmem()] * 3,
         compiler_params=limit(60),
         cost_estimate=about(2),
         name="packs",
     )(charges, panel_mask, geometry, targets, remote_source[0], remote_live[0])
-    masked, geo, packs = made[0], made[1], made[2:]
+    masked, geo, packs = made
     pieces = [masked] + [send(masked, (("sub", d),)) for d in range(1, S)]
-    packs = [send(packs[d - 1], (("clu", d),)) for d in range(1, C)]
+    packs = lax.all_to_all(packs, "clu", split_axis=0, concat_axis=0, tiled=True)
 
     *features, up = pl.pallas_call(
         prepare_kernel,
@@ -639,9 +632,9 @@
     made = pl.pallas_call(
         functools.partial(remote_kernel, (C, S, L, slots, clusters, panels)),
         out_shape=[pltpu.VMEM((clusters, panels), F32)]
-        + [pltpu.VMEM((slots + par_dev, L), F32)] * (C - 1),
-        in_specs=[vmem()] * (3 + S + C - 1),
-        out_specs=[vmem()] * C,
+        + [pltpu.VMEM((C, slots + par_dev, L), F32)],
+        in_specs=[vmem()] * (4 + S),
+        out_specs=[vmem()] * 2,
         scratch_shapes=[
             pltpu.VMEM((clusters, panels), F32),
             pltpu.VMEM((n, L), F32),
@@ -649,16 +642,17 @@
             pltpu.VMEM((L, whole(n)), F32),
             pltpu.VMEM((1, n * ROWS, L), F32),
             pltpu.SMEM((2 * n + 1,), jnp.int32),
-            pltpu.SMEM((C - 1, 8, L), F32),
-            pltpu.SemaphoreType.DMA((C - 1,)),
+            pltpu.SMEM((C, 8, L), F32),
+            pltpu.SemaphoreType.DMA((C,)),
         ]
-        + [pltpu.VMEM((L, panels), F32)] * 8
+        + [pltpu.VMEM((L, panels), F32)] * 16
         + [pltpu.VMEM((L, 2 * LANES), BF16)] * 4,
         compiler_params=limit(24),
         cost_estimate=about(6),
         name="near_remote",
-    )(*near_by(tables[1], scale, up, *pieces, *packs))
-    acc, sums = made[0], [send(made[d], (("clu", C - d),)) for d in range(1, C)]
+    )(*near_by(tables[1], scale, up, *pieces, packs))
+    acc = made[0]
+    sums = lax.all_to_all(made[1], "clu", split_axis=0, concat_axis=0, tiled=True)
 
     wide = whole(local_pairs.shape[1])
     near = pl.pallas_call(
@@ -671,7 +665,7 @@
             pltpu.VMEM((clusters, panels), F32),
             pltpu.VMEM((panels, wide), F32),
         ]
-        + [pltpu.VMEM((panels, panels), F32)] * 16
+        + [pltpu.VMEM((panels, panels), F32)] * 32
         + [pltpu.VMEM((panels, 2 * LANES), BF16)] * 4,
         compiler_params=limit(24),
         cost_estimate=about(9),
@@ -682,13 +676,13 @@
     parts = pl.pallas_call(
         functools.partial(merge_kernel, (C, S, L, slots, clusters)),
         out_shape=[pltpu.VMEM((height, L), F32)] * S,
-        in_specs=[smem()] + [vmem()] * (6 + C - 1),
+        in_specs=[smem()] + [vmem()] * 6,
         out_specs=[vmem()] * S,
         scratch_shapes=[pltpu.VMEM((C * par_dev, rank), F32)],
         compiler_params=limit(16),
         cost_estimate=about(1),
         name="merge",
-    )(far_list.T, *near_by(targets, near, coupling, transfer_t, parent, up, *sums))
+    )(far_list.T, *near_by(targets, near, coupling, transfer_t, parent, sums))
     others = [send(parts[d], (("sub", d),)) for d in range(1, S)]
 
     near = pl.pallas_call(

time: 39.2 us -> 53.4 us (1.36)
  local copies, waits for them, and re-layouts: 0.03 us -> 13 us
  starting transfers between devices: 13 us -> 14.6 us
  waiting for transfers between devices: 0.68 us -> 0.11 us
    unnamed x16 -> x34, local copies, waits for them, and re-layouts: 0.03 us -> 13 us
    all_to_all x0 -> x2, starting transfers between devices: none -> 11.4 us  [the longest x1 6.32 us: on_device(): lax.all_to_all(packs, 'clu', split_axis=0, concat_axis=0, tiled=True)]
    ppermute x9 -> x3, starting transfers between devices: 13 us -> 3.23 us  [send(): return lax.ppermute(value, names if len(names) > 1 else names[0], perm)]
    pallas_call x1, Pallas kernels: 1.37 us -> 2.02 us  [on_device(): pl.pallas_call(functools.partial(pack_kernel, (C, S, L, slots)), out_shap...]
    ppermute x9 -> x3, waiting for transfers between devices: 0.68 us -> 0.1 us  [send(): return lax.ppermute(value, names if len(names) > 1 else names[0], perm)]
  transfers between devices with their start and end apart: 9 -> 5, of which waited for: 2 -> 1; matrix products, arithmetic and copies ran while one was open for 0% -> 0% of each run, Pallas kernels for 41% -> 30%
where the time goes in v19:
time: 53.4 us; the launch traced here: 53.2 us
  Pallas kernels  24.6 us (46%)
  starting transfers between devices  14.6 us (27%)
  local copies, waits for them, and re-layouts  13 us (24%)
  other arithmetic  0.65 us (1%)
    unnamed x34, local copies, waits for them, and re-layouts  13 us
    pallas_call x1, Pallas kernels, on_device(): pl.pallas_call(functools.partial(local_kernel, (S, L, R, clusters, panels...  8.13 us
    all_to_all x1, starting transfers between devices, on_device(): lax.all_to_all(packs, 'clu', split_axis=0, concat_axis=0, tiled=True)  6.32 us
    pallas_call x1, Pallas kernels, on_device(): pl.pallas_call(functools.partial(remote_kernel, (C, S, L, slots, clusters...  5.71 us
    all_to_all x1, starting transfers between devices, on_device(): lax.all_to_all(made[1], 'clu', split_axis=0, concat_axis=0, tiled=True)  5.09 us
    pallas_call x1, Pallas kernels, on_device(): pl.pallas_call(functools.partial(self_kernel, (S, L, R, clusters, panels)...  4.3 us
    ppermute x3, starting transfers between devices, send(): return lax.ppermute(value, names if len(names) > 1 else names[0], perm)  3.23 us
    pallas_call x1, Pallas kernels, on_device(): pl.pallas_call(prepare_kernel, out_shape=[pltpu.VMEM((panels // LANES, cl...  2.48 us
  transfers between devices with their start and end apart: 5, of which 1 were waited for; matrix products, arithmetic and copies ran while one was open for 0% of the time, Pallas kernels for 30%

profile of v19, /device:TPU:0, one launch (start us, length us, event | category | flops | bytes accessed | tf_op | source)
XLA Modules:
  0.0 53.2 jit_solution(9532762535005959865)
XLA Ops:
  0.0 2.0 %packs.1 = (f32[128,128]{1,0:T(8,128)S(1)}, f32[2,512,128]{2,1,0:T(8,128)S(1)}, f32[4,88,128]{2,1,0:T(8,128)}) custom-call(f32[128,128]{1,0:T(8,128)} %charges.1, s32[128,128]{1,0:T(8,128)} %mask.1, f32[128,4,256]{2,1,0:T(4,128)} %geo.1, s32[4,16]{1,0:T(4,128)} %bitcast.14, s32[4,16]{1,0:T(4,128)} %bitcast.21, s32[4,16]{1,0:T(4,128)} %bitcast.22), custom_call_target="tpu_custom_call" | custom-call | bytes 7000000 | tf_op jit(solution)/shard_map/packs/pallas_call | solution.py:596
  2.0 0.0 copy-start.6
  2.0 0.8 %copy-done.6 = f32[2,512,128]{2,1,0:T(8,128)} copy-done((f32[2,512,128]{2,1,0:T(8,128)}, f32[2,512,128]{2,1,0:T(8,128)S(1)}, u32[]{:S(2)}) %copy-start.6) | copy-done | bytes 524312
  2.8 6.3 %all-to-all-start = ((f32[4,88,128]{2,1,0:T(8,128)}), f32[4,88,128]{2,1,0:T(8,128)S(1)}, u32[]{:S(2)}, u32[]{:S(2)}) async-start(f32[4,88,128]{2,1,0:T(8,128)} %get-tuple-element.24), calls=%async_computation | async-start | bytes 360448 | tf_op jit(solution)/shard_map/all_to_all | solution.py:608
  9.2 1.5 %collective-permute-start = (f32[128,128]{1,0:T(8,128)S(1)}, f32[128,128]{1,0:T(8,128)S(1)}, u32[]{:S(2)}, u32[]{:S(2)}) collective-permute-start(f32[128,128]{1,0:T(8,128)S(1)} %get-tuple-element.18.masked.rest_0_), channel_id=1, source_target_pairs={{0,2},{2,0},{1,3},{3,1},{4,6},{6,4},{5,7},{7,5},{8,10},{10,8},{9,1... | collective-permute-start | bytes 196616 | tf_op jit(solution)/shard_map/ppermute | solution.py:567
  10.6 0.0 copy-start.7
  10.6 1.0 %copy-done.7 = f32[2,512,128]{2,1,0:T(8,128)S(1)} copy-done((f32[2,512,128]{2,1,0:T(8,128)S(1)}, f32[2,512,128]{2,1,0:T(8,128)}, u32[]{:S(2)}) %copy-start.7) | copy-done | bytes 524312
  11.7 0.0 copy-start.14
  11.7 2.5 %prepare.1 = (f32[2,3072,128]{2,1,0:T(8,128)S(1)}, f32[2,3072,128]{2,1,0:T(8,128)S(1)}, f32[128,256]{1,0:T(8,128)S(1)}, f32[8,128]{1,0:T(8,128)S(1)}, f32[16,32]{1,0:T(8,128)S(1)}) custom-call(f32[2,512,128]{2,1,0:T(8,128)S(1)} %copy-done.7, f32[128,128]{1,0:T(8,128)S(1)} %get-tuple-element.18.masked.rest_0_, f32[128,32,128]{2,1,0:T(8,128)} %bitcast.10, ...), custom_call_target="tpu_custom_call" | custom-call | bytes 14000000 | tf_op jit(solution)/shard_map/prepare/pallas_call | solution.py:610
  14.2 0.0 copy-start
  14.2 1.6 %copy-done = f32[2,3072,128]{2,1,0:T(8,128)} copy-done((f32[2,3072,128]{2,1,0:T(8,128)}, f32[2,3072,128]{2,1,0:T(8,128)S(1)}, u32[]{:S(2)}) %copy-start) | copy-done | bytes 3145752
  15.8 0.0 copy-start.8
  15.8 0.6 %copy-done.8 = f32[128,256]{1,0:T(8,128)} copy-done((f32[128,256]{1,0:T(8,128)}, f32[128,256]{1,0:T(8,128)S(1)}, u32[]{:S(2)}) %copy-start.8) | copy-done | bytes 131096
  16.5 0.0 collective-permute-done.rest_1_
  16.5 0.0 all-to-all-done.rest_2_
  16.5 5.7 %near_remote.1 = (f32[128,256]{1,0:T(8,128)S(1)}, f32[4,32,128]{2,1,0:T(8,128)}) custom-call(f32[2,3072,128]{2,1,0:T(8,128)S(1)} %get-tuple-element.20.fb, f32[8,128]{1,0:T(8,128)S(1)} %get-tuple-element.22.scale, f32[16,32]{1,0:T(8,128)S(1)} %get-tuple-element.23.up, f32[128,128]{1,0:T(8,128)S(1)} %get-tuple-element.18.masked.rest_0_, ...), custom_call_target="tpu_custom_call" | custom-call | bytes 21000000 | tf_op jit(solution)/shard_map/near_remote/pallas_call | solution.py:632
  22.2 0.0 copy-start.10
  22.2 0.6 %copy-done.10 = f32[128,256]{1,0:T(8,128)} copy-done((f32[128,256]{1,0:T(8,128)}, f32[128,256]{1,0:T(8,128)S(1)}, u32[]{:S(2)}) %copy-start.10) | copy-done | bytes 131096
  22.8 5.1 %all-to-all-start.1 = ((f32[4,32,128]{2,1,0:T(8,128)}), f32[4,32,128]{2,1,0:T(8,128)S(1)}, u32[]{:S(2)}, u32[]{:S(2)}) async-start(f32[4,32,128]{2,1,0:T(8,128)} %get-tuple-element.26), calls=%async_computation.1 | async-start | bytes 131072 | tf_op jit(solution)/shard_map/all_to_all | solution.py:655
  27.9 0.0 copy-done.14
  27.9 0.0 copy-start.1
  27.9 1.9 %copy-done.1 = f32[2,3072,128]{2,1,0:T(8,128)S(1)} copy-done((f32[2,3072,128]{2,1,0:T(8,128)S(1)}, f32[2,3072,128]{2,1,0:T(8,128)}, u32[]{:S(2)}) %copy-start.1) | copy-done | bytes 3145752
  29.8 0.0 copy-start.11
  29.8 0.9 %copy-done.11 = f32[128,256]{1,0:T(8,128)S(1)} copy-done((f32[128,256]{1,0:T(8,128)S(1)}, f32[128,256]{1,0:T(8,128)}, u32[]{:S(2)}) %copy-start.11) | copy-done | bytes 131096
  30.7 0.0 copy-start.12
  30.7 0.0 copy-start.13
  30.7 0.0 copy-start.15
  30.7 8.1 %near_local.1.near = f32[128,256]{1,0:T(8,128)S(1)} custom-call(s32[2,128]{1,0:T(2,128)S(1)} %bitcast.17, s32[2,128]{1,0:T(2,128)S(1)} %bitcast.18, f32[2,3072,128]{2,1,0:T(8,128)S(1)} %copy-done.1, f32[2,3072,128]{2,1,0:T(8,128)S(1)} %get-tuple-element.20.fb, f32[8,128]{1,0:T(8,128)S(1)} %get-tuple-element.22.scale, f32[128,256]{1,0:T(8,128)S(1)} %copy-done.11, ...), custom_call_target="tpu_custom_call" | custom-call | bytes 31500000 | tf_op jit(solution)/shard_map/near_local/pallas_call | solution.py:658
  38.9 0.0 all-to-all-done.1.sums
  38.9 0.0 copy-done.12
  38.9 0.0 copy-done.13
  38.9 0.0 copy-done.15
  38.9 0.0 copy-start.4
  38.9 1.6 %copy-done.4 = f32[16,8,32,32]{3,2,1,0:T(8,128)S(1)} copy-done((f32[16,8,32,32]{3,2,1,0:T(8,128)S(1)}, f32[16,8,32,32]{3,2,1,0:T(8,128)}, u32[]{:S(2)}) %copy-start.4) | copy-done | bytes 524312
  40.5 0.0 copy-start.5
  40.5 1.0 %copy-done.5 = f32[128,32,32]{0,2,1:T(8,128)S(1)} copy-done((f32[128,32,32]{0,2,1:T(8,128)S(1)}, f32[128,32,32]{0,2,1:T(8,128)}, u32[]{:S(2)}) %copy-start.5) | copy-done | bytes 524312
  41.5 1.2 %merge.1 = (f32[160,128]{1,0:T(8,128)S(1)}, f32[160,128]{1,0:T(8,128)S(1)}) custom-call(s32[8,16]{1,0:T(8,128)S(1)} %bitcast.16, s32[4,16]{1,0:T(4,128)S(1)} %bitcast.15, f32[128,256]{1,0:T(8,128)S(1)} %near_local.1.near, f32[16,8,32,32]{3,2,1,0:T(8,128)S(1)} %copy-done.4, f32[32,32,128]{2,1,0:T(8,128)S(1)} %bitcast.13, s32[1,128]{1,0:T(1,128)S(1)} %bitcast.20, ...), custom_call_target="tpu_custom_call" | custom-call | bytes 3500000 | tf_op jit(solution)/shard_map/merge/pallas_call | solution.py:676
  42.7 0.6 %collective-permute-start.1 = (f32[160,128]{1,0:T(8,128)S(1)}, f32[160,128]{1,0:T(8,128)S(1)}, u32[]{:S(2)}, u32[]{:S(2)}) collective-permute-start(f32[160,128]{1,0:T(8,128)S(1)} %get-tuple-element.28), channel_id=1, source_target_pairs={{0,2},{2,0},{1,3},{3,1},{4,6},{6,4},{5,7},{7,5},{8,10},{10,8},{9,1... | collective-permute-start | bytes 245768 | tf_op jit(solution)/shard_map/ppermute | solution.py:567
  43.3 1.9 %copy-done.2 = f32[2,3072,128]{2,1,0:T(8,128)S(1)} copy-done((f32[2,3072,128]{2,1,0:T(8,128)S(1)}, f32[2,3072,128]{2,1,0:T(8,128)}, u32[]{:S(2)}) %copy-start.2) | copy-done | bytes 3145752
  45.2 0.9 %copy-done.9 = f32[128,256]{1,0:T(8,128)S(1)} copy-done((f32[128,256]{1,0:T(8,128)S(1)}, f32[128,256]{1,0:T(8,128)}, u32[]{:S(2)}) %copy-start.9) | copy-done | bytes 131096
  46.1 4.3 %near_self.1 = f32[160,128]{1,0:T(8,128)S(1)} custom-call(f32[2,3072,128]{2,1,0:T(8,128)S(1)} %copy-done.2, f32[2,3072,128]{2,1,0:T(8,128)S(1)} %get-tuple-element.20.fb, f32[128,256]{1,0:T(8,128)S(1)} %copy-done.9, f32[8,128]{1,0:T(8,128)S(1)} %get-tuple-element.22.scale, f32[160,128]{1,0:T(8,128)S(1)} %get-tuple-element.27.part, ...), custom_call_target="tpu_custom_call" | custom-call | bytes 14000000 | tf_op jit(solution)/shard_map/near_self/pallas_call | solution.py:688
  50.4 0.0 collective-permute-done.1
  50.5 1.1 %collective-permute-start.2 = (f32[160,128]{1,0:T(8,128)S(1)}, f32[160,128]{1,0:T(8,128)S(1)}, u32[]{:S(2)}, u32[]{:S(2)}) collective-permute-start(f32[160,128]{1,0:T(8,128)S(1)} %add.6.near), channel_id=1, source_target_pairs={{0,1},{1,0},{2,3},{3,2},{4,5},{5,4},{6,7},{7,6},{8,9},{9,8},{10,11... | collective-permute-start | bytes 245768 | tf_op jit(solution)/shard_map/ppermute | solution.py:567
  51.6 0.0 copy-done.3
  51.6 0.8 %far_down.1 = f32[128,128]{1,0:T(8,128)S(1)} custom-call(f32[128,32,128]{2,1,0:T(8,128)S(1)} %bitcast.11, f32[160,128]{1,0:T(8,128)S(1)} %add.6.near), custom_call_target="tpu_custom_call" | custom-call | bytes 3500000 | tf_op jit(solution)/shard_map/far_down/pallas_call | solution.py:709
  52.4 0.1 collective-permute-done.2
  52.5 0.0 copy-done.16
  52.5 0.6 %fusion = f32[128,128]{1,0:T(8,128)} fusion(f32[128,128]{1,0:T(8,128)S(1)} %far_down.1, f32[160,128]{1,0:T(8,128)S(1)} %collective-permute-done.2, s32[128,128]{1,0:T(8,128)S(1)} %copy-done.16), kind=kLoop, calls=%fused_computation.1 | loop fusion | flops 49152 | bytes 262144 | tf_op jit(solution)/shard_map/mul | solution.py:720
  (5 shorter events, 0.0 us)
Async XLA Ops:
  2.0 0.8 %copy-start.6 = (f32[2,512,128]{2,1,0:T(8,128)}, f32[2,512,128]{2,1,0:T(8,128)S(1)}, u32[]{:S(2)}) copy-start(f32[2,512,128]{2,1,0:T(8,128)S(1)} %get-tuple-element.17.geo) | copy-start | bytes 1572868
  2.8 13.6 %all-to-all-start = ((f32[4,88,128]{2,1,0:T(8,128)}), f32[4,88,128]{2,1,0:T(8,128)S(1)}, u32[]{:S(2)}, u32[]{:S(2)}) async-start(f32[4,88,128]{2,1,0:T(8,128)} %get-tuple-element.24), calls=%async_computation | async-start | bytes 360448 | tf_op jit(solution)/shard_map/all_to_all | solution.py:608
  9.2 7.3 %collective-permute-start = (f32[128,128]{1,0:T(8,128)S(1)}, f32[128,128]{1,0:T(8,128)S(1)}, u32[]{:S(2)}, u32[]{:S(2)}) collective-permute-start(f32[128,128]{1,0:T(8,128)S(1)} %get-tuple-element.18.masked.rest_0_), channel_id=1, source_target_pairs={{0,2},{2,0},{1,3},{3,1},{4,6},{6,4},{5,7},{7,5},{8,10},{10,8},{9,1... | collective-permute-start | bytes 196616 | tf_op jit(solution)/shard_map/ppermute | solution.py:567
  10.6 1.0 %copy-start.7 = (f32[2,512,128]{2,1,0:T(8,128)S(1)}, f32[2,512,128]{2,1,0:T(8,128)}, u32[]{:S(2)}) copy-start(f32[2,512,128]{2,1,0:T(8,128)} %copy-done.6) | copy-start | bytes 1572868
  11.7 16.2 %copy-start.14 = (s32[1,128,2]{1,2,0:T(2,128)S(1)}, s32[1,128,2]{1,2,0:T(2,128)}, u32[]{:S(2)}) copy-start(s32[1,128,2]{1,2,0:T(2,128)} %param.18) | copy-start | bytes 3076
  14.2 1.6 %copy-start = (f32[2,3072,128]{2,1,0:T(8,128)}, f32[2,3072,128]{2,1,0:T(8,128)S(1)}, u32[]{:S(2)}) copy-start(f32[2,3072,128]{2,1,0:T(8,128)S(1)} %get-tuple-element.19.fa) | copy-start | bytes 9437188
  15.8 0.6 %copy-start.8 = (f32[128,256]{1,0:T(8,128)}, f32[128,256]{1,0:T(8,128)S(1)}, u32[]{:S(2)}) copy-start(f32[128,256]{1,0:T(8,128)S(1)} %get-tuple-element.21.diags) | copy-start | bytes 393220
  22.2 0.6 %copy-start.10 = (f32[128,256]{1,0:T(8,128)}, f32[128,256]{1,0:T(8,128)S(1)}, u32[]{:S(2)}) copy-start(f32[128,256]{1,0:T(8,128)S(1)} %get-tuple-element.25.acc_in) | copy-start | bytes 393220
  22.8 16.0 %all-to-all-start.1 = ((f32[4,32,128]{2,1,0:T(8,128)}), f32[4,32,128]{2,1,0:T(8,128)S(1)}, u32[]{:S(2)}, u32[]{:S(2)}) async-start(f32[4,32,128]{2,1,0:T(8,128)} %get-tuple-element.26), calls=%async_computation.1 | async-start | bytes 131072 | tf_op jit(solution)/shard_map/all_to_all | solution.py:655
  27.9 1.9 %copy-start.1 = (f32[2,3072,128]{2,1,0:T(8,128)S(1)}, f32[2,3072,128]{2,1,0:T(8,128)}, u32[]{:S(2)}) copy-start(f32[2,3072,128]{2,1,0:T(8,128)} %copy-done) | copy-start | bytes 9437188
  29.8 0.9 %copy-start.11 = (f32[128,256]{1,0:T(8,128)S(1)}, f32[128,256]{1,0:T(8,128)}, u32[]{:S(2)}) copy-start(f32[128,256]{1,0:T(8,128)} %copy-done.10) | copy-start | bytes 393220
  30.7 8.2 %copy-start.12 = (s32[1,4,16]{2,1,0:T(4,128)S(1)}, s32[1,4,16]{2,1,0:T(4,128)}, u32[]{:S(2)}) copy-start(s32[1,4,16]{2,1,0:T(4,128)} %param.16) | copy-start | bytes 772
  30.7 8.2 %copy-start.13 = (s32[16,8]{0,1:T(8,128)S(1)}, s32[16,8]{0,1:T(8,128)}, u32[]{:S(2)}) copy-start(s32[16,8]{0,1:T(8,128)} %param.22) | copy-start | bytes 1540
  30.7 8.2 %copy-start.15 = (s32[128]{0:T(128)S(1)}, s32[128]{0:T(128)}, u32[]{:S(2)}) copy-start(s32[128]{0:T(128)} %param.21) | copy-start | bytes 1540
  38.9 1.6 %copy-start.4 = (f32[16,8,32,32]{3,2,1,0:T(8,128)S(1)}, f32[16,8,32,32]{3,2,1,0:T(8,128)}, u32[]{:S(2)}) copy-start(f32[16,8,32,32]{3,2,1,0:T(8,128)} %coupling.1) | copy-start | bytes 1572868
  40.5 1.0 %copy-start.5 = (f32[128,32,32]{0,2,1:T(8,128)S(1)}, f32[128,32,32]{0,2,1:T(8,128)}, u32[]{:S(2)}) copy-start(f32[128,32,32]{0,2,1:T(8,128)} %param.20) | copy-start | bytes 1572868
  42.7 7.7 %collective-permute-start.1 = (f32[160,128]{1,0:T(8,128)S(1)}, f32[160,128]{1,0:T(8,128)S(1)}, u32[]{:S(2)}, u32[]{:S(2)}) collective-permute-start(f32[160,128]{1,0:T(8,128)S(1)} %get-tuple-element.28), channel_id=1, source_target_pairs={{0,2},{2,0},{1,3},{3,1},{4,6},{6,4},{5,7},{7,5},{8,10},{10,8},{9,1... | collective-permute-start | bytes 245768 | tf_op jit(solution)/shard_map/ppermute | solution.py:567
  43.3 1.9 %copy-start.2 = (f32[2,3072,128]{2,1,0:T(8,128)S(1)}, f32[2,3072,128]{2,1,0:T(8,128)}, u32[]{:S(2)}) copy-start(f32[2,3072,128]{2,1,0:T(8,128)} %copy-done) | copy-start | bytes 9437188
  45.2 0.9 %copy-start.9 = (f32[128,256]{1,0:T(8,128)S(1)}, f32[128,256]{1,0:T(8,128)}, u32[]{:S(2)}) copy-start(f32[128,256]{1,0:T(8,128)} %copy-done.8) | copy-start | bytes 393220
  46.1 5.5 %copy-start.3 = (f32[128,128,32]{1,2,0:T(8,128)S(1)}, f32[128,128,32]{1,2,0:T(8,128)}, u32[]{:S(2)}) copy-start(f32[128,128,32]{1,2,0:T(8,128)} %param.19) | copy-start | bytes 6291460
  46.1 6.4 %copy-start.16 = (s32[128,128]{1,0:T(8,128)S(1)}, s32[128,128]{1,0:T(8,128)}, u32[]{:S(2)}) copy-start(s32[128,128]{1,0:T(8,128)} %mask.1) | copy-start | bytes 196612
  50.5 2.1 %collective-permute-start.2 = (f32[160,128]{1,0:T(8,128)S(1)}, f32[160,128]{1,0:T(8,128)S(1)}, u32[]{:S(2)}, u32[]{:S(2)}) collective-permute-start(f32[160,128]{1,0:T(8,128)S(1)} %add.6.near), channel_id=1, source_target_pairs={{0,1},{1,0},{2,3},{3,2},{4,5},{5,4},{6,7},{7,6},{8,9},{9,8},{10,11... | collective-permute-start | bytes 245768 | tf_op jit(solution)/shard_map/ppermute | solution.py:567

commit v20 on v18

--- a/solution.py
+++ b/solution.py
@@ -224,16 +224,16 @@
     return jnp.concatenate([jnp.sum(b, axis=0, keepdims=True) for b in back], axis=1)
 
 
-def pipeline(total, begin, finish, table, ring, parts):
-    size = len(ring)
-    ahead = min(2, size - 1)
+def pipeline(total, begin, finish, table, size, ring, parts):
+    ring = ring[: min(len(ring), size)]
+    ahead = min(2, len(ring) - 1)
     group = min(2, size)
 
     def body(i, carry):
         indices = []
         for k in range(size):
-            begin(i * size + k + ahead, ring[(k + ahead) % size])
-            indices.append(finish(i * size + k, ring[k], parts[k % len(parts)]))
+            begin(i * size + k + ahead, ring[(k + ahead) % len(ring)])
+            indices.append(finish(i * size + k, ring[k % len(ring)], parts[k % len(parts)]))
             if len(indices) == group:
                 done = [parts[(k - n) % len(parts)] for n in reversed(range(group))]
                 add_columns(table, done, indices)
@@ -245,8 +245,8 @@
     lax.fori_loop(0, (total + size - 1) // size, body, 0)
 
 
-def ring_size(total):
-    return next(size for size in (16, 8, 4, 2, 1) if total % size == 0)
+def body_size(total, most):
+    return next(size for size in (32, 16, 8, 4, 2, 1) if size <= most and total % size == 0)
 
 
 def assemble(sub, S, L, q, pieces):
@@ -289,7 +289,8 @@
         pl.when(sub == s)(functools.partial(fill, s))
 
 
-def remote_kernel(sizes, fb, scale, up, *rest):
+def remote_kernel(sizes, fb, scale, up, before, *rest):
+    del before
     C, S, L, slots, clusters, panels = sizes
     pieces = rest[:S]
     packs = rest[S : S + C - 1]
@@ -338,7 +339,7 @@
         acc[pl.ds(source, 1), :] += jnp.where(ok, back, 0.0)
         return jnp.where(ok, slot, -1)
 
-    pipeline(found, begin, finish, fwdt, work[:8], work[8:])
+    pipeline(found, begin, finish, fwdt, 8, work[:4], work[4:])
     acc_out[...] = acc[...] * inv
     fwd = (fwdt[...] * inv).T
     rank = up.shape[1]
@@ -387,7 +388,7 @@
     pieces = rest[:S]
     acc_out = rest[S]
     q, acc, pair_sums, *work = rest[S + 1 :]
-    ring, sums = work[:16], work[16:]
+    ring, sums = work[:8], work[8:]
     sub = lax.axis_index("sub")
     assemble(sub, S, L, q, pieces)
     acc[...] = jnp.zeros_like(acc)
@@ -407,23 +408,19 @@
         )
         return start + i
 
-    pipeline(count, begin, finish, pair_sums, ring[: ring_size(count)], sums)
+    pipeline(count, begin, finish, pair_sums, body_size(count, 32), ring, sums)
     width = pair_rows.shape[1]
     total = acc[...] + select_rows(pair_rows[0:1, :], pair_sums[...].T[:width, :], clusters)
     acc_out[...] = acc_in[...] + total * scale[0:1, 0:1]
 
 
-def self_shares(clusters, S, R):
-    base = clusters // R
-    unit = base // 4 if R > 1 else 0
-    return base, unit
-
-
-def self_kernel(sizes, fa, fb, diags, scale, part, *rest):
+def self_kernel(sizes, early, fa, fb, diags, scale, *rest):
     S, L, R, clusters, panels = sizes
+    if not early:
+        part, before, *rest = rest
     pieces = rest[:S]
     out, q, fs, spots, self_sums, *work = rest[S:]
-    ring, sums = work[:16], work[16:]
+    ring, sums = work[:8], work[8:]
     sub, rep = lax.axis_index("sub"), lax.axis_index("rep")
     self_sums[...] = jnp.zeros_like(self_sums)
     blocks = L == LANES
@@ -443,9 +440,17 @@
 
     for s in range(S):
         pl.when(sub == s)(functools.partial(place, s))
-    base, unit = self_shares(clusters, S, R)
-    first = rep * base - jnp.where(rep > 0, unit, 0)
-    share = base + jnp.where(rep == R - 1, unit, 0) - jnp.where(rep == 0, unit, 0)
+    base = clusters // R
+    unit = base // 4
+    first = rep * base
+    share = base
+    if R > 1:
+        first = first - jnp.where(rep > 0, unit, 0)
+        share = share + jnp.where(rep == R - 1, unit, 0) - jnp.where(rep == 0, unit, 0)
+    if early:
+        share = unit
+    else:
+        first, share = first + unit, share - unit
 
     def begin(i, dist):
         c = first + jnp.minimum(i, share - 1)
@@ -473,9 +478,13 @@
         staged(spans_of(L), root, partial)
         return c
 
-    pipeline(share, begin, finish, self_sums, ring[: ring_size(unit or base)], sums)
-    out[...] = part[...]
-    out[:clusters, :] = part[:clusters, :] + self_sums[...].T * scale[0:1, 0:1]
+    pipeline(share, begin, finish, self_sums, body_size(unit, 16), ring, sums)
+    total = self_sums[...].T * scale[0:1, 0:1]
+    if early:
+        out[...] = total
+    else:
+        out[...] = part[...]
+        out[:clusters, :] = (part[:clusters, :] + before[...]) + total
 
 
 def merge_kernel(sizes, far_list, targets, near, coupling, transfer, parent, up, *rest):
@@ -636,11 +645,32 @@
     )(*near_by(geo, masked), *far_off(basis_t, transfer_t, parent))
     *tables, diags, scale = features
 
+    def own_tiles(early, height, *added):
+        return pl.pallas_call(
+            functools.partial(self_kernel, (S, L, R, clusters, panels), early),
+            out_shape=pltpu.VMEM((height, L), F32),
+            in_specs=[vmem()] * (4 + len(added) + S),
+            out_specs=vmem(),
+            scratch_shapes=[
+                pltpu.VMEM((clusters, panels), F32),
+                pltpu.VMEM((1, 8 if L == LANES else clusters * ROWS, L), F32),
+                pltpu.VMEM((clusters, L), F32),
+                pltpu.VMEM((L, clusters), F32),
+            ]
+            + [pltpu.VMEM((L, panels), F32)] * 8
+            + [pltpu.VMEM((L, 2 * LANES), BF16)] * 4,
+            compiler_params=limit(24),
+            cost_estimate=about(2 if early else 4),
+            name="near_self_early" if early else "near_self",
+        )(*near_by(*tables, diags, scale, *added, *pieces))
+
+    before = own_tiles(True, clusters)
+
     made = pl.pallas_call(
         functools.partial(remote_kernel, (C, S, L, slots, clusters, panels)),
         out_shape=[pltpu.VMEM((clusters, panels), F32)]
         + [pltpu.VMEM((slots + par_dev, L), F32)] * (C - 1),
-        in_specs=[vmem()] * (3 + S + C - 1),
+        in_specs=[vmem()] * (4 + S + C - 1),
         out_specs=[vmem()] * C,
         scratch_shapes=[
             pltpu.VMEM((clusters, panels), F32),
@@ -652,12 +682,12 @@
             pltpu.SMEM((C - 1, 8, L), F32),
             pltpu.SemaphoreType.DMA((C - 1,)),
         ]
-        + [pltpu.VMEM((L, panels), F32)] * 8
+        + [pltpu.VMEM((L, panels), F32)] * 4
         + [pltpu.VMEM((L, 2 * LANES), BF16)] * 4,
         compiler_params=limit(24),
         cost_estimate=about(6),
         name="near_remote",
-    )(*near_by(tables[1], scale, up, *pieces, *packs))
+    )(*near_by(tables[1], scale, up, before, *pieces, *packs))
     acc, sums = made[0], [send(made[d], (("clu", C - d),)) for d in range(1, C)]
 
     wide = whole(local_pairs.shape[1])
@@ -671,7 +701,7 @@
             pltpu.VMEM((clusters, panels), F32),
             pltpu.VMEM((panels, wide), F32),
         ]
-        + [pltpu.VMEM((panels, panels), F32)] * 16
+        + [pltpu.VMEM((panels, panels), F32)] * 8
         + [pltpu.VMEM((panels, 2 * LANES), BF16)] * 4,
         compiler_params=limit(24),
         cost_estimate=about(9),
@@ -691,23 +721,7 @@
     )(far_list.T, *near_by(targets, near, coupling, transfer_t, parent, up, *sums))
     others = [send(parts[d], (("sub", d),)) for d in range(1, S)]
 
-    near = pl.pallas_call(
-        functools.partial(self_kernel, (S, L, R, clusters, panels)),
-        out_shape=pltpu.VMEM((height, L), F32),
-        in_specs=[vmem()] * (5 + S),
-        out_specs=vmem(),
-        scratch_shapes=[
-            pltpu.VMEM((clusters, panels), F32),
-            pltpu.VMEM((1, 8 if L == LANES else clusters * ROWS, L), F32),
-            pltpu.VMEM((clusters, L), F32),
-            pltpu.VMEM((L, clusters), F32),
-        ]
-        + [pltpu.VMEM((L, panels), F32)] * 16
-        + [pltpu.VMEM((L, 2 * LANES), BF16)] * 4,
-        compiler_params=limit(24),
-        cost_estimate=about(4),
-        name="near_self",
-    )(*near_by(*tables, diags, scale, parts[0], *pieces))
+    near = own_tiles(False, height, parts[0], before)
     for other in others:
         near = near + other
     others = [send(near, (("rep", e),)) for e in range(1, R)]

time: 39.2 us -> 38.5 us (0.982)
  starting transfers between devices: 13 us -> 11.8 us
  waiting for transfers between devices: 0.68 us -> 1.41 us
    ppermute x9, starting transfers between devices: 13 us -> 11.8 us  [send(): return lax.ppermute(value, names if len(names) > 1 else names[0], perm)]
    ppermute x9, waiting for transfers between devices: 0.68 us -> 1.41 us  [send(): return lax.ppermute(value, names if len(names) > 1 else names[0], perm)]
    pallas_call x1 -> x2, Pallas kernels: 4.3 us -> 4.37 us  [own_tiles(): pl.pallas_call(functools.partial(self_kernel, (S, L, R, clusters, panels)...]
where the time goes in v20:
time: 38.5 us; the launch traced here: 38.2 us
  Pallas kernels  24.1 us (63%)
  starting transfers between devices  11.8 us (31%)
  waiting for transfers between devices  1.41 us (4%)
  other arithmetic  0.65 us (2%)
    ppermute x9, starting transfers between devices, send(): return lax.ppermute(value, names if len(names) > 1 else names[0], perm)  11.8 us
    pallas_call x1, Pallas kernels, on_device(): pl.pallas_call(functools.partial(local_kernel, (S, L, R, clusters, panels...  8.13 us
    pallas_call x1, Pallas kernels, on_device(): pl.pallas_call(functools.partial(remote_kernel, (C, S, L, slots, clusters...  5.71 us
    pallas_call x2, Pallas kernels, own_tiles(): pl.pallas_call(functools.partial(self_kernel, (S, L, R, clusters, panels)...  4.37 us
    pallas_call x1, Pallas kernels, on_device(): pl.pallas_call(prepare_kernel, out_shape=[pltpu.VMEM((panels // LANES, cl...  2.47 us
    ppermute x9, waiting for transfers between devices, send(): return lax.ppermute(value, names if len(names) > 1 else names[0], perm)  1.41 us
    pallas_call x1, Pallas kernels, on_device(): pl.pallas_call(functools.partial(pack_kernel, (C, S, L, slots)), out_shap...  1.37 us
    pallas_call x1, Pallas kernels, on_device(): pl.pallas_call(functools.partial(merge_kernel, (C, S, L, slots, clusters)...  1.26 us
  transfers between devices with their start and end apart: 9, of which 2 were waited for; matrix products, arithmetic and copies ran while one was open for 0% of the time, Pallas kernels for 41%

profile of v20, /device:TPU:0, one launch (start us, length us, event | category | flops | bytes accessed | tf_op | source)
XLA Modules:
  0.0 38.2 jit_solution(16027772729029307872)
XLA Ops:
  0.0 1.4 %packs.1 = (f32[128,128]{1,0:T(8,128)S(1)}, f32[2,512,128]{2,1,0:T(8,128)S(1)}, f32[88,128]{1,0:T(8,128)S(1)}, f32[88,128]{1,0:T(8,128)S(1)}, f32[88,128]{1,0:T(8,128)S(1)}) custom-call(f32[128,128]{1,0:T(8,128)} %charges.1, s32[128,128]{1,0:T(8,128)} %mask.1, f32[128,4,256]{2,1,0:T(4,128)} %geo.1, s32[4,16]{1,0:T(4,128)} %bitcast.14, s32[4,16]{1,0:T(4,128)} %bitcast.21, ...), custom_call_target="tpu_custom_call" | custom-call | bytes 7000000 | tf_op jit(solution)/shard_map/packs/pallas_call | solution.py:612
  1.4 3.0 %collective-permute-start = (f32[128,128]{1,0:T(8,128)S(1)}, f32[128,128]{1,0:T(8,128)S(1)}, u32[]{:S(2)}, u32[]{:S(2)}) collective-permute-start(f32[128,128]{1,0:T(8,128)S(1)} %get-tuple-element.22.masked.rest_0_.rest_2_), channel_id=1, source_target_pairs={{0,2},{2,0},{1,3},{3,1},{4,6},{6,4},{5,7},{7,5},{8,10},{10,8},{9,1... | collective-permute-start | bytes 196616 | tf_op jit(solution)/shard_map/ppermute | solution.py:583
  4.4 1.6 %collective-permute-start.1 = (f32[88,128]{1,0:T(8,128)S(1)}, f32[88,128]{1,0:T(8,128)S(1)}, u32[]{:S(2)}, u32[]{:S(2)}) collective-permute-start(f32[88,128]{1,0:T(8,128)S(1)} %get-tuple-element.28), channel_id=1, source_target_pairs={{0,4},{4,8},{8,12},{12,0},{1,5},{5,9},{9,13},{13,1},{2,6},{6,10},{... | collective-permute-start | bytes 135176 | tf_op jit(solution)/shard_map/ppermute | solution.py:583
  6.0 2.6 %collective-permute-start.2 = (f32[88,128]{1,0:T(8,128)S(1)}, f32[88,128]{1,0:T(8,128)S(1)}, u32[]{:S(2)}, u32[]{:S(2)}) collective-permute-start(f32[88,128]{1,0:T(8,128)S(1)} %get-tuple-element.29), channel_id=1, source_target_pairs={{0,8},{4,12},{8,0},{12,4},{1,9},{5,13},{9,1},{13,5},{2,10},{6,14},... | collective-permute-start | bytes 135176 | tf_op jit(solution)/shard_map/ppermute | solution.py:583
  8.6 1.3 %collective-permute-start.3 = (f32[88,128]{1,0:T(8,128)S(1)}, f32[88,128]{1,0:T(8,128)S(1)}, u32[]{:S(2)}, u32[]{:S(2)}) collective-permute-start(f32[88,128]{1,0:T(8,128)S(1)} %get-tuple-element.30), channel_id=1, source_target_pairs={{0,12},{4,0},{8,4},{12,8},{1,13},{5,1},{9,5},{13,9},{2,14},{6,2},{... | collective-permute-start | bytes 135176 | tf_op jit(solution)/shard_map/ppermute | solution.py:583
  9.9 2.5 %prepare.1 = (f32[2,3072,128]{2,1,0:T(8,128)S(1)}, f32[2,3072,128]{2,1,0:T(8,128)S(1)}, f32[128,256]{1,0:T(8,128)S(1)}, f32[8,128]{1,0:T(8,128)S(1)}, f32[16,32]{1,0:T(8,128)S(1)}) custom-call(f32[2,512,128]{2,1,0:T(8,128)S(1)} %get-tuple-element.21.geo, f32[128,128]{1,0:T(8,128)S(1)} %get-tuple-element.22.masked.rest_0_.rest_2_, f32[128,32,128]{2,1,0:T(8,128)} %bitcast.10, ...), custom_call_target="tpu_custom_call" | custom-call | bytes 14000000 | tf_op jit(solution)/shard_map/prepare/pallas_call | solution.py:626
  12.4 0.0 collective-permute-done.rest_1_.rest_3_
  12.4 1.4 %near_self_early.1.before.rest_1_ = f32[128,128]{1,0:T(8,128)S(1)} custom-call(f32[2,3072,128]{2,1,0:T(8,128)S(1)} %get-tuple-element.23.fa, f32[2,3072,128]{2,1,0:T(8,128)S(1)} %get-tuple-element.24.fb, f32[128,256]{1,0:T(8,128)S(1)} %get-tuple-element.25.diags, f32[8,128]{1,0:T(8,128)S(1)} %get-tuple-element.26.scale, ...), custom_call_target="tpu_custom_call" | custom-call | bytes 7000000 | tf_op jit(solution)/shard_map/near_self_early/pallas_call | solution.py:649
  13.8 0.0 copy-start.5
  13.8 0.0 collective-permute-done.1.rest_2_
  13.8 0.0 collective-permute-done.2.rest_3_
  13.9 0.0 collective-permute-done.3.rest_4_
  13.9 5.7 %near_remote.1 = (f32[128,256]{1,0:T(8,128)S(1)}, f32[32,128]{1,0:T(8,128)S(1)}, f32[32,128]{1,0:T(8,128)S(1)}, f32[32,128]{1,0:T(8,128)S(1)}) custom-call(f32[2,3072,128]{2,1,0:T(8,128)S(1)} %get-tuple-element.24.fb, f32[8,128]{1,0:T(8,128)S(1)} %get-tuple-element.26.scale, f32[16,32]{1,0:T(8,128)S(1)} %get-tuple-element.27.up, ...), custom_call_target="tpu_custom_call" | custom-call | bytes 21000000 | tf_op jit(solution)/shard_map/near_remote/pallas_call | solution.py:669
  19.6 1.9 %collective-permute-start.4 = (f32[32,128]{1,0:T(8,128)S(1)}, f32[32,128]{1,0:T(8,128)S(1)}, u32[]{:S(2)}, u32[]{:S(2)}) collective-permute-start(f32[32,128]{1,0:T(8,128)S(1)} %get-tuple-element.32), channel_id=1, source_target_pairs={{0,12},{4,0},{8,4},{12,8},{1,13},{5,1},{9,5},{13,9},{2,14},{6,2},{... | collective-permute-start | bytes 49160 | tf_op jit(solution)/shard_map/ppermute | solution.py:583
  21.5 0.2 collective-permute-start.5
  21.8 0.4 %collective-permute-start.6 = (f32[32,128]{1,0:T(8,128)S(1)}, f32[32,128]{1,0:T(8,128)S(1)}, u32[]{:S(2)}, u32[]{:S(2)}) collective-permute-start(f32[32,128]{1,0:T(8,128)S(1)} %get-tuple-element.34), channel_id=1, source_target_pairs={{0,4},{4,8},{8,12},{12,0},{1,5},{5,9},{9,13},{13,1},{2,6},{6,10},{... | collective-permute-start | bytes 49160 | tf_op jit(solution)/shard_map/ppermute | solution.py:583
  22.2 0.0 copy-done.5
  22.2 0.0 copy-start.1
  22.2 0.0 copy-start.2
  22.2 0.0 copy-start.3
  22.2 0.0 copy-start.4
  22.2 0.0 copy-start.6
  22.2 8.1 %near_local.1.near = f32[128,256]{1,0:T(8,128)S(1)} custom-call(s32[2,128]{1,0:T(2,128)S(1)} %bitcast.17, s32[2,128]{1,0:T(2,128)S(1)} %bitcast.18, f32[2,3072,128]{2,1,0:T(8,128)S(1)} %get-tuple-element.23.fa, f32[2,3072,128]{2,1,0:T(8,128)S(1)} %get-tuple-element.24.fb, f32[8,128]{1,0:T(8,128)S(1)} %get-tuple-element.26.scale, ...), custom_call_target="tpu_custom_call" | custom-call | bytes 31500000 | tf_op jit(solution)/shard_map/near_local/pallas_call | solution.py:694
  30.3 0.0 collective-permute-done.4.rest_0_
  30.4 0.0 collective-permute-done.5.rest_1_
  30.4 0.0 collective-permute-done.6.rest_2_
  30.4 0.0 copy-done.1
  30.4 0.0 copy-done.2
  30.4 0.0 copy-done.3
  30.4 0.0 copy-done.4
  30.4 0.0 copy-done.6
  30.4 1.3 %merge.1 = (f32[160,128]{1,0:T(8,128)S(1)}, f32[160,128]{1,0:T(8,128)S(1)}) custom-call(s32[8,16]{1,0:T(8,128)S(1)} %bitcast.16, s32[4,16]{1,0:T(4,128)S(1)} %bitcast.15, f32[128,256]{1,0:T(8,128)S(1)} %near_local.1.near, f32[16,8,32,32]{3,2,1,0:T(8,128)S(1)} %copy-done.1, f32[32,32,128]{2,1,0:T(8,128)S(1)} %bitcast.13, s32[1,128]{1,0:T(1,128)S(1)} %bitcast.20, ...), custom_call_target="tpu_custom_call" | custom-call | bytes 3500000 | tf_op jit(solution)/shard_map/merge/pallas_call | solution.py:712
  31.7 0.6 %collective-permute-start.7 = (f32[160,128]{1,0:T(8,128)S(1)}, f32[160,128]{1,0:T(8,128)S(1)}, u32[]{:S(2)}, u32[]{:S(2)}) collective-permute-start(f32[160,128]{1,0:T(8,128)S(1)} %get-tuple-element.36), channel_id=1, source_target_pairs={{0,2},{2,0},{1,3},{3,1},{4,6},{6,4},{5,7},{7,5},{8,10},{10,8},{9,1... | collective-permute-start | bytes 245768 | tf_op jit(solution)/shard_map/ppermute | solution.py:583
  32.3 0.0 copy-start
  32.3 0.0 copy-start.7
  32.3 2.9 %near_self.1 = f32[160,128]{1,0:T(8,128)S(1)} custom-call(f32[2,3072,128]{2,1,0:T(8,128)S(1)} %get-tuple-element.23.fa, f32[2,3072,128]{2,1,0:T(8,128)S(1)} %get-tuple-element.24.fb, f32[128,256]{1,0:T(8,128)S(1)} %get-tuple-element.25.diags, f32[8,128]{1,0:T(8,128)S(1)} %get-tuple-element.26.scale, f32[160,128]{1,0:T(8,128)S(1)} %get-tuple-element.35.rest_0_, ...), custom_call_target="tpu_custom_call" | custom-call | bytes 14000000 | tf_op jit(solution)/shard_map/near_self/pallas_call | solution.py:649
  35.2 1.0 %collective-permute-done.7 = f32[160,128]{1,0:T(8,128)S(1)} collective-permute-done((f32[160,128]{1,0:T(8,128)S(1)}, f32[160,128]{1,0:T(8,128)S(1)}, u32[]{:S(2)}, u32[]{:S(2)}) %collective-permute-start.7) | collective-permute-done | bytes 81952 | tf_op jit(solution)/shard_map/ppermute | solution.py:583
  36.2 0.1 collective-permute-start.8
  36.3 0.0 copy-done
  36.3 0.8 %far_down.1 = f32[128,128]{1,0:T(8,128)S(1)} custom-call(f32[128,32,128]{2,1,0:T(8,128)S(1)} %bitcast.11, f32[160,128]{1,0:T(8,128)S(1)} %add.6.near), custom_call_target="tpu_custom_call" | custom-call | bytes 3500000 | tf_op jit(solution)/shard_map/far_down/pallas_call | solution.py:729
  37.1 0.4 %collective-permute-done.8 = f32[160,128]{1,0:T(8,128)S(1)} collective-permute-done((f32[160,128]{1,0:T(8,128)S(1)}, f32[160,128]{1,0:T(8,128)S(1)}, u32[]{:S(2)}, u32[]{:S(2)}) %collective-permute-start.8) | collective-permute-done | bytes 81952 | tf_op jit(solution)/shard_map/ppermute | solution.py:583
  37.6 0.0 copy-done.7
  37.6 0.6 %fusion = f32[128,128]{1,0:T(8,128)} fusion(f32[128,128]{1,0:T(8,128)S(1)} %far_down.1, f32[160,128]{1,0:T(8,128)S(1)} %collective-permute-done.8, s32[128,128]{1,0:T(8,128)S(1)} %copy-done.7), kind=kLoop, calls=%fused_computation.1 | loop fusion | flops 49152 | bytes 262144 | tf_op jit(solution)/shard_map/mul | solution.py:740
  (1 shorter events, 0.0 us)
Async XLA Ops:
  1.4 11.0 %collective-permute-start = (f32[128,128]{1,0:T(8,128)S(1)}, f32[128,128]{1,0:T(8,128)S(1)}, u32[]{:S(2)}, u32[]{:S(2)}) collective-permute-start(f32[128,128]{1,0:T(8,128)S(1)} %get-tuple-element.22.masked.rest_0_.rest_2_), channel_id=1, source_target_pairs={{0,2},{2,0},{1,3},{3,1},{4,6},{6,4},{5,7},{7,5},{8,10},{10,8},{9,1... | collective-permute-start | bytes 196616 | tf_op jit(solution)/shard_map/ppermute | solution.py:583
  4.4 9.4 %collective-permute-start.1 = (f32[88,128]{1,0:T(8,128)S(1)}, f32[88,128]{1,0:T(8,128)S(1)}, u32[]{:S(2)}, u32[]{:S(2)}) collective-permute-start(f32[88,128]{1,0:T(8,128)S(1)} %get-tuple-element.28), channel_id=1, source_target_pairs={{0,4},{4,8},{8,12},{12,0},{1,5},{5,9},{9,13},{13,1},{2,6},{6,10},{... | collective-permute-start | bytes 135176 | tf_op jit(solution)/shard_map/ppermute | solution.py:583
  6.0 7.9 %collective-permute-start.2 = (f32[88,128]{1,0:T(8,128)S(1)}, f32[88,128]{1,0:T(8,128)S(1)}, u32[]{:S(2)}, u32[]{:S(2)}) collective-permute-start(f32[88,128]{1,0:T(8,128)S(1)} %get-tuple-element.29), channel_id=1, source_target_pairs={{0,8},{4,12},{8,0},{12,4},{1,9},{5,13},{9,1},{13,5},{2,10},{6,14},... | collective-permute-start | bytes 135176 | tf_op jit(solution)/shard_map/ppermute | solution.py:583
  8.6 5.3 %collective-permute-start.3 = (f32[88,128]{1,0:T(8,128)S(1)}, f32[88,128]{1,0:T(8,128)S(1)}, u32[]{:S(2)}, u32[]{:S(2)}) collective-permute-start(f32[88,128]{1,0:T(8,128)S(1)} %get-tuple-element.30), channel_id=1, source_target_pairs={{0,12},{4,0},{8,4},{12,8},{1,13},{5,1},{9,5},{13,9},{2,14},{6,2},{... | collective-permute-start | bytes 135176 | tf_op jit(solution)/shard_map/ppermute | solution.py:583
  13.8 8.3 %copy-start.5 = (s32[1,128,2]{1,2,0:T(2,128)S(1)}, s32[1,128,2]{1,2,0:T(2,128)}, u32[]{:S(2)}) copy-start(s32[1,128,2]{1,2,0:T(2,128)} %param.18) | copy-start | bytes 3076
  19.6 10.8 %collective-permute-start.4 = (f32[32,128]{1,0:T(8,128)S(1)}, f32[32,128]{1,0:T(8,128)S(1)}, u32[]{:S(2)}, u32[]{:S(2)}) collective-permute-start(f32[32,128]{1,0:T(8,128)S(1)} %get-tuple-element.32), channel_id=1, source_target_pairs={{0,12},{4,0},{8,4},{12,8},{1,13},{5,1},{9,5},{13,9},{2,14},{6,2},{... | collective-permute-start | bytes 49160 | tf_op jit(solution)/shard_map/ppermute | solution.py:583
  21.5 8.8 %collective-permute-start.5 = (f32[32,128]{1,0:T(8,128)S(1)}, f32[32,128]{1,0:T(8,128)S(1)}, u32[]{:S(2)}, u32[]{:S(2)}) collective-permute-start(f32[32,128]{1,0:T(8,128)S(1)} %get-tuple-element.33), channel_id=1, source_target_pairs={{0,8},{4,12},{8,0},{12,4},{1,9},{5,13},{9,1},{13,5},{2,10},{6,14},... | collective-permute-start | bytes 49160 | tf_op jit(solution)/shard_map/ppermute | solution.py:583
  21.8 8.6 %collective-permute-start.6 = (f32[32,128]{1,0:T(8,128)S(1)}, f32[32,128]{1,0:T(8,128)S(1)}, u32[]{:S(2)}, u32[]{:S(2)}) collective-permute-start(f32[32,128]{1,0:T(8,128)S(1)} %get-tuple-element.34), channel_id=1, source_target_pairs={{0,4},{4,8},{8,12},{12,0},{1,5},{5,9},{9,13},{13,1},{2,6},{6,10},{... | collective-permute-start | bytes 49160 | tf_op jit(solution)/shard_map/ppermute | solution.py:583
  22.2 8.2 %copy-start.1 = (f32[16,8,32,32]{3,2,1,0:T(8,128)S(1)}, f32[16,8,32,32]{3,2,1,0:T(8,128)}, u32[]{:S(2)}) copy-start(f32[16,8,32,32]{3,2,1,0:T(8,128)} %coupling.1) | copy-start | bytes 1572868
  22.2 8.2 %copy-start.2 = (f32[128,32,32]{0,2,1:T(8,128)S(1)}, f32[128,32,32]{0,2,1:T(8,128)}, u32[]{:S(2)}) copy-start(f32[128,32,32]{0,2,1:T(8,128)} %param.20) | copy-start | bytes 1572868
  22.2 8.2 %copy-start.3 = (s32[1,4,16]{2,1,0:T(4,128)S(1)}, s32[1,4,16]{2,1,0:T(4,128)}, u32[]{:S(2)}) copy-start(s32[1,4,16]{2,1,0:T(4,128)} %param.16) | copy-start | bytes 772
  22.2 8.2 %copy-start.4 = (s32[16,8]{0,1:T(8,128)S(1)}, s32[16,8]{0,1:T(8,128)}, u32[]{:S(2)}) copy-start(s32[16,8]{0,1:T(8,128)} %param.22) | copy-start | bytes 1540
  22.2 8.2 %copy-start.6 = (s32[128]{0:T(128)S(1)}, s32[128]{0:T(128)}, u32[]{:S(2)}) copy-start(s32[128]{0:T(128)} %param.21) | copy-start | bytes 1540
  31.7 4.5 %collective-permute-start.7 = (f32[160,128]{1,0:T(8,128)S(1)}, f32[160,128]{1,0:T(8,128)S(1)}, u32[]{:S(2)}, u32[]{:S(2)}) collective-permute-start(f32[160,128]{1,0:T(8,128)S(1)} %get-tuple-element.36), channel_id=1, source_target_pairs={{0,2},{2,0},{1,3},{3,1},{4,6},{6,4},{5,7},{7,5},{8,10},{10,8},{9,1... | collective-permute-start | bytes 245768 | tf_op jit(solution)/shard_map/ppermute | solution.py:583
  32.3 4.0 %copy-start = (f32[128,128,32]{1,2,0:T(8,128)S(1)}, f32[128,128,32]{1,2,0:T(8,128)}, u32[]{:S(2)}) copy-start(f32[128,128,32]{1,2,0:T(8,128)} %param.19) | copy-start | bytes 6291460
  32.3 5.3 %copy-start.7 = (s32[128,128]{1,0:T(8,128)S(1)}, s32[128,128]{1,0:T(8,128)}, u32[]{:S(2)}) copy-start(s32[128,128]{1,0:T(8,128)} %mask.1) | copy-start | bytes 196612
  36.2 1.3 %collective-permute-start.8 = (f32[160,128]{1,0:T(8,128)S(1)}, f32[160,128]{1,0:T(8,128)S(1)}, u32[]{:S(2)}, u32[]{:S(2)}) collective-permute-start(f32[160,128]{1,0:T(8,128)S(1)} %add.6.near), channel_id=1, source_target_pairs={{0,1},{1,0},{2,3},{3,2},{4,5},{5,4},{6,7},{7,6},{8,9},{9,8},{10,11... | collective-permute-start | bytes 245768 | tf_op jit(solution)/shard_map/ppermute | solution.py:583

commit v21 on v20

--- a/solution.py
+++ b/solution.py
@@ -9,7 +9,6 @@
 
 F32 = jnp.float32
 BF16 = jnp.bfloat16
-HIGHEST = lax.Precision.HIGHEST
 ROWS = 24
 LANES = 128
 
@@ -116,7 +115,7 @@
 def products(left, right):
     a, b, c = [left[k : k + 8, :] for k in (0, 8, 16)]
     x, y, z = [right[k : k + 8, :] for k in (0, 8, 16)]
-    pairs = [(a, x), (b, x), (a, y), (c, x), (a, z), (b, y), (b, z), (c, y)]
+    pairs = [(a, x), (b, x), (a, y), (c, x), (a, z), (b, y)]
     return [jnp.concatenate(v, axis=0).astype(BF16) for v in zip(*pairs)]
 
 
@@ -139,16 +138,19 @@
     return jnp.dot(left, right, preferred_element_type=F32)
 
 
+def pieces_of(value):
+    high = value.astype(BF16)
+    rest = value - high.astype(F32)
+    mid = rest.astype(BF16)
+    return [high, mid, (rest - mid.astype(F32)).astype(BF16)]
+
+
 def select_rows(index, value, count):
     row = lax.broadcasted_iota(jnp.int32, (count, index.shape[1]), 0)
     left = jnp.where(row == index, 1.0, 0.0).astype(BF16)
-    high = value.astype(BF16)
-    rest = value - high.astype(F32)
-    mid = rest.astype(BF16)
-    low = (rest - mid.astype(F32)).astype(BF16)
     return jnp.dot(
         jnp.concatenate([left] * 3, axis=1),
-        jnp.concatenate([high, mid, low], axis=0),
+        jnp.concatenate(pieces_of(value), axis=0),
         preferred_element_type=F32,
     )
 
@@ -511,8 +513,12 @@
             part = part + coupling[p, k] * parents[pl.ds(far_list[k, p], 1), :]
         field = jnp.where(lane == p, jnp.sum(part, axis=1, keepdims=True), field)
     which = lax.broadcasted_iota(jnp.int32, (LANES, clusters), 0)
-    onehot = (parent[...] == which).astype(F32)
-    down = jnp.dot(field, onehot, precision=HIGHEST, preferred_element_type=F32)
+    onehot = jnp.where(parent[...] == which, 1.0, 0.0).astype(BF16)
+    down = jnp.dot(
+        jnp.concatenate(pieces_of(field), axis=1),
+        jnp.concatenate([onehot] * 3, axis=0),
+        preferred_element_type=F32,
+    )
     fields = jnp.concatenate(
         [jnp.sum(transfer[r] * down, axis=0, keepdims=True) for r in range(rank)], axis=0
     )
@@ -542,9 +548,12 @@
     for r in range(rank):
         lifted = lifted + transfer[r] * leaf[r : r + 1, :]
     which = lax.broadcasted_iota(jnp.int32, (count, clusters), 0)
-    onehot = (parent[...] == which).astype(F32)
+    onehot = jnp.where(parent[...] == which, 1.0, 0.0).astype(BF16)
     return lax.dot_general(
-        onehot, lifted, (((1,), (1,)), ((), ())), precision=HIGHEST, preferred_element_type=F32
+        jnp.concatenate([onehot] * 3, axis=1),
+        jnp.concatenate(pieces_of(lifted), axis=1),
+        (((1,), (1,)), ((), ())),
+        preferred_element_type=F32,
     )
 
 

time: 38.5 us -> 38.3 us (level)
  transfers between devices with their start and end apart: 9 -> 9, of which waited for: 2 -> 2; matrix products, arithmetic and copies ran while one was open for 0% -> 0% of each run, Pallas kernels for 41% -> 42%
where the time goes in v21:
time: 38.3 us; the launch traced here: 38 us
  Pallas kernels  24.1 us (63%)
  starting transfers between devices  11.6 us (30%)
  waiting for transfers between devices  1.41 us (4%)
  other arithmetic  0.65 us (2%)
    ppermute x9, starting transfers between devices, send(): return lax.ppermute(value, names if len(names) > 1 else names[0], perm)  11.6 us
    pallas_call x1, Pallas kernels, on_device(): pl.pallas_call(functools.partial(local_kernel, (S, L, R, clusters, panels...  8.01 us
    pallas_call x1, Pallas kernels, on_device(): pl.pallas_call(functools.partial(remote_kernel, (C, S, L, slots, clusters...  5.72 us
    pallas_call x2, Pallas kernels, own_tiles(): pl.pallas_call(functools.partial(self_kernel, (S, L, R, clusters, panels)...  4.5 us
    pallas_call x1, Pallas kernels, on_device(): pl.pallas_call(prepare_kernel, out_shape=[pltpu.VMEM((panels // LANES, cl...  2.46 us
    ppermute x9, waiting for transfers between devices, send(): return lax.ppermute(value, names if len(names) > 1 else names[0], perm)  1.41 us
    pallas_call x1, Pallas kernels, on_device(): pl.pallas_call(functools.partial(pack_kernel, (C, S, L, slots)), out_shap...  1.37 us
    pallas_call x1, Pallas kernels, on_device(): pl.pallas_call(functools.partial(merge_kernel, (C, S, L, slots, clusters)...  1.2 us
  transfers between devices with their start and end apart: 9, of which 2 were waited for; matrix products, arithmetic and copies ran while one was open for 0% of the time, Pallas kernels for 42%

profile of v21, /device:TPU:0, one launch (start us, length us, event | category | flops | bytes accessed | tf_op | source)
XLA Modules:
  0.0 38.0 jit_solution(2839608623993828821)
XLA Ops:
  0.0 1.4 %packs.1 = (f32[128,128]{1,0:T(8,128)S(1)}, f32[2,512,128]{2,1,0:T(8,128)S(1)}, f32[88,128]{1,0:T(8,128)S(1)}, f32[88,128]{1,0:T(8,128)S(1)}, f32[88,128]{1,0:T(8,128)S(1)}) custom-call(f32[128,128]{1,0:T(8,128)} %charges.1, s32[128,128]{1,0:T(8,128)} %mask.1, f32[128,4,256]{2,1,0:T(4,128)} %geo.1, s32[4,16]{1,0:T(4,128)} %bitcast.14, s32[4,16]{1,0:T(4,128)} %bitcast.21, ...), custom_call_target="tpu_custom_call" | custom-call | bytes 7000000 | tf_op jit(solution)/shard_map/packs/pallas_call | solution.py:621
  1.4 3.0 %collective-permute-start = (f32[128,128]{1,0:T(8,128)S(1)}, f32[128,128]{1,0:T(8,128)S(1)}, u32[]{:S(2)}, u32[]{:S(2)}) collective-permute-start(f32[128,128]{1,0:T(8,128)S(1)} %get-tuple-element.22.masked.rest_0_.rest_2_), channel_id=1, source_target_pairs={{0,2},{2,0},{1,3},{3,1},{4,6},{6,4},{5,7},{7,5},{8,10},{10,8},{9,1... | collective-permute-start | bytes 196616 | tf_op jit(solution)/shard_map/ppermute | solution.py:592
  4.4 1.6 %collective-permute-start.1 = (f32[88,128]{1,0:T(8,128)S(1)}, f32[88,128]{1,0:T(8,128)S(1)}, u32[]{:S(2)}, u32[]{:S(2)}) collective-permute-start(f32[88,128]{1,0:T(8,128)S(1)} %get-tuple-element.28), channel_id=1, source_target_pairs={{0,4},{4,8},{8,12},{12,0},{1,5},{5,9},{9,13},{13,1},{2,6},{6,10},{... | collective-permute-start | bytes 135176 | tf_op jit(solution)/shard_map/ppermute | solution.py:592
  6.0 2.6 %collective-permute-start.2 = (f32[88,128]{1,0:T(8,128)S(1)}, f32[88,128]{1,0:T(8,128)S(1)}, u32[]{:S(2)}, u32[]{:S(2)}) collective-permute-start(f32[88,128]{1,0:T(8,128)S(1)} %get-tuple-element.29), channel_id=1, source_target_pairs={{0,8},{4,12},{8,0},{12,4},{1,9},{5,13},{9,1},{13,5},{2,10},{6,14},... | collective-permute-start | bytes 135176 | tf_op jit(solution)/shard_map/ppermute | solution.py:592
  8.6 1.3 %collective-permute-start.3 = (f32[88,128]{1,0:T(8,128)S(1)}, f32[88,128]{1,0:T(8,128)S(1)}, u32[]{:S(2)}, u32[]{:S(2)}) collective-permute-start(f32[88,128]{1,0:T(8,128)S(1)} %get-tuple-element.30), channel_id=1, source_target_pairs={{0,12},{4,0},{8,4},{12,8},{1,13},{5,1},{9,5},{13,9},{2,14},{6,2},{... | collective-permute-start | bytes 135176 | tf_op jit(solution)/shard_map/ppermute | solution.py:592
  9.9 2.5 %prepare.1 = (f32[2,3072,128]{2,1,0:T(8,128)S(1)}, f32[2,3072,128]{2,1,0:T(8,128)S(1)}, f32[128,256]{1,0:T(8,128)S(1)}, f32[8,128]{1,0:T(8,128)S(1)}, f32[16,32]{1,0:T(8,128)S(1)}) custom-call(f32[2,512,128]{2,1,0:T(8,128)S(1)} %get-tuple-element.21.geo, f32[128,128]{1,0:T(8,128)S(1)} %get-tuple-element.22.masked.rest_0_.rest_2_, f32[128,32,128]{2,1,0:T(8,128)} %bitcast.10, ...), custom_call_target="tpu_custom_call" | custom-call | bytes 14000000 | tf_op jit(solution)/shard_map/prepare/pallas_call | solution.py:635
  12.4 0.0 collective-permute-done.rest_1_.rest_3_
  12.4 1.6 %near_self_early.1.before.rest_1_ = f32[128,128]{1,0:T(8,128)S(1)} custom-call(f32[2,3072,128]{2,1,0:T(8,128)S(1)} %get-tuple-element.23.fa, f32[2,3072,128]{2,1,0:T(8,128)S(1)} %get-tuple-element.24.fb, f32[128,256]{1,0:T(8,128)S(1)} %get-tuple-element.25.diags, f32[8,128]{1,0:T(8,128)S(1)} %get-tuple-element.26.scale, ...), custom_call_target="tpu_custom_call" | custom-call | bytes 7000000 | tf_op jit(solution)/shard_map/near_self_early/pallas_call | solution.py:658
  13.9 0.0 copy-start.5
  14.0 0.0 collective-permute-done.1.rest_2_
  14.0 0.0 collective-permute-done.2.rest_3_
  14.0 0.0 collective-permute-done.3.rest_4_
  14.0 5.7 %near_remote.1 = (f32[128,256]{1,0:T(8,128)S(1)}, f32[32,128]{1,0:T(8,128)S(1)}, f32[32,128]{1,0:T(8,128)S(1)}, f32[32,128]{1,0:T(8,128)S(1)}) custom-call(f32[2,3072,128]{2,1,0:T(8,128)S(1)} %get-tuple-element.24.fb, f32[8,128]{1,0:T(8,128)S(1)} %get-tuple-element.26.scale, f32[16,32]{1,0:T(8,128)S(1)} %get-tuple-element.27.up, ...), custom_call_target="tpu_custom_call" | custom-call | bytes 21000000 | tf_op jit(solution)/shard_map/near_remote/pallas_call | solution.py:678
  19.7 1.8 %collective-permute-start.4 = (f32[32,128]{1,0:T(8,128)S(1)}, f32[32,128]{1,0:T(8,128)S(1)}, u32[]{:S(2)}, u32[]{:S(2)}) collective-permute-start(f32[32,128]{1,0:T(8,128)S(1)} %get-tuple-element.32), channel_id=1, source_target_pairs={{0,12},{4,0},{8,4},{12,8},{1,13},{5,1},{9,5},{13,9},{2,14},{6,2},{... | collective-permute-start | bytes 49160 | tf_op jit(solution)/shard_map/ppermute | solution.py:592
  21.5 0.4 %collective-permute-start.5 = (f32[32,128]{1,0:T(8,128)S(1)}, f32[32,128]{1,0:T(8,128)S(1)}, u32[]{:S(2)}, u32[]{:S(2)}) collective-permute-start(f32[32,128]{1,0:T(8,128)S(1)} %get-tuple-element.33), channel_id=1, source_target_pairs={{0,8},{4,12},{8,0},{12,4},{1,9},{5,13},{9,1},{13,5},{2,10},{6,14},... | collective-permute-start | bytes 49160 | tf_op jit(solution)/shard_map/ppermute | solution.py:592
  21.9 0.3 collective-permute-start.6
  22.2 0.0 copy-done.5
  22.2 0.0 copy-start.1
  22.2 0.0 copy-start.2
  22.2 0.0 copy-start.3
  22.2 0.0 copy-start.4
  22.2 0.0 copy-start.6
  22.2 8.0 %near_local.1.near = f32[128,256]{1,0:T(8,128)S(1)} custom-call(s32[2,128]{1,0:T(2,128)S(1)} %bitcast.17, s32[2,128]{1,0:T(2,128)S(1)} %bitcast.18, f32[2,3072,128]{2,1,0:T(8,128)S(1)} %get-tuple-element.23.fa, f32[2,3072,128]{2,1,0:T(8,128)S(1)} %get-tuple-element.24.fb, f32[8,128]{1,0:T(8,128)S(1)} %get-tuple-element.26.scale, ...), custom_call_target="tpu_custom_call" | custom-call | bytes 31500000 | tf_op jit(solution)/shard_map/near_local/pallas_call | solution.py:703
  30.2 0.0 collective-permute-done.4.rest_0_
  30.2 0.0 collective-permute-done.5.rest_1_
  30.2 0.0 collective-permute-done.6.rest_2_
  30.2 0.0 copy-done.1
  30.3 0.0 copy-done.2
  30.3 0.0 copy-done.3
  30.3 0.0 copy-done.4
  30.3 0.0 copy-done.6
  30.3 1.2 %merge.1 = (f32[160,128]{1,0:T(8,128)S(1)}, f32[160,128]{1,0:T(8,128)S(1)}) custom-call(s32[8,16]{1,0:T(8,128)S(1)} %bitcast.16, s32[4,16]{1,0:T(4,128)S(1)} %bitcast.15, f32[128,256]{1,0:T(8,128)S(1)} %near_local.1.near, f32[16,8,32,32]{3,2,1,0:T(8,128)S(1)} %copy-done.1, f32[32,32,128]{2,1,0:T(8,128)S(1)} %bitcast.13, s32[1,128]{1,0:T(1,128)S(1)} %bitcast.20, ...), custom_call_target="tpu_custom_call" | custom-call | bytes 3500000 | tf_op jit(solution)/shard_map/merge/pallas_call | solution.py:721
  31.5 0.6 %collective-permute-start.7 = (f32[160,128]{1,0:T(8,128)S(1)}, f32[160,128]{1,0:T(8,128)S(1)}, u32[]{:S(2)}, u32[]{:S(2)}) collective-permute-start(f32[160,128]{1,0:T(8,128)S(1)} %get-tuple-element.36), channel_id=1, source_target_pairs={{0,2},{2,0},{1,3},{3,1},{4,6},{6,4},{5,7},{7,5},{8,10},{10,8},{9,1... | collective-permute-start | bytes 245768 | tf_op jit(solution)/shard_map/ppermute | solution.py:592
  32.1 0.0 copy-start
  32.1 0.0 copy-start.7
  32.1 2.9 %near_self.1 = f32[160,128]{1,0:T(8,128)S(1)} custom-call(f32[2,3072,128]{2,1,0:T(8,128)S(1)} %get-tuple-element.23.fa, f32[2,3072,128]{2,1,0:T(8,128)S(1)} %get-tuple-element.24.fb, f32[128,256]{1,0:T(8,128)S(1)} %get-tuple-element.25.diags, f32[8,128]{1,0:T(8,128)S(1)} %get-tuple-element.26.scale, f32[160,128]{1,0:T(8,128)S(1)} %get-tuple-element.35.rest_0_, ...), custom_call_target="tpu_custom_call" | custom-call | bytes 14000000 | tf_op jit(solution)/shard_map/near_self/pallas_call | solution.py:658
  35.1 1.0 %collective-permute-done.7 = f32[160,128]{1,0:T(8,128)S(1)} collective-permute-done((f32[160,128]{1,0:T(8,128)S(1)}, f32[160,128]{1,0:T(8,128)S(1)}, u32[]{:S(2)}, u32[]{:S(2)}) %collective-permute-start.7) | collective-permute-done | bytes 81952 | tf_op jit(solution)/shard_map/ppermute | solution.py:592
  36.0 0.1 collective-permute-start.8
  36.1 0.0 copy-done
  36.1 0.8 %far_down.1 = f32[128,128]{1,0:T(8,128)S(1)} custom-call(f32[128,32,128]{2,1,0:T(8,128)S(1)} %bitcast.11, f32[160,128]{1,0:T(8,128)S(1)} %add.6.near), custom_call_target="tpu_custom_call" | custom-call | bytes 3500000 | tf_op jit(solution)/shard_map/far_down/pallas_call | solution.py:738
  36.9 0.4 %collective-permute-done.8 = f32[160,128]{1,0:T(8,128)S(1)} collective-permute-done((f32[160,128]{1,0:T(8,128)S(1)}, f32[160,128]{1,0:T(8,128)S(1)}, u32[]{:S(2)}, u32[]{:S(2)}) %collective-permute-start.8) | collective-permute-done | bytes 81952 | tf_op jit(solution)/shard_map/ppermute | solution.py:592
  37.4 0.0 copy-done.7
  37.4 0.6 %fusion = f32[128,128]{1,0:T(8,128)} fusion(f32[128,128]{1,0:T(8,128)S(1)} %far_down.1, f32[160,128]{1,0:T(8,128)S(1)} %collective-permute-done.8, s32[128,128]{1,0:T(8,128)S(1)} %copy-done.7), kind=kLoop, calls=%fused_computation.1 | loop fusion | flops 49152 | bytes 262144 | tf_op jit(solution)/shard_map/mul | solution.py:749
  (1 shorter events, 0.0 us)
Async XLA Ops:
  1.4 11.0 %collective-permute-start = (f32[128,128]{1,0:T(8,128)S(1)}, f32[128,128]{1,0:T(8,128)S(1)}, u32[]{:S(2)}, u32[]{:S(2)}) collective-permute-start(f32[128,128]{1,0:T(8,128)S(1)} %get-tuple-element.22.masked.rest_0_.rest_2_), channel_id=1, source_target_pairs={{0,2},{2,0},{1,3},{3,1},{4,6},{6,4},{5,7},{7,5},{8,10},{10,8},{9,1... | collective-permute-start | bytes 196616 | tf_op jit(solution)/shard_map/ppermute | solution.py:592
  4.4 9.6 %collective-permute-start.1 = (f32[88,128]{1,0:T(8,128)S(1)}, f32[88,128]{1,0:T(8,128)S(1)}, u32[]{:S(2)}, u32[]{:S(2)}) collective-permute-start(f32[88,128]{1,0:T(8,128)S(1)} %get-tuple-element.28), channel_id=1, source_target_pairs={{0,4},{4,8},{8,12},{12,0},{1,5},{5,9},{9,13},{13,1},{2,6},{6,10},{... | collective-permute-start | bytes 135176 | tf_op jit(solution)/shard_map/ppermute | solution.py:592
  6.0 8.0 %collective-permute-start.2 = (f32[88,128]{1,0:T(8,128)S(1)}, f32[88,128]{1,0:T(8,128)S(1)}, u32[]{:S(2)}, u32[]{:S(2)}) collective-permute-start(f32[88,128]{1,0:T(8,128)S(1)} %get-tuple-element.29), channel_id=1, source_target_pairs={{0,8},{4,12},{8,0},{12,4},{1,9},{5,13},{9,1},{13,5},{2,10},{6,14},... | collective-permute-start | bytes 135176 | tf_op jit(solution)/shard_map/ppermute | solution.py:592
  8.6 5.4 %collective-permute-start.3 = (f32[88,128]{1,0:T(8,128)S(1)}, f32[88,128]{1,0:T(8,128)S(1)}, u32[]{:S(2)}, u32[]{:S(2)}) collective-permute-start(f32[88,128]{1,0:T(8,128)S(1)} %get-tuple-element.30), channel_id=1, source_target_pairs={{0,12},{4,0},{8,4},{12,8},{1,13},{5,1},{9,5},{13,9},{2,14},{6,2},{... | collective-permute-start | bytes 135176 | tf_op jit(solution)/shard_map/ppermute | solution.py:592
  13.9 8.2 %copy-start.5 = (s32[1,128,2]{1,2,0:T(2,128)S(1)}, s32[1,128,2]{1,2,0:T(2,128)}, u32[]{:S(2)}) copy-start(s32[1,128,2]{1,2,0:T(2,128)} %param.18) | copy-start | bytes 3076
  19.7 10.5 %collective-permute-start.4 = (f32[32,128]{1,0:T(8,128)S(1)}, f32[32,128]{1,0:T(8,128)S(1)}, u32[]{:S(2)}, u32[]{:S(2)}) collective-permute-start(f32[32,128]{1,0:T(8,128)S(1)} %get-tuple-element.32), channel_id=1, source_target_pairs={{0,12},{4,0},{8,4},{12,8},{1,13},{5,1},{9,5},{13,9},{2,14},{6,2},{... | collective-permute-start | bytes 49160 | tf_op jit(solution)/shard_map/ppermute | solution.py:592
  21.5 8.7 %collective-permute-start.5 = (f32[32,128]{1,0:T(8,128)S(1)}, f32[32,128]{1,0:T(8,128)S(1)}, u32[]{:S(2)}, u32[]{:S(2)}) collective-permute-start(f32[32,128]{1,0:T(8,128)S(1)} %get-tuple-element.33), channel_id=1, source_target_pairs={{0,8},{4,12},{8,0},{12,4},{1,9},{5,13},{9,1},{13,5},{2,10},{6,14},... | collective-permute-start | bytes 49160 | tf_op jit(solution)/shard_map/ppermute | solution.py:592
  21.9 8.3 %collective-permute-start.6 = (f32[32,128]{1,0:T(8,128)S(1)}, f32[32,128]{1,0:T(8,128)S(1)}, u32[]{:S(2)}, u32[]{:S(2)}) collective-permute-start(f32[32,128]{1,0:T(8,128)S(1)} %get-tuple-element.34), channel_id=1, source_target_pairs={{0,4},{4,8},{8,12},{12,0},{1,5},{5,9},{9,13},{13,1},{2,6},{6,10},{... | collective-permute-start | bytes 49160 | tf_op jit(solution)/shard_map/ppermute | solution.py:592
  22.2 8.1 %copy-start.1 = (f32[16,8,32,32]{3,2,1,0:T(8,128)S(1)}, f32[16,8,32,32]{3,2,1,0:T(8,128)}, u32[]{:S(2)}) copy-start(f32[16,8,32,32]{3,2,1,0:T(8,128)} %coupling.1) | copy-start | bytes 1572868
  22.2 8.1 %copy-start.2 = (f32[128,32,32]{0,2,1:T(8,128)S(1)}, f32[128,32,32]{0,2,1:T(8,128)}, u32[]{:S(2)}) copy-start(f32[128,32,32]{0,2,1:T(8,128)} %param.20) | copy-start | bytes 1572868
  22.2 8.1 %copy-start.3 = (s32[1,4,16]{2,1,0:T(4,128)S(1)}, s32[1,4,16]{2,1,0:T(4,128)}, u32[]{:S(2)}) copy-start(s32[1,4,16]{2,1,0:T(4,128)} %param.16) | copy-start | bytes 772
  22.2 8.1 %copy-start.4 = (s32[16,8]{0,1:T(8,128)S(1)}, s32[16,8]{0,1:T(8,128)}, u32[]{:S(2)}) copy-start(s32[16,8]{0,1:T(8,128)} %param.22) | copy-start | bytes 1540
  22.2 8.1 %copy-start.6 = (s32[128]{0:T(128)S(1)}, s32[128]{0:T(128)}, u32[]{:S(2)}) copy-start(s32[128]{0:T(128)} %param.21) | copy-start | bytes 1540
  31.5 4.5 %collective-permute-start.7 = (f32[160,128]{1,0:T(8,128)S(1)}, f32[160,128]{1,0:T(8,128)S(1)}, u32[]{:S(2)}, u32[]{:S(2)}) collective-permute-start(f32[160,128]{1,0:T(8,128)S(1)} %get-tuple-element.36), channel_id=1, source_target_pairs={{0,2},{2,0},{1,3},{3,1},{4,6},{6,4},{5,7},{7,5},{8,10},{10,8},{9,1... | collective-permute-start | bytes 245768 | tf_op jit(solution)/shard_map/ppermute | solution.py:592
  32.1 4.0 %copy-start = (f32[128,128,32]{1,2,0:T(8,128)S(1)}, f32[128,128,32]{1,2,0:T(8,128)}, u32[]{:S(2)}) copy-start(f32[128,128,32]{1,2,0:T(8,128)} %param.19) | copy-start | bytes 6291460
  32.1 5.3 %copy-start.7 = (s32[128,128]{1,0:T(8,128)S(1)}, s32[128,128]{1,0:T(8,128)}, u32[]{:S(2)}) copy-start(s32[128,128]{1,0:T(8,128)} %mask.1) | copy-start | bytes 196612
  36.0 1.3 %collective-permute-start.8 = (f32[160,128]{1,0:T(8,128)S(1)}, f32[160,128]{1,0:T(8,128)S(1)}, u32[]{:S(2)}, u32[]{:S(2)}) collective-permute-start(f32[160,128]{1,0:T(8,128)S(1)} %add.6.near), channel_id=1, source_target_pairs={{0,1},{1,0},{2,3},{3,2},{4,5},{5,4},{6,7},{7,6},{8,9},{9,8},{10,11... | collective-permute-start | bytes 245768 | tf_op jit(solution)/shard_map/ppermute | solution.py:592

commit v22 on v20

--- a/solution.py
+++ b/solution.py
@@ -442,15 +442,19 @@
         pl.when(sub == s)(functools.partial(place, s))
     base = clusters // R
     unit = base // 4
+    half = unit // 2
     first = rep * base
     share = base
+    ahead = unit
     if R > 1:
-        first = first - jnp.where(rep > 0, unit, 0)
-        share = share + jnp.where(rep == R - 1, unit, 0) - jnp.where(rep == 0, unit, 0)
+        first = first - jnp.where(rep > 0, unit + half, 0)
+        more = jnp.where(rep == R - 1, 1, 0) - jnp.where(rep == 0, 1, 0)
+        share = share + more * (unit + half)
+        ahead = unit + more * half
     if early:
-        share = unit
+        share = ahead
     else:
-        first, share = first + unit, share - unit
+        first, share = first + ahead, share - ahead
 
     def begin(i, dist):
         c = first + jnp.minimum(i, share - 1)
@@ -478,7 +482,7 @@
         staged(spans_of(L), root, partial)
         return c
 
-    pipeline(share, begin, finish, self_sums, body_size(unit, 16), ring, sums)
+    pipeline(share, begin, finish, self_sums, body_size(half if early else unit, 16), ring, sums)
     total = self_sums[...].T * scale[0:1, 0:1]
     if early:
         out[...] = total

time: 38.5 us -> 38.5 us (level)
  no operation moved by 1% of the time
where the time goes in v22:
time: 38.5 us; the launch traced here: 38.2 us
  Pallas kernels  23.8 us (62%)
  starting transfers between devices  12 us (31%)
  waiting for transfers between devices  1.39 us (4%)
  other arithmetic  0.65 us (2%)
    ppermute x9, starting transfers between devices, send(): return lax.ppermute(value, names if len(names) > 1 else names[0], perm)  12 us
    pallas_call x1, Pallas kernels, on_device(): pl.pallas_call(functools.partial(local_kernel, (S, L, R, clusters, panels...  8.12 us
    pallas_call x1, Pallas kernels, on_device(): pl.pallas_call(functools.partial(remote_kernel, (C, S, L, slots, clusters...  5.72 us
    pallas_call x2, Pallas kernels, own_tiles(): pl.pallas_call(functools.partial(self_kernel, (S, L, R, clusters, panels)...  4.1 us
    pallas_call x1, Pallas kernels, on_device(): pl.pallas_call(prepare_kernel, out_shape=[pltpu.VMEM((panels // LANES, cl...  2.47 us
    ppermute x9, waiting for transfers between devices, send(): return lax.ppermute(value, names if len(names) > 1 else names[0], perm)  1.39 us
    pallas_call x1, Pallas kernels, on_device(): pl.pallas_call(functools.partial(pack_kernel, (C, S, L, slots)), out_shap...  1.37 us
    pallas_call x1, Pallas kernels, on_device(): pl.pallas_call(functools.partial(merge_kernel, (C, S, L, slots, clusters)...  1.25 us
  transfers between devices with their start and end apart: 9, of which 2 were waited for; matrix products, arithmetic and copies ran while one was open for 0% of the time, Pallas kernels for 41%

profile of v22, /device:TPU:0, one launch (start us, length us, event | category | flops | bytes accessed | tf_op | source)
XLA Modules:
  0.0 38.2 jit_solution(15434310928197640733)
XLA Ops:
  0.0 1.4 %packs.1 = (f32[128,128]{1,0:T(8,128)S(1)}, f32[2,512,128]{2,1,0:T(8,128)S(1)}, f32[88,128]{1,0:T(8,128)S(1)}, f32[88,128]{1,0:T(8,128)S(1)}, f32[88,128]{1,0:T(8,128)S(1)}) custom-call(f32[128,128]{1,0:T(8,128)} %charges.1, s32[128,128]{1,0:T(8,128)} %mask.1, f32[128,4,256]{2,1,0:T(4,128)} %geo.1, s32[4,16]{1,0:T(4,128)} %bitcast.14, s32[4,16]{1,0:T(4,128)} %bitcast.21, ...), custom_call_target="tpu_custom_call" | custom-call | bytes 7000000 | tf_op jit(solution)/shard_map/packs/pallas_call | solution.py:616
  1.4 3.0 %collective-permute-start = (f32[128,128]{1,0:T(8,128)S(1)}, f32[128,128]{1,0:T(8,128)S(1)}, u32[]{:S(2)}, u32[]{:S(2)}) collective-permute-start(f32[128,128]{1,0:T(8,128)S(1)} %get-tuple-element.22.masked.rest_0_.rest_2_), channel_id=1, source_target_pairs={{0,2},{2,0},{1,3},{3,1},{4,6},{6,4},{5,7},{7,5},{8,10},{10,8},{9,1... | collective-permute-start | bytes 196616 | tf_op jit(solution)/shard_map/ppermute | solution.py:587
  4.4 1.6 %collective-permute-start.1 = (f32[88,128]{1,0:T(8,128)S(1)}, f32[88,128]{1,0:T(8,128)S(1)}, u32[]{:S(2)}, u32[]{:S(2)}) collective-permute-start(f32[88,128]{1,0:T(8,128)S(1)} %get-tuple-element.28), channel_id=1, source_target_pairs={{0,4},{4,8},{8,12},{12,0},{1,5},{5,9},{9,13},{13,1},{2,6},{6,10},{... | collective-permute-start | bytes 135176 | tf_op jit(solution)/shard_map/ppermute | solution.py:587
  6.0 2.6 %collective-permute-start.2 = (f32[88,128]{1,0:T(8,128)S(1)}, f32[88,128]{1,0:T(8,128)S(1)}, u32[]{:S(2)}, u32[]{:S(2)}) collective-permute-start(f32[88,128]{1,0:T(8,128)S(1)} %get-tuple-element.29), channel_id=1, source_target_pairs={{0,8},{4,12},{8,0},{12,4},{1,9},{5,13},{9,1},{13,5},{2,10},{6,14},... | collective-permute-start | bytes 135176 | tf_op jit(solution)/shard_map/ppermute | solution.py:587
  8.6 1.3 %collective-permute-start.3 = (f32[88,128]{1,0:T(8,128)S(1)}, f32[88,128]{1,0:T(8,128)S(1)}, u32[]{:S(2)}, u32[]{:S(2)}) collective-permute-start(f32[88,128]{1,0:T(8,128)S(1)} %get-tuple-element.30), channel_id=1, source_target_pairs={{0,12},{4,0},{8,4},{12,8},{1,13},{5,1},{9,5},{13,9},{2,14},{6,2},{... | collective-permute-start | bytes 135176 | tf_op jit(solution)/shard_map/ppermute | solution.py:587
  9.9 2.5 %prepare.1 = (f32[2,3072,128]{2,1,0:T(8,128)S(1)}, f32[2,3072,128]{2,1,0:T(8,128)S(1)}, f32[128,256]{1,0:T(8,128)S(1)}, f32[8,128]{1,0:T(8,128)S(1)}, f32[16,32]{1,0:T(8,128)S(1)}) custom-call(f32[2,512,128]{2,1,0:T(8,128)S(1)} %get-tuple-element.21.geo, f32[128,128]{1,0:T(8,128)S(1)} %get-tuple-element.22.masked.rest_0_.rest_2_, f32[128,32,128]{2,1,0:T(8,128)} %bitcast.10, ...), custom_call_target="tpu_custom_call" | custom-call | bytes 14000000 | tf_op jit(solution)/shard_map/prepare/pallas_call | solution.py:630
  12.4 0.0 collective-permute-done.rest_1_.rest_3_
  12.4 1.2 %near_self_early.1.before.rest_1_ = f32[128,128]{1,0:T(8,128)S(1)} custom-call(f32[2,3072,128]{2,1,0:T(8,128)S(1)} %get-tuple-element.23.fa, f32[2,3072,128]{2,1,0:T(8,128)S(1)} %get-tuple-element.24.fb, f32[128,256]{1,0:T(8,128)S(1)} %get-tuple-element.25.diags, f32[8,128]{1,0:T(8,128)S(1)} %get-tuple-element.26.scale, ...), custom_call_target="tpu_custom_call" | custom-call | bytes 7000000 | tf_op jit(solution)/shard_map/near_self_early/pallas_call | solution.py:653
  13.5 0.0 copy-start.5
  13.6 0.0 collective-permute-done.1.rest_2_
  13.6 0.0 collective-permute-done.2.rest_3_
  13.6 0.0 collective-permute-done.3.rest_4_
  13.6 5.7 %near_remote.1 = (f32[128,256]{1,0:T(8,128)S(1)}, f32[32,128]{1,0:T(8,128)S(1)}, f32[32,128]{1,0:T(8,128)S(1)}, f32[32,128]{1,0:T(8,128)S(1)}) custom-call(f32[2,3072,128]{2,1,0:T(8,128)S(1)} %get-tuple-element.24.fb, f32[8,128]{1,0:T(8,128)S(1)} %get-tuple-element.26.scale, f32[16,32]{1,0:T(8,128)S(1)} %get-tuple-element.27.up, ...), custom_call_target="tpu_custom_call" | custom-call | bytes 21000000 | tf_op jit(solution)/shard_map/near_remote/pallas_call | solution.py:673
  19.3 2.2 %collective-permute-start.4 = (f32[32,128]{1,0:T(8,128)S(1)}, f32[32,128]{1,0:T(8,128)S(1)}, u32[]{:S(2)}, u32[]{:S(2)}) collective-permute-start(f32[32,128]{1,0:T(8,128)S(1)} %get-tuple-element.32), channel_id=1, source_target_pairs={{0,12},{4,0},{8,4},{12,8},{1,13},{5,1},{9,5},{13,9},{2,14},{6,2},{... | collective-permute-start | bytes 49160 | tf_op jit(solution)/shard_map/ppermute | solution.py:587
  21.5 0.0 collective-permute-start.5
  21.5 0.6 %collective-permute-start.6 = (f32[32,128]{1,0:T(8,128)S(1)}, f32[32,128]{1,0:T(8,128)S(1)}, u32[]{:S(2)}, u32[]{:S(2)}) collective-permute-start(f32[32,128]{1,0:T(8,128)S(1)} %get-tuple-element.34), channel_id=1, source_target_pairs={{0,4},{4,8},{8,12},{12,0},{1,5},{5,9},{9,13},{13,1},{2,6},{6,10},{... | collective-permute-start | bytes 49160 | tf_op jit(solution)/shard_map/ppermute | solution.py:587
  22.2 0.0 copy-done.5
  22.2 0.0 copy-start.1
  22.2 0.0 copy-start.2
  22.2 0.0 copy-start.3
  22.2 0.0 copy-start.4
  22.2 0.0 copy-start.6
  22.2 8.1 %near_local.1.near = f32[128,256]{1,0:T(8,128)S(1)} custom-call(s32[2,128]{1,0:T(2,128)S(1)} %bitcast.17, s32[2,128]{1,0:T(2,128)S(1)} %bitcast.18, f32[2,3072,128]{2,1,0:T(8,128)S(1)} %get-tuple-element.23.fa, f32[2,3072,128]{2,1,0:T(8,128)S(1)} %get-tuple-element.24.fb, f32[8,128]{1,0:T(8,128)S(1)} %get-tuple-element.26.scale, ...), custom_call_target="tpu_custom_call" | custom-call | bytes 31500000 | tf_op jit(solution)/shard_map/near_local/pallas_call | solution.py:698
  30.3 0.0 collective-permute-done.4.rest_0_
  30.3 0.0 collective-permute-done.5.rest_1_
  30.3 0.0 collective-permute-done.6.rest_2_
  30.3 0.0 copy-done.1
  30.4 0.0 copy-done.2
  30.4 0.0 copy-done.3
  30.4 0.0 copy-done.4
  30.4 0.0 copy-done.6
  30.4 1.3 %merge.1 = (f32[160,128]{1,0:T(8,128)S(1)}, f32[160,128]{1,0:T(8,128)S(1)}) custom-call(s32[8,16]{1,0:T(8,128)S(1)} %bitcast.16, s32[4,16]{1,0:T(4,128)S(1)} %bitcast.15, f32[128,256]{1,0:T(8,128)S(1)} %near_local.1.near, f32[16,8,32,32]{3,2,1,0:T(8,128)S(1)} %copy-done.1, f32[32,32,128]{2,1,0:T(8,128)S(1)} %bitcast.13, s32[1,128]{1,0:T(1,128)S(1)} %bitcast.20, ...), custom_call_target="tpu_custom_call" | custom-call | bytes 3500000 | tf_op jit(solution)/shard_map/merge/pallas_call | solution.py:716
  31.7 0.6 %collective-permute-start.7 = (f32[160,128]{1,0:T(8,128)S(1)}, f32[160,128]{1,0:T(8,128)S(1)}, u32[]{:S(2)}, u32[]{:S(2)}) collective-permute-start(f32[160,128]{1,0:T(8,128)S(1)} %get-tuple-element.36), channel_id=1, source_target_pairs={{0,2},{2,0},{1,3},{3,1},{4,6},{6,4},{5,7},{7,5},{8,10},{10,8},{9,1... | collective-permute-start | bytes 245768 | tf_op jit(solution)/shard_map/ppermute | solution.py:587
  32.3 0.0 copy-start
  32.3 0.0 copy-start.7
  32.3 2.9 %near_self.1 = f32[160,128]{1,0:T(8,128)S(1)} custom-call(f32[2,3072,128]{2,1,0:T(8,128)S(1)} %get-tuple-element.23.fa, f32[2,3072,128]{2,1,0:T(8,128)S(1)} %get-tuple-element.24.fb, f32[128,256]{1,0:T(8,128)S(1)} %get-tuple-element.25.diags, f32[8,128]{1,0:T(8,128)S(1)} %get-tuple-element.26.scale, f32[160,128]{1,0:T(8,128)S(1)} %get-tuple-element.35.rest_0_, ...), custom_call_target="tpu_custom_call" | custom-call | bytes 14000000 | tf_op jit(solution)/shard_map/near_self/pallas_call | solution.py:653
  35.2 0.9 %collective-permute-done.7 = f32[160,128]{1,0:T(8,128)S(1)} collective-permute-done((f32[160,128]{1,0:T(8,128)S(1)}, f32[160,128]{1,0:T(8,128)S(1)}, u32[]{:S(2)}, u32[]{:S(2)}) %collective-permute-start.7) | collective-permute-done | bytes 81952 | tf_op jit(solution)/shard_map/ppermute | solution.py:587
  36.2 0.1 collective-permute-start.8
  36.3 0.0 copy-done
  36.3 0.8 %far_down.1 = f32[128,128]{1,0:T(8,128)S(1)} custom-call(f32[128,32,128]{2,1,0:T(8,128)S(1)} %bitcast.11, f32[160,128]{1,0:T(8,128)S(1)} %add.6.near), custom_call_target="tpu_custom_call" | custom-call | bytes 3500000 | tf_op jit(solution)/shard_map/far_down/pallas_call | solution.py:733
  37.1 0.4 %collective-permute-done.8 = f32[160,128]{1,0:T(8,128)S(1)} collective-permute-done((f32[160,128]{1,0:T(8,128)S(1)}, f32[160,128]{1,0:T(8,128)S(1)}, u32[]{:S(2)}, u32[]{:S(2)}) %collective-permute-start.8) | collective-permute-done | bytes 81952 | tf_op jit(solution)/shard_map/ppermute | solution.py:587
  37.5 0.0 copy-done.7
  37.5 0.6 %fusion = f32[128,128]{1,0:T(8,128)} fusion(f32[128,128]{1,0:T(8,128)S(1)} %far_down.1, f32[160,128]{1,0:T(8,128)S(1)} %collective-permute-done.8, s32[128,128]{1,0:T(8,128)S(1)} %copy-done.7), kind=kLoop, calls=%fused_computation.1 | loop fusion | flops 49152 | bytes 262144 | tf_op jit(solution)/shard_map/mul | solution.py:744
  (1 shorter events, 0.0 us)
Async XLA Ops:
  1.4 11.0 %collective-permute-start = (f32[128,128]{1,0:T(8,128)S(1)}, f32[128,128]{1,0:T(8,128)S(1)}, u32[]{:S(2)}, u32[]{:S(2)}) collective-permute-start(f32[128,128]{1,0:T(8,128)S(1)} %get-tuple-element.22.masked.rest_0_.rest_2_), channel_id=1, source_target_pairs={{0,2},{2,0},{1,3},{3,1},{4,6},{6,4},{5,7},{7,5},{8,10},{10,8},{9,1... | collective-permute-start | bytes 196616 | tf_op jit(solution)/shard_map/ppermute | solution.py:587
  4.4 9.2 %collective-permute-start.1 = (f32[88,128]{1,0:T(8,128)S(1)}, f32[88,128]{1,0:T(8,128)S(1)}, u32[]{:S(2)}, u32[]{:S(2)}) collective-permute-start(f32[88,128]{1,0:T(8,128)S(1)} %get-tuple-element.28), channel_id=1, source_target_pairs={{0,4},{4,8},{8,12},{12,0},{1,5},{5,9},{9,13},{13,1},{2,6},{6,10},{... | collective-permute-start | bytes 135176 | tf_op jit(solution)/shard_map/ppermute | solution.py:587
  6.0 7.6 %collective-permute-start.2 = (f32[88,128]{1,0:T(8,128)S(1)}, f32[88,128]{1,0:T(8,128)S(1)}, u32[]{:S(2)}, u32[]{:S(2)}) collective-permute-start(f32[88,128]{1,0:T(8,128)S(1)} %get-tuple-element.29), channel_id=1, source_target_pairs={{0,8},{4,12},{8,0},{12,4},{1,9},{5,13},{9,1},{13,5},{2,10},{6,14},... | collective-permute-start | bytes 135176 | tf_op jit(solution)/shard_map/ppermute | solution.py:587
  8.6 5.0 %collective-permute-start.3 = (f32[88,128]{1,0:T(8,128)S(1)}, f32[88,128]{1,0:T(8,128)S(1)}, u32[]{:S(2)}, u32[]{:S(2)}) collective-permute-start(f32[88,128]{1,0:T(8,128)S(1)} %get-tuple-element.30), channel_id=1, source_target_pairs={{0,12},{4,0},{8,4},{12,8},{1,13},{5,1},{9,5},{13,9},{2,14},{6,2},{... | collective-permute-start | bytes 135176 | tf_op jit(solution)/shard_map/ppermute | solution.py:587
  13.5 8.6 %copy-start.5 = (s32[1,128,2]{1,2,0:T(2,128)S(1)}, s32[1,128,2]{1,2,0:T(2,128)}, u32[]{:S(2)}) copy-start(s32[1,128,2]{1,2,0:T(2,128)} %param.18) | copy-start | bytes 3076
  19.3 11.0 %collective-permute-start.4 = (f32[32,128]{1,0:T(8,128)S(1)}, f32[32,128]{1,0:T(8,128)S(1)}, u32[]{:S(2)}, u32[]{:S(2)}) collective-permute-start(f32[32,128]{1,0:T(8,128)S(1)} %get-tuple-element.32), channel_id=1, source_target_pairs={{0,12},{4,0},{8,4},{12,8},{1,13},{5,1},{9,5},{13,9},{2,14},{6,2},{... | collective-permute-start | bytes 49160 | tf_op jit(solution)/shard_map/ppermute | solution.py:587
  21.5 8.8 %collective-permute-start.5 = (f32[32,128]{1,0:T(8,128)S(1)}, f32[32,128]{1,0:T(8,128)S(1)}, u32[]{:S(2)}, u32[]{:S(2)}) collective-permute-start(f32[32,128]{1,0:T(8,128)S(1)} %get-tuple-element.33), channel_id=1, source_target_pairs={{0,8},{4,12},{8,0},{12,4},{1,9},{5,13},{9,1},{13,5},{2,10},{6,14},... | collective-permute-start | bytes 49160 | tf_op jit(solution)/shard_map/ppermute | solution.py:587
  21.5 8.8 %collective-permute-start.6 = (f32[32,128]{1,0:T(8,128)S(1)}, f32[32,128]{1,0:T(8,128)S(1)}, u32[]{:S(2)}, u32[]{:S(2)}) collective-permute-start(f32[32,128]{1,0:T(8,128)S(1)} %get-tuple-element.34), channel_id=1, source_target_pairs={{0,4},{4,8},{8,12},{12,0},{1,5},{5,9},{9,13},{13,1},{2,6},{6,10},{... | collective-permute-start | bytes 49160 | tf_op jit(solution)/shard_map/ppermute | solution.py:587
  22.2 8.2 %copy-start.1 = (f32[16,8,32,32]{3,2,1,0:T(8,128)S(1)}, f32[16,8,32,32]{3,2,1,0:T(8,128)}, u32[]{:S(2)}) copy-start(f32[16,8,32,32]{3,2,1,0:T(8,128)} %coupling.1) | copy-start | bytes 1572868
  22.2 8.2 %copy-start.2 = (f32[128,32,32]{0,2,1:T(8,128)S(1)}, f32[128,32,32]{0,2,1:T(8,128)}, u32[]{:S(2)}) copy-start(f32[128,32,32]{0,2,1:T(8,128)} %param.20) | copy-start | bytes 1572868
  22.2 8.2 %copy-start.3 = (s32[1,4,16]{2,1,0:T(4,128)S(1)}, s32[1,4,16]{2,1,0:T(4,128)}, u32[]{:S(2)}) copy-start(s32[1,4,16]{2,1,0:T(4,128)} %param.16) | copy-start | bytes 772
  22.2 8.2 %copy-start.4 = (s32[16,8]{0,1:T(8,128)S(1)}, s32[16,8]{0,1:T(8,128)}, u32[]{:S(2)}) copy-start(s32[16,8]{0,1:T(8,128)} %param.22) | copy-start | bytes 1540
  22.2 8.2 %copy-start.6 = (s32[128]{0:T(128)S(1)}, s32[128]{0:T(128)}, u32[]{:S(2)}) copy-start(s32[128]{0:T(128)} %param.21) | copy-start | bytes 1540
  31.7 4.5 %collective-permute-start.7 = (f32[160,128]{1,0:T(8,128)S(1)}, f32[160,128]{1,0:T(8,128)S(1)}, u32[]{:S(2)}, u32[]{:S(2)}) collective-permute-start(f32[160,128]{1,0:T(8,128)S(1)} %get-tuple-element.36), channel_id=1, source_target_pairs={{0,2},{2,0},{1,3},{3,1},{4,6},{6,4},{5,7},{7,5},{8,10},{10,8},{9,1... | collective-permute-start | bytes 245768 | tf_op jit(solution)/shard_map/ppermute | solution.py:587
  32.3 4.0 %copy-start = (f32[128,128,32]{1,2,0:T(8,128)S(1)}, f32[128,128,32]{1,2,0:T(8,128)}, u32[]{:S(2)}) copy-start(f32[128,128,32]{1,2,0:T(8,128)} %param.19) | copy-start | bytes 6291460
  32.3 5.2 %copy-start.7 = (s32[128,128]{1,0:T(8,128)S(1)}, s32[128,128]{1,0:T(8,128)}, u32[]{:S(2)}) copy-start(s32[128,128]{1,0:T(8,128)} %mask.1) | copy-start | bytes 196612
  36.2 1.3 %collective-permute-start.8 = (f32[160,128]{1,0:T(8,128)S(1)}, f32[160,128]{1,0:T(8,128)S(1)}, u32[]{:S(2)}, u32[]{:S(2)}) collective-permute-start(f32[160,128]{1,0:T(8,128)S(1)} %add.6.near), channel_id=1, source_target_pairs={{0,1},{1,0},{2,3},{3,2},{4,5},{5,4},{6,7},{7,6},{8,9},{9,8},{10,11... | collective-permute-start | bytes 245768 | tf_op jit(solution)/shard_map/ppermute | solution.py:587

commit v23 on v20

--- a/solution.py
+++ b/solution.py
@@ -339,7 +339,7 @@
         acc[pl.ds(source, 1), :] += jnp.where(ok, back, 0.0)
         return jnp.where(ok, slot, -1)
 
-    pipeline(found, begin, finish, fwdt, 8, work[:4], work[4:])
+    pipeline(found, begin, finish, fwdt, 16, work[:4], work[4:])
     acc_out[...] = acc[...] * inv
     fwd = (fwdt[...] * inv).T
     rank = up.shape[1]

time: 38.5 us -> 37.7 us (0.979)
  Pallas kernels: 24.1 us -> 23.3 us
    pallas_call x1, Pallas kernels: 5.71 us -> 4.88 us  [on_device(): pl.pallas_call(functools.partial(remote_kernel, (C, S, L, slots, clusters...]
  transfers between devices with their start and end apart: 9 -> 9, of which waited for: 2 -> 2; matrix products, arithmetic and copies ran while one was open for 0% -> 0% of each run, Pallas kernels for 41% -> 42%
where the time goes in v23:
time: 37.7 us; the launch traced here: 37.3 us
  Pallas kernels  23.3 us (62%)
  starting transfers between devices  11.8 us (31%)
  waiting for transfers between devices  1.4 us (4%)
  other arithmetic  0.65 us (2%)
    ppermute x9, starting transfers between devices, send(): return lax.ppermute(value, names if len(names) > 1 else names[0], perm)  11.8 us
    pallas_call x1, Pallas kernels, on_device(): pl.pallas_call(functools.partial(local_kernel, (S, L, R, clusters, panels...  8.12 us
    pallas_call x1, Pallas kernels, on_device(): pl.pallas_call(functools.partial(remote_kernel, (C, S, L, slots, clusters...  4.88 us
    pallas_call x2, Pallas kernels, own_tiles(): pl.pallas_call(functools.partial(self_kernel, (S, L, R, clusters, panels)...  4.37 us
    pallas_call x1, Pallas kernels, on_device(): pl.pallas_call(prepare_kernel, out_shape=[pltpu.VMEM((panels // LANES, cl...  2.47 us
    ppermute x9, waiting for transfers between devices, send(): return lax.ppermute(value, names if len(names) > 1 else names[0], perm)  1.4 us
    pallas_call x1, Pallas kernels, on_device(): pl.pallas_call(functools.partial(pack_kernel, (C, S, L, slots)), out_shap...  1.37 us
    pallas_call x1, Pallas kernels, on_device(): pl.pallas_call(functools.partial(merge_kernel, (C, S, L, slots, clusters)...  1.25 us
  transfers between devices with their start and end apart: 9, of which 2 were waited for; matrix products, arithmetic and copies ran while one was open for 0% of the time, Pallas kernels for 42%

profile of v23, /device:TPU:0, one launch (start us, length us, event | category | flops | bytes accessed | tf_op | source)
XLA Modules:
  0.0 37.3 jit_solution(2595276257870385788)
XLA Ops:
  0.0 1.4 %packs.1 = (f32[128,128]{1,0:T(8,128)S(1)}, f32[2,512,128]{2,1,0:T(8,128)S(1)}, f32[88,128]{1,0:T(8,128)S(1)}, f32[88,128]{1,0:T(8,128)S(1)}, f32[88,128]{1,0:T(8,128)S(1)}) custom-call(f32[128,128]{1,0:T(8,128)} %charges.1, s32[128,128]{1,0:T(8,128)} %mask.1, f32[128,4,256]{2,1,0:T(4,128)} %geo.1, s32[4,16]{1,0:T(4,128)} %bitcast.14, s32[4,16]{1,0:T(4,128)} %bitcast.21, ...), custom_call_target="tpu_custom_call" | custom-call | bytes 7000000 | tf_op jit(solution)/shard_map/packs/pallas_call | solution.py:612
  1.4 3.0 %collective-permute-start = (f32[128,128]{1,0:T(8,128)S(1)}, f32[128,128]{1,0:T(8,128)S(1)}, u32[]{:S(2)}, u32[]{:S(2)}) collective-permute-start(f32[128,128]{1,0:T(8,128)S(1)} %get-tuple-element.22.masked.rest_0_.rest_2_), channel_id=1, source_target_pairs={{0,2},{2,0},{1,3},{3,1},{4,6},{6,4},{5,7},{7,5},{8,10},{10,8},{9,1... | collective-permute-start | bytes 196616 | tf_op jit(solution)/shard_map/ppermute | solution.py:583
  4.4 1.6 %collective-permute-start.1 = (f32[88,128]{1,0:T(8,128)S(1)}, f32[88,128]{1,0:T(8,128)S(1)}, u32[]{:S(2)}, u32[]{:S(2)}) collective-permute-start(f32[88,128]{1,0:T(8,128)S(1)} %get-tuple-element.28), channel_id=1, source_target_pairs={{0,4},{4,8},{8,12},{12,0},{1,5},{5,9},{9,13},{13,1},{2,6},{6,10},{... | collective-permute-start | bytes 135176 | tf_op jit(solution)/shard_map/ppermute | solution.py:583
  6.0 2.6 %collective-permute-start.2 = (f32[88,128]{1,0:T(8,128)S(1)}, f32[88,128]{1,0:T(8,128)S(1)}, u32[]{:S(2)}, u32[]{:S(2)}) collective-permute-start(f32[88,128]{1,0:T(8,128)S(1)} %get-tuple-element.29), channel_id=1, source_target_pairs={{0,8},{4,12},{8,0},{12,4},{1,9},{5,13},{9,1},{13,5},{2,10},{6,14},... | collective-permute-start | bytes 135176 | tf_op jit(solution)/shard_map/ppermute | solution.py:583
  8.6 1.3 %collective-permute-start.3 = (f32[88,128]{1,0:T(8,128)S(1)}, f32[88,128]{1,0:T(8,128)S(1)}, u32[]{:S(2)}, u32[]{:S(2)}) collective-permute-start(f32[88,128]{1,0:T(8,128)S(1)} %get-tuple-element.30), channel_id=1, source_target_pairs={{0,12},{4,0},{8,4},{12,8},{1,13},{5,1},{9,5},{13,9},{2,14},{6,2},{... | collective-permute-start | bytes 135176 | tf_op jit(solution)/shard_map/ppermute | solution.py:583
  9.9 2.5 %prepare.1 = (f32[2,3072,128]{2,1,0:T(8,128)S(1)}, f32[2,3072,128]{2,1,0:T(8,128)S(1)}, f32[128,256]{1,0:T(8,128)S(1)}, f32[8,128]{1,0:T(8,128)S(1)}, f32[16,32]{1,0:T(8,128)S(1)}) custom-call(f32[2,512,128]{2,1,0:T(8,128)S(1)} %get-tuple-element.21.geo, f32[128,128]{1,0:T(8,128)S(1)} %get-tuple-element.22.masked.rest_0_.rest_2_, f32[128,32,128]{2,1,0:T(8,128)} %bitcast.10, ...), custom_call_target="tpu_custom_call" | custom-call | bytes 14000000 | tf_op jit(solution)/shard_map/prepare/pallas_call | solution.py:626
  12.4 0.0 collective-permute-done.rest_1_.rest_3_
  12.4 1.4 %near_self_early.1.before.rest_1_ = f32[128,128]{1,0:T(8,128)S(1)} custom-call(f32[2,3072,128]{2,1,0:T(8,128)S(1)} %get-tuple-element.23.fa, f32[2,3072,128]{2,1,0:T(8,128)S(1)} %get-tuple-element.24.fb, f32[128,256]{1,0:T(8,128)S(1)} %get-tuple-element.25.diags, f32[8,128]{1,0:T(8,128)S(1)} %get-tuple-element.26.scale, ...), custom_call_target="tpu_custom_call" | custom-call | bytes 7000000 | tf_op jit(solution)/shard_map/near_self_early/pallas_call | solution.py:649
  13.8 0.0 copy-start.5
  13.8 0.0 collective-permute-done.1.rest_2_
  13.8 0.0 collective-permute-done.2.rest_3_
  13.9 0.0 collective-permute-done.3.rest_4_
  13.9 4.9 %near_remote.1 = (f32[128,256]{1,0:T(8,128)S(1)}, f32[32,128]{1,0:T(8,128)S(1)}, f32[32,128]{1,0:T(8,128)S(1)}, f32[32,128]{1,0:T(8,128)S(1)}) custom-call(f32[2,3072,128]{2,1,0:T(8,128)S(1)} %get-tuple-element.24.fb, f32[8,128]{1,0:T(8,128)S(1)} %get-tuple-element.26.scale, f32[16,32]{1,0:T(8,128)S(1)} %get-tuple-element.27.up, ...), custom_call_target="tpu_custom_call" | custom-call | bytes 21000000 | tf_op jit(solution)/shard_map/near_remote/pallas_call | solution.py:669
  18.8 1.9 %collective-permute-start.4 = (f32[32,128]{1,0:T(8,128)S(1)}, f32[32,128]{1,0:T(8,128)S(1)}, u32[]{:S(2)}, u32[]{:S(2)}) collective-permute-start(f32[32,128]{1,0:T(8,128)S(1)} %get-tuple-element.32), channel_id=1, source_target_pairs={{0,12},{4,0},{8,4},{12,8},{1,13},{5,1},{9,5},{13,9},{2,14},{6,2},{... | collective-permute-start | bytes 49160 | tf_op jit(solution)/shard_map/ppermute | solution.py:583
  20.7 0.3 collective-permute-start.5
  20.9 0.4 %collective-permute-start.6 = (f32[32,128]{1,0:T(8,128)S(1)}, f32[32,128]{1,0:T(8,128)S(1)}, u32[]{:S(2)}, u32[]{:S(2)}) collective-permute-start(f32[32,128]{1,0:T(8,128)S(1)} %get-tuple-element.34), channel_id=1, source_target_pairs={{0,4},{4,8},{8,12},{12,0},{1,5},{5,9},{9,13},{13,1},{2,6},{6,10},{... | collective-permute-start | bytes 49160 | tf_op jit(solution)/shard_map/ppermute | solution.py:583
  21.3 0.0 copy-done.5
  21.3 0.0 copy-start.1
  21.3 0.0 copy-start.2
  21.3 0.0 copy-start.3
  21.3 0.0 copy-start.4
  21.3 0.0 copy-start.6
  21.4 8.1 %near_local.1.near = f32[128,256]{1,0:T(8,128)S(1)} custom-call(s32[2,128]{1,0:T(2,128)S(1)} %bitcast.17, s32[2,128]{1,0:T(2,128)S(1)} %bitcast.18, f32[2,3072,128]{2,1,0:T(8,128)S(1)} %get-tuple-element.23.fa, f32[2,3072,128]{2,1,0:T(8,128)S(1)} %get-tuple-element.24.fb, f32[8,128]{1,0:T(8,128)S(1)} %get-tuple-element.26.scale, ...), custom_call_target="tpu_custom_call" | custom-call | bytes 31500000 | tf_op jit(solution)/shard_map/near_local/pallas_call | solution.py:694
  29.5 0.0 collective-permute-done.4.rest_0_
  29.5 0.0 collective-permute-done.5.rest_1_
  29.5 0.0 collective-permute-done.6.rest_2_
  29.5 0.0 copy-done.1
  29.5 0.0 copy-done.2
  29.5 0.0 copy-done.3
  29.5 0.0 copy-done.4
  29.6 0.0 copy-done.6
  29.6 1.3 %merge.1 = (f32[160,128]{1,0:T(8,128)S(1)}, f32[160,128]{1,0:T(8,128)S(1)}) custom-call(s32[8,16]{1,0:T(8,128)S(1)} %bitcast.16, s32[4,16]{1,0:T(4,128)S(1)} %bitcast.15, f32[128,256]{1,0:T(8,128)S(1)} %near_local.1.near, f32[16,8,32,32]{3,2,1,0:T(8,128)S(1)} %copy-done.1, f32[32,32,128]{2,1,0:T(8,128)S(1)} %bitcast.13, s32[1,128]{1,0:T(1,128)S(1)} %bitcast.20, ...), custom_call_target="tpu_custom_call" | custom-call | bytes 3500000 | tf_op jit(solution)/shard_map/merge/pallas_call | solution.py:712
  30.8 0.6 %collective-permute-start.7 = (f32[160,128]{1,0:T(8,128)S(1)}, f32[160,128]{1,0:T(8,128)S(1)}, u32[]{:S(2)}, u32[]{:S(2)}) collective-permute-start(f32[160,128]{1,0:T(8,128)S(1)} %get-tuple-element.36), channel_id=1, source_target_pairs={{0,2},{2,0},{1,3},{3,1},{4,6},{6,4},{5,7},{7,5},{8,10},{10,8},{9,1... | collective-permute-start | bytes 245768 | tf_op jit(solution)/shard_map/ppermute | solution.py:583
  31.4 0.0 copy-start
  31.4 0.0 copy-start.7
  31.4 2.9 %near_self.1 = f32[160,128]{1,0:T(8,128)S(1)} custom-call(f32[2,3072,128]{2,1,0:T(8,128)S(1)} %get-tuple-element.23.fa, f32[2,3072,128]{2,1,0:T(8,128)S(1)} %get-tuple-element.24.fb, f32[128,256]{1,0:T(8,128)S(1)} %get-tuple-element.25.diags, f32[8,128]{1,0:T(8,128)S(1)} %get-tuple-element.26.scale, f32[160,128]{1,0:T(8,128)S(1)} %get-tuple-element.35.rest_0_, ...), custom_call_target="tpu_custom_call" | custom-call | bytes 14000000 | tf_op jit(solution)/shard_map/near_self/pallas_call | solution.py:649
  34.4 1.0 %collective-permute-done.7 = f32[160,128]{1,0:T(8,128)S(1)} collective-permute-done((f32[160,128]{1,0:T(8,128)S(1)}, f32[160,128]{1,0:T(8,128)S(1)}, u32[]{:S(2)}, u32[]{:S(2)}) %collective-permute-start.7) | collective-permute-done | bytes 81952 | tf_op jit(solution)/shard_map/ppermute | solution.py:583
  35.4 0.1 collective-permute-start.8
  35.4 0.0 copy-done
  35.4 0.8 %far_down.1 = f32[128,128]{1,0:T(8,128)S(1)} custom-call(f32[128,32,128]{2,1,0:T(8,128)S(1)} %bitcast.11, f32[160,128]{1,0:T(8,128)S(1)} %add.6.near), custom_call_target="tpu_custom_call" | custom-call | bytes 3500000 | tf_op jit(solution)/shard_map/far_down/pallas_call | solution.py:729
  36.3 0.4 %collective-permute-done.8 = f32[160,128]{1,0:T(8,128)S(1)} collective-permute-done((f32[160,128]{1,0:T(8,128)S(1)}, f32[160,128]{1,0:T(8,128)S(1)}, u32[]{:S(2)}, u32[]{:S(2)}) %collective-permute-start.8) | collective-permute-done | bytes 81952 | tf_op jit(solution)/shard_map/ppermute | solution.py:583
  36.7 0.0 copy-done.7
  36.7 0.6 %fusion = f32[128,128]{1,0:T(8,128)} fusion(f32[128,128]{1,0:T(8,128)S(1)} %far_down.1, f32[160,128]{1,0:T(8,128)S(1)} %collective-permute-done.8, s32[128,128]{1,0:T(8,128)S(1)} %copy-done.7), kind=kLoop, calls=%fused_computation.1 | loop fusion | flops 49152 | bytes 262144 | tf_op jit(solution)/shard_map/mul | solution.py:740
  (1 shorter events, 0.0 us)
Async XLA Ops:
  1.4 11.0 %collective-permute-start = (f32[128,128]{1,0:T(8,128)S(1)}, f32[128,128]{1,0:T(8,128)S(1)}, u32[]{:S(2)}, u32[]{:S(2)}) collective-permute-start(f32[128,128]{1,0:T(8,128)S(1)} %get-tuple-element.22.masked.rest_0_.rest_2_), channel_id=1, source_target_pairs={{0,2},{2,0},{1,3},{3,1},{4,6},{6,4},{5,7},{7,5},{8,10},{10,8},{9,1... | collective-permute-start | bytes 196616 | tf_op jit(solution)/shard_map/ppermute | solution.py:583
  4.4 9.4 %collective-permute-start.1 = (f32[88,128]{1,0:T(8,128)S(1)}, f32[88,128]{1,0:T(8,128)S(1)}, u32[]{:S(2)}, u32[]{:S(2)}) collective-permute-start(f32[88,128]{1,0:T(8,128)S(1)} %get-tuple-element.28), channel_id=1, source_target_pairs={{0,4},{4,8},{8,12},{12,0},{1,5},{5,9},{9,13},{13,1},{2,6},{6,10},{... | collective-permute-start | bytes 135176 | tf_op jit(solution)/shard_map/ppermute | solution.py:583
  6.0 7.9 %collective-permute-start.2 = (f32[88,128]{1,0:T(8,128)S(1)}, f32[88,128]{1,0:T(8,128)S(1)}, u32[]{:S(2)}, u32[]{:S(2)}) collective-permute-start(f32[88,128]{1,0:T(8,128)S(1)} %get-tuple-element.29), channel_id=1, source_target_pairs={{0,8},{4,12},{8,0},{12,4},{1,9},{5,13},{9,1},{13,5},{2,10},{6,14},... | collective-permute-start | bytes 135176 | tf_op jit(solution)/shard_map/ppermute | solution.py:583
  8.6 5.3 %collective-permute-start.3 = (f32[88,128]{1,0:T(8,128)S(1)}, f32[88,128]{1,0:T(8,128)S(1)}, u32[]{:S(2)}, u32[]{:S(2)}) collective-permute-start(f32[88,128]{1,0:T(8,128)S(1)} %get-tuple-element.30), channel_id=1, source_target_pairs={{0,12},{4,0},{8,4},{12,8},{1,13},{5,1},{9,5},{13,9},{2,14},{6,2},{... | collective-permute-start | bytes 135176 | tf_op jit(solution)/shard_map/ppermute | solution.py:583
  13.8 7.5 %copy-start.5 = (s32[1,128,2]{1,2,0:T(2,128)S(1)}, s32[1,128,2]{1,2,0:T(2,128)}, u32[]{:S(2)}) copy-start(s32[1,128,2]{1,2,0:T(2,128)} %param.18) | copy-start | bytes 3076
  18.8 10.7 %collective-permute-start.4 = (f32[32,128]{1,0:T(8,128)S(1)}, f32[32,128]{1,0:T(8,128)S(1)}, u32[]{:S(2)}, u32[]{:S(2)}) collective-permute-start(f32[32,128]{1,0:T(8,128)S(1)} %get-tuple-element.32), channel_id=1, source_target_pairs={{0,12},{4,0},{8,4},{12,8},{1,13},{5,1},{9,5},{13,9},{2,14},{6,2},{... | collective-permute-start | bytes 49160 | tf_op jit(solution)/shard_map/ppermute | solution.py:583
  20.7 8.8 %collective-permute-start.5 = (f32[32,128]{1,0:T(8,128)S(1)}, f32[32,128]{1,0:T(8,128)S(1)}, u32[]{:S(2)}, u32[]{:S(2)}) collective-permute-start(f32[32,128]{1,0:T(8,128)S(1)} %get-tuple-element.33), channel_id=1, source_target_pairs={{0,8},{4,12},{8,0},{12,4},{1,9},{5,13},{9,1},{13,5},{2,10},{6,14},... | collective-permute-start | bytes 49160 | tf_op jit(solution)/shard_map/ppermute | solution.py:583
  20.9 8.6 %collective-permute-start.6 = (f32[32,128]{1,0:T(8,128)S(1)}, f32[32,128]{1,0:T(8,128)S(1)}, u32[]{:S(2)}, u32[]{:S(2)}) collective-permute-start(f32[32,128]{1,0:T(8,128)S(1)} %get-tuple-element.34), channel_id=1, source_target_pairs={{0,4},{4,8},{8,12},{12,0},{1,5},{5,9},{9,13},{13,1},{2,6},{6,10},{... | collective-permute-start | bytes 49160 | tf_op jit(solution)/shard_map/ppermute | solution.py:583
  21.3 8.2 %copy-start.1 = (f32[16,8,32,32]{3,2,1,0:T(8,128)S(1)}, f32[16,8,32,32]{3,2,1,0:T(8,128)}, u32[]{:S(2)}) copy-start(f32[16,8,32,32]{3,2,1,0:T(8,128)} %coupling.1) | copy-start | bytes 1572868
  21.3 8.2 %copy-start.2 = (f32[128,32,32]{0,2,1:T(8,128)S(1)}, f32[128,32,32]{0,2,1:T(8,128)}, u32[]{:S(2)}) copy-start(f32[128,32,32]{0,2,1:T(8,128)} %param.20) | copy-start | bytes 1572868
  21.3 8.2 %copy-start.3 = (s32[1,4,16]{2,1,0:T(4,128)S(1)}, s32[1,4,16]{2,1,0:T(4,128)}, u32[]{:S(2)}) copy-start(s32[1,4,16]{2,1,0:T(4,128)} %param.16) | copy-start | bytes 772
  21.3 8.2 %copy-start.4 = (s32[16,8]{0,1:T(8,128)S(1)}, s32[16,8]{0,1:T(8,128)}, u32[]{:S(2)}) copy-start(s32[16,8]{0,1:T(8,128)} %param.22) | copy-start | bytes 1540
  21.3 8.2 %copy-start.6 = (s32[128]{0:T(128)S(1)}, s32[128]{0:T(128)}, u32[]{:S(2)}) copy-start(s32[128]{0:T(128)} %param.21) | copy-start | bytes 1540
  30.8 4.5 %collective-permute-start.7 = (f32[160,128]{1,0:T(8,128)S(1)}, f32[160,128]{1,0:T(8,128)S(1)}, u32[]{:S(2)}, u32[]{:S(2)}) collective-permute-start(f32[160,128]{1,0:T(8,128)S(1)} %get-tuple-element.36), channel_id=1, source_target_pairs={{0,2},{2,0},{1,3},{3,1},{4,6},{6,4},{5,7},{7,5},{8,10},{10,8},{9,1... | collective-permute-start | bytes 245768 | tf_op jit(solution)/shard_map/ppermute | solution.py:583
  31.4 4.0 %copy-start = (f32[128,128,32]{1,2,0:T(8,128)S(1)}, f32[128,128,32]{1,2,0:T(8,128)}, u32[]{:S(2)}) copy-start(f32[128,128,32]{1,2,0:T(8,128)} %param.19) | copy-start | bytes 6291460
  31.4 5.3 %copy-start.7 = (s32[128,128]{1,0:T(8,128)S(1)}, s32[128,128]{1,0:T(8,128)}, u32[]{:S(2)}) copy-start(s32[128,128]{1,0:T(8,128)} %mask.1) | copy-start | bytes 196612
  35.4 1.3 %collective-permute-start.8 = (f32[160,128]{1,0:T(8,128)S(1)}, f32[160,128]{1,0:T(8,128)S(1)}, u32[]{:S(2)}, u32[]{:S(2)}) collective-permute-start(f32[160,128]{1,0:T(8,128)S(1)} %add.6.near), channel_id=1, source_target_pairs={{0,1},{1,0},{2,3},{3,2},{4,5},{5,4},{6,7},{7,6},{8,9},{9,8},{10,11... | collective-permute-start | bytes 245768 | tf_op jit(solution)/shard_map/ppermute | solution.py:583
